TPU v7x, 32 devices: a whole 2x2x4 slice. The times are simulated.
32 devices in a mesh: seq: 8 (over y, x, core), exp: 4 (over z).
Axes of the slice: x: 2, y: 2, z: 4, core: 2. Of those that a mesh axis runs over, the one named last changes fastest.
Arguments:
- tokens: bfloat16 [48, 4, 1024], P('exp'), may hold values from -48 to 48
- attn_gain: float32 [1024], replicated, may hold values from 0.1 to 1.9
- w_qkv: bfloat16 [3072, 1024], P('seq'), may hold values from -0.1875 to 0.1875
- window_cache: bfloat16 [2, 48, 4096, 1024], P(None, 'exp', 'seq'), may hold values from -180 to 180
- sink_cache: bfloat16 [2, 48, 4, 1024], P(None, 'exp'), may hold values from -6 to 6
- lengths: int32 [48], P('exp'), may hold values from 8 to 16384, as said below
- w_out: bfloat16 [1024, 1024], P('seq'), may hold values from -0.1875 to 0.1875
- moe_gain: float32 [1024], replicated, may hold values from 0.1 to 1.9
- router: bfloat16 [1024, 16], replicated, may hold values from -0.1875 to 0.1875
- expert_ids: int32 [48, 4, 2], P('exp'), may hold values from 0 to 15, all different within a row
- slot_order: int32 [4, 48], P('exp'), may hold values from 0 to 47, each once within a row
- expert_in: bfloat16 [2, 4, 11264, 1024], P(None, 'exp', 'seq'), may hold values from -0.1875 to 0.1875
- expert_down: bfloat16 [4, 11264, 1024], P('exp', 'seq'), may hold values from -0.109375 to 0.109375
Outputs:
- output: bfloat16 [48, 4, 1024], P('exp')
Inputs may be any that keep to these rules, and one draw needn't show every extreme that they name: `lengths`: at least one request holds 16384 tokens. `expert_ids`: the 2 experts of a token differ, and every expert is named by some token. `slot_order`: each group's row holds every number of 0 to 47 once.
All inputs are finite; a program needn't handle non-finite values.
Results may differ from a plain program's by a relative error of at most 0.0083.
The roundings to bfloat16 on the way count: a program that leaves them out, or rounds other values in their place, can miss the bound.
Values may be sent and summed in bfloat16 or wider, within the bound.
No kernel may reach another device: no remote copies, remote signals or barrier semaphores. Data moves between devices by JAX's collectives and lax.ppermute only.
A program may use at most 128 MiB of HBM per device.

v0:
```python
import jax
import jax.numpy as jnp
from jax import lax
from jax.sharding import PartitionSpec as P

HEADS = 16
HD = 64
EXPERTS = 16
TOPK = 2
SINKS = 4
WIN = 4096
CAP = 8


EPSILON = 1e-06
MASKED = -1e30


def rms_scale(values, gain_row):
    widened = values.astype(jnp.float32)
    inverse = lax.rsqrt(jnp.mean(widened * widened, axis=-1, keepdims=True) + EPSILON)
    return (widened * inverse * gain_row).astype(jnp.bfloat16)


def by_heads(values, factor):
    shaped = values.reshape(factor.shape + (values.shape[-1] // factor.shape[-1],))
    return (shaped * factor[..., None]).reshape(values.shape)


def expert_tail(gate_up, down_rows, own_expert, local_experts):
    hidden = (jax.nn.gelu(gate_up[0], approximate=True) * gate_up[1]).astype(jnp.bfloat16)
    outputs = jnp.einsum("nkf,fd->nkd", hidden, down_rows, preferred_element_type=jnp.float32)
    placing = (jnp.arange(local_experts, dtype=jnp.int32) == own_expert).astype(jnp.float32)
    return outputs[:, None, :, :] * placing[None, :, None, None]


def body(
    tokens,
    attn_gain,
    w_qkv,
    window_cache,
    sink_cache,
    lengths,
    w_out,
    moe_gain,
    router,
    expert_ids,
    slot_order,
    expert_in,
    expert_down,
):
    requests, step_count, model_width = tokens.shape
    row_count = requests * step_count
    seq_index = lax.axis_index("seq")
    seq_count = lax.axis_size("seq")
    group_count = lax.axis_size("exp")
    local_experts = EXPERTS // group_count
    own_expert = seq_index // (seq_count // local_experts)
    in_rows = expert_in[:, 0]
    down_rows = expert_down[0]
    contract = (((1,), (1,)), ((), ()))
    flat_rows = tokens.reshape(row_count, model_width)
    normed_attn = rms_scale(flat_rows, attn_gain)
    local_mix = lax.dot_general(
        normed_attn, w_qkv, contract, preferred_element_type=jnp.float32
    ).astype(jnp.bfloat16)
    mixed_rows = lax.all_gather(local_mix, "seq", axis=1, tiled=True).reshape(
        requests, step_count, 3, HEADS, HD
    )
    queries = mixed_rows[:, :, 0]
    new_keys = mixed_rows[:, :, 1]
    new_values = mixed_rows[:, :, 2]
    score_scale = HD ** (-0.5)
    slot_span = window_cache.shape[2]
    slot_ids = seq_index * slot_span + jnp.arange(slot_span, dtype=jnp.int32)
    cache_keys = window_cache[0].reshape(requests, slot_span, HEADS, HD)
    cache_values = window_cache[1].reshape(requests, slot_span, HEADS, HD)
    window_scores = (
        jnp.einsum("rshe,rwhe->rshw", queries, cache_keys, preferred_element_type=jnp.float32)
        * score_scale
    )
    filled = jnp.minimum(WIN, lengths - SINKS)
    step_ids = jnp.arange(step_count, dtype=jnp.int32)
    written = (lengths[:, None] + step_ids[None, :] - SINKS) % WIN
    overwritten = (
        jnp.cumsum((slot_ids[None, None, :] == written[:, :, None]).astype(jnp.int32), axis=1) > 0
    )
    window_live = (
        (slot_ids[None, None, :] < filled[:, None, None]) & jnp.logical_not(overwritten)
    )[:, :, None, :]
    sink_keys = sink_cache[0].reshape(requests, SINKS, HEADS, HD)
    sink_values = sink_cache[1].reshape(requests, SINKS, HEADS, HD)
    local_keys = jnp.concatenate([sink_keys, new_keys], axis=1)
    local_values = jnp.concatenate([sink_values, new_values], axis=1)
    local_scores = (
        jnp.einsum("rshe,rkhe->rshk", queries, local_keys, preferred_element_type=jnp.float32)
        * score_scale
    )
    causal = jnp.concatenate(
        [jnp.ones((step_count, SINKS), jnp.bool_), step_ids[None, :] <= step_ids[:, None]], axis=1
    )
    local_live = causal[None, :, None, :] & (seq_index == 0)
    peak_score = jnp.maximum(
        jnp.max(jnp.where(window_live, window_scores, MASKED), axis=-1),
        jnp.max(jnp.where(local_live, local_scores, MASKED), axis=-1),
    )
    window_exp = jnp.where(window_live, jnp.exp(window_scores - peak_score[..., None]), 0.0)
    local_exp = jnp.where(local_live, jnp.exp(local_scores - peak_score[..., None]), 0.0)
    weight_sum = jnp.sum(window_exp, axis=-1) + jnp.sum(local_exp, axis=-1)
    weighted = jnp.einsum(
        "rshw,rwhe->rshe",
        window_exp.astype(jnp.bfloat16),
        cache_values,
        preferred_element_type=jnp.float32,
    )
    weighted = weighted + jnp.einsum(
        "rshk,rkhe->rshe",
        local_exp.astype(jnp.bfloat16),
        local_values,
        preferred_element_type=jnp.float32,
    )
    weighted = weighted.reshape(requests, step_count, model_width)
    overall = lax.pmax(peak_score, "seq")
    factor = jnp.exp(peak_score - overall)
    weight_sum, weighted = (
        lax.psum((weight_sum * factor).astype(jnp.bfloat16), "seq").astype(jnp.float32),
        lax.psum(by_heads(weighted, factor).astype(jnp.bfloat16), "seq").astype(jnp.float32),
    )
    attended = by_heads(weighted, 1.0 / weight_sum).astype(jnp.bfloat16)
    local_proj = lax.dot_general(
        attended.reshape(row_count, model_width),
        w_out,
        contract,
        preferred_element_type=jnp.float32,
    ).astype(jnp.bfloat16)
    projected = lax.all_gather(local_proj, "seq", axis=1, tiled=True)
    residual = flat_rows.astype(jnp.float32) + projected.astype(jnp.float32)
    normed_moe = rms_scale(residual, moe_gain)
    logits = jnp.dot(normed_moe, router, preferred_element_type=jnp.float32)
    chosen = expert_ids.reshape(row_count, TOPK)
    onehot = (chosen[:, :, None] == jnp.arange(EXPERTS, dtype=jnp.int32)).astype(jnp.float32)
    gate_values = jax.nn.sigmoid(jnp.sum(onehot * logits[:, None, :], axis=-1))
    priority = slot_order[0]
    earlier = (priority[None, :] < priority[:, None]).astype(jnp.float32)
    counts = jnp.dot(earlier, jnp.sum(onehot, axis=1), precision=lax.Precision.HIGHEST)
    position = jnp.sum(onehot * counts[:, None, :], axis=-1).astype(jnp.int32)
    column = chosen * CAP + position
    select = (
        (column[:, :, None] == jnp.arange(EXPERTS * CAP, dtype=jnp.int32))
        & (position < CAP)[:, :, None]
    ).astype(jnp.bfloat16)
    dispatch = jnp.sum(select, axis=1)
    buffer = lax.dot_general(
        dispatch, normed_moe, (((0,), (0,)), ((), ())), preferred_element_type=jnp.float32
    ).astype(jnp.bfloat16)
    buffer = buffer.reshape(group_count, local_experts, CAP, model_width)
    own_rows = lax.dynamic_index_in_dim(
        lax.all_to_all(buffer, "exp", split_axis=0, concat_axis=0, tiled=True),
        own_expert,
        1,
        keepdims=False,
    )
    gate_up = jnp.einsum("nkd,pfd->pnkf", own_rows, in_rows, preferred_element_type=jnp.float32)
    expert_part = expert_tail(gate_up, down_rows, own_expert, local_experts)
    summed = lax.psum(expert_part.astype(jnp.bfloat16), "seq")
    returned = lax.all_to_all(summed, "exp", split_axis=0, concat_axis=0, tiled=True).reshape(
        EXPERTS * CAP, model_width
    )
    picked = jnp.einsum("rkc,cd->rkd", select, returned, preferred_element_type=jnp.float32)
    final_rows = (residual + jnp.sum(gate_values[:, :, None] * picked, axis=1)).astype(jnp.bfloat16)
    result = final_rows.reshape(requests, step_count, model_width)
    return result


def solution(mesh):
    in_specs = (
        P("exp", None, None),
        P(),
        P("seq", None),
        P(None, "exp", "seq", None),
        P(None, "exp", None, None),
        P("exp"),
        P("seq", None),
        P(),
        P(),
        P("exp", None, None),
        P("exp", None),
        P(None, "exp", "seq", None),
        P("exp", "seq", None),
    )
    out_specs = P("exp", None, None)
    return jax.shard_map(body, mesh=mesh, in_specs=in_specs, out_specs=out_specs, check_vma=False)
```

profile of v0, /device:TPU:0, one launch (start us, length us, event | category | flops | bytes accessed | tf_op | source)
XLA Modules:
  0.0 299.7 jit_solution(16767786420879056118)
XLA Ops:
  6.5 0.9 add_select_fusion
  7.4 0.7 add_minimum_fusion
  8.1 0.9 reshape.165
  9.0 1.0 multiply_reduce_fusion.1
  10.1 0.8 reduce_window_sum.11
  11.0 17.4 %fusion.71 = (bf16[1,12,512,1024]{3,2,1,0:T(8,128)(2,1)}, bf16[1,12,512,1024]{3,2,1,0:T(8,128)(2,1)}) fusion(bf16[2,12,512,1024]{3,2,1,0:T(8,128)(2,1)} %param.16), kind=kLoop, calls=%fused_computation.113 | loop fusion | bytes 50331648 | tf_op jit(solution)/shard_map/slice | solution.py:77
  28.4 16.7 %copy.60 = bf16[1,12,512,1024]{2,3,1,0:T(8,128)(2,1)} copy(bf16[1,12,512,1024]{3,2,1,0:T(8,128)(2,1)} %get-tuple-element.10) | data formatting | bytes 25165824 | tf_op jit(solution)/shard_map/slice | solution.py:76
  45.2 1.5 convolution_convert_fusion.1
  46.7 11.0 %all_gather.6 = bf16[48,3072]{1,0:T(8,128)(2,1)S(1)} all-gather(bf16[48,384]{1,0:T(8,128)(2,1)S(1)} %convolution_convert_fusion.1), channel_id=1, replica_groups=mesh['seq'=8,'exp'=4] {'seq'}, dimensions={1}, use_global_device_ids=true | all-gather | bytes 331776 | tf_op jit(solution)/shard_map/all_gather | solution.py:67
  57.7 1.2 reshape.160
  58.9 1.9 fusion.72
  60.8 0.9 not_and_fusion
  61.8 8.2 %fusion.7 = (f32[12,4,16]{1,2,0:T(8,128)}, f32[12,16,4,512]{3,2,1,0:T(4,128)}) fusion(pred[12,4,512]{2,1,0:T(4,128)(4,1)S(1)} %not_and_fusion, bf16[12,512,16,64]{1,3,2,0:T(8,128)(2,1)} %bitcast.85, bf16[12,4,1,16,64]{4,3,2,1,0:T(8,128)(2,1)S(1)} %get-tuple-element.13), kind=kOutput, calls=%fused_computation.7 | convolution fusion | flops 51510528 | bytes 14281728 | tf_op jit(solution)/shard_map/rshe,rwhe->rshw/dot_general | solution.py:79
  70.0 1.0 copy.63
  71.0 1.7 copy.89
  72.7 1.7 fusion.73
  74.4 1.8 reshape_squeeze.13
  76.2 1.0 copy.62
  77.3 2.8 select_reduce_fusion
  80.0 1.0 copy.64
  81.2 23.6 %pmax.7 = f32[12,4,16]{2,1,0:T(4,128)S(1)} all-reduce(f32[12,4,16]{2,1,0:T(4,128)S(1)} %max.9), channel_id=1, replica_groups=mesh['seq'=8,'exp'=4] {'seq'}, use_global_device_ids=true, to_apply=%region_4.5 | all-reduce | flops 768 | bytes 6144 | tf_op jit(solution)/shard_map/pmax | solution.py:123
  104.8 2.4 fusion.15
  107.3 0.7 copy.72
  108.0 1.5 fusion.27
  109.5 0.7 copy.73
  110.3 0.8 copy.88
  111.0 1.1 reshape_squeeze.15
  112.1 0.7 copy.68
  112.9 16.7 %copy.66 = bf16[1,12,512,1024]{2,3,1,0:T(8,128)(2,1)} copy(bf16[1,12,512,1024]{3,2,1,0:T(8,128)(2,1)} %get-tuple-element.9) | data formatting | bytes 25165824 | tf_op jit(solution)/shard_map/slice | solution.py:77
  130.2 0.8 copy.70
  131.0 1.6 convolution_bitcast_fusion.1
  132.7 8.5 %fusion.13 = bf16[12,4,16,64]{3,1,2,0:T(4,128)(2,1)S(1)} fusion(f32[12,4,16,64]{3,1,2,0:T(4,128)S(1)} %convolution_bitcast_fusion.1, bf16[12,512,16,64]{1,3,2,0:T(8,128)(2,1)} %bitcast.86, f32[12,16,4,512]{3,2,1,0:T(4,128)} %get-tuple-element.17, f32[12,4,16]{1,2,0:T(8,128)S(1)} %copy.65, pred[12,4,512]{2,1,0:T(4,128)(4,1)S(1)} %not_and_fusion, ...), kind=kOutput, calls=%fused_computation.19 | convolution fusion | flops 51658752 | bytes 14481408 | tf_op jit(solution)/shard_map/rshw,rwhe->rshe/dot_general | solution.py:110
  141.2 0.8 convert_element_type.106
  142.1 22.3 %psum.22 = bf16[12,4,16]{2,1,0:T(4,128)(2,1)S(1)} all-reduce(bf16[12,4,16]{2,1,0:T(4,128)(2,1)S(1)} %copy-done.4), channel_id=1, replica_groups=mesh['seq'=8,'exp'=4] {'seq'}, use_global_device_ids=true, to_apply=%region_8.9 | all-reduce | flops 768 | bytes 3072 | tf_op jit(solution)/shard_map/psum | solution.py:126
  165.0 0.9 mul.171
  165.9 28.1 %all-reduce.4.cloned.1.call-done = bf16[12,4,1024]{2,1,0:T(4,128)(2,1)} async-done(((bf16[12,4,1024]{2,1,0:T(4,128)(2,1)}), bf16[12,4,1024]{2,1,0:T(4,128)(2,1)}) %all-reduce.4.cloned.1.call-update) | async-done | bytes 98320 | tf_op jit(solution)/shard_map/psum | solution.py:127
  194.0 1.0 multiply_convert_fusion.2
  195.1 1.1 convolution_convert_fusion.2
  196.2 9.7 %all_gather.7 = bf16[48,1024]{1,0:T(8,128)(2,1)S(1)} all-gather(bf16[48,128]{1,0:T(8,128)(2,1)S(1)} %convolution_convert_fusion.2), channel_id=1, replica_groups=mesh['seq'=8,'exp'=4] {'seq'}, dimensions={1}, use_global_device_ids=true | all-gather | bytes 110592 | tf_op jit(solution)/shard_map/all_gather | solution.py:136
  206.5 0.9 convolution_convert_fusion
  207.4 4.6 %all-to-all-start = ((bf16[4,4,8,1024]{3,2,1,0:T(8,128)(2,1)}), bf16[4,4,8,1024]{3,2,1,0:T(8,128)(2,1)S(1)}, u32[]{:S(2)}, u32[]{:S(2)}) async-start(bf16[4,4,8,1024]{3,2,1,0:T(8,128)(2,1)} %bitcast.10), calls=%async_computation | async-start | bytes 524288 | tf_op jit(solution)/shard_map/all_to_all | solution.py:158
  212.1 9.4 %all-to-all-done = bf16[4,4,8,1024]{3,2,1,0:T(8,128)(2,1)S(1)} async-done(((bf16[4,4,8,1024]{3,2,1,0:T(8,128)(2,1)}), bf16[4,4,8,1024]{3,2,1,0:T(8,128)(2,1)S(1)}, u32[]{:S(2)}, u32[]{:S(2)}) %all-to-all-start) | async-done | bytes 262176 | tf_op jit(solution)/shard_map/all_to_all | solution.py:158
  221.4 4.4 %fusion.4 = f32[2,4,8,1408]{3,2,0,1:T(8,128)S(1)} fusion(bf16[2,1,1408,1024]{3,2,1,0:T(8,128)(2,1)} %param.24, bf16[4,4,8,1024]{3,2,1,0:T(8,128)(2,1)S(1)} %all-to-all-done, s32[]{:T(128)S(6)} %select_n.39), kind=kOutput, calls=%fused_computation.4 | convolution fusion | flops 184549376 | bytes 6193156 | tf_op jit(solution)/shard_map/nkd,pfd->pnkf/dot_general | solution.py:163
  226.4 0.8 multiply_convert_fusion
  227.2 51.8 %all-reduce.6.cloned.1.call-done = bf16[4,4,8,1024]{3,2,1,0:T(8,128)(2,1)} async-done(((bf16[4,4,8,1024]{3,2,1,0:T(8,128)(2,1)}), bf16[4,4,8,1024]{3,2,1,0:T(8,128)(2,1)}) %all-reduce.6.cloned.1.call-update) | async-done | bytes 262160 | tf_op jit(solution)/shard_map/psum | solution.py:165
  279.1 4.6 %all-to-all-start.1 = ((bf16[4,4,8,1024]{3,2,1,0:T(8,128)(2,1)}), bf16[4,4,8,1024]{3,2,1,0:T(8,128)(2,1)S(1)}, u32[]{:S(2)}, u32[]{:S(2)}) async-start(bf16[4,4,8,1024]{3,2,1,0:T(8,128)(2,1)} %all-reduce.6.cloned.1.call-done), calls=%async_computation.1 | async-start | bytes 524288 | tf_op jit(solution)/shard_map/all_to_all | solution.py:166
  283.7 8.2 %all-to-all-done.1 = bf16[4,4,8,1024]{3,2,1,0:T(8,128)(2,1)S(1)} async-done(((bf16[4,4,8,1024]{3,2,1,0:T(8,128)(2,1)}), bf16[4,4,8,1024]{3,2,1,0:T(8,128)(2,1)S(1)}, u32[]{:S(2)}, u32[]{:S(2)}) %all-to-all-start.1) | async-done | bytes 262176 | tf_op jit(solution)/shard_map/all_to_all | solution.py:166
  292.1 0.7 reshape.164
  (55 shorter events, 3.2 us)
Async XLA Ops:
  6.5 219.3 %copy-start = (bf16[1,1408,1024]{2,1,0:T(8,128)(2,1)S(1)}, bf16[1,1408,1024]{2,1,0:T(8,128)(2,1)}, u32[]{:S(2)}) copy-start(bf16[1,1408,1024]{2,1,0:T(8,128)(2,1)} %param.25) | copy-start | bytes 8650756
  6.5 187.5 %all-reduce.4.cloned.1.call-start = ((), (), s32[]{:S(2)}) async-start(), calls=%async_computation.2 | async-start | bytes 196608 | tf_op jit(solution)/shard_map/psum | solution.py:127
  28.4 16.8 %copy-start.6 = (f32[1024]{0:T(1024)S(1)}, f32[1024]{0:T(1024)}, u32[]{:S(2)}) copy-start(f32[1024]{0:T(1024)} %param.14) | copy-start | bytes 12292
  112.9 16.7 %copy-start.2 = (f32[12,4,16]{2,1,0:T(4,128)S(1)}, f32[12,4,16]{2,1,0:T(4,128)}, u32[]{:S(2)}) copy-start(f32[12,4,16]{2,1,0:T(4,128)} %copy.72) | copy-start | bytes 9220
  112.9 16.7 %copy-start.3 = (f32[12,4,16]{2,1,0:T(4,128)S(1)}, f32[12,4,16]{2,1,0:T(4,128)}, u32[]{:S(2)}) copy-start(f32[12,4,16]{2,1,0:T(4,128)} %copy.73) | copy-start | bytes 9220
  112.9 18.1 %copy-start.1 = (bf16[12,4,1,16,64]{4,1,3,0,2:T(4,128)(2,1)S(1)}, bf16[12,4,1,16,64]{4,1,3,0,2:T(4,128)(2,1)}, u32[]{:S(2)}) copy-start(bf16[12,4,1,16,64]{4,1,3,0,2:T(4,128)(2,1)} %copy.88) | copy-start | bytes 294916
  132.6 9.4 %copy-start.4 = (bf16[12,4,16]{2,1,0:T(4,128)(2,1)S(1)}, bf16[12,4,16]{2,1,0:T(4,128)(2,1)}, u32[]{:S(2)}) copy-start(bf16[12,4,16]{2,1,0:T(4,128)(2,1)} %get-tuple-element.7) | copy-start | bytes 4612
  132.6 31.8 %copy-start.8 = (s32[12,4,2]{0,2,1:T(2,128)S(1)}, s32[12,4,2]{0,2,1:T(2,128)}, u32[]{:S(2)}) copy-start(s32[12,4,2]{0,2,1:T(2,128)} %param.22) | copy-start | bytes 1156
  132.6 32.0 %copy-start.9 = (s32[1,48]{1,0:T(1,128)S(1)}, s32[1,48]{1,0:T(1,128)}, u32[]{:S(2)}) copy-start(s32[1,48]{1,0:T(1,128)} %param.23) | copy-start | bytes 580
  141.1 65.0 %copy-start.7 = (f32[1024]{0:T(1024)S(1)}, f32[1024]{0:T(1024)}, u32[]{:S(2)}) copy-start(f32[1024]{0:T(1024)} %param.20) | copy-start | bytes 12292
  141.2 65.0 %copy-start.5 = (bf16[1024,16]{0,1:T(8,128)(2,1)S(1)}, bf16[1024,16]{0,1:T(8,128)(2,1)}, u32[]{:S(2)}) copy-start(bf16[1024,16]{0,1:T(8,128)(2,1)} %param.21) | copy-start | bytes 98308
  207.4 14.0 %all-to-all-start = ((bf16[4,4,8,1024]{3,2,1,0:T(8,128)(2,1)}), bf16[4,4,8,1024]{3,2,1,0:T(8,128)(2,1)S(1)}, u32[]{:S(2)}, u32[]{:S(2)}) async-start(bf16[4,4,8,1024]{3,2,1,0:T(8,128)(2,1)} %bitcast.10), calls=%async_computation | async-start | bytes 524288 | tf_op jit(solution)/shard_map/all_to_all | solution.py:158
  212.0 67.0 %all-reduce.6.cloned.1.call-start = ((), (), s32[]{:S(2)}) async-start(), calls=%async_computation.3 | async-start | bytes 524288 | tf_op jit(solution)/shard_map/psum | solution.py:165
  279.1 12.8 %all-to-all-start.1 = ((bf16[4,4,8,1024]{3,2,1,0:T(8,128)(2,1)}), bf16[4,4,8,1024]{3,2,1,0:T(8,128)(2,1)S(1)}, u32[]{:S(2)}, u32[]{:S(2)}) async-start(bf16[4,4,8,1024]{3,2,1,0:T(8,128)(2,1)} %all-reduce.6.cloned.1.call-done), calls=%async_computation.1 | async-start | bytes 524288 | tf_op jit(solution)/shard_map/all_to_all | solution.py:166
Sparse Core Ops, SparseCore 0:
  142.2 51.7 all-reduce.3
  227.4 51.6 all-reduce.5
where the time goes:
time: 301 us; the launch traced here: 300 us
  waiting for transfers between devices  97.5 us (32%)
  local copies, waits for them, and re-layouts  71 us (24%)
  blocking collectives  66.6 us (22%)
  matrix products  30.2 us (10%)
  between operations  13.7 us (5%)
  other arithmetic  11.4 us (4%)
  starting transfers between devices  9.2 us (3%)
    psum x1, waiting for transfers between devices, body(): summed = lax.psum(expert_part.astype(jnp.bfloat16), 'seq')  51.8 us
    slice x2, local copies, waits for them, and re-layouts, body(): cache_values = window_cache[1].reshape(requests, slot_span, HEADS, HD)  34.1 us
    psum x1, waiting for transfers between devices, body(): lax.psum(by_heads(weighted, factor).astype(jnp.bfloat16), 'seq')  28.1 us
    pmax x1, blocking collectives, body(): overall = lax.pmax(peak_score, 'seq')  23.6 us
    psum x1, blocking collectives, body(): lax.psum((weight_sum * factor).astype(jnp.bfloat16), 'seq')  22.3 us
    slice x1, local copies, waits for them, and re-layouts, body(): cache_keys = window_cache[0].reshape(requests, slot_span, HEADS, HD)  16.7 us
    all_gather x1, blocking collectives, body(): lax.all_gather(local_mix, 'seq', axis=1, tiled=True)  11 us
    all_gather x1, blocking collectives, body(): projected = lax.all_gather(local_proj, 'seq', axis=1, tiled=True)  9.72 us
  transfers between devices with their start and end apart: 4, of which 4 were waited for; matrix products, arithmetic and copies ran while one was open for 0% of the time, Pallas kernels for 0%

commit v1 on v0

v1 whole, which is shorter than its diff:
```python
import functools

import jax
import jax.numpy as jnp
from jax import lax
from jax.experimental import pallas as pl
from jax.experimental.pallas import tpu as pltpu
from jax.sharding import PartitionSpec as P

HEADS = 16
HD = 64
EXPERTS = 16
TOPK = 2
SINKS = 4
WIN = 4096
CAP = 8
LANES = 128
PIECES = 3

EPSILON = 1e-06
MASKED = -1e30
MIB = 1 << 20
ROWS_BY_ROWS = (((1,), (1,)), ((), ()))
ROWS_BY_COLS = (((1,), (0,)), ((), ()))


def dot(a, b, dims=ROWS_BY_COLS):
    return lax.dot_general(a, b, dims, preferred_element_type=jnp.float32)


def params(limit_mib=32):
    return pltpu.CompilerParams(vmem_limit_bytes=limit_mib * MIB)


def split(value, count):
    parts = []
    for _ in range(count):
        part = value.astype(jnp.bfloat16)
        parts.append(part)
        value = value - part.astype(jnp.float32)
    return parts


def rms_rows(widened, gain_row):
    inverse = lax.rsqrt(jnp.mean(widened * widened, axis=-1, keepdims=True) + EPSILON)
    return (widened * inverse * gain_row).astype(jnp.bfloat16)


def qkv_kernel(tokens_ref, gain_ref, weight_ref, out_ref, rows_ref):
    requests, steps, _ = tokens_ref.shape
    for r in range(requests):
        rows_ref[r * steps : (r + 1) * steps, :] = tokens_ref[r].astype(jnp.float32)
    normed = rms_rows(rows_ref[...], gain_ref[...])
    out_ref[...] = dot(normed, weight_ref[...], ROWS_BY_ROWS).astype(jnp.bfloat16)


def attention_kernel(
    lengths_ref,
    place_ref,
    mixed_ref,
    keys_ref,
    values_ref,
    sinks_ref,
    out_ref,
    flat_ref,
    query_ref,
    extra_ref,
    part_ref,
):
    request = pl.program_id(0)
    requests = pl.num_programs(0)
    devices, rows, share = mixed_ref.shape
    steps = query_ref.shape[1]
    width = keys_ref.shape[-1]
    span = keys_ref.shape[2]
    groups = steps * HEADS

    @pl.when(request == 0)
    def _():
        for d in range(devices):
            flat_ref[:, d * share : (d + 1) * share] = mixed_ref[d].astype(jnp.float32)
        for r in range(query_ref.shape[0]):
            own = slice(r * steps, (r + 1) * steps)
            query_ref[r] = flat_ref[own, 0:width]
            for p in range(2):
                extra_ref[p, r, 0:SINKS] = sinks_ref[p, r].astype(jnp.float32)
                extra_ref[p, r, SINKS : SINKS + steps] = flat_ref[
                    own, (p + 1) * width : (p + 2) * width
                ]

    length = lengths_ref[request]
    base = place_ref[0] * span
    head_of_row = lax.broadcasted_iota(jnp.int32, (HEADS, width), 0)
    head_of_col = lax.broadcasted_iota(jnp.int32, (HEADS, width), 1) // HD
    own_head = (head_of_row == head_of_col).astype(jnp.float32)
    queries = query_ref[request]
    spread = jnp.concatenate([queries[t : t + 1] * own_head for t in range(steps)], axis=0).astype(
        jnp.bfloat16
    )
    scale = HD ** (-0.5)
    scores = dot(spread, keys_ref[0, 0], ROWS_BY_ROWS) * scale
    extra_keys = extra_ref[0, request].astype(jnp.bfloat16)
    extra_scores = dot(spread, extra_keys, ROWS_BY_ROWS) * scale

    slot = base + lax.broadcasted_iota(jnp.int32, (groups, span), 1)
    step = lax.broadcasted_iota(jnp.int32, (groups, span), 0) // HEADS
    age = jnp.bitwise_and(slot - (length - SINKS), WIN - 1)
    live = (slot < jnp.minimum(WIN, length - SINKS)) & (age > step)
    count = SINKS + steps
    extra_at = lax.broadcasted_iota(jnp.int32, (groups, count), 1)
    extra_step = lax.broadcasted_iota(jnp.int32, (groups, count), 0) // HEADS
    extra_live = (extra_at - SINKS <= extra_step) & (place_ref[0] == 0)

    scores = jnp.where(live, scores, MASKED)
    extra_scores = jnp.where(extra_live, extra_scores, MASKED)
    peak = jnp.maximum(
        jnp.max(scores, axis=-1, keepdims=True), jnp.max(extra_scores, axis=-1, keepdims=True)
    )
    weight = jnp.where(live, jnp.exp(scores - peak), 0.0)
    extra_weight = jnp.where(extra_live, jnp.exp(extra_scores - peak), 0.0)
    total = jnp.sum(weight, axis=-1, keepdims=True) + jnp.sum(extra_weight, axis=-1, keepdims=True)
    mixed = dot(weight.astype(jnp.bfloat16), values_ref[0, 0])
    mixed = mixed + dot(
        extra_weight.astype(jnp.bfloat16), extra_ref[1, request].astype(jnp.bfloat16)
    )
    lane = lax.broadcasted_iota(jnp.int32, (HEADS, LANES), 1)
    row_head = lax.broadcasted_iota(jnp.int32, (HEADS, LANES), 0)
    rows_out = []
    for t in range(steps):
        own = slice(t * HEADS, (t + 1) * HEADS)
        rows_out.append(jnp.sum(mixed[own] * own_head, axis=0, keepdims=True))
        stats = jnp.zeros((HEADS, LANES), jnp.float32)
        parts = split(peak[own], PIECES) + split(total[own], PIECES)
        for i, part in enumerate(parts):
            stats = jnp.where(lane == row_head + i * HEADS, part.astype(jnp.float32), stats)
        rows_out.append(jnp.sum(stats, axis=0, keepdims=True))
    part_ref[request] = jnp.concatenate(
        [
            jnp.concatenate(rows_out[0::2], axis=0),
            jnp.concatenate(rows_out[1::2], axis=0),
        ],
        axis=1,
    )

    @pl.when(request == requests - 1)
    def _():
        for r in range(part_ref.shape[0]):
            flat_ref[r * steps : (r + 1) * steps, 0 : width + LANES] = part_ref[r]
        out_ref[...] = flat_ref[:, 0 : width + LANES].astype(jnp.bfloat16)


def combine(parts_ref):
    devices, rows, padded = parts_ref.shape
    width = padded - LANES
    stats = [parts_ref[d][:, width:].astype(jnp.float32) for d in range(devices)]

    def joined(stat, first):
        return sum(
            stat[:, (first + i) * HEADS : (first + i + 1) * HEADS] for i in range(PIECES)
        )

    peaks = [joined(stat, 0) for stat in stats]
    totals = [joined(stat, PIECES) for stat in stats]
    overall = functools.reduce(jnp.maximum, peaks)
    factors = [jnp.exp(peak - overall) for peak in peaks]
    total = sum(f * t for f, t in zip(factors, totals))
    inverse = 1.0 / total
    head_of_row = lax.broadcasted_iota(jnp.int32, (HEADS, width), 0)
    head_of_col = lax.broadcasted_iota(jnp.int32, (HEADS, width), 1) // HD
    expand = (head_of_row == head_of_col).astype(jnp.bfloat16)
    attended = jnp.zeros((rows, width), jnp.float32)
    for d in range(devices):
        share = sum(dot(part, expand) for part in split(factors[d] * inverse, 2))
        attended = attended + share * parts_ref[d][:, :width].astype(jnp.float32)
    return attended.astype(jnp.bfloat16)


def project_kernel(parts_ref, weight_ref, out_ref):
    attended = combine(parts_ref)
    out_ref[...] = dot(attended, weight_ref[...], ROWS_BY_ROWS).astype(jnp.bfloat16)


def routing_kernel(ids_ref, order_ref, select_ref, turned_ref, chosen_ref, rows_ref):
    requests, steps, _ = ids_ref.shape
    rows = requests * steps
    for r in range(requests):
        rows_ref[r * steps : (r + 1) * steps, :] = ids_ref[r]
    lane = lax.broadcasted_iota(jnp.int32, (rows, LANES), 1)
    chosen = [rows_ref[:, c : c + 1] for c in range(TOPK)]
    onehot = [(lane == ids).astype(jnp.float32) for ids in chosen]
    across = order_ref[...]
    square_row = lax.broadcasted_iota(jnp.int32, (rows, rows), 0)
    square_col = lax.broadcasted_iota(jnp.int32, (rows, rows), 1)
    order_wide = jnp.broadcast_to(across, (rows, rows))
    down = jnp.sum(
        jnp.where(square_row == square_col, order_wide, 0).astype(jnp.float32),
        axis=1,
        keepdims=True,
    )
    earlier = (order_wide.astype(jnp.float32) < down).astype(jnp.bfloat16)
    counts = dot(earlier, sum(onehot).astype(jnp.bfloat16))
    slot = lax.broadcasted_iota(jnp.int32, (rows, EXPERTS * CAP), 1)
    both = jnp.zeros((rows, EXPERTS * CAP), jnp.float32)
    for c in range(TOPK):
        position = jnp.sum(onehot[c] * counts, axis=-1, keepdims=True).astype(jnp.int32)
        column = chosen[c] * CAP + position
        select = ((column == slot) & (position < CAP)).astype(jnp.float32)
        select_ref[c] = select
        chosen_ref[c] = onehot[c]
        both = both + select
    turned_ref[...] = jnp.transpose(both)


def residual_kernel(
    own_ref, projected_ref, tokens_ref, gain_ref, turned_ref, normed_ref, residual_ref, send_ref
):
    requests, steps, _ = tokens_ref.shape
    devices, rows, share = projected_ref.shape
    for r in range(requests):
        residual_ref[r * steps : (r + 1) * steps, :] = tokens_ref[r].astype(jnp.float32)
    for d in range(devices):
        own = slice(d * share, (d + 1) * share)
        residual_ref[:, own] = residual_ref[:, own] + projected_ref[d].astype(jnp.float32)
    normed = rms_rows(residual_ref[...], gain_ref[...])
    normed_ref[...] = normed
    groups = send_ref.shape[0]
    local_experts = EXPERTS // groups
    for g in range(groups):
        first = pl.multiple_of((g * local_experts + own_ref[0]) * CAP, CAP)
        picking = turned_ref[pl.ds(first, CAP), :].astype(jnp.bfloat16)
        send_ref[g] = dot(picking, normed).astype(jnp.bfloat16)


def gate_kernel(normed_ref, router_ref, select_ref, chosen_ref, out_ref):
    logits = dot(normed_ref[...], router_ref[...])
    gates = jnp.zeros(select_ref.shape[1:], jnp.float32)
    for c in range(TOPK):
        logit = jnp.sum(chosen_ref[c][:, :EXPERTS] * logits, axis=-1, keepdims=True)
        gates = gates + jax.nn.sigmoid(logit) * select_ref[c]
    out_ref[...] = gates


def expert_kernel(rows_ref, in_ref, down_ref, out_ref):
    groups, slots, width = rows_ref.shape
    rows = rows_ref[...].reshape(groups * slots, width)
    gate = dot(rows, in_ref[0, 0], ROWS_BY_ROWS)
    up = dot(rows, in_ref[1, 0], ROWS_BY_ROWS)
    hidden = (jax.nn.gelu(gate, approximate=True) * up).astype(jnp.bfloat16)
    out_ref[...] = dot(hidden, down_ref[0])


def final_kernel(gates_ref, returned_ref, residual_ref, out_ref):
    requests, steps, width = out_ref.shape
    returned = returned_ref[...]
    moe = sum(dot(part, returned) for part in split(gates_ref[...], 2))
    total = residual_ref[...] + moe
    for r in range(requests):
        out_ref[r] = total[r * steps : (r + 1) * steps].astype(jnp.bfloat16)


def shape(dims, dtype):
    return jax.ShapeDtypeStruct(dims, dtype)


def body(
    tokens,
    attn_gain,
    w_qkv,
    window_cache,
    sink_cache,
    lengths,
    w_out,
    moe_gain,
    router,
    expert_ids,
    slot_order,
    expert_in,
    expert_down,
):
    requests, steps, width = tokens.shape
    rows = requests * steps
    seq_index = lax.axis_index("seq")
    seq_count = lax.axis_size("seq")
    groups = lax.axis_size("exp")
    local_experts = EXPERTS // groups
    sharers = seq_count // local_experts
    own_expert = (seq_index // sharers).astype(jnp.int32).reshape(1)
    place = seq_index.astype(jnp.int32).reshape(1)
    span = window_cache.shape[2]
    share = w_qkv.shape[0]
    slots = EXPERTS * CAP
    f32, bf16 = jnp.float32, jnp.bfloat16

    local_mix = pl.pallas_call(
        qkv_kernel,
        out_shape=shape((rows, share), bf16),
        scratch_shapes=[pltpu.VMEM((rows, width), f32)],
        compiler_params=params(),
        name="qkv",
    )(tokens, attn_gain.reshape(1, width), w_qkv)
    mixed = lax.all_gather(local_mix, "seq", axis=0)

    padded = width + LANES
    part = pl.pallas_call(
        attention_kernel,
        grid_spec=pltpu.PrefetchScalarGridSpec(
            num_scalar_prefetch=2,
            grid=(requests,),
            in_specs=[
                pl.BlockSpec((seq_count, rows, share), lambda i, *_: (0, 0, 0)),
                pl.BlockSpec((1, 1, span, width), lambda i, *_: (0, i, 0, 0)),
                pl.BlockSpec((1, 1, span, width), lambda i, *_: (1, i, 0, 0)),
                pl.BlockSpec(sink_cache.shape, lambda i, *_: (0, 0, 0, 0)),
            ],
            out_specs=pl.BlockSpec((rows, padded), lambda i, *_: (0, 0)),
            scratch_shapes=[
                pltpu.VMEM((rows, 3 * width), f32),
                pltpu.VMEM((requests, steps, width), f32),
                pltpu.VMEM((2, requests, SINKS + steps, width), f32),
                pltpu.VMEM((requests, steps, padded), f32),
            ],
        ),
        out_shape=shape((rows, padded), bf16),
        compiler_params=params(),
        name="attention",
    )(lengths, place, mixed, window_cache, window_cache, sink_cache)
    parts = lax.all_gather(part, "seq", axis=0)

    local_proj = pl.pallas_call(
        project_kernel,
        out_shape=shape((rows, w_out.shape[0]), bf16),
        compiler_params=params(),
        name="project",
    )(parts, w_out)
    projected = lax.all_gather(local_proj, "seq", axis=0)

    select, turned, chosen = pl.pallas_call(
        routing_kernel,
        out_shape=(
            shape((TOPK, rows, slots), f32),
            shape((slots, rows), f32),
            shape((TOPK, rows, LANES), f32),
        ),
        scratch_shapes=[pltpu.VMEM((rows, TOPK), jnp.int32)],
        compiler_params=params(),
        name="routing",
    )(expert_ids, slot_order)

    smem = pl.BlockSpec(memory_space=pltpu.SMEM)
    vmem = pl.BlockSpec(memory_space=pltpu.VMEM)
    normed, residual, send = pl.pallas_call(
        residual_kernel,
        in_specs=[smem] + [vmem] * 4,
        out_shape=(
            shape((rows, width), bf16),
            shape((rows, width), f32),
            shape((groups, CAP, width), bf16),
        ),
        compiler_params=params(),
        name="residual",
    )(own_expert, projected, tokens, moe_gain.reshape(1, width), turned)
    received = lax.all_to_all(send, "exp", split_axis=0, concat_axis=0, tiled=True)

    gates = pl.pallas_call(
        gate_kernel,
        out_shape=shape((rows, slots), f32),
        compiler_params=params(),
        name="gate",
    )(normed, router, select, chosen)

    outputs = pl.pallas_call(
        expert_kernel,
        out_shape=shape((groups * CAP, width), f32),
        compiler_params=params(),
        name="expert",
    )(received, expert_in, expert_down)

    reach = 1
    while reach < sharers:
        other = lax.ppermute(outputs, "seq", [(i, i ^ reach) for i in range(seq_count)])
        outputs = outputs + other
        reach *= 2
    returned = lax.all_to_all(
        outputs.astype(bf16).reshape(groups, CAP, width),
        "exp",
        split_axis=0,
        concat_axis=0,
        tiled=True,
    )
    gathered = lax.all_gather(returned, "seq", axis=0)[::sharers]
    everyone = gathered.transpose(1, 0, 2, 3).reshape(slots, width)

    return pl.pallas_call(
        final_kernel,
        out_shape=shape((requests, steps, width), bf16),
        compiler_params=params(),
        name="final",
    )(gates, everyone, residual)


def solution(mesh):
    in_specs = (
        P("exp", None, None),
        P(),
        P("seq", None),
        P(None, "exp", "seq", None),
        P(None, "exp", None, None),
        P("exp"),
        P("seq", None),
        P(),
        P(),
        P("exp", None, None),
        P("exp", None),
        P(None, "exp", "seq", None),
        P("exp", "seq", None),
    )
    out_specs = P("exp", None, None)
    return jax.shard_map(body, mesh=mesh, in_specs=in_specs, out_specs=out_specs, check_vma=False)
```

time: 301 us -> 93.3 us (0.31)
  waiting for transfers between devices: 97.5 us -> 6.6 us
  local copies, waits for them, and re-layouts: 71 us -> 7.28 us
  matrix products: 30.2 us -> 0 us
  Pallas kernels: 0 us -> 24.6 us
  blocking collectives: 66.6 us -> 50.1 us
  between operations: 13.7 us -> 0.13 us
  other arithmetic: 11.4 us -> 0.64 us
  starting transfers between devices: 9.2 us -> 3.3 us
    psum x2 -> x0, waiting for transfers between devices: 80 us -> none  [the longest x1 51.8 us: body(): summed = lax.psum(expert_part.astype(jnp.bfloat16), 'seq')]
    slice x5 -> x0, local copies, waits for them, and re-layouts: 54.4 us -> none  [the longest x2 34.1 us: body(): cache_values = window_cache[1].reshape(requests, slot_span, HEADS, HD)]
    dot_general x12 -> x0, matrix products: 30.2 us -> none  [the longest x1 8.48 us: body(): jnp.einsum('rshw,rwhe->rshe', window_exp.astype(jnp.bfloat16), cache_valu...]
    pallas_call x0 -> x8, Pallas kernels: none -> 24.6 us  [the longest x1 19.1 us: body(): pl.pallas_call(attention_kernel, grid_spec=pltpu.PrefetchScalarGridSpec(n...]
    pmax x1 -> x0, blocking collectives: 23.6 us -> none  [body(): overall = lax.pmax(peak_score, 'seq')]
    psum x1 -> x0, blocking collectives: 22.3 us -> none  [body(): lax.psum((weight_sum * factor).astype(jnp.bfloat16), 'seq')]
    all_gather x2 -> x4, blocking collectives: 20.7 us -> 39.6 us  [the longest x1 10.9 us: body(): mixed = lax.all_gather(local_mix, 'seq', axis=0)]
    all_to_all x2 -> x1, waiting for transfers between devices: 17.6 us -> 5.25 us  [body(): lax.all_to_all(outputs.astype(bf16).reshape(groups, CAP, width), 'exp', s...]
  transfers between devices with their start and end apart: 4 -> 2, of which waited for: 4 -> 2; matrix products, arithmetic and copies ran while one was open for 0% -> 0% of each run, Pallas kernels for 0% -> 0%
where the time goes in v1:
time: 93.3 us; the launch traced here: 92.6 us
  blocking collectives  50.1 us (54%)
  Pallas kernels  24.6 us (26%)
  local copies, waits for them, and re-layouts  7.28 us (8%)
  waiting for transfers between devices  6.6 us (7%)
  starting transfers between devices  3.3 us (4%)
    pallas_call x1, Pallas kernels, body(): pl.pallas_call(attention_kernel, grid_spec=pltpu.PrefetchScalarGridSpec(n...  19.1 us
    all_gather x1, blocking collectives, body(): mixed = lax.all_gather(local_mix, 'seq', axis=0)  10.9 us
    all_gather x1, blocking collectives, body(): parts = lax.all_gather(part, 'seq', axis=0)  10.7 us
    all_to_all x1, blocking collectives, body(): lax.all_to_all(send, 'exp', split_axis=0, concat_axis=0, tiled=True)  10.4 us
    all_gather x1, blocking collectives, body(): gathered = lax.all_gather(returned, 'seq', axis=0)[::sharers]  9.82 us
    all_gather x1, blocking collectives, body(): projected = lax.all_gather(local_proj, 'seq', axis=0)  8.27 us
    unnamed x28, local copies, waits for them, and re-layouts  7.24 us
    all_to_all x1, waiting for transfers between devices, body(): lax.all_to_all(outputs.astype(bf16).reshape(groups, CAP, width), 'exp', s...  5.25 us
  transfers between devices with their start and end apart: 2, of which 2 were waited for; matrix products, arithmetic and copies ran while one was open for 0% of the time, Pallas kernels for 0%

profile of v1, /device:TPU:0, one launch (start us, length us, event | category | flops | bytes accessed | tf_op | source)
XLA Modules:
  0.0 92.6 jit_solution(10876539713011408767)
XLA Ops:
  0.0 0.0 copy-start.2
  0.0 1.1 %copy-done.2 = bf16[384,1024]{1,0:T(8,128)(2,1)S(1)} copy-done((bf16[384,1024]{1,0:T(8,128)(2,1)S(1)}, bf16[384,1024]{1,0:T(8,128)(2,1)}, u32[]{:S(2)}) %copy-start.2) | copy-done | bytes 786456
  1.1 0.0 copy-start.3
  1.1 0.9 copy-done.3
  2.0 0.0 copy-start.7
  2.0 0.7 copy-done.7
  2.7 0.4 qkv.1
  3.1 10.9 %all-gather = bf16[384,384]{1,0:T(8,128)(2,1)S(1)} all-gather(bf16[48,384]{1,0:T(8,128)(2,1)S(1)} %qkv.1), channel_id=2, replica_groups=mesh['seq'=8,'exp'=4] {'seq'}, dimensions={0}, use_global_device_ids=true | all-gather | bytes 331776 | tf_op jit(solution)/shard_map/all_gather | solution.py:301
  14.0 0.0 copy-start.6
  14.0 0.9 copy-done.6
  14.9 0.0 copy-start.9
  14.9 0.7 copy-done.9
  15.6 0.0 copy-start.5
  15.6 0.0 copy-start.12
  15.6 0.0 copy-start.10
  15.6 0.0 copy-start.4
  15.6 0.0 copy-start.8
  15.6 0.0 copy-start.1
  15.6 19.1 %attention.1 = bf16[48,1152]{1,0:T(8,128)(2,1)S(1)} custom-call(s32[12]{0:T(128)S(1)} %copy-done.9, s32[1]{0:T(128)} %bitcast.1.place_ref, bf16[8,48,384]{2,1,0:T(8,128)(2,1)S(1)} %bitcast.14, bf16[2,12,512,1024]{3,2,1,0:T(8,128)(2,1)} %values_ref.1, bf16[2,12,512,1024]{3,2,1,0:T(8,128)(2,1)} %values_ref.1, bf16[2,12,4,1024]{3,2,1,0:T(4,128)(2,1)S(1)} %copy-done.6), custom_call_target="tpu_custom_call" | custom-call | tf_op jit(solution)/shard_map/attention/pallas_call | solution.py:304
  34.7 10.7 %all-gather.1 = bf16[384,1152]{1,0:T(8,128)(2,1)S(1)} all-gather(bf16[48,1152]{1,0:T(8,128)(2,1)S(1)} %attention.1), channel_id=3, replica_groups=mesh['seq'=8,'exp'=4] {'seq'}, dimensions={0}, use_global_device_ids=true | all-gather | bytes 995328 | tf_op jit(solution)/shard_map/all_gather | solution.py:327
  45.4 0.0 copy-start.11
  45.4 0.0 copy-done.5
  45.4 0.9 project.1
  46.3 8.3 %all-gather.2 = bf16[384,128]{1,0:T(8,128)(2,1)S(1)} all-gather(bf16[48,128]{1,0:T(8,128)(2,1)S(1)} %project.1), channel_id=4, replica_groups=mesh['seq'=8,'exp'=4] {'seq'}, dimensions={0}, use_global_device_ids=true | all-gather | bytes 110592 | tf_op jit(solution)/shard_map/all_gather | solution.py:335
  54.5 0.0 copy-done.12
  54.5 0.1 copy.19.ids_ref
  54.6 0.0 copy-done.10
  54.7 0.5 routing.1
  55.2 0.0 copy-done.4
  55.2 0.0 copy-done.8
  55.2 0.3 residual.1
  55.5 10.4 %all_to_all.10.rows_ref = bf16[4,8,1024]{2,1,0:T(8,128)(2,1)S(1)} all-to-all(bf16[4,8,1024]{2,1,0:T(8,128)(2,1)S(1)} %get-tuple-element.15), channel_id=1, replica_groups=mesh['seq'=8,'exp'=4] {'exp'}, dimensions={0} | all-to-all | bytes 131072 | tf_op jit(solution)/shard_map/all_to_all | solution.py:362
  65.9 0.0 copy-done.1
  65.9 0.0 copy-start
  65.9 2.6 %copy-done = bf16[2,1,1408,1024]{3,2,1,0:T(8,128)(2,1)S(1)} copy-done((bf16[2,1,1408,1024]{3,2,1,0:T(8,128)(2,1)S(1)}, bf16[2,1,1408,1024]{3,2,1,0:T(8,128)(2,1)}, u32[]{:S(2)}) %copy-start) | copy-done | bytes 5767192
  68.6 2.3 %expert.1 = f32[32,1024]{1,0:T(8,128)S(1)} custom-call(bf16[4,8,1024]{2,1,0:T(8,128)(2,1)S(1)} %all_to_all.10.rows_ref, bf16[2,1,1408,1024]{3,2,1,0:T(8,128)(2,1)S(1)} %copy-done, bf16[1,1408,1024]{2,1,0:T(8,128)(2,1)S(1)} %copy-done.1), custom_call_target="tpu_custom_call" | custom-call | tf_op jit(solution)/shard_map/expert/pallas_call | solution.py:371
  70.8 0.0 collective-permute-start
  70.8 1.3 %collective-permute-done = f32[32,1024]{1,0:T(8,128)S(1)} collective-permute-done((f32[32,1024]{1,0:T(8,128)S(1)}, f32[32,1024]{1,0:T(8,128)S(1)}, u32[]{:S(2)}, u32[]{:S(2)}) %collective-permute-start) | collective-permute-done | bytes 131104 | tf_op jit(solution)/shard_map/ppermute | solution.py:380
  72.2 0.6 fusion
  72.8 3.3 %all-to-all-start.1 = ((bf16[4,8,1024]{2,1,0:T(8,128)(2,1)}), bf16[4,8,1024]{2,1,0:T(8,128)(2,1)S(1)}, u32[]{:S(2)}, u32[]{:S(2)}) async-start(bf16[4,8,1024]{2,1,0:T(8,128)(2,1)} %fusion), calls=%async_computation.1 | async-start | bytes 131072 | tf_op jit(solution)/shard_map/all_to_all | solution.py:383
  76.1 0.0 copy-done.11
  76.1 0.2 copy.20.router_ref
  76.3 0.3 gate.1.gates_ref
  76.6 5.3 %all-to-all-done.1 = bf16[4,8,1024]{2,1,0:T(8,128)(2,1)S(1)} async-done(((bf16[4,8,1024]{2,1,0:T(8,128)(2,1)}), bf16[4,8,1024]{2,1,0:T(8,128)(2,1)S(1)}, u32[]{:S(2)}, u32[]{:S(2)}) %all-to-all-start.1) | async-done | bytes 65568 | tf_op jit(solution)/shard_map/all_to_all | solution.py:383
  81.8 9.8 %all-gather.3 = bf16[32,8,1024]{2,1,0:T(8,128)(2,1)S(1)} all-gather(bf16[4,8,1024]{2,1,0:T(8,128)(2,1)S(1)} %all-to-all-done.1), channel_id=5, replica_groups=mesh['seq'=8,'exp'=4] {'seq'}, dimensions={0}, use_global_device_ids=true | all-gather | bytes 589824 | tf_op jit(solution)/shard_map/all_gather | solution.py:390
  91.7 0.9 final.1
  (2 shorter events, 0.0 us)
Async XLA Ops:
  0.0 1.1 %copy-start.2 = (bf16[384,1024]{1,0:T(8,128)(2,1)S(1)}, bf16[384,1024]{1,0:T(8,128)(2,1)}, u32[]{:S(2)}) copy-start(bf16[384,1024]{1,0:T(8,128)(2,1)} %weight_ref.2) | copy-start | bytes 2359300
  1.1 0.9 copy-start.3
  2.0 0.7 copy-start.7
  14.0 0.9 %copy-start.6 = (bf16[2,12,4,1024]{3,2,1,0:T(4,128)(2,1)S(1)}, bf16[2,12,4,1024]{3,2,1,0:T(4,128)(2,1)}, u32[]{:S(2)}) copy-start(bf16[2,12,4,1024]{3,2,1,0:T(4,128)(2,1)} %sinks_ref.1) | copy-start | bytes 589828
  14.9 0.7 copy-start.9
  15.6 29.8 %copy-start.5 = (bf16[128,1024]{1,0:T(8,128)(2,1)S(1)}, bf16[128,1024]{1,0:T(8,128)(2,1)}, u32[]{:S(2)}) copy-start(bf16[128,1024]{1,0:T(8,128)(2,1)} %weight_ref.3) | copy-start | bytes 786436
  15.6 38.9 %copy-start.12 = (s32[12,4,2]{0,2,1:T(2,128)S(1)}, s32[12,4,2]{0,2,1:T(2,128)}, u32[]{:S(2)}) copy-start(s32[12,4,2]{0,2,1:T(2,128)} %param.22) | copy-start | bytes 1156
  15.6 39.1 %copy-start.10 = (s32[1,48]{1,0:T(1,128)S(1)}, s32[1,48]{1,0:T(1,128)}, u32[]{:S(2)}) copy-start(s32[1,48]{1,0:T(1,128)} %order_ref.1) | copy-start | bytes 580
  15.6 39.6 %copy-start.4 = (bf16[12,4,1024]{2,1,0:T(4,128)(2,1)S(1)}, bf16[12,4,1024]{2,1,0:T(4,128)(2,1)}, u32[]{:S(2)}) copy-start(bf16[12,4,1024]{2,1,0:T(4,128)(2,1)} %tokens_ref.3) | copy-start | bytes 294916
  15.6 39.6 %copy-start.8 = (f32[1024]{0:T(1024)S(1)}, f32[1024]{0:T(1024)}, u32[]{:S(2)}) copy-start(f32[1024]{0:T(1024)} %param.20) | copy-start | bytes 12292
  15.6 50.3 %copy-start.1 = (bf16[1,1408,1024]{2,1,0:T(8,128)(2,1)S(1)}, bf16[1,1408,1024]{2,1,0:T(8,128)(2,1)}, u32[]{:S(2)}) copy-start(bf16[1,1408,1024]{2,1,0:T(8,128)(2,1)} %down_ref.1) | copy-start | bytes 8650756
  45.4 30.7 %copy-start.11 = (bf16[1024,16]{0,1:T(8,128)(2,1)S(1)}, bf16[1024,16]{0,1:T(8,128)(2,1)}, u32[]{:S(2)}) copy-start(bf16[1024,16]{0,1:T(8,128)(2,1)} %param.21) | copy-start | bytes 98308
  65.9 2.6 %copy-start = (bf16[2,1,1408,1024]{3,2,1,0:T(8,128)(2,1)S(1)}, bf16[2,1,1408,1024]{3,2,1,0:T(8,128)(2,1)}, u32[]{:S(2)}) copy-start(bf16[2,1,1408,1024]{3,2,1,0:T(8,128)(2,1)} %in_ref.1) | copy-start | bytes 17301508
  70.8 1.4 %collective-permute-start = (f32[32,1024]{1,0:T(8,128)S(1)}, f32[32,1024]{1,0:T(8,128)S(1)}, u32[]{:S(2)}, u32[]{:S(2)}) collective-permute-start(f32[32,1024]{1,0:T(8,128)S(1)} %expert.1), channel_id=1, source_target_pairs={{0,4},{4,0},{8,12},{12,8},{16,20},{20,16},{24,28},{28,24},{1,5},{5... | collective-permute-start | bytes 393224 | tf_op jit(solution)/shard_map/ppermute | solution.py:380
  72.8 9.0 %all-to-all-start.1 = ((bf16[4,8,1024]{2,1,0:T(8,128)(2,1)}), bf16[4,8,1024]{2,1,0:T(8,128)(2,1)S(1)}, u32[]{:S(2)}, u32[]{:S(2)}) async-start(bf16[4,8,1024]{2,1,0:T(8,128)(2,1)} %fusion), calls=%async_computation.1 | async-start | bytes 131072 | tf_op jit(solution)/shard_map/all_to_all | solution.py:383

commit v2 on v1

v2 whole, which is shorter than its diff:
```python
import functools

import jax
import jax.numpy as jnp
from jax import lax
from jax.experimental import pallas as pl
from jax.experimental.pallas import tpu as pltpu
from jax.sharding import PartitionSpec as P

HEADS = 16
HD = 64
EXPERTS = 16
TOPK = 2
SINKS = 4
WIN = 4096
CAP = 8
LANES = 128
PIECES = 3
BLOCK = 256
BLOCK_HEADS = BLOCK // HD

EPSILON = 1e-06
MASKED = -1e30
MIB = 1 << 20
ROWS_BY_ROWS = (((1,), (1,)), ((), ()))
ROWS_BY_COLS = (((1,), (0,)), ((), ()))


def dot(a, b, dims=ROWS_BY_COLS):
    return lax.dot_general(a, b, dims, preferred_element_type=jnp.float32)


def params(limit_mib=32):
    return pltpu.CompilerParams(vmem_limit_bytes=limit_mib * MIB)


def split(value, count):
    parts = []
    for _ in range(count):
        part = value.astype(jnp.bfloat16)
        parts.append(part)
        value = value - part.astype(jnp.float32)
    return parts


def rms_rows(widened, gain_row):
    inverse = lax.rsqrt(jnp.mean(widened * widened, axis=-1, keepdims=True) + EPSILON)
    return (widened * inverse * gain_row).astype(jnp.bfloat16)


def copy_rows(source_ref, rows_ref):
    requests, steps, _ = source_ref.shape
    for r in range(requests):
        rows_ref[r * steps : (r + 1) * steps, :] = source_ref[r].astype(rows_ref.dtype)


def qkv_kernel(tokens_ref, gain_ref, weight_ref, out_ref, token_buf, gain_buf, weight_buf, rows_ref, sems):
    copies = [
        pltpu.make_async_copy(source, target, sems.at[i])
        for i, (source, target) in enumerate(
            ((tokens_ref, token_buf), (gain_ref, gain_buf), (weight_ref, weight_buf))
        )
    ]
    for copy in copies:
        copy.start()
    for copy in copies:
        copy.wait()
    copy_rows(token_buf, rows_ref)
    normed = rms_rows(rows_ref[...], gain_buf[...])
    out_ref[...] = dot(normed, weight_buf[...], ROWS_BY_ROWS).astype(jnp.bfloat16)


def in_order(place, near_ref, far_ref, ordered_ref):
    for j in range(near_ref.shape[0]):
        ordered_ref[jnp.bitwise_xor(place, 2 * j)] = near_ref[j]
        ordered_ref[jnp.bitwise_xor(place, 2 * j + 1)] = far_ref[j]


def head_masks(rows, width, steps):
    row_head = lax.broadcasted_iota(jnp.int32, (rows, width), 0) // steps % BLOCK_HEADS
    col_head = lax.broadcasted_iota(jnp.int32, (rows, width), 1) // HD % BLOCK_HEADS
    return (row_head == col_head).astype(jnp.float32)


def attention_kernel(
    place_ref, lengths_ref, near_ref, far_ref, window_ref, out_ref, ordered_ref, flat_ref, query_ref
):
    devices, rows, share = ordered_ref.shape
    _, requests, span, width = window_ref.shape
    steps = rows // requests
    block_rows = BLOCK_HEADS * steps
    place = place_ref[0]
    in_order(place, near_ref, far_ref, ordered_ref)
    for d in range(devices):
        if d * share < width:
            flat_ref[:, d * share : (d + 1) * share] = ordered_ref[d].astype(jnp.float32)
    own_head = head_masks(block_rows, width, steps)
    for r in range(requests):
        queries = flat_ref[r * steps : (r + 1) * steps, 0:width]
        query_ref[r] = (jnp.concatenate([queries] * BLOCK_HEADS, axis=0) * own_head).astype(
            jnp.bfloat16
        )
    base = place * span
    scale = HD ** (-0.5)
    pair = 2 * steps
    tiles = HEADS * steps // pair
    slot = base + lax.broadcasted_iota(jnp.int32, (pair, span), 1)
    step = lax.broadcasted_iota(jnp.int32, (pair, span), 0) % steps
    stat_lane = lax.broadcasted_iota(jnp.int32, (HEADS * steps, LANES), 1)
    stat_head = lax.broadcasted_iota(jnp.int32, (HEADS * steps, LANES), 0) // steps
    cols = [slice(c, c + BLOCK) for c in range(0, width, BLOCK)]

    def score(r):
        return jnp.concatenate(
            [dot(query_ref[r, :, c], window_ref[0, r, :, c], ROWS_BY_ROWS) for c in cols], axis=0
        )

    scores = score(0)
    for r in range(requests):
        following = score(r + 1) if r + 1 < requests else None
        length = lengths_ref[r]
        age = jnp.bitwise_and(slot - (length - SINKS), WIN - 1)
        live = ((slot < jnp.minimum(WIN, length - SINKS)) & (age > step))[None]
        scores = jnp.where(live, scores.reshape(tiles, pair, span) * scale, MASKED)
        peak = jnp.max(scores, axis=-1, keepdims=True)
        weight = jnp.where(live, jnp.exp(scores - peak), 0.0)
        total = jnp.sum(weight, axis=-1, keepdims=True)
        weight = weight.reshape(HEADS * steps, span).astype(jnp.bfloat16)
        outs = []
        for b, c in enumerate(cols):
            own = slice(b * block_rows, (b + 1) * block_rows)
            mixed = dot(weight[own], window_ref[1, r, :, c]) * own_head[:, c]
            mixed = sum(mixed[i : i + pair] for i in range(0, block_rows, pair))
            outs.append(mixed[:steps] + mixed[steps:])
        stats = jnp.zeros((HEADS * steps, LANES), jnp.float32)
        parts = split(peak.reshape(HEADS * steps, 1), PIECES)
        parts = parts + split(total.reshape(HEADS * steps, 1), PIECES)
        for i, part in enumerate(parts):
            stats = jnp.where(
                stat_lane == stat_head + i * HEADS, part.astype(jnp.float32), stats
            )
        stats = jnp.sum(stats.reshape(tiles, pair, LANES), axis=0)
        outs.append(stats[:steps] + stats[steps:])
        flat_ref[r * steps : (r + 1) * steps, :] = jnp.concatenate(outs, axis=1)
        scores = following
    out_ref[...] = flat_ref[...].astype(jnp.bfloat16)


def extra_kernel(
    place_ref, near_ref, far_ref, sinks_ref, out_ref, stats_ref, ordered_ref, flat_ref, query_ref, keys_ref
):
    devices, rows, share = ordered_ref.shape
    _, requests, sinks, width = sinks_ref.shape
    steps = rows // requests
    block_rows = BLOCK_HEADS * steps
    count = sinks + steps
    in_order(place_ref[0], near_ref, far_ref, ordered_ref)
    for d in range(devices):
        flat_ref[:, d * share : (d + 1) * share] = ordered_ref[d].astype(jnp.float32)
    own_head = head_masks(block_rows, width, steps)
    for r in range(requests):
        own = slice(r * steps, (r + 1) * steps)
        queries = jnp.concatenate([flat_ref[own, 0:width]] * BLOCK_HEADS, axis=0) * own_head
        query_ref[r * block_rows : (r + 1) * block_rows, :] = queries
        for p in range(2):
            keys_ref[p, r * count : r * count + sinks] = sinks_ref[p, r].astype(jnp.float32)
            keys_ref[p, r * count + sinks : (r + 1) * count] = flat_ref[
                own, (p + 1) * width : (p + 2) * width
            ]
    all_rows = requests * block_rows
    all_keys = requests * count
    row = lax.broadcasted_iota(jnp.int32, (all_rows, all_keys), 0)
    key = lax.broadcasted_iota(jnp.int32, (all_rows, all_keys), 1)
    live = (row // block_rows == key // count) & (key % count - sinks <= row % steps)
    stat_lane = lax.broadcasted_iota(jnp.int32, (all_rows, LANES), 1)
    stat_head = lax.broadcasted_iota(jnp.int32, (all_rows, LANES), 0) % block_rows // steps
    whole_mask = jnp.concatenate([own_head[:, :BLOCK]] * requests, axis=0)
    stats = jnp.zeros((all_rows, LANES), jnp.float32)
    pair = 2 * steps

    def by_request(values):
        values = jnp.sum(values.reshape(requests, block_rows // pair, pair, values.shape[-1]), axis=1)
        return values[:, :steps] + values[:, steps:]

    for b in range(width // BLOCK):
        c = slice(b * BLOCK, (b + 1) * BLOCK)
        scores = dot(
            query_ref[:, c].astype(jnp.bfloat16), keys_ref[0, :, c].astype(jnp.bfloat16), ROWS_BY_ROWS
        )
        scores = jnp.where(live, scores * HD ** (-0.5), MASKED)
        peak = jnp.max(scores, axis=-1, keepdims=True)
        weight = jnp.where(live, jnp.exp(scores - peak), 0.0)
        total = jnp.sum(weight, axis=-1, keepdims=True)
        mixed = dot(weight.astype(jnp.bfloat16), keys_ref[1, :, c].astype(jnp.bfloat16))
        mixed = by_request(mixed * whole_mask)
        for r in range(requests):
            out_ref[r * steps : (r + 1) * steps, c] = mixed[r]
        stats = jnp.where(stat_lane == stat_head + b * BLOCK_HEADS, peak, stats)
        stats = jnp.where(stat_lane == stat_head + b * BLOCK_HEADS + HEADS, total, stats)
    stats = by_request(stats)
    for r in range(requests):
        stats_ref[r * steps : (r + 1) * steps, :] = stats[r]


def project_kernel(
    place_ref, near_ref, far_ref, extra_ref, extra_stats_ref, weight_ref, out_ref, ordered_ref
):
    devices, rows, padded = ordered_ref.shape
    width = padded - LANES
    in_order(place_ref[0], near_ref, far_ref, ordered_ref)
    stats = [ordered_ref[d][:, width:].astype(jnp.float32) for d in range(devices)]

    def joined(stat, first):
        return sum(
            stat[:, (first + i) * HEADS : (first + i + 1) * HEADS] for i in range(PIECES)
        )

    peaks = [joined(stat, 0) for stat in stats] + [extra_stats_ref[:, :HEADS]]
    totals = [joined(stat, PIECES) for stat in stats] + [extra_stats_ref[:, HEADS : 2 * HEADS]]
    overall = functools.reduce(jnp.maximum, peaks)
    factors = [jnp.exp(peak - overall) for peak in peaks]
    total = sum(f * t for f, t in zip(factors, totals))
    inverse = 1.0 / total
    head_of_row = lax.broadcasted_iota(jnp.int32, (HEADS, width), 0)
    head_of_col = lax.broadcasted_iota(jnp.int32, (HEADS, width), 1) // HD
    expand = (head_of_row == head_of_col).astype(jnp.bfloat16)

    def spread(factor):
        return sum(dot(part, expand) for part in split(factor * inverse, 2))

    attended = spread(factors[-1]) * extra_ref[...]
    for d in range(devices):
        attended = attended + spread(factors[d]) * ordered_ref[d][:, :width].astype(jnp.float32)
    out_ref[...] = dot(attended.astype(jnp.bfloat16), weight_ref[...], ROWS_BY_ROWS).astype(
        jnp.bfloat16
    )


def routing_kernel(ids_ref, order_ref, select_ref, turned_ref, chosen_ref, rows_ref):
    requests, steps, _ = ids_ref.shape
    rows = requests * steps
    for r in range(requests):
        rows_ref[r * steps : (r + 1) * steps, :] = ids_ref[r]
    lane = lax.broadcasted_iota(jnp.int32, (rows, LANES), 1)
    chosen = [rows_ref[:, c : c + 1] for c in range(TOPK)]
    onehot = [(lane == ids).astype(jnp.float32) for ids in chosen]
    across = order_ref[...]
    square_row = lax.broadcasted_iota(jnp.int32, (rows, rows), 0)
    square_col = lax.broadcasted_iota(jnp.int32, (rows, rows), 1)
    order_wide = jnp.broadcast_to(across, (rows, rows))
    down = jnp.sum(
        jnp.where(square_row == square_col, order_wide, 0).astype(jnp.float32),
        axis=1,
        keepdims=True,
    )
    earlier = (order_wide.astype(jnp.float32) < down).astype(jnp.bfloat16)
    counts = dot(earlier, sum(onehot).astype(jnp.bfloat16))
    slot = lax.broadcasted_iota(jnp.int32, (rows, EXPERTS * CAP), 1)
    both = jnp.zeros((rows, EXPERTS * CAP), jnp.float32)
    for c in range(TOPK):
        position = jnp.sum(onehot[c] * counts, axis=-1, keepdims=True).astype(jnp.int32)
        column = chosen[c] * CAP + position
        select = ((column == slot) & (position < CAP)).astype(jnp.float32)
        select_ref[c] = select
        chosen_ref[c] = onehot[c]
        both = both + select
    turned_ref[...] = jnp.transpose(both)


def residual_kernel(
    place_ref,
    own_ref,
    near_ref,
    far_ref,
    tokens_ref,
    gain_ref,
    turned_ref,
    normed_ref,
    residual_ref,
    send_ref,
    ordered_ref,
):
    devices, rows, share = ordered_ref.shape
    in_order(place_ref[0], near_ref, far_ref, ordered_ref)
    copy_rows(tokens_ref, residual_ref)
    for d in range(devices):
        own = slice(d * share, (d + 1) * share)
        residual_ref[:, own] = residual_ref[:, own] + ordered_ref[d].astype(jnp.float32)
    normed = rms_rows(residual_ref[...], gain_ref[...])
    normed_ref[...] = normed
    groups = send_ref.shape[0]
    local_experts = EXPERTS // groups
    for g in range(groups):
        first = pl.multiple_of((g * local_experts + own_ref[0]) * CAP, CAP)
        picking = turned_ref[pl.ds(first, CAP), :].astype(jnp.bfloat16)
        send_ref[g] = dot(picking, normed).astype(jnp.bfloat16)


def gate_kernel(normed_ref, router_ref, select_ref, chosen_ref, out_ref):
    logits = dot(normed_ref[...], router_ref[...])
    gates = jnp.zeros(select_ref.shape[1:], jnp.float32)
    for c in range(TOPK):
        logit = jnp.sum(chosen_ref[c][:, :EXPERTS] * logits, axis=-1, keepdims=True)
        gates = gates + jax.nn.sigmoid(logit) * select_ref[c]
    out_ref[...] = gates


def expert_kernel(odd_ref, rows_ref, in_ref, down_ref, keep_ref, send_ref):
    groups, slots, width = rows_ref.shape
    rows = rows_ref[...].reshape(groups * slots, width)
    gate = dot(rows, in_ref[0, 0], ROWS_BY_ROWS)
    up = dot(rows, in_ref[1, 0], ROWS_BY_ROWS)
    hidden = (jax.nn.gelu(gate, approximate=True) * up).astype(jnp.bfloat16)
    outputs = dot(hidden, down_ref[0])
    half = width // 2
    odd = odd_ref[0] == 1
    keep_ref[...] = jnp.where(odd, outputs[:, half:], outputs[:, :half])
    send_ref[...] = jnp.where(odd, outputs[:, :half], outputs[:, half:])


def column_block(sharer, sharers):
    block = 0
    while sharers > 1:
        sharers //= 2
        block += (sharer & 1) * sharers
        sharer >>= 1
    return block


def final_kernel(gates_ref, returned_ref, residual_ref, out_ref, table_ref):
    requests, steps, width = out_ref.shape
    devices, groups, slots, part = returned_ref.shape
    local_experts = EXPERTS // groups
    sharers = devices // local_experts
    for s in range(devices):
        first = column_block(s % sharers, sharers) * part
        for x in range(groups):
            row = (x * local_experts + s // sharers) * slots
            table_ref[row : row + slots, first : first + part] = returned_ref[s, x].astype(jnp.float32)
    table = table_ref[...].astype(jnp.bfloat16)
    moe = sum(dot(part, table) for part in split(gates_ref[...], 2))
    total = residual_ref[...] + moe
    for r in range(requests):
        out_ref[r] = total[r * steps : (r + 1) * steps].astype(jnp.bfloat16)


def gather_seq(values):
    count = lax.axis_size("seq")
    others = [
        lax.ppermute(values, "seq", [(i, i ^ k) for i in range(count)]) for k in range(2, count, 2)
    ]
    near = jnp.stack([values] + others)
    far = lax.ppermute(near, "seq", [(i, i ^ 1) for i in range(count)])
    return near, far


def shape(dims, dtype):
    return jax.ShapeDtypeStruct(dims, dtype)


def body(
    tokens,
    attn_gain,
    w_qkv,
    window_cache,
    sink_cache,
    lengths,
    w_out,
    moe_gain,
    router,
    expert_ids,
    slot_order,
    expert_in,
    expert_down,
):
    requests, steps, width = tokens.shape
    rows = requests * steps
    seq_index = lax.axis_index("seq")
    seq_count = lax.axis_size("seq")
    groups = lax.axis_size("exp")
    local_experts = EXPERTS // groups
    sharers = seq_count // local_experts
    own_expert = (seq_index // sharers).astype(jnp.int32).reshape(1)
    place = seq_index.astype(jnp.int32).reshape(1)
    span = window_cache.shape[2]
    share = w_qkv.shape[0]
    slots = EXPERTS * CAP
    f32, bf16 = jnp.float32, jnp.bfloat16

    smem = pl.BlockSpec(memory_space=pltpu.SMEM)
    vmem = pl.BlockSpec(memory_space=pltpu.VMEM)
    anywhere = pl.BlockSpec(memory_space=pl.ANY)

    gain_row = attn_gain.reshape(1, width)
    local_mix = pl.pallas_call(
        qkv_kernel,
        in_specs=[anywhere] * 3,
        out_shape=shape((rows, share), bf16),
        scratch_shapes=[
            pltpu.VMEM(tokens.shape, bf16),
            pltpu.VMEM(gain_row.shape, f32),
            pltpu.VMEM(w_qkv.shape, bf16),
            pltpu.VMEM((rows, width), f32),
            pltpu.SemaphoreType.DMA((3,)),
        ],
        compiler_params=params(4),
        name="qkv",
    )(tokens, gain_row, w_qkv)
    near_mix, far_mix = gather_seq(local_mix)

    padded = width + LANES
    part = pl.pallas_call(
        attention_kernel,
        in_specs=[smem, smem, vmem, vmem, vmem],
        out_shape=shape((rows, padded), bf16),
        scratch_shapes=[
            pltpu.VMEM((seq_count, rows, share), bf16),
            pltpu.VMEM((rows, padded), f32),
            pltpu.VMEM((requests, BLOCK_HEADS * steps, width), bf16),
        ],
        compiler_params=params(8),
        name="attention",
    )(place, lengths, near_mix, far_mix, window_cache)
    near_part, far_part = gather_seq(part)

    extra, extra_stats = pl.pallas_call(
        extra_kernel,
        in_specs=[smem, vmem, vmem, vmem],
        out_shape=(shape((rows, width), f32), shape((rows, LANES), f32)),
        scratch_shapes=[
            pltpu.VMEM((seq_count, rows, share), bf16),
            pltpu.VMEM((rows, 3 * width), f32),
            pltpu.VMEM((rows * BLOCK_HEADS, width), f32),
            pltpu.VMEM((2, requests * (SINKS + steps), width), f32),
        ],
        compiler_params=params(8),
        name="extra",
    )(place, near_mix, far_mix, sink_cache)

    local_proj = pl.pallas_call(
        project_kernel,
        in_specs=[smem] + [vmem] * 5,
        out_shape=shape((rows, w_out.shape[0]), bf16),
        scratch_shapes=[pltpu.VMEM((seq_count, rows, padded), bf16)],
        compiler_params=params(8),
        name="project",
    )(place, near_part, far_part, extra, extra_stats, w_out)
    near_proj, far_proj = gather_seq(local_proj)

    select, turned, chosen = pl.pallas_call(
        routing_kernel,
        out_shape=(
            shape((TOPK, rows, slots), f32),
            shape((slots, rows), f32),
            shape((TOPK, rows, LANES), f32),
        ),
        scratch_shapes=[pltpu.VMEM((rows, TOPK), jnp.int32)],
        compiler_params=params(8),
        name="routing",
    )(expert_ids, slot_order)

    normed, residual, send = pl.pallas_call(
        residual_kernel,
        in_specs=[smem, smem] + [vmem] * 5,
        out_shape=(
            shape((rows, width), bf16),
            shape((rows, width), f32),
            shape((groups, CAP, width), bf16),
        ),
        scratch_shapes=[pltpu.VMEM((seq_count, rows, w_out.shape[0]), bf16)],
        compiler_params=params(8),
        name="residual",
    )(place, own_expert, near_proj, far_proj, tokens, moe_gain.reshape(1, width), turned)
    received = lax.all_to_all(send, "exp", split_axis=0, concat_axis=0, tiled=True)

    gates = pl.pallas_call(
        gate_kernel,
        out_shape=shape((rows, slots), f32),
        compiler_params=params(8),
        name="gate",
    )(normed, router, select, chosen)

    odd = jnp.bitwise_and(place, 1)
    kept, sent = pl.pallas_call(
        expert_kernel,
        in_specs=[smem] + [vmem] * 3,
        out_shape=(
            shape((groups * CAP, width // 2), f32),
            shape((groups * CAP, width // 2), f32),
        ),
        compiler_params=params(8),
        name="expert",
    )(odd, received, expert_in, expert_down)

    reach = 1
    while True:
        kept = kept + lax.ppermute(sent, "seq", [(i, i ^ reach) for i in range(seq_count)])
        reach *= 2
        if reach >= sharers:
            break
        upper = (seq_index // reach) % 2 == 1
        low, high = jnp.split(kept, 2, axis=1)
        kept, sent = jnp.where(upper, high, low), jnp.where(upper, low, high)
    columns = kept.shape[1]
    outgoing = kept.astype(bf16).reshape(1, groups, CAP, columns)
    outgoing = jnp.broadcast_to(outgoing, (seq_count, groups, CAP, columns))
    returned = lax.all_to_all(
        outgoing.reshape(seq_count * groups, CAP, columns),
        ("seq", "exp"),
        split_axis=0,
        concat_axis=0,
        tiled=True,
    ).reshape(seq_count, groups, CAP, columns)

    return pl.pallas_call(
        final_kernel,
        out_shape=shape((requests, steps, width), bf16),
        scratch_shapes=[pltpu.VMEM((slots, width), f32)],
        compiler_params=params(8),
        name="final",
    )(gates, returned, residual)


def solution(mesh):
    in_specs = (
        P("exp", None, None),
        P(),
        P("seq", None),
        P(None, "exp", "seq", None),
        P(None, "exp", None, None),
        P("exp"),
        P("seq", None),
        P(),
        P(),
        P("exp", None, None),
        P("exp", None),
        P(None, "exp", "seq", None),
        P("exp", "seq", None),
    )
    out_specs = P("exp", None, None)
    return jax.shard_map(body, mesh=mesh, in_specs=in_specs, out_specs=out_specs, check_vma=False)
```

time: 93.3 us -> 80.4 us (0.86)
  blocking collectives: 50.1 us -> 0 us
  waiting for transfers between devices: 6.6 us -> 31.4 us
  starting transfers between devices: 3.3 us -> 19.9 us
  Pallas kernels: 24.6 us -> 13.1 us
  local copies, waits for them, and re-layouts: 7.28 us -> 15.2 us
    all_gather x4 -> x0, blocking collectives: 39.6 us -> none  [the longest x1 10.9 us: body(): mixed = lax.all_gather(local_mix, 'seq', axis=0)]
    ppermute x1 -> x13, waiting for transfers between devices: 1.34 us -> 16 us  [the longest x9 11.9 us: gather_seq(): lax.ppermute(values, 'seq', [(i, i ^ k) for i in range(count)])]
    ppermute x1 -> x13, starting transfers between devices: 0.01 us -> 11.9 us  [the longest x9 11.7 us: gather_seq(): lax.ppermute(values, 'seq', [(i, i ^ k) for i in range(count)])]
    pallas_call x5 -> x6, Pallas kernels: 22.9 us -> 11.5 us  [the longest x1 5.77 us: body(): pl.pallas_call(attention_kernel, in_specs=[smem, smem, vmem, vmem, vmem],...]
    all_to_all x1 -> x0, blocking collectives: 10.4 us -> none  [body(): lax.all_to_all(send, 'exp', split_axis=0, concat_axis=0, tiled=True)]
    all_to_all x1 -> x2, waiting for transfers between devices: 5.25 us -> 15.5 us  [the longest x1 9.74 us: body(): lax.all_to_all(outgoing.reshape(seq_count * groups, CAP, columns), ('seq'...]
    unnamed x28 -> x30, local copies, waits for them, and re-layouts: 7.24 us -> 14.5 us
    all_to_all x1 -> x2, starting transfers between devices: 3.28 us -> 7.97 us  [the longest x1 4.87 us: body(): lax.all_to_all(send, 'exp', split_axis=0, concat_axis=0, tiled=True)]
  transfers between devices with their start and end apart: 2 -> 15, of which waited for: 2 -> 15; matrix products, arithmetic and copies ran while one was open for 0% -> 0% of each run, Pallas kernels for 0% -> 2%
where the time goes in v2:
time: 80.4 us; the launch traced here: 80 us
  waiting for transfers between devices  31.4 us (39%)
  starting transfers between devices  19.9 us (25%)
  local copies, waits for them, and re-layouts  15.2 us (19%)
  Pallas kernels  13.1 us (16%)
    unnamed x30, local copies, waits for them, and re-layouts  14.5 us
    ppermute x9, waiting for transfers between devices, gather_seq(): lax.ppermute(values, 'seq', [(i, i ^ k) for i in range(count)])  11.9 us
    ppermute x9, starting transfers between devices, gather_seq(): lax.ppermute(values, 'seq', [(i, i ^ k) for i in range(count)])  11.7 us
    all_to_all x1, waiting for transfers between devices, body(): lax.all_to_all(outgoing.reshape(seq_count * groups, CAP, columns), ('seq'...  9.74 us
    pallas_call x1, Pallas kernels, body(): pl.pallas_call(attention_kernel, in_specs=[smem, smem, vmem, vmem, vmem],...  5.77 us
    all_to_all x1, waiting for transfers between devices, body(): lax.all_to_all(send, 'exp', split_axis=0, concat_axis=0, tiled=True)  5.74 us
    all_to_all x1, starting transfers between devices, body(): lax.all_to_all(send, 'exp', split_axis=0, concat_axis=0, tiled=True)  4.87 us
    all_to_all x1, starting transfers between devices, body(): lax.all_to_all(outgoing.reshape(seq_count * groups, CAP, columns), ('seq'...  3.1 us
  transfers between devices with their start and end apart: 15, of which 15 were waited for; matrix products, arithmetic and copies ran while one was open for 0% of the time, Pallas kernels for 2%

profile of v2, /device:TPU:0, one launch (start us, length us, event | category | flops | bytes accessed | tf_op | source)
XLA Modules:
  0.0 80.0 jit_solution(7999338988047896900)
XLA Ops:
  0.0 1.1 %copy-done.3 = bf16[384,1024]{1,0:T(8,128)(2,1)S(1)} copy-done((bf16[384,1024]{1,0:T(8,128)(2,1)S(1)}, bf16[384,1024]{1,0:T(8,128)(2,1)}, u32[]{:S(2)}) %copy-start.3) | copy-done | bytes 786456
  1.1 0.9 %copy-done.4 = bf16[12,4,1024]{2,1,0:T(4,128)(2,1)S(1)} copy-done((bf16[12,4,1024]{2,1,0:T(4,128)(2,1)S(1)}, bf16[12,4,1024]{2,1,0:T(4,128)(2,1)}, u32[]{:S(2)}) %copy-start.4) | copy-done | bytes 98328
  2.0 0.7 copy-done.8
  2.7 0.6 qkv.1
  3.3 3.0 %collective-permute-start = (bf16[48,384]{1,0:T(8,128)(2,1)S(1)}, bf16[48,384]{1,0:T(8,128)(2,1)S(1)}, u32[]{:S(2)}, u32[]{:S(2)}) collective-permute-start(bf16[48,384]{1,0:T(8,128)(2,1)S(1)} %qkv.1), channel_id=1, source_target_pairs={{0,8},{4,12},{8,0},{12,4},{16,24},{20,28},{24,16},{28,20},{1,9},{5... | collective-permute-start | bytes 110600 | tf_op jit(solution)/shard_map/ppermute | solution.py:350
  6.3 1.5 %collective-permute-start.1 = (bf16[48,384]{1,0:T(8,128)(2,1)S(1)}, bf16[48,384]{1,0:T(8,128)(2,1)S(1)}, u32[]{:S(2)}, u32[]{:S(2)}) collective-permute-start(bf16[48,384]{1,0:T(8,128)(2,1)S(1)} %qkv.1), channel_id=1, source_target_pairs={{0,16},{4,20},{8,24},{12,28},{16,0},{20,4},{24,8},{28,12},{1,17},{... | collective-permute-start | bytes 110600 | tf_op jit(solution)/shard_map/ppermute | solution.py:350
  7.8 0.4 collective-permute-done
  8.2 2.0 %collective-permute-done.1 = bf16[48,384]{1,0:T(8,128)(2,1)S(1)} collective-permute-done((bf16[48,384]{1,0:T(8,128)(2,1)S(1)}, bf16[48,384]{1,0:T(8,128)(2,1)S(1)}, u32[]{:S(2)}, u32[]{:S(2)}) %collective-permute-start.1) | collective-permute-done | bytes 36896 | tf_op jit(solution)/shard_map/ppermute | solution.py:350
  10.3 2.4 %collective-permute-done.2 = bf16[48,384]{1,0:T(8,128)(2,1)S(1)} collective-permute-done((bf16[48,384]{1,0:T(8,128)(2,1)S(1)}, bf16[48,384]{1,0:T(8,128)(2,1)S(1)}, u32[]{:S(2)}, u32[]{:S(2)}) %collective-permute-start.2) | collective-permute-done | bytes 36896 | tf_op jit(solution)/shard_map/ppermute | solution.py:350
  12.7 0.1 collective-permute-start.3
  12.8 1.4 %collective-permute-done.3.far_ref = bf16[4,48,384]{2,1,0:T(8,128)(2,1)S(1)} collective-permute-done((bf16[4,48,384]{2,1,0:T(8,128)(2,1)S(1)}, bf16[4,48,384]{2,1,0:T(8,128)(2,1)S(1)}, u32[]{:S(2)}, u32[]{:S(2)}) %collective-permute-start.3) | collective-permute-done | bytes 147488 | tf_op jit(solution)/shard_map/ppermute | solution.py:353
  14.1 8.2 %copy-done = bf16[2,12,512,1024]{3,2,1,0:T(8,128)(2,1)S(1)} copy-done((bf16[2,12,512,1024]{3,2,1,0:T(8,128)(2,1)S(1)}, bf16[2,12,512,1024]{3,2,1,0:T(8,128)(2,1)}, u32[]{:S(2)}) %copy-start) | copy-done | bytes 25165848
  22.3 0.7 copy-done.10
  23.0 5.8 %attention.1 = bf16[48,1152]{1,0:T(8,128)(2,1)S(1)} custom-call(s32[1]{0:T(128)} %bitcast.place_ref, s32[12]{0:T(128)S(1)} %copy-done.10, bf16[4,48,384]{2,1,0:T(8,128)(2,1)S(1)} %pad_maximum_fusion.1.near_ref, bf16[4,48,384]{2,1,0:T(8,128)(2,1)S(1)} %collective-permute-done.3.far_ref, bf16[2,12,512,1024]{3,2,1,0:T(8,128)(2,1)S(1)} %copy-done), custom_call_target="tpu_custom_call" | custom-call | tf_op jit(solution)/shard_map/attention/pallas_call | solution.py:412
  28.8 0.1 collective-permute-start.6
  28.9 1.9 %collective-permute-start.4 = (bf16[48,1152]{1,0:T(8,128)(2,1)S(1)}, bf16[48,1152]{1,0:T(8,128)(2,1)S(1)}, u32[]{:S(2)}, u32[]{:S(2)}) collective-permute-start(bf16[48,1152]{1,0:T(8,128)(2,1)S(1)} %attention.1), channel_id=1, source_target_pairs={{0,8},{4,12},{8,0},{12,4},{16,24},{20,28},{24,16},{28,20},{1,9},{5... | collective-permute-start | bytes 331784 | tf_op jit(solution)/shard_map/ppermute | solution.py:350
  30.8 1.5 %collective-permute-start.5 = (bf16[48,1152]{1,0:T(8,128)(2,1)S(1)}, bf16[48,1152]{1,0:T(8,128)(2,1)S(1)}, u32[]{:S(2)}, u32[]{:S(2)}) collective-permute-start(bf16[48,1152]{1,0:T(8,128)(2,1)S(1)} %attention.1), channel_id=1, source_target_pairs={{0,16},{4,20},{8,24},{12,28},{16,0},{20,4},{24,8},{28,12},{1,17},{... | collective-permute-start | bytes 331784 | tf_op jit(solution)/shard_map/ppermute | solution.py:350
  32.3 3.3 %collective-permute-done.6 = bf16[48,1152]{1,0:T(8,128)(2,1)S(1)} collective-permute-done((bf16[48,1152]{1,0:T(8,128)(2,1)S(1)}, bf16[48,1152]{1,0:T(8,128)(2,1)S(1)}, u32[]{:S(2)}, u32[]{:S(2)}) %collective-permute-start.6) | collective-permute-done | bytes 110624 | tf_op jit(solution)/shard_map/ppermute | solution.py:350
  35.6 0.6 collective-permute-done.4
  36.3 1.0 %collective-permute-done.5 = bf16[48,1152]{1,0:T(8,128)(2,1)S(1)} collective-permute-done((bf16[48,1152]{1,0:T(8,128)(2,1)S(1)}, bf16[48,1152]{1,0:T(8,128)(2,1)S(1)}, u32[]{:S(2)}, u32[]{:S(2)}) %collective-permute-start.5) | collective-permute-done | bytes 110624 | tf_op jit(solution)/shard_map/ppermute | solution.py:350
  37.2 0.1 pad_maximum_fusion.near_ref
  37.3 0.1 collective-permute-start.7
  37.4 0.9 %extra.1 = (f32[48,1024]{1,0:T(8,128)S(1)}, f32[48,128]{1,0:T(8,128)S(1)}) custom-call(s32[1]{0:T(128)} %bitcast.place_ref, bf16[4,48,384]{2,1,0:T(8,128)(2,1)S(1)} %pad_maximum_fusion.1.near_ref, bf16[4,48,384]{2,1,0:T(8,128)(2,1)S(1)} %collective-permute-done.3.far_ref, bf16[2,12,4,1024]{3,2,1,0:T(4,128)(2,1)S(1)} %copy-done.7), custom_call_target="tpu_custom_call" | custom-call | tf_op jit(solution)/shard_map/extra/pallas_call | solution.py:426
  38.3 0.9 %collective-permute-done.7.far_ref = bf16[4,48,1152]{2,1,0:T(8,128)(2,1)S(1)} collective-permute-done((bf16[4,48,1152]{2,1,0:T(8,128)(2,1)S(1)}, bf16[4,48,1152]{2,1,0:T(8,128)(2,1)S(1)}, u32[]{:S(2)}, u32[]{:S(2)}) %collective-permute-start.7) | collective-permute-done | bytes 442400 | tf_op jit(solution)/shard_map/ppermute | solution.py:353
  39.2 1.0 %project.1 = bf16[48,128]{1,0:T(8,128)(2,1)S(1)} custom-call(s32[1]{0:T(128)} %bitcast.place_ref, bf16[4,48,1152]{2,1,0:T(8,128)(2,1)S(1)} %pad_maximum_fusion.near_ref, bf16[4,48,1152]{2,1,0:T(8,128)(2,1)S(1)} %collective-permute-done.7.far_ref, f32[48,1024]{1,0:T(8,128)S(1)} %get-tuple-element.15.extra_ref, ...), custom_call_target="tpu_custom_call" | custom-call | tf_op jit(solution)/shard_map/project/pallas_call | solution.py:440
  40.2 0.6 collective-permute-start.8
  40.8 0.6 collective-permute-start.9
  41.3 2.4 %collective-permute-start.10 = (bf16[48,128]{1,0:T(8,128)(2,1)S(1)}, bf16[48,128]{1,0:T(8,128)(2,1)S(1)}, u32[]{:S(2)}, u32[]{:S(2)}) collective-permute-start(bf16[48,128]{1,0:T(8,128)(2,1)S(1)} %project.1), channel_id=1, source_target_pairs={{0,24},{4,28},{8,16},{12,20},{16,8},{20,12},{24,0},{28,4},{1,25},{... | collective-permute-start | bytes 36872 | tf_op jit(solution)/shard_map/ppermute | solution.py:350
  43.7 0.2 collective-permute-done.8
  43.9 0.5 collective-permute-done.9
  44.5 1.5 %collective-permute-done.10 = bf16[48,128]{1,0:T(8,128)(2,1)S(1)} collective-permute-done((bf16[48,128]{1,0:T(8,128)(2,1)S(1)}, bf16[48,128]{1,0:T(8,128)(2,1)S(1)}, u32[]{:S(2)}, u32[]{:S(2)}) %collective-permute-start.10) | collective-permute-done | bytes 12320 | tf_op jit(solution)/shard_map/ppermute | solution.py:350
  45.9 0.1 collective-permute-start.11
  46.0 0.1 copy.14.ids_ref
  46.2 0.5 routing.1
  46.7 0.6 collective-permute-done.11.far_ref
  47.2 1.0 %residual.1 = (bf16[48,1024]{1,0:T(8,128)(2,1)S(1)}, f32[48,1024]{1,0:T(8,128)S(1)}, bf16[4,8,1024]{2,1,0:T(8,128)(2,1)}) custom-call(s32[1]{0:T(128)} %bitcast.place_ref, s32[1]{0:T(128)} %bitcast.1.own_ref, bf16[4,48,128]{2,1,0:T(8,128)(2,1)S(1)} %pad_maximum_fusion.2.near_ref, bf16[4,48,128]{2,1,0:T(8,128)(2,1)S(1)} %collective-permute-done.11.far_ref, ...), custom_call_target="tpu_custom_call" | custom-call | tf_op jit(solution)/shard_map/residual/pallas_call | solution.py:462
  48.2 4.9 %all-to-all-start = ((bf16[4,8,1024]{2,1,0:T(8,128)(2,1)}), bf16[4,8,1024]{2,1,0:T(8,128)(2,1)S(1)}, u32[]{:S(2)}, u32[]{:S(2)}) async-start(bf16[4,8,1024]{2,1,0:T(8,128)(2,1)} %get-tuple-element.21), calls=%async_computation | async-start | bytes 131072 | tf_op jit(solution)/shard_map/all_to_all | solution.py:474
  53.1 5.7 %all-to-all-done.rows_ref = bf16[4,8,1024]{2,1,0:T(8,128)(2,1)S(1)} async-done(((bf16[4,8,1024]{2,1,0:T(8,128)(2,1)}), bf16[4,8,1024]{2,1,0:T(8,128)(2,1)S(1)}, u32[]{:S(2)}, u32[]{:S(2)}) %all-to-all-start) | async-done | bytes 65568 | tf_op jit(solution)/shard_map/all_to_all | solution.py:474
  58.8 2.6 %copy-done.1 = bf16[2,1,1408,1024]{3,2,1,0:T(8,128)(2,1)S(1)} copy-done((bf16[2,1,1408,1024]{3,2,1,0:T(8,128)(2,1)S(1)}, bf16[2,1,1408,1024]{3,2,1,0:T(8,128)(2,1)}, u32[]{:S(2)}) %copy-start.1) | copy-done | bytes 5767192
  61.5 2.3 %expert.1 = (f32[32,512]{1,0:T(8,128)S(1)}, f32[32,512]{1,0:T(8,128)S(1)}) custom-call(s32[1]{0:T(128)S(6)} %and.10.odd_ref, bf16[4,8,1024]{2,1,0:T(8,128)(2,1)S(1)} %all-to-all-done.rows_ref, bf16[2,1,1408,1024]{3,2,1,0:T(8,128)(2,1)S(1)} %copy-done.1, bf16[1,1408,1024]{2,1,0:T(8,128)(2,1)S(1)} %copy-done.2), custom_call_target="tpu_custom_call" | custom-call | tf_op jit(solution)/shard_map/expert/pallas_call | solution.py:484
  63.7 0.1 collective-permute-start.12
  63.8 1.2 %collective-permute-done.12 = f32[32,512]{1,0:T(8,128)S(1)} collective-permute-done((f32[32,512]{1,0:T(8,128)S(1)}, f32[32,512]{1,0:T(8,128)S(1)}, u32[]{:S(2)}, u32[]{:S(2)}) %collective-permute-start.12) | collective-permute-done | bytes 65568 | tf_op jit(solution)/shard_map/ppermute | solution.py:497
  65.1 0.7 broadcast_in_dim.8
  65.8 3.1 %all-to-all-start.1 = ((bf16[32,8,512]{2,1,0:T(8,128)(2,1)}), bf16[32,8,512]{2,1,0:T(8,128)(2,1)S(1)}, u32[]{:S(2)}, u32[]{:S(2)}) async-start(bf16[32,8,512]{2,1,0:T(8,128)(2,1)} %bitcast.17), calls=%async_computation.1 | async-start | bytes 524288 | tf_op jit(solution)/shard_map/all_to_all | solution.py:507
  68.9 0.2 copy.15.router_ref
  69.1 0.3 gate.1.gates_ref
  69.4 9.7 %all-to-all-done.1 = bf16[32,8,512]{2,1,0:T(8,128)(2,1)S(1)} async-done(((bf16[32,8,512]{2,1,0:T(8,128)(2,1)}), bf16[32,8,512]{2,1,0:T(8,128)(2,1)S(1)}, u32[]{:S(2)}, u32[]{:S(2)}) %all-to-all-start.1) | async-done | bytes 262176 | tf_op jit(solution)/shard_map/all_to_all | solution.py:507
  79.1 0.9 %final.1 = bf16[12,4,1024]{2,1,0:T(4,128)(2,1)} custom-call(f32[48,128]{1,0:T(8,128)S(1)} %gate.1.gates_ref, bf16[8,4,8,512]{3,2,1,0:T(8,128)(2,1)S(1)} %bitcast.20, f32[48,1024]{1,0:T(8,128)S(1)} %get-tuple-element.24.residual_ref), custom_call_target="tpu_custom_call" | custom-call | tf_op jit(solution)/shard_map/final/pallas_call | solution.py:515
  (26 shorter events, 0.1 us)
Async XLA Ops:
  0.0 1.1 %copy-start.3 = (bf16[384,1024]{1,0:T(8,128)(2,1)S(1)}, bf16[384,1024]{1,0:T(8,128)(2,1)}, u32[]{:S(2)}) copy-start(bf16[384,1024]{1,0:T(8,128)(2,1)} %weight_ref.2) | copy-start | bytes 2359300
  1.1 0.9 %copy-start.4 = (bf16[12,4,1024]{2,1,0:T(4,128)(2,1)S(1)}, bf16[12,4,1024]{2,1,0:T(4,128)(2,1)}, u32[]{:S(2)}) copy-start(bf16[12,4,1024]{2,1,0:T(4,128)(2,1)} %tokens_ref.3) | copy-start | bytes 294916
  2.0 0.7 copy-start.8
  3.3 4.9 %collective-permute-start = (bf16[48,384]{1,0:T(8,128)(2,1)S(1)}, bf16[48,384]{1,0:T(8,128)(2,1)S(1)}, u32[]{:S(2)}, u32[]{:S(2)}) collective-permute-start(bf16[48,384]{1,0:T(8,128)(2,1)S(1)} %qkv.1), channel_id=1, source_target_pairs={{0,8},{4,12},{8,0},{12,4},{16,24},{20,28},{24,16},{28,20},{1,9},{5... | collective-permute-start | bytes 110600 | tf_op jit(solution)/shard_map/ppermute | solution.py:350
  6.3 4.0 %collective-permute-start.1 = (bf16[48,384]{1,0:T(8,128)(2,1)S(1)}, bf16[48,384]{1,0:T(8,128)(2,1)S(1)}, u32[]{:S(2)}, u32[]{:S(2)}) collective-permute-start(bf16[48,384]{1,0:T(8,128)(2,1)S(1)} %qkv.1), channel_id=1, source_target_pairs={{0,16},{4,20},{8,24},{12,28},{16,0},{20,4},{24,8},{28,12},{1,17},{... | collective-permute-start | bytes 110600 | tf_op jit(solution)/shard_map/ppermute | solution.py:350
  7.8 4.9 %collective-permute-start.2 = (bf16[48,384]{1,0:T(8,128)(2,1)S(1)}, bf16[48,384]{1,0:T(8,128)(2,1)S(1)}, u32[]{:S(2)}, u32[]{:S(2)}) collective-permute-start(bf16[48,384]{1,0:T(8,128)(2,1)S(1)} %qkv.1), channel_id=1, source_target_pairs={{0,24},{4,28},{8,16},{12,20},{16,8},{20,12},{24,0},{28,4},{1,25},{... | collective-permute-start | bytes 110600 | tf_op jit(solution)/shard_map/ppermute | solution.py:350
  12.7 1.4 %collective-permute-start.3 = (bf16[4,48,384]{2,1,0:T(8,128)(2,1)S(1)}, bf16[4,48,384]{2,1,0:T(8,128)(2,1)S(1)}, u32[]{:S(2)}, u32[]{:S(2)}) collective-permute-start(bf16[4,48,384]{2,1,0:T(8,128)(2,1)S(1)} %pad_maximum_fusion.1.near_ref), channel_id=1, source_target_pairs={{0,4},{4,0},{8,12},{12,8},{16,20},{20,16},{24,28},{28,24},{1,5},{5... | collective-permute-start | bytes 442376 | tf_op jit(solution)/shard_map/ppermute | solution.py:353
  14.1 8.2 %copy-start = (bf16[2,12,512,1024]{3,2,1,0:T(8,128)(2,1)S(1)}, bf16[2,12,512,1024]{3,2,1,0:T(8,128)(2,1)}, u32[]{:S(2)}) copy-start(bf16[2,12,512,1024]{3,2,1,0:T(8,128)(2,1)} %window_ref.1) | copy-start | bytes 75497472
  22.3 0.7 copy-start.10
  23.0 14.4 %copy-start.7 = (bf16[2,12,4,1024]{3,2,1,0:T(4,128)(2,1)S(1)}, bf16[2,12,4,1024]{3,2,1,0:T(4,128)(2,1)}, u32[]{:S(2)}) copy-start(bf16[2,12,4,1024]{3,2,1,0:T(4,128)(2,1)} %sinks_ref.1) | copy-start | bytes 589828
  23.0 16.2 %copy-start.6 = (bf16[128,1024]{1,0:T(8,128)(2,1)S(1)}, bf16[128,1024]{1,0:T(8,128)(2,1)}, u32[]{:S(2)}) copy-start(bf16[128,1024]{1,0:T(8,128)(2,1)} %weight_ref.3) | copy-start | bytes 786436
  23.0 23.1 %copy-start.13 = (s32[12,4,2]{0,2,1:T(2,128)S(1)}, s32[12,4,2]{0,2,1:T(2,128)}, u32[]{:S(2)}) copy-start(s32[12,4,2]{0,2,1:T(2,128)} %param.22) | copy-start | bytes 1156
  23.0 23.2 %copy-start.11 = (s32[1,48]{1,0:T(1,128)S(1)}, s32[1,48]{1,0:T(1,128)}, u32[]{:S(2)}) copy-start(s32[1,48]{1,0:T(1,128)} %order_ref.1) | copy-start | bytes 580
  23.0 24.3 %copy-start.5 = (bf16[12,4,1024]{2,1,0:T(4,128)(2,1)S(1)}, bf16[12,4,1024]{2,1,0:T(4,128)(2,1)}, u32[]{:S(2)}) copy-start(bf16[12,4,1024]{2,1,0:T(4,128)(2,1)} %tokens_ref.3) | copy-start | bytes 294916
  23.0 24.3 %copy-start.9 = (f32[1024]{0:T(1024)S(1)}, f32[1024]{0:T(1024)}, u32[]{:S(2)}) copy-start(f32[1024]{0:T(1024)} %param.20) | copy-start | bytes 12292
  23.0 35.8 %copy-start.2 = (bf16[1,1408,1024]{2,1,0:T(8,128)(2,1)S(1)}, bf16[1,1408,1024]{2,1,0:T(8,128)(2,1)}, u32[]{:S(2)}) copy-start(bf16[1,1408,1024]{2,1,0:T(8,128)(2,1)} %down_ref.1) | copy-start | bytes 8650756
  28.8 6.9 %collective-permute-start.6 = (bf16[48,1152]{1,0:T(8,128)(2,1)S(1)}, bf16[48,1152]{1,0:T(8,128)(2,1)S(1)}, u32[]{:S(2)}, u32[]{:S(2)}) collective-permute-start(bf16[48,1152]{1,0:T(8,128)(2,1)S(1)} %attention.1), channel_id=1, source_target_pairs={{0,24},{4,28},{8,16},{12,20},{16,8},{20,12},{24,0},{28,4},{1,25},{... | collective-permute-start | bytes 331784 | tf_op jit(solution)/shard_map/ppermute | solution.py:350
  28.9 7.4 %collective-permute-start.4 = (bf16[48,1152]{1,0:T(8,128)(2,1)S(1)}, bf16[48,1152]{1,0:T(8,128)(2,1)S(1)}, u32[]{:S(2)}, u32[]{:S(2)}) collective-permute-start(bf16[48,1152]{1,0:T(8,128)(2,1)S(1)} %attention.1), channel_id=1, source_target_pairs={{0,8},{4,12},{8,0},{12,4},{16,24},{20,28},{24,16},{28,20},{1,9},{5... | collective-permute-start | bytes 331784 | tf_op jit(solution)/shard_map/ppermute | solution.py:350
  30.8 6.4 %collective-permute-start.5 = (bf16[48,1152]{1,0:T(8,128)(2,1)S(1)}, bf16[48,1152]{1,0:T(8,128)(2,1)S(1)}, u32[]{:S(2)}, u32[]{:S(2)}) collective-permute-start(bf16[48,1152]{1,0:T(8,128)(2,1)S(1)} %attention.1), channel_id=1, source_target_pairs={{0,16},{4,20},{8,24},{12,28},{16,0},{20,4},{24,8},{28,12},{1,17},{... | collective-permute-start | bytes 331784 | tf_op jit(solution)/shard_map/ppermute | solution.py:350
  37.3 1.9 %collective-permute-start.7 = (bf16[4,48,1152]{2,1,0:T(8,128)(2,1)S(1)}, bf16[4,48,1152]{2,1,0:T(8,128)(2,1)S(1)}, u32[]{:S(2)}, u32[]{:S(2)}) collective-permute-start(bf16[4,48,1152]{2,1,0:T(8,128)(2,1)S(1)} %pad_maximum_fusion.near_ref), channel_id=1, source_target_pairs={{0,4},{4,0},{8,12},{12,8},{16,20},{20,16},{24,28},{28,24},{1,5},{5... | collective-permute-start | bytes 1327112 | tf_op jit(solution)/shard_map/ppermute | solution.py:353
  39.2 29.7 %copy-start.12 = (bf16[1024,16]{0,1:T(8,128)(2,1)S(1)}, bf16[1024,16]{0,1:T(8,128)(2,1)}, u32[]{:S(2)}) copy-start(bf16[1024,16]{0,1:T(8,128)(2,1)} %param.21) | copy-start | bytes 98308
  40.2 3.8 %collective-permute-start.8 = (bf16[48,128]{1,0:T(8,128)(2,1)S(1)}, bf16[48,128]{1,0:T(8,128)(2,1)S(1)}, u32[]{:S(2)}, u32[]{:S(2)}) collective-permute-start(bf16[48,128]{1,0:T(8,128)(2,1)S(1)} %project.1), channel_id=1, source_target_pairs={{0,8},{4,12},{8,0},{12,4},{16,24},{20,28},{24,16},{28,20},{1,9},{5... | collective-permute-start | bytes 36872 | tf_op jit(solution)/shard_map/ppermute | solution.py:350
  40.8 3.7 %collective-permute-start.9 = (bf16[48,128]{1,0:T(8,128)(2,1)S(1)}, bf16[48,128]{1,0:T(8,128)(2,1)S(1)}, u32[]{:S(2)}, u32[]{:S(2)}) collective-permute-start(bf16[48,128]{1,0:T(8,128)(2,1)S(1)} %project.1), channel_id=1, source_target_pairs={{0,16},{4,20},{8,24},{12,28},{16,0},{20,4},{24,8},{28,12},{1,17},{... | collective-permute-start | bytes 36872 | tf_op jit(solution)/shard_map/ppermute | solution.py:350
  41.3 4.6 %collective-permute-start.10 = (bf16[48,128]{1,0:T(8,128)(2,1)S(1)}, bf16[48,128]{1,0:T(8,128)(2,1)S(1)}, u32[]{:S(2)}, u32[]{:S(2)}) collective-permute-start(bf16[48,128]{1,0:T(8,128)(2,1)S(1)} %project.1), channel_id=1, source_target_pairs={{0,24},{4,28},{8,16},{12,20},{16,8},{20,12},{24,0},{28,4},{1,25},{... | collective-permute-start | bytes 36872 | tf_op jit(solution)/shard_map/ppermute | solution.py:350
  45.9 1.3 %collective-permute-start.11 = (bf16[4,48,128]{2,1,0:T(8,128)(2,1)S(1)}, bf16[4,48,128]{2,1,0:T(8,128)(2,1)S(1)}, u32[]{:S(2)}, u32[]{:S(2)}) collective-permute-start(bf16[4,48,128]{2,1,0:T(8,128)(2,1)S(1)} %pad_maximum_fusion.2.near_ref), channel_id=1, source_target_pairs={{0,4},{4,0},{8,12},{12,8},{16,20},{20,16},{24,28},{28,24},{1,5},{5... | collective-permute-start | bytes 147464 | tf_op jit(solution)/shard_map/ppermute | solution.py:353
  48.2 10.6 %all-to-all-start = ((bf16[4,8,1024]{2,1,0:T(8,128)(2,1)}), bf16[4,8,1024]{2,1,0:T(8,128)(2,1)S(1)}, u32[]{:S(2)}, u32[]{:S(2)}) async-start(bf16[4,8,1024]{2,1,0:T(8,128)(2,1)} %get-tuple-element.21), calls=%async_computation | async-start | bytes 131072 | tf_op jit(solution)/shard_map/all_to_all | solution.py:474
  58.8 2.6 %copy-start.1 = (bf16[2,1,1408,1024]{3,2,1,0:T(8,128)(2,1)S(1)}, bf16[2,1,1408,1024]{3,2,1,0:T(8,128)(2,1)}, u32[]{:S(2)}) copy-start(bf16[2,1,1408,1024]{3,2,1,0:T(8,128)(2,1)} %in_ref.1) | copy-start | bytes 17301508
  63.7 1.3 %collective-permute-start.12 = (f32[32,512]{1,0:T(8,128)S(1)}, f32[32,512]{1,0:T(8,128)S(1)}, u32[]{:S(2)}, u32[]{:S(2)}) collective-permute-start(f32[32,512]{1,0:T(8,128)S(1)} %get-tuple-element.23), channel_id=1, source_target_pairs={{0,4},{4,0},{8,12},{12,8},{16,20},{20,16},{24,28},{28,24},{1,5},{5... | collective-permute-start | bytes 196616 | tf_op jit(solution)/shard_map/ppermute | solution.py:497
  65.8 13.3 %all-to-all-start.1 = ((bf16[32,8,512]{2,1,0:T(8,128)(2,1)}), bf16[32,8,512]{2,1,0:T(8,128)(2,1)S(1)}, u32[]{:S(2)}, u32[]{:S(2)}) async-start(bf16[32,8,512]{2,1,0:T(8,128)(2,1)} %bitcast.17), calls=%async_computation.1 | async-start | bytes 524288 | tf_op jit(solution)/shard_map/all_to_all | solution.py:507

commit v3 on v2

--- a/solution.py
+++ b/solution.py
@@ -16,6 +16,7 @@
 CAP = 8
 LANES = 128
 PIECES = 3
+EARLY = 3
 BLOCK = 256
 BLOCK_HEADS = BLOCK // HD
 
@@ -32,6 +33,14 @@
 
 def params(limit_mib=32):
     return pltpu.CompilerParams(vmem_limit_bytes=limit_mib * MIB)
+
+
+def moving(count):
+    return pl.CostEstimate(flops=0, bytes_accessed=count, transcendentals=0)
+
+
+def in_hbm(value):
+    return pltpu.with_memory_space_constraint(value, pltpu.HBM)
 
 
 def split(value, count):
@@ -82,11 +91,60 @@
     return (row_head == col_head).astype(jnp.float32)
 
 
+def fetch_window_kernel(
+    early, sent_ref, window_ref, lengths_ref, held_ref, keys_ref, values_ref, spans_ref, numbers_ref, sems
+):
+    copies = [
+        pltpu.make_async_copy(lengths_ref, numbers_ref, sems.at[0]),
+        pltpu.make_async_copy(window_ref.at[0], keys_ref, sems.at[1]),
+        pltpu.make_async_copy(window_ref.at[1, pl.ds(0, early)], values_ref, sems.at[2]),
+    ]
+    for copy in copies:
+        copy.start()
+    held_ref[...] = sent_ref[...]
+    copies[0].wait()
+    for r in range(spans_ref.shape[0]):
+        spans_ref[r : r + 1, :] = jnp.full((1, LANES), numbers_ref[r], jnp.int32)
+    copies[1].wait()
+    copies[2].wait()
+
+
+def fetch_experts_kernel(sent_ref, in_ref, down_ref, held_ref, in_out, down_out, sems):
+    copies = [
+        pltpu.make_async_copy(in_ref, in_out, sems.at[0]),
+        pltpu.make_async_copy(down_ref, down_out, sems.at[1]),
+    ]
+    for copy in copies:
+        copy.start()
+    held_ref[...] = sent_ref[...]
+    for copy in copies:
+        copy.wait()
+
+
 def attention_kernel(
-    place_ref, lengths_ref, near_ref, far_ref, window_ref, out_ref, ordered_ref, flat_ref, query_ref
+    place_ref,
+    spans_ref,
+    near_ref,
+    far_ref,
+    keys_ref,
+    values_ref,
+    window_ref,
+    out_ref,
+    ordered_ref,
+    flat_ref,
+    query_ref,
+    late_ref,
+    sems,
 ):
     devices, rows, share = ordered_ref.shape
-    _, requests, span, width = window_ref.shape
+    requests, span, width = keys_ref.shape
+    early = values_ref.shape[0]
+    late = [
+        pltpu.make_async_copy(window_ref.at[1, r], late_ref.at[r - early], sems.at[r - early])
+        for r in range(early, requests)
+    ]
+    for copy in late:
+        copy.start()
     steps = rows // requests
     block_rows = BLOCK_HEADS * steps
     place = place_ref[0]
@@ -112,13 +170,13 @@
 
     def score(r):
         return jnp.concatenate(
-            [dot(query_ref[r, :, c], window_ref[0, r, :, c], ROWS_BY_ROWS) for c in cols], axis=0
+            [dot(query_ref[r, :, c], keys_ref[r, :, c], ROWS_BY_ROWS) for c in cols], axis=0
         )
 
     scores = score(0)
     for r in range(requests):
         following = score(r + 1) if r + 1 < requests else None
-        length = lengths_ref[r]
+        length = spans_ref[r : r + 1, 0:1]
         age = jnp.bitwise_and(slot - (length - SINKS), WIN - 1)
         live = ((slot < jnp.minimum(WIN, length - SINKS)) & (age > step))[None]
         scores = jnp.where(live, scores.reshape(tiles, pair, span) * scale, MASKED)
@@ -126,10 +184,13 @@
         weight = jnp.where(live, jnp.exp(scores - peak), 0.0)
         total = jnp.sum(weight, axis=-1, keepdims=True)
         weight = weight.reshape(HEADS * steps, span).astype(jnp.bfloat16)
+        if r >= early:
+            late[r - early].wait()
+        values = values_ref.at[r] if r < early else late_ref.at[r - early]
         outs = []
         for b, c in enumerate(cols):
             own = slice(b * block_rows, (b + 1) * block_rows)
-            mixed = dot(weight[own], window_ref[1, r, :, c]) * own_head[:, c]
+            mixed = dot(weight[own], values[:, c]) * own_head[:, c]
             mixed = sum(mixed[i : i + pair] for i in range(0, block_rows, pair))
             outs.append(mixed[:steps] + mixed[steps:])
         stats = jnp.zeros((HEADS * steps, LANES), jnp.float32)
@@ -277,9 +338,9 @@
     turned_ref,
     normed_ref,
     residual_ref,
-    send_ref,
-    ordered_ref,
+    *send_and_ordered_refs,
 ):
+    *send_refs, ordered_ref = send_and_ordered_refs
     devices, rows, share = ordered_ref.shape
     in_order(place_ref[0], near_ref, far_ref, ordered_ref)
     copy_rows(tokens_ref, residual_ref)
@@ -288,12 +349,11 @@
         residual_ref[:, own] = residual_ref[:, own] + ordered_ref[d].astype(jnp.float32)
     normed = rms_rows(residual_ref[...], gain_ref[...])
     normed_ref[...] = normed
-    groups = send_ref.shape[0]
-    local_experts = EXPERTS // groups
-    for g in range(groups):
-        first = pl.multiple_of((g * local_experts + own_ref[0]) * CAP, CAP)
-        picking = turned_ref[pl.ds(first, CAP), :].astype(jnp.bfloat16)
-        send_ref[g] = dot(picking, normed).astype(jnp.bfloat16)
+    local_experts = EXPERTS // len(send_refs)
+    for k, send_ref in enumerate(send_refs):
+        expert = jnp.bitwise_xor(own_ref[1], k) * local_experts + own_ref[0]
+        picking = turned_ref[pl.ds(pl.multiple_of(expert * CAP, CAP), CAP), :].astype(jnp.bfloat16)
+        send_ref[...] = dot(picking, normed).astype(jnp.bfloat16)
 
 
 def gate_kernel(normed_ref, router_ref, select_ref, chosen_ref, out_ref):
@@ -305,17 +365,29 @@
     out_ref[...] = gates
 
 
-def expert_kernel(odd_ref, rows_ref, in_ref, down_ref, keep_ref, send_ref):
+def expert_kernel(place_ref, own_ref, in_ref, down_ref, *refs):
+    *received_refs, keep_ref, send_ref, rows_ref = refs
     groups, slots, width = rows_ref.shape
-    rows = rows_ref[...].reshape(groups * slots, width)
+    for k, received_ref in enumerate(received_refs):
+        rows_ref[jnp.bitwise_xor(own_ref[1], k)] = received_ref[...].astype(jnp.float32)
+    rows = rows_ref[...].reshape(groups * slots, width).astype(jnp.bfloat16)
     gate = dot(rows, in_ref[0, 0], ROWS_BY_ROWS)
     up = dot(rows, in_ref[1, 0], ROWS_BY_ROWS)
     hidden = (jax.nn.gelu(gate, approximate=True) * up).astype(jnp.bfloat16)
     outputs = dot(hidden, down_ref[0])
     half = width // 2
-    odd = odd_ref[0] == 1
+    odd = jnp.bitwise_and(place_ref[0], 1) == 1
     keep_ref[...] = jnp.where(odd, outputs[:, half:], outputs[:, :half])
     send_ref[...] = jnp.where(odd, outputs[:, :half], outputs[:, half:])
+
+
+def spread_kernel(kept_ref, other_ref, out_ref):
+    slots = out_ref.shape[1]
+    groups = kept_ref.shape[0] // slots
+    outputs = kept_ref[...] + other_ref[...]
+    for block in range(out_ref.shape[0]):
+        first = block % groups * slots
+        out_ref[block] = outputs[first : first + slots].astype(jnp.bfloat16)
 
 
 def column_block(sharer, sharers):
@@ -344,11 +416,13 @@
         out_ref[r] = total[r * steps : (r + 1) * steps].astype(jnp.bfloat16)
 
 
-def gather_seq(values):
+def gather_seq(values, meanwhile=None):
     count = lax.axis_size("seq")
     others = [
         lax.ppermute(values, "seq", [(i, i ^ k) for i in range(count)]) for k in range(2, count, 2)
     ]
+    if meanwhile is not None:
+        values = meanwhile(values)
     near = jnp.stack([values] + others)
     far = lax.ppermute(near, "seq", [(i, i ^ 1) for i in range(count)])
     return near, far
@@ -380,7 +454,7 @@
     groups = lax.axis_size("exp")
     local_experts = EXPERTS // groups
     sharers = seq_count // local_experts
-    own_expert = (seq_index // sharers).astype(jnp.int32).reshape(1)
+    own_expert = jnp.stack([seq_index // sharers, lax.axis_index("exp")]).astype(jnp.int32)
     place = seq_index.astype(jnp.int32).reshape(1)
     span = window_cache.shape[2]
     share = w_qkv.shape[0]
@@ -389,12 +463,12 @@
 
     smem = pl.BlockSpec(memory_space=pltpu.SMEM)
     vmem = pl.BlockSpec(memory_space=pltpu.VMEM)
-    anywhere = pl.BlockSpec(memory_space=pl.ANY)
+    hbm = pl.BlockSpec(memory_space=pltpu.HBM)
 
     gain_row = attn_gain.reshape(1, width)
     local_mix = pl.pallas_call(
         qkv_kernel,
-        in_specs=[anywhere] * 3,
+        in_specs=[hbm] * 3,
         out_shape=shape((rows, share), bf16),
         scratch_shapes=[
             pltpu.VMEM(tokens.shape, bf16),
@@ -405,23 +479,63 @@
         ],
         compiler_params=params(4),
         name="qkv",
-    )(tokens, gain_row, w_qkv)
-    near_mix, far_mix = gather_seq(local_mix)
+    )(in_hbm(tokens), in_hbm(gain_row), in_hbm(w_qkv))
+    early = min(EARLY, requests - 1)
+    fetched = {}
+
+    def fetch_window(values):
+        held, *fetched["window"] = pl.pallas_call(
+            functools.partial(fetch_window_kernel, early),
+            in_specs=[vmem, hbm, hbm],
+            out_shape=(
+                shape(values.shape, bf16),
+                shape((requests, span, width), bf16),
+                shape((early, span, width), bf16),
+                shape((requests, LANES), jnp.int32),
+            ),
+            scratch_shapes=[pltpu.SMEM((requests,), jnp.int32), pltpu.SemaphoreType.DMA((3,))],
+            compiler_params=params(8),
+            cost_estimate=moving(window_cache.size),
+            name="fetch_window",
+        )(values, in_hbm(window_cache), in_hbm(lengths))
+        return held
+
+    def fetch_experts(values):
+        held, *fetched["experts"] = pl.pallas_call(
+            fetch_experts_kernel,
+            in_specs=[vmem, hbm, hbm],
+            out_shape=(
+                shape(values.shape, bf16),
+                shape(expert_in.shape, bf16),
+                shape(expert_down.shape, bf16),
+            ),
+            scratch_shapes=[pltpu.SemaphoreType.DMA((2,))],
+            compiler_params=params(8),
+            cost_estimate=moving(2 * (expert_in.size + expert_down.size)),
+            name="fetch_experts",
+        )(values, in_hbm(expert_in), in_hbm(expert_down))
+        return held
+
+    near_mix, far_mix = gather_seq(local_mix, fetch_window)
+    keys, values, spans = fetched["window"]
 
     padded = width + LANES
     part = pl.pallas_call(
         attention_kernel,
-        in_specs=[smem, smem, vmem, vmem, vmem],
+        in_specs=[smem] + [vmem] * 5 + [hbm],
         out_shape=shape((rows, padded), bf16),
         scratch_shapes=[
             pltpu.VMEM((seq_count, rows, share), bf16),
             pltpu.VMEM((rows, padded), f32),
             pltpu.VMEM((requests, BLOCK_HEADS * steps, width), bf16),
+            pltpu.VMEM((requests - early, span, width), bf16),
+            pltpu.SemaphoreType.DMA((requests - early,)),
         ],
-        compiler_params=params(8),
+        compiler_params=params(20),
         name="attention",
-    )(place, lengths, near_mix, far_mix, window_cache)
-    near_part, far_part = gather_seq(part)
+    )(place, spans, near_mix, far_mix, keys, values, in_hbm(window_cache))
+    near_part, far_part = gather_seq(part, fetch_experts)
+    local_in, local_down = fetched["experts"]
 
     extra, extra_stats = pl.pallas_call(
         extra_kernel,
@@ -459,19 +573,22 @@
         name="routing",
     )(expert_ids, slot_order)
 
-    normed, residual, send = pl.pallas_call(
+    normed, residual, *send = pl.pallas_call(
         residual_kernel,
         in_specs=[smem, smem] + [vmem] * 5,
         out_shape=(
             shape((rows, width), bf16),
             shape((rows, width), f32),
-            shape((groups, CAP, width), bf16),
+            *[shape((CAP, width), bf16)] * groups,
         ),
         scratch_shapes=[pltpu.VMEM((seq_count, rows, w_out.shape[0]), bf16)],
         compiler_params=params(8),
         name="residual",
     )(place, own_expert, near_proj, far_proj, tokens, moe_gain.reshape(1, width), turned)
-    received = lax.all_to_all(send, "exp", split_axis=0, concat_axis=0, tiled=True)
+    received = [
+        lax.ppermute(block, "exp", [(i, i ^ k) for i in range(groups)]) if k else block
+        for k, block in enumerate(send)
+    ]
 
     gates = pl.pallas_call(
         gate_kernel,
@@ -480,32 +597,36 @@
         name="gate",
     )(normed, router, select, chosen)
 
-    odd = jnp.bitwise_and(place, 1)
     kept, sent = pl.pallas_call(
         expert_kernel,
-        in_specs=[smem] + [vmem] * 3,
+        in_specs=[smem, smem] + [vmem] * (2 + groups),
         out_shape=(
             shape((groups * CAP, width // 2), f32),
             shape((groups * CAP, width // 2), f32),
         ),
+        scratch_shapes=[pltpu.VMEM((groups, CAP, width), f32)],
         compiler_params=params(8),
         name="expert",
-    )(odd, received, expert_in, expert_down)
+    )(place, own_expert, local_in, local_down, *received)
 
     reach = 1
     while True:
-        kept = kept + lax.ppermute(sent, "seq", [(i, i ^ reach) for i in range(seq_count)])
+        other = lax.ppermute(sent, "seq", [(i, i ^ reach) for i in range(seq_count)])
         reach *= 2
         if reach >= sharers:
             break
         upper = (seq_index // reach) % 2 == 1
-        low, high = jnp.split(kept, 2, axis=1)
+        low, high = jnp.split(kept + other, 2, axis=1)
         kept, sent = jnp.where(upper, high, low), jnp.where(upper, low, high)
     columns = kept.shape[1]
-    outgoing = kept.astype(bf16).reshape(1, groups, CAP, columns)
-    outgoing = jnp.broadcast_to(outgoing, (seq_count, groups, CAP, columns))
+    outgoing = pl.pallas_call(
+        spread_kernel,
+        out_shape=shape((seq_count * groups, CAP, columns), bf16),
+        compiler_params=params(8),
+        name="spread",
+    )(kept, other)
     returned = lax.all_to_all(
-        outgoing.reshape(seq_count * groups, CAP, columns),
+        outgoing,
         ("seq", "exp"),
         split_axis=0,
         concat_axis=0,

time: 80.4 us -> 82.9 us (1.031)
  Pallas kernels: 13.1 us -> 25.1 us
  waiting for transfers between devices: 31.4 us -> 23.6 us
  starting transfers between devices: 19.9 us -> 19 us
    pallas_call x3 -> x6, Pallas kernels: 8.61 us -> 20.8 us  [the longest x1 6.56 us: body(): pl.pallas_call(attention_kernel, in_specs=[smem] + [vmem] * 5 + [hbm], ou...]
    ppermute x9, waiting for transfers between devices: 11.9 us -> 4.57 us  [gather_seq(): lax.ppermute(values, 'seq', [(i, i ^ k) for i in range(count)])]
    all_to_all x2 -> x1, waiting for transfers between devices: 15.5 us -> 9.74 us  [body(): lax.all_to_all(outgoing, ('seq', 'exp'), split_axis=0, concat_axis=0, til...]
    all_to_all x2 -> x1, starting transfers between devices: 7.97 us -> 2.58 us  [body(): lax.all_to_all(outgoing, ('seq', 'exp'), split_axis=0, concat_axis=0, til...]
    ppermute x0 -> x3, waiting for transfers between devices: none -> 5.31 us  [body(): lax.ppermute(block, 'exp', [(i, i ^ k) for i in range(groups)])]
    ppermute x0 -> x3, starting transfers between devices: none -> 4.45 us  [body(): lax.ppermute(block, 'exp', [(i, i ^ k) for i in range(groups)])]
    unnamed x30 -> x24, local copies, waits for them, and re-layouts: 14.5 us -> 14.5 us
  transfers between devices with their start and end apart: 15 -> 17, of which waited for: 15 -> 10; matrix products, arithmetic and copies ran while one was open for 0% -> 0% of each run, Pallas kernels for 2% -> 13%
where the time goes in v3:
time: 82.9 us; the launch traced here: 82.7 us
  Pallas kernels  25.1 us (30%)
  waiting for transfers between devices  23.6 us (28%)
  starting transfers between devices  19 us (23%)
  local copies, waits for them, and re-layouts  14.5 us (17%)
    unnamed x24, local copies, waits for them, and re-layouts  14.5 us
    ppermute x9, starting transfers between devices, gather_seq(): lax.ppermute(values, 'seq', [(i, i ^ k) for i in range(count)])  11.7 us
    all_to_all x1, waiting for transfers between devices, body(): lax.all_to_all(outgoing, ('seq', 'exp'), split_axis=0, concat_axis=0, til...  9.74 us
    pallas_call x1, Pallas kernels, body(): pl.pallas_call(attention_kernel, in_specs=[smem] + [vmem] * 5 + [hbm], ou...  6.56 us
    pallas_call x1, Pallas kernels, fetch_window(): pl.pallas_call(functools.partial(fetch_window_kernel, early), in_specs=[v...  5.5 us
    ppermute x3, waiting for transfers between devices, body(): lax.ppermute(block, 'exp', [(i, i ^ k) for i in range(groups)])  5.31 us
    ppermute x9, waiting for transfers between devices, gather_seq(): lax.ppermute(values, 'seq', [(i, i ^ k) for i in range(count)])  4.57 us
    ppermute x3, starting transfers between devices, body(): lax.ppermute(block, 'exp', [(i, i ^ k) for i in range(groups)])  4.45 us
  transfers between devices with their start and end apart: 17, of which 10 were waited for; matrix products, arithmetic and copies ran while one was open for 0% of the time, Pallas kernels for 13%

profile of v3, /device:TPU:0, one launch (start us, length us, event | category | flops | bytes accessed | tf_op | source)
XLA Modules:
  0.0 82.7 jit_solution(5852572389639669828)
XLA Ops:
  0.0 1.6 %qkv.1.sent_ref = bf16[48,384]{1,0:T(8,128)(2,1)S(1)} custom-call(bf16[12,4,1024]{2,1,0:T(4,128)(2,1)} %tokens_ref.3, f32[1,1024]{1,0:T(1,128)} %bitcast.32, bf16[384,1024]{1,0:T(8,128)(2,1)} %weight_ref.2), custom_call_target="tpu_custom_call" | custom-call | tf_op jit(solution)/shard_map/qkv/pallas_call | solution.py:469
  1.6 3.0 %collective-permute-start = (bf16[48,384]{1,0:T(8,128)(2,1)S(1)}, bf16[48,384]{1,0:T(8,128)(2,1)S(1)}, u32[]{:S(2)}, u32[]{:S(2)}) collective-permute-start(bf16[48,384]{1,0:T(8,128)(2,1)S(1)} %qkv.1.sent_ref), channel_id=1, source_target_pairs={{0,8},{4,12},{8,0},{12,4},{16,24},{20,28},{24,16},{28,20},{1,9},{5... | collective-permute-start | bytes 110600 | tf_op jit(solution)/shard_map/ppermute | solution.py:422
  4.6 1.5 %collective-permute-start.1 = (bf16[48,384]{1,0:T(8,128)(2,1)S(1)}, bf16[48,384]{1,0:T(8,128)(2,1)S(1)}, u32[]{:S(2)}, u32[]{:S(2)}) collective-permute-start(bf16[48,384]{1,0:T(8,128)(2,1)S(1)} %qkv.1.sent_ref), channel_id=1, source_target_pairs={{0,16},{4,20},{8,24},{12,28},{16,0},{20,4},{24,8},{28,12},{1,17},{... | collective-permute-start | bytes 110600 | tf_op jit(solution)/shard_map/ppermute | solution.py:422
  6.2 0.0 collective-permute-start.2
  6.2 5.5 %fetch_window.1 = (bf16[48,384]{1,0:T(8,128)(2,1)S(1)}, bf16[12,512,1024]{2,1,0:T(8,128)(2,1)S(1)}, bf16[3,512,1024]{2,1,0:T(8,128)(2,1)S(1)}, s32[12,128]{1,0:T(8,128)S(1)}) custom-call(bf16[48,384]{1,0:T(8,128)(2,1)S(1)} %qkv.1.sent_ref, bf16[2,12,512,1024]{3,2,1,0:T(8,128)(2,1)} %window_ref.3, s32[12]{0:T(128)} %lengths_ref.1), custom_call_target="tpu_custom_call" | custom-call | bytes 12582912 | tf_op jit(solution)/shard_map/fetch_window/pallas_call | solution.py:487
  11.7 4.5 %copy-done = bf16[12,512,1024]{2,1,0:T(8,128)(2,1)} copy-done((bf16[12,512,1024]{2,1,0:T(8,128)(2,1)}, bf16[12,512,1024]{2,1,0:T(8,128)(2,1)S(1)}, u32[]{:S(2)}) %copy-start) | copy-done | bytes 12582936
  16.2 0.1 collective-permute-start.3
  16.3 1.4 %collective-permute-done.3.far_ref = bf16[4,48,384]{2,1,0:T(8,128)(2,1)S(1)} collective-permute-done((bf16[4,48,384]{2,1,0:T(8,128)(2,1)S(1)}, bf16[4,48,384]{2,1,0:T(8,128)(2,1)S(1)}, u32[]{:S(2)}, u32[]{:S(2)}) %collective-permute-start.3) | collective-permute-done | bytes 147488 | tf_op jit(solution)/shard_map/ppermute | solution.py:427
  17.7 4.6 %copy-done.1 = bf16[12,512,1024]{2,1,0:T(8,128)(2,1)S(1)} copy-done((bf16[12,512,1024]{2,1,0:T(8,128)(2,1)S(1)}, bf16[12,512,1024]{2,1,0:T(8,128)(2,1)}, u32[]{:S(2)}) %copy-start.1) | copy-done | bytes 12582936
  22.3 6.6 %attention.1.sent_ref = bf16[48,1152]{1,0:T(8,128)(2,1)S(1)} custom-call(s32[1]{0:T(128)} %bitcast.place_ref, s32[12,128]{1,0:T(8,128)S(1)} %get-tuple-element.25.spans_ref, bf16[4,48,384]{2,1,0:T(8,128)(2,1)S(1)} %pad_maximum_fusion.1.near_ref, bf16[4,48,384]{2,1,0:T(8,128)(2,1)S(1)} %collective-permute-done.3.far_ref, ...), custom_call_target="tpu_custom_call" | custom-call | tf_op jit(solution)/shard_map/attention/pallas_call | solution.py:523
  28.8 0.0 copy-start.6
  28.9 2.0 %collective-permute-start.5 = (bf16[48,1152]{1,0:T(8,128)(2,1)S(1)}, bf16[48,1152]{1,0:T(8,128)(2,1)S(1)}, u32[]{:S(2)}, u32[]{:S(2)}) collective-permute-start(bf16[48,1152]{1,0:T(8,128)(2,1)S(1)} %attention.1.sent_ref), channel_id=1, source_target_pairs={{0,16},{4,20},{8,24},{12,28},{16,0},{20,4},{24,8},{28,12},{1,17},{... | collective-permute-start | bytes 331784 | tf_op jit(solution)/shard_map/ppermute | solution.py:422
  30.9 1.4 %collective-permute-start.6 = (bf16[48,1152]{1,0:T(8,128)(2,1)S(1)}, bf16[48,1152]{1,0:T(8,128)(2,1)S(1)}, u32[]{:S(2)}, u32[]{:S(2)}) collective-permute-start(bf16[48,1152]{1,0:T(8,128)(2,1)S(1)} %attention.1.sent_ref), channel_id=1, source_target_pairs={{0,24},{4,28},{8,16},{12,20},{16,8},{20,12},{24,0},{28,4},{1,25},{... | collective-permute-start | bytes 331784 | tf_op jit(solution)/shard_map/ppermute | solution.py:422
  32.4 0.1 collective-permute-start.4
  32.5 3.5 %fetch_experts.1 = (bf16[48,1152]{1,0:T(8,128)(2,1)S(1)}, bf16[2,1,1408,1024]{3,2,1,0:T(8,128)(2,1)S(1)}, bf16[1,1408,1024]{2,1,0:T(8,128)(2,1)S(1)}) custom-call(bf16[48,1152]{1,0:T(8,128)(2,1)S(1)} %attention.1.sent_ref, bf16[2,1,1408,1024]{3,2,1,0:T(8,128)(2,1)} %in_ref.1, bf16[1,1408,1024]{2,1,0:T(8,128)(2,1)} %down_ref.1), custom_call_target="tpu_custom_call" | custom-call | bytes 8650752 | tf_op jit(solution)/shard_map/fetch_experts/pallas_call | solution.py:504
  36.0 2.5 %copy-done.2 = bf16[2,1,1408,1024]{3,2,1,0:T(8,128)(2,1)} copy-done((bf16[2,1,1408,1024]{3,2,1,0:T(8,128)(2,1)}, bf16[2,1,1408,1024]{3,2,1,0:T(8,128)(2,1)S(1)}, u32[]{:S(2)}) %copy-start.2) | copy-done | bytes 5767192
  38.5 0.1 pad_maximum_fusion.near_ref
  38.6 0.1 collective-permute-start.7
  38.7 0.9 %extra.1 = (f32[48,1024]{1,0:T(8,128)S(1)}, f32[48,128]{1,0:T(8,128)S(1)}) custom-call(s32[1]{0:T(128)} %bitcast.place_ref, bf16[4,48,384]{2,1,0:T(8,128)(2,1)S(1)} %pad_maximum_fusion.1.near_ref, bf16[4,48,384]{2,1,0:T(8,128)(2,1)S(1)} %collective-permute-done.3.far_ref, bf16[2,12,4,1024]{3,2,1,0:T(4,128)(2,1)S(1)} %copy-done.6), custom_call_target="tpu_custom_call" | custom-call | tf_op jit(solution)/shard_map/extra/pallas_call | solution.py:540
  39.6 0.8 %collective-permute-done.7.far_ref = bf16[4,48,1152]{2,1,0:T(8,128)(2,1)S(1)} collective-permute-done((bf16[4,48,1152]{2,1,0:T(8,128)(2,1)S(1)}, bf16[4,48,1152]{2,1,0:T(8,128)(2,1)S(1)}, u32[]{:S(2)}, u32[]{:S(2)}) %collective-permute-start.7) | collective-permute-done | bytes 442400 | tf_op jit(solution)/shard_map/ppermute | solution.py:427
  40.5 1.0 %project.1 = bf16[48,128]{1,0:T(8,128)(2,1)S(1)} custom-call(s32[1]{0:T(128)} %bitcast.place_ref, bf16[4,48,1152]{2,1,0:T(8,128)(2,1)S(1)} %pad_maximum_fusion.near_ref, bf16[4,48,1152]{2,1,0:T(8,128)(2,1)S(1)} %collective-permute-done.7.far_ref, f32[48,1024]{1,0:T(8,128)S(1)} %get-tuple-element.30.extra_ref, ...), custom_call_target="tpu_custom_call" | custom-call | tf_op jit(solution)/shard_map/project/pallas_call | solution.py:554
  41.5 2.0 %collective-permute-start.8 = (bf16[48,128]{1,0:T(8,128)(2,1)S(1)}, bf16[48,128]{1,0:T(8,128)(2,1)S(1)}, u32[]{:S(2)}, u32[]{:S(2)}) collective-permute-start(bf16[48,128]{1,0:T(8,128)(2,1)S(1)} %project.1), channel_id=1, source_target_pairs={{0,8},{4,12},{8,0},{12,4},{16,24},{20,28},{24,16},{28,20},{1,9},{5... | collective-permute-start | bytes 36872 | tf_op jit(solution)/shard_map/ppermute | solution.py:422
  43.4 1.5 %collective-permute-start.9 = (bf16[48,128]{1,0:T(8,128)(2,1)S(1)}, bf16[48,128]{1,0:T(8,128)(2,1)S(1)}, u32[]{:S(2)}, u32[]{:S(2)}) collective-permute-start(bf16[48,128]{1,0:T(8,128)(2,1)S(1)} %project.1), channel_id=1, source_target_pairs={{0,16},{4,20},{8,24},{12,28},{16,0},{20,4},{24,8},{28,12},{1,17},{... | collective-permute-start | bytes 36872 | tf_op jit(solution)/shard_map/ppermute | solution.py:422
  45.0 0.0 collective-permute-start.10
  45.0 0.2 collective-permute-done.8
  45.2 1.9 %collective-permute-done.9 = bf16[48,128]{1,0:T(8,128)(2,1)S(1)} collective-permute-done((bf16[48,128]{1,0:T(8,128)(2,1)S(1)}, bf16[48,128]{1,0:T(8,128)(2,1)S(1)}, u32[]{:S(2)}, u32[]{:S(2)}) %collective-permute-start.9) | collective-permute-done | bytes 12320 | tf_op jit(solution)/shard_map/ppermute | solution.py:422
  47.1 2.4 %collective-permute-done.10 = bf16[48,128]{1,0:T(8,128)(2,1)S(1)} collective-permute-done((bf16[48,128]{1,0:T(8,128)(2,1)S(1)}, bf16[48,128]{1,0:T(8,128)(2,1)S(1)}, u32[]{:S(2)}, u32[]{:S(2)}) %collective-permute-start.10) | collective-permute-done | bytes 12320 | tf_op jit(solution)/shard_map/ppermute | solution.py:422
  49.6 0.1 collective-permute-start.11
  49.7 0.1 pad_add_fusion.own_ref
  49.7 0.1 copy.14.ids_ref
  49.8 0.5 routing.1
  50.3 0.5 collective-permute-done.11.far_ref
  50.9 0.9 %residual.1 = (bf16[48,1024]{1,0:T(8,128)(2,1)S(1)}, f32[48,1024]{1,0:T(8,128)S(1)}, bf16[8,1024]{1,0:T(8,128)(2,1)S(1)}, bf16[8,1024]{1,0:T(8,128)(2,1)S(1)}, b...) custom-call(s32[1]{0:T(128)} %bitcast.place_ref, s32[2]{0:T(128)S(1)} %pad_add_fusion.own_ref, ...), custom_call_target="tpu_custom_call" | custom-call | tf_op jit(solution)/shard_map/residual/pallas_call | solution.py:576
  51.7 1.6 %collective-permute-start.12 = (bf16[8,1024]{1,0:T(8,128)(2,1)S(1)}, bf16[8,1024]{1,0:T(8,128)(2,1)S(1)}, u32[]{:S(2)}, u32[]{:S(2)}) collective-permute-start(bf16[8,1024]{1,0:T(8,128)(2,1)S(1)} %get-tuple-element.39), channel_id=1, source_target_pairs={{0,1},{1,0},{2,3},{3,2},{4,5},{5,4},{6,7},{7,6},{8,9},{9,8},{10,11... | collective-permute-start | bytes 49160 | tf_op jit(solution)/shard_map/ppermute | solution.py:589
  53.4 2.6 %collective-permute-start.13 = (bf16[8,1024]{1,0:T(8,128)(2,1)S(1)}, bf16[8,1024]{1,0:T(8,128)(2,1)S(1)}, u32[]{:S(2)}, u32[]{:S(2)}) collective-permute-start(bf16[8,1024]{1,0:T(8,128)(2,1)S(1)} %get-tuple-element.40), channel_id=1, source_target_pairs={{0,2},{1,3},{2,0},{3,1},{4,6},{5,7},{6,4},{7,5},{8,10},{9,11},{10,... | collective-permute-start | bytes 49160 | tf_op jit(solution)/shard_map/ppermute | solution.py:589
  56.0 0.2 collective-permute-start.14
  56.2 1.9 %collective-permute-done.13.refs_2_ = bf16[8,1024]{1,0:T(8,128)(2,1)S(1)} collective-permute-done((bf16[8,1024]{1,0:T(8,128)(2,1)S(1)}, bf16[8,1024]{1,0:T(8,128)(2,1)S(1)}, u32[]{:S(2)}, u32[]{:S(2)}) %collective-permute-start.13) | collective-permute-done | bytes 16416 | tf_op jit(solution)/shard_map/ppermute | solution.py:589
  58.1 3.4 %collective-permute-done.14.refs_3_ = bf16[8,1024]{1,0:T(8,128)(2,1)S(1)} collective-permute-done((bf16[8,1024]{1,0:T(8,128)(2,1)S(1)}, bf16[8,1024]{1,0:T(8,128)(2,1)S(1)}, u32[]{:S(2)}, u32[]{:S(2)}) %collective-permute-start.14) | collective-permute-done | bytes 16416 | tf_op jit(solution)/shard_map/ppermute | solution.py:589
  61.5 2.6 %copy-done.3 = bf16[2,1,1408,1024]{3,2,1,0:T(8,128)(2,1)S(1)} copy-done((bf16[2,1,1408,1024]{3,2,1,0:T(8,128)(2,1)S(1)}, bf16[2,1,1408,1024]{3,2,1,0:T(8,128)(2,1)}, u32[]{:S(2)}) %copy-start.3) | copy-done | bytes 5767192
  64.1 2.8 %expert.1 = (f32[32,512]{1,0:T(8,128)S(1)}, f32[32,512]{1,0:T(8,128)S(1)}) custom-call(s32[1]{0:T(128)} %bitcast.place_ref, s32[2]{0:T(128)S(1)} %pad_add_fusion.own_ref, bf16[2,1,1408,1024]{3,2,1,0:T(8,128)(2,1)S(1)} %copy-done.3, bf16[1,1408,1024]{2,1,0:T(8,128)(2,1)S(1)} %get-tuple-element.37.down_ref, bf16[8,1024]{1,0:T(8,128)(2,1)S(1)} %get-tuple-element.38.refs_0_, ...), custom_call_target="tpu_custom_call" | custom-call | tf_op jit(solution)/shard_map/expert/pallas_call | solution.py:600
  67.0 0.1 collective-permute-start.15
  67.1 1.2 %collective-permute-done.15.other_ref = f32[32,512]{1,0:T(8,128)S(1)} collective-permute-done((f32[32,512]{1,0:T(8,128)S(1)}, f32[32,512]{1,0:T(8,128)S(1)}, u32[]{:S(2)}, u32[]{:S(2)}) %collective-permute-start.15) | collective-permute-done | bytes 65568 | tf_op jit(solution)/shard_map/ppermute | solution.py:614
  68.3 0.7 spread.1
  69.0 2.6 %all-to-all-start = ((bf16[32,8,512]{2,1,0:T(8,128)(2,1)}), bf16[32,8,512]{2,1,0:T(8,128)(2,1)S(1)}, u32[]{:S(2)}, u32[]{:S(2)}) async-start(bf16[32,8,512]{2,1,0:T(8,128)(2,1)} %spread.1), calls=%async_computation | async-start | bytes 524288 | tf_op jit(solution)/shard_map/all_to_all | solution.py:628
  71.6 0.2 copy.15.router_ref
  71.8 0.3 gate.1.gates_ref
  72.1 9.7 %all-to-all-done = bf16[32,8,512]{2,1,0:T(8,128)(2,1)S(1)} async-done(((bf16[32,8,512]{2,1,0:T(8,128)(2,1)}), bf16[32,8,512]{2,1,0:T(8,128)(2,1)S(1)}, u32[]{:S(2)}, u32[]{:S(2)}) %all-to-all-start) | async-done | bytes 262176 | tf_op jit(solution)/shard_map/all_to_all | solution.py:628
  81.8 0.9 %final.1 = bf16[12,4,1024]{2,1,0:T(4,128)(2,1)} custom-call(f32[48,128]{1,0:T(8,128)S(1)} %gate.1.gates_ref, bf16[8,4,8,512]{3,2,1,0:T(8,128)(2,1)S(1)} %bitcast.18, f32[48,1024]{1,0:T(8,128)S(1)} %get-tuple-element.44.residual_ref), custom_call_target="tpu_custom_call" | custom-call | tf_op jit(solution)/shard_map/final/pallas_call | solution.py:636
  (26 shorter events, 0.1 us)
Async XLA Ops:
  1.6 14.6 %collective-permute-start = (bf16[48,384]{1,0:T(8,128)(2,1)S(1)}, bf16[48,384]{1,0:T(8,128)(2,1)S(1)}, u32[]{:S(2)}, u32[]{:S(2)}) collective-permute-start(bf16[48,384]{1,0:T(8,128)(2,1)S(1)} %qkv.1.sent_ref), channel_id=1, source_target_pairs={{0,8},{4,12},{8,0},{12,4},{16,24},{20,28},{24,16},{28,20},{1,9},{5... | collective-permute-start | bytes 110600 | tf_op jit(solution)/shard_map/ppermute | solution.py:422
  4.6 11.6 %collective-permute-start.1 = (bf16[48,384]{1,0:T(8,128)(2,1)S(1)}, bf16[48,384]{1,0:T(8,128)(2,1)S(1)}, u32[]{:S(2)}, u32[]{:S(2)}) collective-permute-start(bf16[48,384]{1,0:T(8,128)(2,1)S(1)} %qkv.1.sent_ref), channel_id=1, source_target_pairs={{0,16},{4,20},{8,24},{12,28},{16,0},{20,4},{24,8},{28,12},{1,17},{... | collective-permute-start | bytes 110600 | tf_op jit(solution)/shard_map/ppermute | solution.py:422
  6.2 10.0 %collective-permute-start.2 = (bf16[48,384]{1,0:T(8,128)(2,1)S(1)}, bf16[48,384]{1,0:T(8,128)(2,1)S(1)}, u32[]{:S(2)}, u32[]{:S(2)}) collective-permute-start(bf16[48,384]{1,0:T(8,128)(2,1)S(1)} %qkv.1.sent_ref), channel_id=1, source_target_pairs={{0,24},{4,28},{8,16},{12,20},{16,8},{20,12},{24,0},{28,4},{1,25},{... | collective-permute-start | bytes 110600 | tf_op jit(solution)/shard_map/ppermute | solution.py:422
  11.7 4.5 %copy-start = (bf16[12,512,1024]{2,1,0:T(8,128)(2,1)}, bf16[12,512,1024]{2,1,0:T(8,128)(2,1)S(1)}, u32[]{:S(2)}) copy-start(bf16[12,512,1024]{2,1,0:T(8,128)(2,1)S(1)} %get-tuple-element.27.keys_ref) | copy-start | bytes 37748740
  16.2 1.4 %collective-permute-start.3 = (bf16[4,48,384]{2,1,0:T(8,128)(2,1)S(1)}, bf16[4,48,384]{2,1,0:T(8,128)(2,1)S(1)}, u32[]{:S(2)}, u32[]{:S(2)}) collective-permute-start(bf16[4,48,384]{2,1,0:T(8,128)(2,1)S(1)} %pad_maximum_fusion.1.near_ref), channel_id=1, source_target_pairs={{0,4},{4,0},{8,12},{12,8},{16,20},{20,16},{24,28},{28,24},{1,5},{5... | collective-permute-start | bytes 442376 | tf_op jit(solution)/shard_map/ppermute | solution.py:427
  17.7 4.6 %copy-start.1 = (bf16[12,512,1024]{2,1,0:T(8,128)(2,1)S(1)}, bf16[12,512,1024]{2,1,0:T(8,128)(2,1)}, u32[]{:S(2)}) copy-start(bf16[12,512,1024]{2,1,0:T(8,128)(2,1)} %copy-done) | copy-start | bytes 37748740
  28.8 9.9 %copy-start.6 = (bf16[2,12,4,1024]{3,2,1,0:T(4,128)(2,1)S(1)}, bf16[2,12,4,1024]{3,2,1,0:T(4,128)(2,1)}, u32[]{:S(2)}) copy-start(bf16[2,12,4,1024]{3,2,1,0:T(4,128)(2,1)} %sinks_ref.1) | copy-start | bytes 589828
  28.8 11.6 %copy-start.5 = (bf16[128,1024]{1,0:T(8,128)(2,1)S(1)}, bf16[128,1024]{1,0:T(8,128)(2,1)}, u32[]{:S(2)}) copy-start(bf16[128,1024]{1,0:T(8,128)(2,1)} %weight_ref.3) | copy-start | bytes 786436
  28.8 20.9 %copy-start.10 = (s32[12,4,2]{0,2,1:T(2,128)S(1)}, s32[12,4,2]{0,2,1:T(2,128)}, u32[]{:S(2)}) copy-start(s32[12,4,2]{0,2,1:T(2,128)} %param.22) | copy-start | bytes 1156
  28.9 21.0 %copy-start.8 = (s32[1,48]{1,0:T(1,128)S(1)}, s32[1,48]{1,0:T(1,128)}, u32[]{:S(2)}) copy-start(s32[1,48]{1,0:T(1,128)} %order_ref.1) | copy-start | bytes 580
  28.9 22.0 %copy-start.4 = (bf16[12,4,1024]{2,1,0:T(4,128)(2,1)S(1)}, bf16[12,4,1024]{2,1,0:T(4,128)(2,1)}, u32[]{:S(2)}) copy-start(bf16[12,4,1024]{2,1,0:T(4,128)(2,1)} %tokens_ref.3) | copy-start | bytes 294916
  28.9 22.0 %copy-start.7 = (f32[1024]{0:T(1024)S(1)}, f32[1024]{0:T(1024)}, u32[]{:S(2)}) copy-start(f32[1024]{0:T(1024)} %param.20) | copy-start | bytes 12292
  28.9 9.6 %collective-permute-start.5 = (bf16[48,1152]{1,0:T(8,128)(2,1)S(1)}, bf16[48,1152]{1,0:T(8,128)(2,1)S(1)}, u32[]{:S(2)}, u32[]{:S(2)}) collective-permute-start(bf16[48,1152]{1,0:T(8,128)(2,1)S(1)} %attention.1.sent_ref), channel_id=1, source_target_pairs={{0,16},{4,20},{8,24},{12,28},{16,0},{20,4},{24,8},{28,12},{1,17},{... | collective-permute-start | bytes 331784 | tf_op jit(solution)/shard_map/ppermute | solution.py:422
  30.9 7.6 %collective-permute-start.6 = (bf16[48,1152]{1,0:T(8,128)(2,1)S(1)}, bf16[48,1152]{1,0:T(8,128)(2,1)S(1)}, u32[]{:S(2)}, u32[]{:S(2)}) collective-permute-start(bf16[48,1152]{1,0:T(8,128)(2,1)S(1)} %attention.1.sent_ref), channel_id=1, source_target_pairs={{0,24},{4,28},{8,16},{12,20},{16,8},{20,12},{24,0},{28,4},{1,25},{... | collective-permute-start | bytes 331784 | tf_op jit(solution)/shard_map/ppermute | solution.py:422
  32.4 6.1 %collective-permute-start.4 = (bf16[48,1152]{1,0:T(8,128)(2,1)S(1)}, bf16[48,1152]{1,0:T(8,128)(2,1)S(1)}, u32[]{:S(2)}, u32[]{:S(2)}) collective-permute-start(bf16[48,1152]{1,0:T(8,128)(2,1)S(1)} %attention.1.sent_ref), channel_id=1, source_target_pairs={{0,8},{4,12},{8,0},{12,4},{16,24},{20,28},{24,16},{28,20},{1,9},{5... | collective-permute-start | bytes 331784 | tf_op jit(solution)/shard_map/ppermute | solution.py:422
  36.0 2.5 %copy-start.2 = (bf16[2,1,1408,1024]{3,2,1,0:T(8,128)(2,1)}, bf16[2,1,1408,1024]{3,2,1,0:T(8,128)(2,1)S(1)}, u32[]{:S(2)}) copy-start(bf16[2,1,1408,1024]{3,2,1,0:T(8,128)(2,1)S(1)} %get-tuple-element.36.in_ref) | copy-start | bytes 17301508
  38.6 1.9 %collective-permute-start.7 = (bf16[4,48,1152]{2,1,0:T(8,128)(2,1)S(1)}, bf16[4,48,1152]{2,1,0:T(8,128)(2,1)S(1)}, u32[]{:S(2)}, u32[]{:S(2)}) collective-permute-start(bf16[4,48,1152]{2,1,0:T(8,128)(2,1)S(1)} %pad_maximum_fusion.near_ref), channel_id=1, source_target_pairs={{0,4},{4,0},{8,12},{12,8},{16,20},{20,16},{24,28},{28,24},{1,5},{5... | collective-permute-start | bytes 1327112 | tf_op jit(solution)/shard_map/ppermute | solution.py:427
  39.6 32.0 %copy-start.9 = (bf16[1024,16]{0,1:T(8,128)(2,1)S(1)}, bf16[1024,16]{0,1:T(8,128)(2,1)}, u32[]{:S(2)}) copy-start(bf16[1024,16]{0,1:T(8,128)(2,1)} %param.21) | copy-start | bytes 98308
  41.5 3.8 %collective-permute-start.8 = (bf16[48,128]{1,0:T(8,128)(2,1)S(1)}, bf16[48,128]{1,0:T(8,128)(2,1)S(1)}, u32[]{:S(2)}, u32[]{:S(2)}) collective-permute-start(bf16[48,128]{1,0:T(8,128)(2,1)S(1)} %project.1), channel_id=1, source_target_pairs={{0,8},{4,12},{8,0},{12,4},{16,24},{20,28},{24,16},{28,20},{1,9},{5... | collective-permute-start | bytes 36872 | tf_op jit(solution)/shard_map/ppermute | solution.py:422
  43.4 3.7 %collective-permute-start.9 = (bf16[48,128]{1,0:T(8,128)(2,1)S(1)}, bf16[48,128]{1,0:T(8,128)(2,1)S(1)}, u32[]{:S(2)}, u32[]{:S(2)}) collective-permute-start(bf16[48,128]{1,0:T(8,128)(2,1)S(1)} %project.1), channel_id=1, source_target_pairs={{0,16},{4,20},{8,24},{12,28},{16,0},{20,4},{24,8},{28,12},{1,17},{... | collective-permute-start | bytes 36872 | tf_op jit(solution)/shard_map/ppermute | solution.py:422
  45.0 4.6 %collective-permute-start.10 = (bf16[48,128]{1,0:T(8,128)(2,1)S(1)}, bf16[48,128]{1,0:T(8,128)(2,1)S(1)}, u32[]{:S(2)}, u32[]{:S(2)}) collective-permute-start(bf16[48,128]{1,0:T(8,128)(2,1)S(1)} %project.1), channel_id=1, source_target_pairs={{0,24},{4,28},{8,16},{12,20},{16,8},{20,12},{24,0},{28,4},{1,25},{... | collective-permute-start | bytes 36872 | tf_op jit(solution)/shard_map/ppermute | solution.py:422
  49.6 1.3 %collective-permute-start.11 = (bf16[4,48,128]{2,1,0:T(8,128)(2,1)S(1)}, bf16[4,48,128]{2,1,0:T(8,128)(2,1)S(1)}, u32[]{:S(2)}, u32[]{:S(2)}) collective-permute-start(bf16[4,48,128]{2,1,0:T(8,128)(2,1)S(1)} %pad_maximum_fusion.2.near_ref), channel_id=1, source_target_pairs={{0,4},{4,0},{8,12},{12,8},{16,20},{20,16},{24,28},{28,24},{1,5},{5... | collective-permute-start | bytes 147464 | tf_op jit(solution)/shard_map/ppermute | solution.py:427
  51.7 4.5 %collective-permute-start.12 = (bf16[8,1024]{1,0:T(8,128)(2,1)S(1)}, bf16[8,1024]{1,0:T(8,128)(2,1)S(1)}, u32[]{:S(2)}, u32[]{:S(2)}) collective-permute-start(bf16[8,1024]{1,0:T(8,128)(2,1)S(1)} %get-tuple-element.39), channel_id=1, source_target_pairs={{0,1},{1,0},{2,3},{3,2},{4,5},{5,4},{6,7},{7,6},{8,9},{9,8},{10,11... | collective-permute-start | bytes 49160 | tf_op jit(solution)/shard_map/ppermute | solution.py:589
  53.4 4.7 %collective-permute-start.13 = (bf16[8,1024]{1,0:T(8,128)(2,1)S(1)}, bf16[8,1024]{1,0:T(8,128)(2,1)S(1)}, u32[]{:S(2)}, u32[]{:S(2)}) collective-permute-start(bf16[8,1024]{1,0:T(8,128)(2,1)S(1)} %get-tuple-element.40), channel_id=1, source_target_pairs={{0,2},{1,3},{2,0},{3,1},{4,6},{5,7},{6,4},{7,5},{8,10},{9,11},{10,... | collective-permute-start | bytes 49160 | tf_op jit(solution)/shard_map/ppermute | solution.py:589
  56.0 5.5 %collective-permute-start.14 = (bf16[8,1024]{1,0:T(8,128)(2,1)S(1)}, bf16[8,1024]{1,0:T(8,128)(2,1)S(1)}, u32[]{:S(2)}, u32[]{:S(2)}) collective-permute-start(bf16[8,1024]{1,0:T(8,128)(2,1)S(1)} %get-tuple-element.41), channel_id=1, source_target_pairs={{0,3},{1,2},{2,1},{3,0},{4,7},{5,6},{6,5},{7,4},{8,11},{9,10},{10,... | collective-permute-start | bytes 49160 | tf_op jit(solution)/shard_map/ppermute | solution.py:589
  61.5 2.6 %copy-start.3 = (bf16[2,1,1408,1024]{3,2,1,0:T(8,128)(2,1)S(1)}, bf16[2,1,1408,1024]{3,2,1,0:T(8,128)(2,1)}, u32[]{:S(2)}) copy-start(bf16[2,1,1408,1024]{3,2,1,0:T(8,128)(2,1)} %copy-done.2) | copy-start | bytes 17301508
  67.0 1.3 %collective-permute-start.15 = (f32[32,512]{1,0:T(8,128)S(1)}, f32[32,512]{1,0:T(8,128)S(1)}, u32[]{:S(2)}, u32[]{:S(2)}) collective-permute-start(f32[32,512]{1,0:T(8,128)S(1)} %get-tuple-element.43), channel_id=1, source_target_pairs={{0,4},{4,0},{8,12},{12,8},{16,20},{20,16},{24,28},{28,24},{1,5},{5... | collective-permute-start | bytes 196616 | tf_op jit(solution)/shard_map/ppermute | solution.py:614
  69.0 12.8 %all-to-all-start = ((bf16[32,8,512]{2,1,0:T(8,128)(2,1)}), bf16[32,8,512]{2,1,0:T(8,128)(2,1)S(1)}, u32[]{:S(2)}, u32[]{:S(2)}) async-start(bf16[32,8,512]{2,1,0:T(8,128)(2,1)} %spread.1), calls=%async_computation | async-start | bytes 524288 | tf_op jit(solution)/shard_map/all_to_all | solution.py:628

commit v4 on v3

--- a/solution.py
+++ b/solution.py
@@ -79,10 +79,10 @@
     out_ref[...] = dot(normed, weight_buf[...], ROWS_BY_ROWS).astype(jnp.bfloat16)
 
 
-def in_order(place, near_ref, far_ref, ordered_ref):
-    for j in range(near_ref.shape[0]):
-        ordered_ref[jnp.bitwise_xor(place, 2 * j)] = near_ref[j]
-        ordered_ref[jnp.bitwise_xor(place, 2 * j + 1)] = far_ref[j]
+def in_order(sent_refs, ordered_ref):
+    place = lax.axis_index("seq")
+    for k, sent_ref in enumerate(sent_refs):
+        ordered_ref[jnp.bitwise_xor(place, k)] = sent_ref[...]
 
 
 def head_masks(rows, width, steps):
@@ -121,21 +121,9 @@
         copy.wait()
 
 
-def attention_kernel(
-    place_ref,
-    spans_ref,
-    near_ref,
-    far_ref,
-    keys_ref,
-    values_ref,
-    window_ref,
-    out_ref,
-    ordered_ref,
-    flat_ref,
-    query_ref,
-    late_ref,
-    sems,
-):
+def attention_kernel(*refs):
+    *mixed_refs, spans_ref, keys_ref, values_ref, window_ref = refs[:-6]
+    out_ref, ordered_ref, flat_ref, query_ref, late_ref, sems = refs[-6:]
     devices, rows, share = ordered_ref.shape
     requests, span, width = keys_ref.shape
     early = values_ref.shape[0]
@@ -147,8 +135,8 @@
         copy.start()
     steps = rows // requests
     block_rows = BLOCK_HEADS * steps
-    place = place_ref[0]
-    in_order(place, near_ref, far_ref, ordered_ref)
+    place = lax.axis_index("seq")
+    in_order(mixed_refs, ordered_ref)
     for d in range(devices):
         if d * share < width:
             flat_ref[:, d * share : (d + 1) * share] = ordered_ref[d].astype(jnp.float32)
@@ -207,15 +195,15 @@
     out_ref[...] = flat_ref[...].astype(jnp.bfloat16)
 
 
-def extra_kernel(
-    place_ref, near_ref, far_ref, sinks_ref, out_ref, stats_ref, ordered_ref, flat_ref, query_ref, keys_ref
-):
+def extra_kernel(*refs):
+    *mixed_refs, sinks_ref = refs[:-6]
+    out_ref, stats_ref, ordered_ref, flat_ref, query_ref, keys_ref = refs[-6:]
     devices, rows, share = ordered_ref.shape
     _, requests, sinks, width = sinks_ref.shape
     steps = rows // requests
     block_rows = BLOCK_HEADS * steps
     count = sinks + steps
-    in_order(place_ref[0], near_ref, far_ref, ordered_ref)
+    in_order(mixed_refs, ordered_ref)
     for d in range(devices):
         flat_ref[:, d * share : (d + 1) * share] = ordered_ref[d].astype(jnp.float32)
     own_head = head_masks(block_rows, width, steps)
@@ -263,12 +251,11 @@
         stats_ref[r * steps : (r + 1) * steps, :] = stats[r]
 
 
-def project_kernel(
-    place_ref, near_ref, far_ref, extra_ref, extra_stats_ref, weight_ref, out_ref, ordered_ref
-):
+def project_kernel(*refs):
+    *part_refs, extra_ref, extra_stats_ref, weight_ref, out_ref, ordered_ref = refs
     devices, rows, padded = ordered_ref.shape
     width = padded - LANES
-    in_order(place_ref[0], near_ref, far_ref, ordered_ref)
+    in_order(part_refs, ordered_ref)
     stats = [ordered_ref[d][:, width:].astype(jnp.float32) for d in range(devices)]
 
     def joined(stat, first):
@@ -297,13 +284,18 @@
     )
 
 
-def routing_kernel(ids_ref, order_ref, select_ref, turned_ref, chosen_ref, rows_ref):
-    requests, steps, _ = ids_ref.shape
+def routing_kernel(ids_ref, order_ref, select_ref, turned_ref, chosen_ref):
+    steps, _, requests = ids_ref.shape
     rows = requests * steps
-    for r in range(requests):
-        rows_ref[r * steps : (r + 1) * steps, :] = ids_ref[r]
     lane = lax.broadcasted_iota(jnp.int32, (rows, LANES), 1)
-    chosen = [rows_ref[:, c : c + 1] for c in range(TOPK)]
+    own_row = lax.broadcasted_iota(jnp.int32, (rows, requests), 0)
+    own_request = lax.broadcasted_iota(jnp.int32, (rows, requests), 1) == own_row // steps
+    chosen = []
+    for c in range(TOPK):
+        ids = jnp.zeros((rows, requests), jnp.int32)
+        for t in range(steps):
+            ids = jnp.where(own_request & (own_row % steps == t), ids_ref[t, c : c + 1, :], ids)
+        chosen.append(jnp.sum(ids.astype(jnp.float32), axis=1, keepdims=True).astype(jnp.int32))
     onehot = [(lane == ids).astype(jnp.float32) for ids in chosen]
     across = order_ref[...]
     square_row = lax.broadcasted_iota(jnp.int32, (rows, rows), 0)
@@ -328,21 +320,11 @@
     turned_ref[...] = jnp.transpose(both)
 
 
-def residual_kernel(
-    place_ref,
-    own_ref,
-    near_ref,
-    far_ref,
-    tokens_ref,
-    gain_ref,
-    turned_ref,
-    normed_ref,
-    residual_ref,
-    *send_and_ordered_refs,
-):
-    *send_refs, ordered_ref = send_and_ordered_refs
-    devices, rows, share = ordered_ref.shape
-    in_order(place_ref[0], near_ref, far_ref, ordered_ref)
+def residual_kernel(devices, *refs):
+    projected_refs, refs = refs[:devices], refs[devices:]
+    tokens_ref, gain_ref, turned_ref, normed_ref, residual_ref, *send_refs, ordered_ref = refs
+    share = ordered_ref.shape[2]
+    in_order(projected_refs, ordered_ref)
     copy_rows(tokens_ref, residual_ref)
     for d in range(devices):
         own = slice(d * share, (d + 1) * share)
@@ -350,14 +332,15 @@
     normed = rms_rows(residual_ref[...], gain_ref[...])
     normed_ref[...] = normed
     local_experts = EXPERTS // len(send_refs)
+    own = lax.axis_index("seq") // (devices // local_experts)
     for k, send_ref in enumerate(send_refs):
-        expert = jnp.bitwise_xor(own_ref[1], k) * local_experts + own_ref[0]
+        expert = jnp.bitwise_xor(lax.axis_index("exp"), k) * local_experts + own
         picking = turned_ref[pl.ds(pl.multiple_of(expert * CAP, CAP), CAP), :].astype(jnp.bfloat16)
         send_ref[...] = dot(picking, normed).astype(jnp.bfloat16)
 
 
 def gate_kernel(normed_ref, router_ref, select_ref, chosen_ref, out_ref):
-    logits = dot(normed_ref[...], router_ref[...])
+    logits = dot(normed_ref[...], router_ref[...], ROWS_BY_ROWS)
     gates = jnp.zeros(select_ref.shape[1:], jnp.float32)
     for c in range(TOPK):
         logit = jnp.sum(chosen_ref[c][:, :EXPERTS] * logits, axis=-1, keepdims=True)
@@ -365,18 +348,18 @@
     out_ref[...] = gates
 
 
-def expert_kernel(place_ref, own_ref, in_ref, down_ref, *refs):
+def expert_kernel(in_ref, down_ref, *refs):
     *received_refs, keep_ref, send_ref, rows_ref = refs
     groups, slots, width = rows_ref.shape
     for k, received_ref in enumerate(received_refs):
-        rows_ref[jnp.bitwise_xor(own_ref[1], k)] = received_ref[...].astype(jnp.float32)
+        rows_ref[jnp.bitwise_xor(lax.axis_index("exp"), k)] = received_ref[...].astype(jnp.float32)
     rows = rows_ref[...].reshape(groups * slots, width).astype(jnp.bfloat16)
     gate = dot(rows, in_ref[0, 0], ROWS_BY_ROWS)
     up = dot(rows, in_ref[1, 0], ROWS_BY_ROWS)
     hidden = (jax.nn.gelu(gate, approximate=True) * up).astype(jnp.bfloat16)
     outputs = dot(hidden, down_ref[0])
     half = width // 2
-    odd = jnp.bitwise_and(place_ref[0], 1) == 1
+    odd = lax.axis_index("seq") % 2 == 1
     keep_ref[...] = jnp.where(odd, outputs[:, half:], outputs[:, :half])
     send_ref[...] = jnp.where(odd, outputs[:, :half], outputs[:, half:])
 
@@ -418,14 +401,15 @@
 
 def gather_seq(values, meanwhile=None):
     count = lax.axis_size("seq")
-    others = [
-        lax.ppermute(values, "seq", [(i, i ^ k) for i in range(count)]) for k in range(2, count, 2)
-    ]
+
+    def exchange(value, bits):
+        return lax.ppermute(value, "seq", [(i, i ^ bits) for i in range(count)])
+
+    near = [exchange(values, k) for k in range(2, count, 2)]
     if meanwhile is not None:
         values = meanwhile(values)
-    near = jnp.stack([values] + others)
-    far = lax.ppermute(near, "seq", [(i, i ^ 1) for i in range(count)])
-    return near, far
+    near = [values] + near
+    return [part for value in near for part in (value, exchange(value, 1))]
 
 
 def shape(dims, dtype):
@@ -454,14 +438,11 @@
     groups = lax.axis_size("exp")
     local_experts = EXPERTS // groups
     sharers = seq_count // local_experts
-    own_expert = jnp.stack([seq_index // sharers, lax.axis_index("exp")]).astype(jnp.int32)
-    place = seq_index.astype(jnp.int32).reshape(1)
     span = window_cache.shape[2]
     share = w_qkv.shape[0]
     slots = EXPERTS * CAP
     f32, bf16 = jnp.float32, jnp.bfloat16
 
-    smem = pl.BlockSpec(memory_space=pltpu.SMEM)
     vmem = pl.BlockSpec(memory_space=pltpu.VMEM)
     hbm = pl.BlockSpec(memory_space=pltpu.HBM)
 
@@ -516,13 +497,13 @@
         )(values, in_hbm(expert_in), in_hbm(expert_down))
         return held
 
-    near_mix, far_mix = gather_seq(local_mix, fetch_window)
+    mixed = gather_seq(local_mix, fetch_window)
     keys, values, spans = fetched["window"]
 
     padded = width + LANES
     part = pl.pallas_call(
         attention_kernel,
-        in_specs=[smem] + [vmem] * 5 + [hbm],
+        in_specs=[vmem] * (seq_count + 3) + [hbm],
         out_shape=shape((rows, padded), bf16),
         scratch_shapes=[
             pltpu.VMEM((seq_count, rows, share), bf16),
@@ -533,13 +514,12 @@
         ],
         compiler_params=params(20),
         name="attention",
-    )(place, spans, near_mix, far_mix, keys, values, in_hbm(window_cache))
-    near_part, far_part = gather_seq(part, fetch_experts)
+    )(*mixed, spans, keys, values, in_hbm(window_cache))
+    parts = gather_seq(part, fetch_experts)
     local_in, local_down = fetched["experts"]
 
     extra, extra_stats = pl.pallas_call(
         extra_kernel,
-        in_specs=[smem, vmem, vmem, vmem],
         out_shape=(shape((rows, width), f32), shape((rows, LANES), f32)),
         scratch_shapes=[
             pltpu.VMEM((seq_count, rows, share), bf16),
@@ -549,17 +529,16 @@
         ],
         compiler_params=params(8),
         name="extra",
-    )(place, near_mix, far_mix, sink_cache)
+    )(*mixed, sink_cache)
 
     local_proj = pl.pallas_call(
         project_kernel,
-        in_specs=[smem] + [vmem] * 5,
         out_shape=shape((rows, w_out.shape[0]), bf16),
         scratch_shapes=[pltpu.VMEM((seq_count, rows, padded), bf16)],
         compiler_params=params(8),
         name="project",
-    )(place, near_part, far_part, extra, extra_stats, w_out)
-    near_proj, far_proj = gather_seq(local_proj)
+    )(*parts, extra, extra_stats, w_out)
+    projected = gather_seq(local_proj)
 
     select, turned, chosen = pl.pallas_call(
         routing_kernel,
@@ -568,14 +547,12 @@
             shape((slots, rows), f32),
             shape((TOPK, rows, LANES), f32),
         ),
-        scratch_shapes=[pltpu.VMEM((rows, TOPK), jnp.int32)],
         compiler_params=params(8),
         name="routing",
-    )(expert_ids, slot_order)
+    )(expert_ids.transpose(1, 2, 0), slot_order)
 
     normed, residual, *send = pl.pallas_call(
-        residual_kernel,
-        in_specs=[smem, smem] + [vmem] * 5,
+        functools.partial(residual_kernel, seq_count),
         out_shape=(
             shape((rows, width), bf16),
             shape((rows, width), f32),
@@ -584,7 +561,7 @@
         scratch_shapes=[pltpu.VMEM((seq_count, rows, w_out.shape[0]), bf16)],
         compiler_params=params(8),
         name="residual",
-    )(place, own_expert, near_proj, far_proj, tokens, moe_gain.reshape(1, width), turned)
+    )(*projected, tokens, moe_gain.reshape(1, width), turned)
     received = [
         lax.ppermute(block, "exp", [(i, i ^ k) for i in range(groups)]) if k else block
         for k, block in enumerate(send)
@@ -595,11 +572,10 @@
         out_shape=shape((rows, slots), f32),
         compiler_params=params(8),
         name="gate",
-    )(normed, router, select, chosen)
+    )(normed, router.T, select, chosen)
 
     kept, sent = pl.pallas_call(
         expert_kernel,
-        in_specs=[smem, smem] + [vmem] * (2 + groups),
         out_shape=(
             shape((groups * CAP, width // 2), f32),
             shape((groups * CAP, width // 2), f32),
@@ -607,7 +583,7 @@
         scratch_shapes=[pltpu.VMEM((groups, CAP, width), f32)],
         compiler_params=params(8),
         name="expert",
-    )(place, own_expert, local_in, local_down, *received)
+    )(local_in, local_down, *received)
 
     reach = 1
     while True:

time: 82.9 us -> 69.3 us (0.84)
  local copies, waits for them, and re-layouts: 14.5 us -> 0.04 us
  starting transfers between devices: 19 us -> 20.8 us
  Pallas kernels: 25.1 us -> 24 us
    unnamed x24 -> x14, local copies, waits for them, and re-layouts: 14.5 us -> 0.04 us
    ppermute x12 -> x21, starting transfers between devices: 11.9 us -> 13.7 us  [exchange(): return lax.ppermute(value, 'seq', [(i, i ^ bits) for i in range(count)])]
    pallas_call x5, Pallas kernels: 12.1 us -> 11.1 us  [the longest x1 6.6 us: body(): pl.pallas_call(attention_kernel, in_specs=[vmem] * (seq_count + 3) + [hbm...]
    ppermute x12 -> x21, waiting for transfers between devices: 7.28 us -> 7.47 us  [exchange(): return lax.ppermute(value, 'seq', [(i, i ^ bits) for i in range(count)])]
  transfers between devices with their start and end apart: 17 -> 26, of which waited for: 10 -> 15; matrix products, arithmetic and copies ran while one was open for 0% -> 0% of each run, Pallas kernels for 13% -> 15%
where the time goes in v4:
time: 69.3 us; the launch traced here: 69 us
  Pallas kernels  24 us (35%)
  waiting for transfers between devices  24 us (35%)
  starting transfers between devices  20.8 us (30%)
    ppermute x21, starting transfers between devices, exchange(): return lax.ppermute(value, 'seq', [(i, i ^ bits) for i in range(count)])  13.7 us
    all_to_all x1, waiting for transfers between devices, body(): lax.all_to_all(outgoing, ('seq', 'exp'), split_axis=0, concat_axis=0, til...  9.94 us
    ppermute x21, waiting for transfers between devices, exchange(): return lax.ppermute(value, 'seq', [(i, i ^ bits) for i in range(count)])  7.47 us
    pallas_call x1, Pallas kernels, body(): pl.pallas_call(attention_kernel, in_specs=[vmem] * (seq_count + 3) + [hbm...  6.6 us
    pallas_call x1, Pallas kernels, fetch_window(): pl.pallas_call(functools.partial(fetch_window_kernel, early), in_specs=[v...  5.5 us
    ppermute x3, waiting for transfers between devices, body(): lax.ppermute(block, 'exp', [(i, i ^ k) for i in range(groups)])  5.32 us
    ppermute x3, starting transfers between devices, body(): lax.ppermute(block, 'exp', [(i, i ^ k) for i in range(groups)])  4.45 us
    pallas_call x1, Pallas kernels, fetch_experts(): pl.pallas_call(fetch_experts_kernel, in_specs=[vmem, hbm, hbm], out_shape...  3.53 us
  transfers between devices with their start and end apart: 26, of which 15 were waited for; matrix products, arithmetic and copies ran while one was open for 0% of the time, Pallas kernels for 15%

profile of v4, /device:TPU:0, one launch (start us, length us, event | category | flops | bytes accessed | tf_op | source)
XLA Modules:
  0.0 69.0 jit_solution(6527210629143782201)
XLA Ops:
  0.0 1.6 %qkv.1.sent_ref = bf16[48,384]{1,0:T(8,128)(2,1)S(1)} custom-call(bf16[12,4,1024]{2,1,0:T(4,128)(2,1)} %refs_8_.3, f32[1,1024]{1,0:T(1,128)} %bitcast.9, bf16[384,1024]{1,0:T(8,128)(2,1)} %weight_ref.1), custom_call_target="tpu_custom_call" | custom-call | tf_op jit(solution)/shard_map/qkv/pallas_call | solution.py:450
  1.6 3.0 %collective-permute-start.1 = (bf16[48,384]{1,0:T(8,128)(2,1)S(1)}, bf16[48,384]{1,0:T(8,128)(2,1)S(1)}, u32[]{:S(2)}, u32[]{:S(2)}) collective-permute-start(bf16[48,384]{1,0:T(8,128)(2,1)S(1)} %qkv.1.sent_ref), channel_id=1, source_target_pairs={{0,8},{4,12},{8,0},{12,4},{16,24},{20,28},{24,16},{28,20},{1,9},{5... | collective-permute-start | bytes 110600 | tf_op jit(solution)/shard_map/ppermute | solution.py:406
  4.6 1.5 %collective-permute-start.3 = (bf16[48,384]{1,0:T(8,128)(2,1)S(1)}, bf16[48,384]{1,0:T(8,128)(2,1)S(1)}, u32[]{:S(2)}, u32[]{:S(2)}) collective-permute-start(bf16[48,384]{1,0:T(8,128)(2,1)S(1)} %qkv.1.sent_ref), channel_id=1, source_target_pairs={{0,16},{4,20},{8,24},{12,28},{16,0},{20,4},{24,8},{28,12},{1,17},{... | collective-permute-start | bytes 110600 | tf_op jit(solution)/shard_map/ppermute | solution.py:406
  6.2 5.5 %fetch_window.1 = (bf16[48,384]{1,0:T(8,128)(2,1)S(1)}, bf16[12,512,1024]{2,1,0:T(8,128)(2,1)S(1)}, bf16[3,512,1024]{2,1,0:T(8,128)(2,1)S(1)}, s32[12,128]{1,0:T(8,128)S(1)}) custom-call(bf16[48,384]{1,0:T(8,128)(2,1)S(1)} %qkv.1.sent_ref, bf16[2,12,512,1024]{3,2,1,0:T(8,128)(2,1)} %refs_11_.1, s32[12]{0:T(128)} %lengths_ref.1), custom_call_target="tpu_custom_call" | custom-call | bytes 12582912 | tf_op jit(solution)/shard_map/fetch_window/pallas_call | solution.py:468
  11.7 0.1 collective-permute-start
  11.8 0.5 collective-permute-start.2
  12.3 0.1 collective-permute-start.4
  12.4 0.4 collective-permute-start.6
  12.8 0.2 collective-permute-done.refs_1_
  13.0 0.2 collective-permute-done.2.refs_3_
  13.1 0.4 collective-permute-done.4.refs_5_
  13.5 0.2 collective-permute-done.6.refs_7_
  13.6 6.6 %attention.1.sent_ref = bf16[48,1152]{1,0:T(8,128)(2,1)S(1)} custom-call(bf16[48,384]{1,0:T(8,128)(2,1)S(1)} %get-tuple-element.25.refs_0_, bf16[48,384]{1,0:T(8,128)(2,1)S(1)} %collective-permute-done.refs_1_, bf16[48,384]{1,0:T(8,128)(2,1)S(1)} %collective-permute-done.1.refs_2_, bf16[48,384]{1,0:T(8,128)(2,1)S(1)} %collective-permute-done.2.refs_3_, ...), custom_call_target="tpu_custom_call" | custom-call | tf_op jit(solution)/shard_map/attention/pallas_call | solution.py:504
  20.3 2.0 %collective-permute-start.10 = (bf16[48,1152]{1,0:T(8,128)(2,1)S(1)}, bf16[48,1152]{1,0:T(8,128)(2,1)S(1)}, u32[]{:S(2)}, u32[]{:S(2)}) collective-permute-start(bf16[48,1152]{1,0:T(8,128)(2,1)S(1)} %attention.1.sent_ref), channel_id=1, source_target_pairs={{0,16},{4,20},{8,24},{12,28},{16,0},{20,4},{24,8},{28,12},{1,17},{... | collective-permute-start | bytes 331784 | tf_op jit(solution)/shard_map/ppermute | solution.py:406
  22.4 1.4 %collective-permute-start.12 = (bf16[48,1152]{1,0:T(8,128)(2,1)S(1)}, bf16[48,1152]{1,0:T(8,128)(2,1)S(1)}, u32[]{:S(2)}, u32[]{:S(2)}) collective-permute-start(bf16[48,1152]{1,0:T(8,128)(2,1)S(1)} %attention.1.sent_ref), channel_id=1, source_target_pairs={{0,24},{4,28},{8,16},{12,20},{16,8},{20,12},{24,0},{28,4},{1,25},{... | collective-permute-start | bytes 331784 | tf_op jit(solution)/shard_map/ppermute | solution.py:406
  23.8 0.1 collective-permute-start.8
  23.9 3.5 %fetch_experts.1 = (bf16[48,1152]{1,0:T(8,128)(2,1)S(1)}, bf16[2,1,1408,1024]{3,2,1,0:T(8,128)(2,1)S(1)}, bf16[1,1408,1024]{2,1,0:T(8,128)(2,1)S(1)}) custom-call(bf16[48,1152]{1,0:T(8,128)(2,1)S(1)} %attention.1.sent_ref, bf16[2,1,1408,1024]{3,2,1,0:T(8,128)(2,1)} %in_ref.1, bf16[1,1408,1024]{2,1,0:T(8,128)(2,1)} %down_ref.1), custom_call_target="tpu_custom_call" | custom-call | bytes 8650752 | tf_op jit(solution)/shard_map/fetch_experts/pallas_call | solution.py:485
  27.5 0.1 collective-permute-start.7
  27.6 0.5 collective-permute-start.11
  28.0 1.2 %collective-permute-done.12.refs_6_ = bf16[48,1152]{1,0:T(8,128)(2,1)S(1)} collective-permute-done((bf16[48,1152]{1,0:T(8,128)(2,1)S(1)}, bf16[48,1152]{1,0:T(8,128)(2,1)S(1)}, u32[]{:S(2)}, u32[]{:S(2)}) %collective-permute-start.12) | collective-permute-done | bytes 110624 | tf_op jit(solution)/shard_map/ppermute | solution.py:406
  29.2 0.4 collective-permute-done.8.refs_2_
  29.6 0.1 collective-permute-start.9
  29.7 0.9 %extra.1 = (f32[48,1024]{1,0:T(8,128)S(1)}, f32[48,128]{1,0:T(8,128)S(1)}) custom-call(bf16[48,384]{1,0:T(8,128)(2,1)S(1)} %get-tuple-element.25.refs_0_, bf16[48,384]{1,0:T(8,128)(2,1)S(1)} %collective-permute-done.refs_1_, bf16[48,384]{1,0:T(8,128)(2,1)S(1)} %collective-permute-done.1.refs_2_, bf16[48,384]{1,0:T(8,128)(2,1)S(1)} %collective-permute-done.2.refs_3_, ...), custom_call_target="tpu_custom_call" | custom-call | tf_op jit(solution)/shard_map/extra/pallas_call | solution.py:521
  30.7 0.3 collective-permute-done.9.refs_3_
  30.9 1.0 %project.1.refs_0_ = bf16[48,128]{1,0:T(8,128)(2,1)S(1)} custom-call(bf16[48,1152]{1,0:T(8,128)(2,1)S(1)} %get-tuple-element.29.refs_0_, bf16[48,1152]{1,0:T(8,128)(2,1)S(1)} %collective-permute-done.7.refs_1_, bf16[48,1152]{1,0:T(8,128)(2,1)S(1)} %collective-permute-done.8.refs_2_, bf16[48,1152]{1,0:T(8,128)(2,1)S(1)} %collective-permute-done.9.refs_3_, ...), custom_call_target="tpu_custom_call" | custom-call | tf_op jit(solution)/shard_map/project/pallas_call | solution.py:534
  32.0 1.7 %collective-permute-start.15 = (bf16[48,128]{1,0:T(8,128)(2,1)S(1)}, bf16[48,128]{1,0:T(8,128)(2,1)S(1)}, u32[]{:S(2)}, u32[]{:S(2)}) collective-permute-start(bf16[48,128]{1,0:T(8,128)(2,1)S(1)} %project.1.refs_0_), channel_id=1, source_target_pairs={{0,8},{4,12},{8,0},{12,4},{16,24},{20,28},{24,16},{28,20},{1,9},{5... | collective-permute-start | bytes 36872 | tf_op jit(solution)/shard_map/ppermute | solution.py:406
  33.7 1.5 %collective-permute-start.17 = (bf16[48,128]{1,0:T(8,128)(2,1)S(1)}, bf16[48,128]{1,0:T(8,128)(2,1)S(1)}, u32[]{:S(2)}, u32[]{:S(2)}) collective-permute-start(bf16[48,128]{1,0:T(8,128)(2,1)S(1)} %project.1.refs_0_), channel_id=1, source_target_pairs={{0,16},{4,20},{8,24},{12,28},{16,0},{20,4},{24,8},{28,12},{1,17},{... | collective-permute-start | bytes 36872 | tf_op jit(solution)/shard_map/ppermute | solution.py:406
  35.2 0.3 collective-permute-start.19
  35.5 0.2 collective-permute-done.15.refs_2_
  35.7 0.3 collective-permute-start.16
  36.0 1.3 %collective-permute-done.17.refs_4_ = bf16[48,128]{1,0:T(8,128)(2,1)S(1)} collective-permute-done((bf16[48,128]{1,0:T(8,128)(2,1)S(1)}, bf16[48,128]{1,0:T(8,128)(2,1)S(1)}, u32[]{:S(2)}, u32[]{:S(2)}) %collective-permute-start.17) | collective-permute-done | bytes 12320 | tf_op jit(solution)/shard_map/ppermute | solution.py:406
  37.4 2.4 %collective-permute-done.19.refs_6_ = bf16[48,128]{1,0:T(8,128)(2,1)S(1)} collective-permute-done((bf16[48,128]{1,0:T(8,128)(2,1)S(1)}, bf16[48,128]{1,0:T(8,128)(2,1)S(1)}, u32[]{:S(2)}, u32[]{:S(2)}) %collective-permute-start.19) | collective-permute-done | bytes 12320 | tf_op jit(solution)/shard_map/ppermute | solution.py:406
  39.8 0.4 routing.1
  40.2 0.7 %collective-permute-done.20.refs_7_ = bf16[48,128]{1,0:T(8,128)(2,1)S(1)} collective-permute-done((bf16[48,128]{1,0:T(8,128)(2,1)S(1)}, bf16[48,128]{1,0:T(8,128)(2,1)S(1)}, u32[]{:S(2)}, u32[]{:S(2)}) %collective-permute-start.20) | collective-permute-done | bytes 12320 | tf_op jit(solution)/shard_map/ppermute | solution.py:406
  41.0 0.3 residual.1
  41.3 1.6 %collective-permute-start.21 = (bf16[8,1024]{1,0:T(8,128)(2,1)S(1)}, bf16[8,1024]{1,0:T(8,128)(2,1)S(1)}, u32[]{:S(2)}, u32[]{:S(2)}) collective-permute-start(bf16[8,1024]{1,0:T(8,128)(2,1)S(1)} %get-tuple-element.39), channel_id=1, source_target_pairs={{0,1},{1,0},{2,3},{3,2},{4,5},{5,4},{6,7},{7,6},{8,9},{9,8},{10,11... | collective-permute-start | bytes 49160 | tf_op jit(solution)/shard_map/ppermute | solution.py:566
  42.9 2.6 %collective-permute-start.22 = (bf16[8,1024]{1,0:T(8,128)(2,1)S(1)}, bf16[8,1024]{1,0:T(8,128)(2,1)S(1)}, u32[]{:S(2)}, u32[]{:S(2)}) collective-permute-start(bf16[8,1024]{1,0:T(8,128)(2,1)S(1)} %get-tuple-element.40), channel_id=1, source_target_pairs={{0,2},{1,3},{2,0},{3,1},{4,6},{5,7},{6,4},{7,5},{8,10},{9,11},{10,... | collective-permute-start | bytes 49160 | tf_op jit(solution)/shard_map/ppermute | solution.py:566
  45.5 0.2 collective-permute-start.23
  45.7 1.9 %collective-permute-done.22.refs_2_ = bf16[8,1024]{1,0:T(8,128)(2,1)S(1)} collective-permute-done((bf16[8,1024]{1,0:T(8,128)(2,1)S(1)}, bf16[8,1024]{1,0:T(8,128)(2,1)S(1)}, u32[]{:S(2)}, u32[]{:S(2)}) %collective-permute-start.22) | collective-permute-done | bytes 16416 | tf_op jit(solution)/shard_map/ppermute | solution.py:566
  47.6 3.4 %collective-permute-done.23.refs_3_ = bf16[8,1024]{1,0:T(8,128)(2,1)S(1)} collective-permute-done((bf16[8,1024]{1,0:T(8,128)(2,1)S(1)}, bf16[8,1024]{1,0:T(8,128)(2,1)S(1)}, u32[]{:S(2)}, u32[]{:S(2)}) %collective-permute-start.23) | collective-permute-done | bytes 16416 | tf_op jit(solution)/shard_map/ppermute | solution.py:566
  51.1 2.3 %expert.1 = (f32[32,512]{1,0:T(8,128)S(1)}, f32[32,512]{1,0:T(8,128)S(1)}) custom-call(bf16[2,1,1408,1024]{3,2,1,0:T(8,128)(2,1)S(1)} %get-tuple-element.36.in_ref, bf16[1,1408,1024]{2,1,0:T(8,128)(2,1)S(1)} %get-tuple-element.37.down_ref, bf16[8,1024]{1,0:T(8,128)(2,1)S(1)} %get-tuple-element.38.refs_0_, ...), custom_call_target="tpu_custom_call" | custom-call | tf_op jit(solution)/shard_map/expert/pallas_call | solution.py:577
  53.3 0.1 collective-permute-start.24
  53.4 1.2 %collective-permute-done.24.other_ref = f32[32,512]{1,0:T(8,128)S(1)} collective-permute-done((f32[32,512]{1,0:T(8,128)S(1)}, f32[32,512]{1,0:T(8,128)S(1)}, u32[]{:S(2)}, u32[]{:S(2)}) %collective-permute-start.24) | collective-permute-done | bytes 65568 | tf_op jit(solution)/shard_map/ppermute | solution.py:590
  54.7 0.7 %spread.1 = bf16[32,8,512]{2,1,0:T(8,128)(2,1)} custom-call(f32[32,512]{1,0:T(8,128)S(1)} %get-tuple-element.42.kept_ref, f32[32,512]{1,0:T(8,128)S(1)} %collective-permute-done.24.other_ref), custom_call_target="tpu_custom_call" | custom-call | tf_op jit(solution)/shard_map/spread/pallas_call | solution.py:598
  55.4 2.6 %all-to-all-start = ((bf16[32,8,512]{2,1,0:T(8,128)(2,1)}), bf16[32,8,512]{2,1,0:T(8,128)(2,1)S(1)}, u32[]{:S(2)}, u32[]{:S(2)}) async-start(bf16[32,8,512]{2,1,0:T(8,128)(2,1)} %spread.1), calls=%async_computation | async-start | bytes 524288 | tf_op jit(solution)/shard_map/all_to_all | solution.py:604
  58.0 0.2 gate.1.gates_ref
  58.2 9.9 %all-to-all-done = bf16[32,8,512]{2,1,0:T(8,128)(2,1)S(1)} async-done(((bf16[32,8,512]{2,1,0:T(8,128)(2,1)}), bf16[32,8,512]{2,1,0:T(8,128)(2,1)S(1)}, u32[]{:S(2)}, u32[]{:S(2)}) %all-to-all-start) | async-done | bytes 262176 | tf_op jit(solution)/shard_map/all_to_all | solution.py:604
  68.2 0.9 %final.1 = bf16[12,4,1024]{2,1,0:T(4,128)(2,1)} custom-call(f32[48,128]{1,0:T(8,128)S(1)} %gate.1.gates_ref, bf16[8,4,8,512]{3,2,1,0:T(8,128)(2,1)S(1)} %bitcast.5, f32[48,1024]{1,0:T(8,128)S(1)} %get-tuple-element.44.residual_ref), custom_call_target="tpu_custom_call" | custom-call | tf_op jit(solution)/shard_map/final/pallas_call | solution.py:612
  (30 shorter events, 0.1 us)
Async XLA Ops:
  1.6 10.1 %collective-permute-start.1 = (bf16[48,384]{1,0:T(8,128)(2,1)S(1)}, bf16[48,384]{1,0:T(8,128)(2,1)S(1)}, u32[]{:S(2)}, u32[]{:S(2)}) collective-permute-start(bf16[48,384]{1,0:T(8,128)(2,1)S(1)} %qkv.1.sent_ref), channel_id=1, source_target_pairs={{0,8},{4,12},{8,0},{12,4},{16,24},{20,28},{24,16},{28,20},{1,9},{5... | collective-permute-start | bytes 110600 | tf_op jit(solution)/shard_map/ppermute | solution.py:406
  4.6 7.6 %collective-permute-start.3 = (bf16[48,384]{1,0:T(8,128)(2,1)S(1)}, bf16[48,384]{1,0:T(8,128)(2,1)S(1)}, u32[]{:S(2)}, u32[]{:S(2)}) collective-permute-start(bf16[48,384]{1,0:T(8,128)(2,1)S(1)} %qkv.1.sent_ref), channel_id=1, source_target_pairs={{0,16},{4,20},{8,24},{12,28},{16,0},{20,4},{24,8},{28,12},{1,17},{... | collective-permute-start | bytes 110600 | tf_op jit(solution)/shard_map/ppermute | solution.py:406
  6.2 6.2 %collective-permute-start.5 = (bf16[48,384]{1,0:T(8,128)(2,1)S(1)}, bf16[48,384]{1,0:T(8,128)(2,1)S(1)}, u32[]{:S(2)}, u32[]{:S(2)}) collective-permute-start(bf16[48,384]{1,0:T(8,128)(2,1)S(1)} %qkv.1.sent_ref), channel_id=1, source_target_pairs={{0,24},{4,28},{8,16},{12,20},{16,8},{20,12},{24,0},{28,4},{1,25},{... | collective-permute-start | bytes 110600 | tf_op jit(solution)/shard_map/ppermute | solution.py:406
  11.7 1.3 %collective-permute-start = (bf16[48,384]{1,0:T(8,128)(2,1)S(1)}, bf16[48,384]{1,0:T(8,128)(2,1)S(1)}, u32[]{:S(2)}, u32[]{:S(2)}) collective-permute-start(bf16[48,384]{1,0:T(8,128)(2,1)S(1)} %get-tuple-element.25.refs_0_), channel_id=1, source_target_pairs={{0,4},{4,0},{8,12},{12,8},{16,20},{20,16},{24,28},{28,24},{1,5},{5... | collective-permute-start | bytes 110600 | tf_op jit(solution)/shard_map/ppermute | solution.py:406
  11.8 1.4 %collective-permute-start.2 = (bf16[48,384]{1,0:T(8,128)(2,1)S(1)}, bf16[48,384]{1,0:T(8,128)(2,1)S(1)}, u32[]{:S(2)}, u32[]{:S(2)}) collective-permute-start(bf16[48,384]{1,0:T(8,128)(2,1)S(1)} %collective-permute-done.1.refs_2_), channel_id=1, source_target_pairs={{0,4},{4,0},{8,12},{12,8},{16,20},{20,16},{24,28},{28,24},{1,5},{5... | collective-permute-start | bytes 110600 | tf_op jit(solution)/shard_map/ppermute | solution.py:406
  12.3 1.2 %collective-permute-start.4 = (bf16[48,384]{1,0:T(8,128)(2,1)S(1)}, bf16[48,384]{1,0:T(8,128)(2,1)S(1)}, u32[]{:S(2)}, u32[]{:S(2)}) collective-permute-start(bf16[48,384]{1,0:T(8,128)(2,1)S(1)} %collective-permute-done.3.refs_4_), channel_id=1, source_target_pairs={{0,4},{4,0},{8,12},{12,8},{16,20},{20,16},{24,28},{28,24},{1,5},{5... | collective-permute-start | bytes 110600 | tf_op jit(solution)/shard_map/ppermute | solution.py:406
  12.4 1.3 %collective-permute-start.6 = (bf16[48,384]{1,0:T(8,128)(2,1)S(1)}, bf16[48,384]{1,0:T(8,128)(2,1)S(1)}, u32[]{:S(2)}, u32[]{:S(2)}) collective-permute-start(bf16[48,384]{1,0:T(8,128)(2,1)S(1)} %collective-permute-done.5.refs_6_), channel_id=1, source_target_pairs={{0,4},{4,0},{8,12},{12,8},{16,20},{20,16},{24,28},{28,24},{1,5},{5... | collective-permute-start | bytes 110600 | tf_op jit(solution)/shard_map/ppermute | solution.py:406
  20.3 9.4 %copy-start.2 = (bf16[2,12,4,1024]{3,2,1,0:T(4,128)(2,1)S(1)}, bf16[2,12,4,1024]{3,2,1,0:T(4,128)(2,1)}, u32[]{:S(2)}) copy-start(bf16[2,12,4,1024]{3,2,1,0:T(4,128)(2,1)} %refs_8_.2) | copy-start | bytes 589828
  20.3 10.7 %copy-start.1 = (bf16[128,1024]{1,0:T(8,128)(2,1)S(1)}, bf16[128,1024]{1,0:T(8,128)(2,1)}, u32[]{:S(2)}) copy-start(bf16[128,1024]{1,0:T(8,128)(2,1)} %refs_10_.1) | copy-start | bytes 786436
  20.3 19.5 %copy-start.5 = (s32[12,4,2]{0,2,1:T(2,128)S(1)}, s32[12,4,2]{0,2,1:T(2,128)}, u32[]{:S(2)}) copy-start(s32[12,4,2]{0,2,1:T(2,128)} %param.22) | copy-start | bytes 1156
  20.3 19.5 %copy-start.6 = (s32[1,48]{1,0:T(1,128)S(1)}, s32[1,48]{1,0:T(1,128)}, u32[]{:S(2)}) copy-start(s32[1,48]{1,0:T(1,128)} %order_ref.1) | copy-start | bytes 580
  20.3 20.6 %copy-start = (bf16[12,4,1024]{2,1,0:T(4,128)(2,1)S(1)}, bf16[12,4,1024]{2,1,0:T(4,128)(2,1)}, u32[]{:S(2)}) copy-start(bf16[12,4,1024]{2,1,0:T(4,128)(2,1)} %refs_8_.3) | copy-start | bytes 294916
  20.3 20.6 %copy-start.4 = (f32[1024]{0:T(1024)S(1)}, f32[1024]{0:T(1024)}, u32[]{:S(2)}) copy-start(f32[1024]{0:T(1024)} %param.20) | copy-start | bytes 12292
  20.3 7.2 %collective-permute-start.10 = (bf16[48,1152]{1,0:T(8,128)(2,1)S(1)}, bf16[48,1152]{1,0:T(8,128)(2,1)S(1)}, u32[]{:S(2)}, u32[]{:S(2)}) collective-permute-start(bf16[48,1152]{1,0:T(8,128)(2,1)S(1)} %attention.1.sent_ref), channel_id=1, source_target_pairs={{0,16},{4,20},{8,24},{12,28},{16,0},{20,4},{24,8},{28,12},{1,17},{... | collective-permute-start | bytes 331784 | tf_op jit(solution)/shard_map/ppermute | solution.py:406
  22.4 6.8 %collective-permute-start.12 = (bf16[48,1152]{1,0:T(8,128)(2,1)S(1)}, bf16[48,1152]{1,0:T(8,128)(2,1)S(1)}, u32[]{:S(2)}, u32[]{:S(2)}) collective-permute-start(bf16[48,1152]{1,0:T(8,128)(2,1)S(1)} %attention.1.sent_ref), channel_id=1, source_target_pairs={{0,24},{4,28},{8,16},{12,20},{16,8},{20,12},{24,0},{28,4},{1,25},{... | collective-permute-start | bytes 331784 | tf_op jit(solution)/shard_map/ppermute | solution.py:406
  23.8 5.8 %collective-permute-start.8 = (bf16[48,1152]{1,0:T(8,128)(2,1)S(1)}, bf16[48,1152]{1,0:T(8,128)(2,1)S(1)}, u32[]{:S(2)}, u32[]{:S(2)}) collective-permute-start(bf16[48,1152]{1,0:T(8,128)(2,1)S(1)} %attention.1.sent_ref), channel_id=1, source_target_pairs={{0,8},{4,12},{8,0},{12,4},{16,24},{20,28},{24,16},{28,20},{1,9},{5... | collective-permute-start | bytes 331784 | tf_op jit(solution)/shard_map/ppermute | solution.py:406
  27.5 3.2 %collective-permute-start.7 = (bf16[48,1152]{1,0:T(8,128)(2,1)S(1)}, bf16[48,1152]{1,0:T(8,128)(2,1)S(1)}, u32[]{:S(2)}, u32[]{:S(2)}) collective-permute-start(bf16[48,1152]{1,0:T(8,128)(2,1)S(1)} %get-tuple-element.29.refs_0_), channel_id=1, source_target_pairs={{0,4},{4,0},{8,12},{12,8},{16,20},{20,16},{24,28},{28,24},{1,5},{5... | collective-permute-start | bytes 331784 | tf_op jit(solution)/shard_map/ppermute | solution.py:406
  27.6 3.1 %collective-permute-start.11 = (bf16[48,1152]{1,0:T(8,128)(2,1)S(1)}, bf16[48,1152]{1,0:T(8,128)(2,1)S(1)}, u32[]{:S(2)}, u32[]{:S(2)}) collective-permute-start(bf16[48,1152]{1,0:T(8,128)(2,1)S(1)} %collective-permute-done.10.refs_4_), channel_id=1, source_target_pairs={{0,4},{4,0},{8,12},{12,8},{16,20},{20,16},{24,28},{28,24},{1,5},{5... | collective-permute-start | bytes 331784 | tf_op jit(solution)/shard_map/ppermute | solution.py:406
  29.2 1.5 %collective-permute-start.13 = (bf16[48,1152]{1,0:T(8,128)(2,1)S(1)}, bf16[48,1152]{1,0:T(8,128)(2,1)S(1)}, u32[]{:S(2)}, u32[]{:S(2)}) collective-permute-start(bf16[48,1152]{1,0:T(8,128)(2,1)S(1)} %collective-permute-done.12.refs_6_), channel_id=1, source_target_pairs={{0,4},{4,0},{8,12},{12,8},{16,20},{20,16},{24,28},{28,24},{1,5},{5... | collective-permute-start | bytes 331784 | tf_op jit(solution)/shard_map/ppermute | solution.py:406
  29.6 1.3 %collective-permute-start.9 = (bf16[48,1152]{1,0:T(8,128)(2,1)S(1)}, bf16[48,1152]{1,0:T(8,128)(2,1)S(1)}, u32[]{:S(2)}, u32[]{:S(2)}) collective-permute-start(bf16[48,1152]{1,0:T(8,128)(2,1)S(1)} %collective-permute-done.8.refs_2_), channel_id=1, source_target_pairs={{0,4},{4,0},{8,12},{12,8},{16,20},{20,16},{24,28},{28,24},{1,5},{5... | collective-permute-start | bytes 331784 | tf_op jit(solution)/shard_map/ppermute | solution.py:406
  30.6 27.4 %copy-start.3 = (bf16[1024,16]{0,1:T(8,128)(2,1)S(1)}, bf16[1024,16]{0,1:T(8,128)(2,1)}, u32[]{:S(2)}) copy-start(bf16[1024,16]{0,1:T(8,128)(2,1)} %param.21) | copy-start | bytes 98308
  32.0 3.8 %collective-permute-start.15 = (bf16[48,128]{1,0:T(8,128)(2,1)S(1)}, bf16[48,128]{1,0:T(8,128)(2,1)S(1)}, u32[]{:S(2)}, u32[]{:S(2)}) collective-permute-start(bf16[48,128]{1,0:T(8,128)(2,1)S(1)} %project.1.refs_0_), channel_id=1, source_target_pairs={{0,8},{4,12},{8,0},{12,4},{16,24},{20,28},{24,16},{28,20},{1,9},{5... | collective-permute-start | bytes 36872 | tf_op jit(solution)/shard_map/ppermute | solution.py:406
  33.7 3.7 %collective-permute-start.17 = (bf16[48,128]{1,0:T(8,128)(2,1)S(1)}, bf16[48,128]{1,0:T(8,128)(2,1)S(1)}, u32[]{:S(2)}, u32[]{:S(2)}) collective-permute-start(bf16[48,128]{1,0:T(8,128)(2,1)S(1)} %project.1.refs_0_), channel_id=1, source_target_pairs={{0,16},{4,20},{8,24},{12,28},{16,0},{20,4},{24,8},{28,12},{1,17},{... | collective-permute-start | bytes 36872 | tf_op jit(solution)/shard_map/ppermute | solution.py:406
  35.2 4.6 %collective-permute-start.19 = (bf16[48,128]{1,0:T(8,128)(2,1)S(1)}, bf16[48,128]{1,0:T(8,128)(2,1)S(1)}, u32[]{:S(2)}, u32[]{:S(2)}) collective-permute-start(bf16[48,128]{1,0:T(8,128)(2,1)S(1)} %project.1.refs_0_), channel_id=1, source_target_pairs={{0,24},{4,28},{8,16},{12,20},{16,8},{20,12},{24,0},{28,4},{1,25},{... | collective-permute-start | bytes 36872 | tf_op jit(solution)/shard_map/ppermute | solution.py:406
  35.5 4.7 %collective-permute-start.14 = (bf16[48,128]{1,0:T(8,128)(2,1)S(1)}, bf16[48,128]{1,0:T(8,128)(2,1)S(1)}, u32[]{:S(2)}, u32[]{:S(2)}) collective-permute-start(bf16[48,128]{1,0:T(8,128)(2,1)S(1)} %project.1.refs_0_), channel_id=1, source_target_pairs={{0,4},{4,0},{8,12},{12,8},{16,20},{20,16},{24,28},{28,24},{1,5},{5... | collective-permute-start | bytes 36872 | tf_op jit(solution)/shard_map/ppermute | solution.py:406
  35.7 4.5 %collective-permute-start.16 = (bf16[48,128]{1,0:T(8,128)(2,1)S(1)}, bf16[48,128]{1,0:T(8,128)(2,1)S(1)}, u32[]{:S(2)}, u32[]{:S(2)}) collective-permute-start(bf16[48,128]{1,0:T(8,128)(2,1)S(1)} %collective-permute-done.15.refs_2_), channel_id=1, source_target_pairs={{0,4},{4,0},{8,12},{12,8},{16,20},{20,16},{24,28},{28,24},{1,5},{5... | collective-permute-start | bytes 36872 | tf_op jit(solution)/shard_map/ppermute | solution.py:406
  37.4 2.8 %collective-permute-start.18 = (bf16[48,128]{1,0:T(8,128)(2,1)S(1)}, bf16[48,128]{1,0:T(8,128)(2,1)S(1)}, u32[]{:S(2)}, u32[]{:S(2)}) collective-permute-start(bf16[48,128]{1,0:T(8,128)(2,1)S(1)} %collective-permute-done.17.refs_4_), channel_id=1, source_target_pairs={{0,4},{4,0},{8,12},{12,8},{16,20},{20,16},{24,28},{28,24},{1,5},{5... | collective-permute-start | bytes 36872 | tf_op jit(solution)/shard_map/ppermute | solution.py:406
  39.8 1.2 %collective-permute-start.20 = (bf16[48,128]{1,0:T(8,128)(2,1)S(1)}, bf16[48,128]{1,0:T(8,128)(2,1)S(1)}, u32[]{:S(2)}, u32[]{:S(2)}) collective-permute-start(bf16[48,128]{1,0:T(8,128)(2,1)S(1)} %collective-permute-done.19.refs_6_), channel_id=1, source_target_pairs={{0,4},{4,0},{8,12},{12,8},{16,20},{20,16},{24,28},{28,24},{1,5},{5... | collective-permute-start | bytes 36872 | tf_op jit(solution)/shard_map/ppermute | solution.py:406
  41.3 4.5 %collective-permute-start.21 = (bf16[8,1024]{1,0:T(8,128)(2,1)S(1)}, bf16[8,1024]{1,0:T(8,128)(2,1)S(1)}, u32[]{:S(2)}, u32[]{:S(2)}) collective-permute-start(bf16[8,1024]{1,0:T(8,128)(2,1)S(1)} %get-tuple-element.39), channel_id=1, source_target_pairs={{0,1},{1,0},{2,3},{3,2},{4,5},{5,4},{6,7},{7,6},{8,9},{9,8},{10,11... | collective-permute-start | bytes 49160 | tf_op jit(solution)/shard_map/ppermute | solution.py:566
  42.9 4.7 %collective-permute-start.22 = (bf16[8,1024]{1,0:T(8,128)(2,1)S(1)}, bf16[8,1024]{1,0:T(8,128)(2,1)S(1)}, u32[]{:S(2)}, u32[]{:S(2)}) collective-permute-start(bf16[8,1024]{1,0:T(8,128)(2,1)S(1)} %get-tuple-element.40), channel_id=1, source_target_pairs={{0,2},{1,3},{2,0},{3,1},{4,6},{5,7},{6,4},{7,5},{8,10},{9,11},{10,... | collective-permute-start | bytes 49160 | tf_op jit(solution)/shard_map/ppermute | solution.py:566
  45.5 5.5 %collective-permute-start.23 = (bf16[8,1024]{1,0:T(8,128)(2,1)S(1)}, bf16[8,1024]{1,0:T(8,128)(2,1)S(1)}, u32[]{:S(2)}, u32[]{:S(2)}) collective-permute-start(bf16[8,1024]{1,0:T(8,128)(2,1)S(1)} %get-tuple-element.41), channel_id=1, source_target_pairs={{0,3},{1,2},{2,1},{3,0},{4,7},{5,6},{6,5},{7,4},{8,11},{9,10},{10,... | collective-permute-start | bytes 49160 | tf_op jit(solution)/shard_map/ppermute | solution.py:566
  53.3 1.3 %collective-permute-start.24 = (f32[32,512]{1,0:T(8,128)S(1)}, f32[32,512]{1,0:T(8,128)S(1)}, u32[]{:S(2)}, u32[]{:S(2)}) collective-permute-start(f32[32,512]{1,0:T(8,128)S(1)} %get-tuple-element.43), channel_id=1, source_target_pairs={{0,4},{4,0},{8,12},{12,8},{16,20},{20,16},{24,28},{28,24},{1,5},{5... | collective-permute-start | bytes 196616 | tf_op jit(solution)/shard_map/ppermute | solution.py:590
  55.4 12.8 %all-to-all-start = ((bf16[32,8,512]{2,1,0:T(8,128)(2,1)}), bf16[32,8,512]{2,1,0:T(8,128)(2,1)S(1)}, u32[]{:S(2)}, u32[]{:S(2)}) async-start(bf16[32,8,512]{2,1,0:T(8,128)(2,1)} %spread.1), calls=%async_computation | async-start | bytes 524288 | tf_op jit(solution)/shard_map/all_to_all | solution.py:604

commit v5 on v4

--- a/solution.py
+++ b/solution.py
@@ -17,6 +17,7 @@
 LANES = 128
 PIECES = 3
 EARLY = 3
+PIECE = 512
 BLOCK = 256
 BLOCK_HEADS = BLOCK // HD
 
@@ -63,15 +64,52 @@
         rows_ref[r * steps : (r + 1) * steps, :] = source_ref[r].astype(rows_ref.dtype)
 
 
-def qkv_kernel(tokens_ref, gain_ref, weight_ref, out_ref, token_buf, gain_buf, weight_buf, rows_ref, sems):
-    copies = [
-        pltpu.make_async_copy(source, target, sems.at[i])
-        for i, (source, target) in enumerate(
-            ((tokens_ref, token_buf), (gain_ref, gain_buf), (weight_ref, weight_buf))
-        )
-    ]
+def started(pairs, sems):
+    copies = [pltpu.make_async_copy(*pair, sems.at[i]) for i, pair in enumerate(pairs)]
     for copy in copies:
         copy.start()
+    return copies
+
+
+def route(ids_ref, order_ref, select_ref, chosen_ref):
+    steps, _, requests = ids_ref.shape
+    rows = requests * steps
+    lane = lax.broadcasted_iota(jnp.int32, (rows, LANES), 1)
+    own_row = lax.broadcasted_iota(jnp.int32, (rows, requests), 0)
+    own_request = lax.broadcasted_iota(jnp.int32, (rows, requests), 1) == own_row // steps
+    chosen = []
+    for c in range(TOPK):
+        ids = jnp.zeros((rows, requests), jnp.int32)
+        for t in range(steps):
+            ids = jnp.where(own_request & (own_row % steps == t), ids_ref[t, c : c + 1, :], ids)
+        chosen.append(jnp.sum(ids.astype(jnp.float32), axis=1, keepdims=True).astype(jnp.int32))
+    onehot = [(lane == ids).astype(jnp.float32) for ids in chosen]
+    square_row = lax.broadcasted_iota(jnp.int32, (rows, rows), 0)
+    square_col = lax.broadcasted_iota(jnp.int32, (rows, rows), 1)
+    order_wide = jnp.broadcast_to(order_ref[...], (rows, rows))
+    down = jnp.sum(
+        jnp.where(square_row == square_col, order_wide, 0).astype(jnp.float32),
+        axis=1,
+        keepdims=True,
+    )
+    earlier = (order_wide.astype(jnp.float32) < down).astype(jnp.bfloat16)
+    counts = dot(earlier, sum(onehot).astype(jnp.bfloat16))
+    slot = lax.broadcasted_iota(jnp.int32, (rows, EXPERTS * CAP), 1)
+    both = jnp.zeros((rows, EXPERTS * CAP), jnp.float32)
+    for c in range(TOPK):
+        position = jnp.sum(onehot[c] * counts, axis=-1, keepdims=True).astype(jnp.int32)
+        column = chosen[c] * CAP + position
+        select = ((column == slot) & (position < CAP)).astype(jnp.float32)
+        select_ref[c] = select
+        chosen_ref[c] = onehot[c]
+        both = both + select
+    return jnp.transpose(both)
+
+
+def qkv_kernel(tokens_ref, gain_ref, weight_ref, out_ref, token_buf, gain_buf, weight_buf, rows_ref, sems):
+    copies = started(
+        ((tokens_ref, token_buf), (gain_ref, gain_buf), (weight_ref, weight_buf)), sems
+    )
     for copy in copies:
         copy.wait()
     copy_rows(token_buf, rows_ref)
@@ -92,32 +130,40 @@
 
 
 def fetch_window_kernel(
-    early, sent_ref, window_ref, lengths_ref, held_ref, keys_ref, values_ref, spans_ref, numbers_ref, sems
+    sent_ref,
+    window_ref,
+    lengths_ref,
+    ids_ref,
+    order_ref,
+    held_ref,
+    keys_ref,
+    values_ref,
+    spans_ref,
+    select_ref,
+    chosen_ref,
+    turned_ref,
+    numbers_ref,
+    ids_buf,
+    order_buf,
+    sems,
 ):
-    copies = [
-        pltpu.make_async_copy(lengths_ref, numbers_ref, sems.at[0]),
-        pltpu.make_async_copy(window_ref.at[0], keys_ref, sems.at[1]),
-        pltpu.make_async_copy(window_ref.at[1, pl.ds(0, early)], values_ref, sems.at[2]),
-    ]
-    for copy in copies:
-        copy.start()
+    copies = started(
+        (
+            (ids_ref, ids_buf),
+            (order_ref, order_buf),
+            (lengths_ref, numbers_ref),
+            (window_ref.at[0], keys_ref),
+            (window_ref.at[1, pl.ds(0, values_ref.shape[0])], values_ref),
+        ),
+        sems,
+    )
     held_ref[...] = sent_ref[...]
-    copies[0].wait()
+    for copy in copies[:3]:
+        copy.wait()
+    turned_ref[...] = route(ids_buf, order_buf, select_ref, chosen_ref)
     for r in range(spans_ref.shape[0]):
         spans_ref[r : r + 1, :] = jnp.full((1, LANES), numbers_ref[r], jnp.int32)
-    copies[1].wait()
-    copies[2].wait()
-
-
-def fetch_experts_kernel(sent_ref, in_ref, down_ref, held_ref, in_out, down_out, sems):
-    copies = [
-        pltpu.make_async_copy(in_ref, in_out, sems.at[0]),
-        pltpu.make_async_copy(down_ref, down_out, sems.at[1]),
-    ]
-    for copy in copies:
-        copy.start()
-    held_ref[...] = sent_ref[...]
-    for copy in copies:
+    for copy in copies[3:]:
         copy.wait()
 
 
@@ -252,7 +298,8 @@
 
 
 def project_kernel(*refs):
-    *part_refs, extra_ref, extra_stats_ref, weight_ref, out_ref, ordered_ref = refs
+    *part_refs, extra_ref, extra_stats_ref, weight_ref, tokens_ref, turned_ref = refs[:-4]
+    out_ref, residual_ref, ordered_ref, rows_ref = refs[-4:]
     devices, rows, padded = ordered_ref.shape
     width = padded - LANES
     in_order(part_refs, ordered_ref)
@@ -279,85 +326,68 @@
     attended = spread(factors[-1]) * extra_ref[...]
     for d in range(devices):
         attended = attended + spread(factors[d]) * ordered_ref[d][:, :width].astype(jnp.float32)
-    out_ref[...] = dot(attended.astype(jnp.bfloat16), weight_ref[...], ROWS_BY_ROWS).astype(
-        jnp.bfloat16
-    )
-
-
-def routing_kernel(ids_ref, order_ref, select_ref, turned_ref, chosen_ref):
-    steps, _, requests = ids_ref.shape
-    rows = requests * steps
-    lane = lax.broadcasted_iota(jnp.int32, (rows, LANES), 1)
-    own_row = lax.broadcasted_iota(jnp.int32, (rows, requests), 0)
-    own_request = lax.broadcasted_iota(jnp.int32, (rows, requests), 1) == own_row // steps
-    chosen = []
-    for c in range(TOPK):
-        ids = jnp.zeros((rows, requests), jnp.int32)
-        for t in range(steps):
-            ids = jnp.where(own_request & (own_row % steps == t), ids_ref[t, c : c + 1, :], ids)
-        chosen.append(jnp.sum(ids.astype(jnp.float32), axis=1, keepdims=True).astype(jnp.int32))
-    onehot = [(lane == ids).astype(jnp.float32) for ids in chosen]
-    across = order_ref[...]
-    square_row = lax.broadcasted_iota(jnp.int32, (rows, rows), 0)
-    square_col = lax.broadcasted_iota(jnp.int32, (rows, rows), 1)
-    order_wide = jnp.broadcast_to(across, (rows, rows))
-    down = jnp.sum(
-        jnp.where(square_row == square_col, order_wide, 0).astype(jnp.float32),
-        axis=1,
-        keepdims=True,
-    )
-    earlier = (order_wide.astype(jnp.float32) < down).astype(jnp.bfloat16)
-    counts = dot(earlier, sum(onehot).astype(jnp.bfloat16))
-    slot = lax.broadcasted_iota(jnp.int32, (rows, EXPERTS * CAP), 1)
-    both = jnp.zeros((rows, EXPERTS * CAP), jnp.float32)
-    for c in range(TOPK):
-        position = jnp.sum(onehot[c] * counts, axis=-1, keepdims=True).astype(jnp.int32)
-        column = chosen[c] * CAP + position
-        select = ((column == slot) & (position < CAP)).astype(jnp.float32)
-        select_ref[c] = select
-        chosen_ref[c] = onehot[c]
-        both = both + select
-    turned_ref[...] = jnp.transpose(both)
-
-
-def residual_kernel(devices, *refs):
-    projected_refs, refs = refs[:devices], refs[devices:]
-    tokens_ref, gain_ref, turned_ref, normed_ref, residual_ref, *send_refs, ordered_ref = refs
-    share = ordered_ref.shape[2]
-    in_order(projected_refs, ordered_ref)
-    copy_rows(tokens_ref, residual_ref)
-    for d in range(devices):
-        own = slice(d * share, (d + 1) * share)
-        residual_ref[:, own] = residual_ref[:, own] + ordered_ref[d].astype(jnp.float32)
-    normed = rms_rows(residual_ref[...], gain_ref[...])
-    normed_ref[...] = normed
-    local_experts = EXPERTS // len(send_refs)
-    own = lax.axis_index("seq") // (devices // local_experts)
-    for k, send_ref in enumerate(send_refs):
-        expert = jnp.bitwise_xor(lax.axis_index("exp"), k) * local_experts + own
-        picking = turned_ref[pl.ds(pl.multiple_of(expert * CAP, CAP), CAP), :].astype(jnp.bfloat16)
-        send_ref[...] = dot(picking, normed).astype(jnp.bfloat16)
-
-
-def gate_kernel(normed_ref, router_ref, select_ref, chosen_ref, out_ref):
-    logits = dot(normed_ref[...], router_ref[...], ROWS_BY_ROWS)
+    projected = dot(attended.astype(jnp.bfloat16), weight_ref[...], ROWS_BY_ROWS).astype(jnp.bfloat16)
+    copy_rows(tokens_ref, rows_ref)
+    share = weight_ref.shape[0]
+    feature = lax.broadcasted_iota(jnp.int32, (width, share), 0)
+    column = lax.broadcasted_iota(jnp.int32, (width, share), 1)
+    own = (feature == column + lax.axis_index("seq") * share).astype(jnp.bfloat16)
+    residual = dot(rows_ref[...].astype(jnp.bfloat16), own) + projected.astype(jnp.float32)
+    residual_ref[...] = residual
+    turned = turned_ref[...].astype(jnp.bfloat16)
+    table = sum(dot(turned, part) for part in split(residual, PIECES))
+    groups = lax.axis_size("exp")
+    local_experts = EXPERTS // groups
+    for s in range(devices):
+        for x in range(groups):
+            row = (x * local_experts + s // (devices // local_experts)) * CAP
+            out_ref[s * groups + x] = table[row : row + CAP]
+
+
+def home_kernel(devices, *refs):
+    residual_refs, refs = refs[:devices], refs[devices:]
+    gain_ref, router_ref, select_ref, chosen_ref, residual_ref, gates_ref, ordered_ref = refs
+    in_order(residual_refs, ordered_ref)
+    residual = jnp.concatenate([ordered_ref[d] for d in range(devices)], axis=1)
+    residual_ref[...] = residual
+    normed = rms_rows(residual, gain_ref[...])
+    logits = dot(normed, router_ref[...], ROWS_BY_ROWS)
     gates = jnp.zeros(select_ref.shape[1:], jnp.float32)
     for c in range(TOPK):
         logit = jnp.sum(chosen_ref[c][:, :EXPERTS] * logits, axis=-1, keepdims=True)
         gates = gates + jax.nn.sigmoid(logit) * select_ref[c]
-    out_ref[...] = gates
-
-
-def expert_kernel(in_ref, down_ref, *refs):
-    *received_refs, keep_ref, send_ref, rows_ref = refs
-    groups, slots, width = rows_ref.shape
-    for k, received_ref in enumerate(received_refs):
-        rows_ref[jnp.bitwise_xor(lax.axis_index("exp"), k)] = received_ref[...].astype(jnp.float32)
-    rows = rows_ref[...].reshape(groups * slots, width).astype(jnp.bfloat16)
-    gate = dot(rows, in_ref[0, 0], ROWS_BY_ROWS)
-    up = dot(rows, in_ref[1, 0], ROWS_BY_ROWS)
-    hidden = (jax.nn.gelu(gate, approximate=True) * up).astype(jnp.bfloat16)
-    outputs = dot(hidden, down_ref[0])
+    gates_ref[...] = gates
+
+
+def expert_kernel(
+    received_ref, gain_ref, in_ref, down_ref, keep_ref, send_ref, in_buf, down_buf, sems
+):
+    hidden_units, width = down_buf.shape
+    pieces = [
+        slice(at, min(at + PIECE, hidden_units)) for at in range(0, hidden_units, PIECE)
+    ]
+    pairs = []
+    for piece in pieces:
+        rows = pl.ds(piece.start, piece.stop - piece.start)
+        pairs += [(in_ref.at[p, 0, rows], in_buf.at[p, rows]) for p in range(2)]
+    copies = started(pairs + [(down_ref.at[0], down_buf)], sems)
+    devices = lax.axis_size("seq")
+    groups = lax.axis_size("exp")
+    columns = []
+    for s in range(devices):
+        columns.append(
+            jnp.concatenate([received_ref[s * groups + g] for g in range(groups)], axis=0)
+        )
+    rows = rms_rows(jnp.concatenate(columns, axis=1), gain_ref[...])
+    hidden = []
+    for i, piece in enumerate(pieces):
+        copies[2 * i].wait()
+        gate = dot(rows, in_buf[0, piece], ROWS_BY_ROWS)
+        copies[2 * i + 1].wait()
+        up = dot(rows, in_buf[1, piece], ROWS_BY_ROWS)
+        hidden.append((jax.nn.gelu(gate, approximate=True) * up).astype(jnp.bfloat16))
+    copies[-1].wait()
+    outputs = dot(jnp.concatenate(hidden, axis=1), down_buf[...])
     half = width // 2
     odd = lax.axis_index("seq") % 2 == 1
     keep_ref[...] = jnp.where(odd, outputs[:, half:], outputs[:, :half])
@@ -462,43 +492,43 @@
         name="qkv",
     )(in_hbm(tokens), in_hbm(gain_row), in_hbm(w_qkv))
     early = min(EARLY, requests - 1)
-    fetched = {}
+
+    fetched = []
 
     def fetch_window(values):
-        held, *fetched["window"] = pl.pallas_call(
-            functools.partial(fetch_window_kernel, early),
-            in_specs=[vmem, hbm, hbm],
+        held, *outputs = pl.pallas_call(
+            fetch_window_kernel,
+            in_specs=[vmem] + [hbm] * 4,
             out_shape=(
                 shape(values.shape, bf16),
                 shape((requests, span, width), bf16),
                 shape((early, span, width), bf16),
                 shape((requests, LANES), jnp.int32),
+                shape((TOPK, rows, slots), f32),
+                shape((TOPK, rows, LANES), f32),
+                shape((slots, rows), f32),
             ),
-            scratch_shapes=[pltpu.SMEM((requests,), jnp.int32), pltpu.SemaphoreType.DMA((3,))],
+            scratch_shapes=[
+                pltpu.SMEM((requests,), jnp.int32),
+                pltpu.VMEM((steps, TOPK, requests), jnp.int32),
+                pltpu.VMEM(slot_order.shape, jnp.int32),
+                pltpu.SemaphoreType.DMA((5,)),
+            ],
             compiler_params=params(8),
             cost_estimate=moving(window_cache.size),
             name="fetch_window",
-        )(values, in_hbm(window_cache), in_hbm(lengths))
+        )(
+            values,
+            in_hbm(window_cache),
+            in_hbm(lengths),
+            in_hbm(expert_ids.transpose(1, 2, 0)),
+            in_hbm(slot_order),
+        )
+        fetched.extend(outputs)
         return held
 
-    def fetch_experts(values):
-        held, *fetched["experts"] = pl.pallas_call(
-            fetch_experts_kernel,
-            in_specs=[vmem, hbm, hbm],
-            out_shape=(
-                shape(values.shape, bf16),
-                shape(expert_in.shape, bf16),
-                shape(expert_down.shape, bf16),
-            ),
-            scratch_shapes=[pltpu.SemaphoreType.DMA((2,))],
-            compiler_params=params(8),
-            cost_estimate=moving(2 * (expert_in.size + expert_down.size)),
-            name="fetch_experts",
-        )(values, in_hbm(expert_in), in_hbm(expert_down))
-        return held
-
     mixed = gather_seq(local_mix, fetch_window)
-    keys, values, spans = fetched["window"]
+    keys, values, spans, select, chosen, turned = fetched
 
     padded = width + LANES
     part = pl.pallas_call(
@@ -515,8 +545,7 @@
         compiler_params=params(20),
         name="attention",
     )(*mixed, spans, keys, values, in_hbm(window_cache))
-    parts = gather_seq(part, fetch_experts)
-    local_in, local_down = fetched["experts"]
+    parts = gather_seq(part)
 
     extra, extra_stats = pl.pallas_call(
         extra_kernel,
@@ -531,59 +560,39 @@
         name="extra",
     )(*mixed, sink_cache)
 
-    local_proj = pl.pallas_call(
+    outgoing, residual_columns = pl.pallas_call(
         project_kernel,
-        out_shape=shape((rows, w_out.shape[0]), bf16),
-        scratch_shapes=[pltpu.VMEM((seq_count, rows, padded), bf16)],
+        out_shape=(
+            shape((seq_count * groups, CAP, w_out.shape[0]), f32),
+            shape((rows, w_out.shape[0]), f32),
+        ),
+        scratch_shapes=[
+            pltpu.VMEM((seq_count, rows, padded), bf16),
+            pltpu.VMEM((rows, width), f32),
+        ],
         compiler_params=params(8),
         name="project",
-    )(*parts, extra, extra_stats, w_out)
-    projected = gather_seq(local_proj)
-
-    select, turned, chosen = pl.pallas_call(
-        routing_kernel,
-        out_shape=(
-            shape((TOPK, rows, slots), f32),
-            shape((slots, rows), f32),
-            shape((TOPK, rows, LANES), f32),
-        ),
-        compiler_params=params(8),
-        name="routing",
-    )(expert_ids.transpose(1, 2, 0), slot_order)
-
-    normed, residual, *send = pl.pallas_call(
-        functools.partial(residual_kernel, seq_count),
-        out_shape=(
-            shape((rows, width), bf16),
-            shape((rows, width), f32),
-            *[shape((CAP, width), bf16)] * groups,
-        ),
-        scratch_shapes=[pltpu.VMEM((seq_count, rows, w_out.shape[0]), bf16)],
-        compiler_params=params(8),
-        name="residual",
-    )(*projected, tokens, moe_gain.reshape(1, width), turned)
-    received = [
-        lax.ppermute(block, "exp", [(i, i ^ k) for i in range(groups)]) if k else block
-        for k, block in enumerate(send)
-    ]
-
-    gates = pl.pallas_call(
-        gate_kernel,
-        out_shape=shape((rows, slots), f32),
-        compiler_params=params(8),
-        name="gate",
-    )(normed, router.T, select, chosen)
-
+    )(*parts, extra, extra_stats, w_out, tokens, turned)
+    received = lax.all_to_all(outgoing, ("seq", "exp"), split_axis=0, concat_axis=0, tiled=True)
+    columns = gather_seq(residual_columns)
+
+    moe_row = moe_gain.reshape(1, width)
+    hidden_units = expert_down.shape[1]
     kept, sent = pl.pallas_call(
         expert_kernel,
+        in_specs=[vmem, vmem, hbm, hbm],
         out_shape=(
             shape((groups * CAP, width // 2), f32),
             shape((groups * CAP, width // 2), f32),
         ),
-        scratch_shapes=[pltpu.VMEM((groups, CAP, width), f32)],
-        compiler_params=params(8),
+        scratch_shapes=[
+            pltpu.VMEM((2, hidden_units, width), bf16),
+            pltpu.VMEM((hidden_units, width), bf16),
+            pltpu.SemaphoreType.DMA((2 * pl.cdiv(hidden_units, PIECE) + 1,)),
+        ],
+        compiler_params=params(20),
         name="expert",
-    )(local_in, local_down, *received)
+    )(received, moe_row, in_hbm(expert_in), in_hbm(expert_down))
 
     reach = 1
     while True:
@@ -594,10 +603,10 @@
         upper = (seq_index // reach) % 2 == 1
         low, high = jnp.split(kept + other, 2, axis=1)
         kept, sent = jnp.where(upper, high, low), jnp.where(upper, low, high)
-    columns = kept.shape[1]
+    part_width = kept.shape[1]
     outgoing = pl.pallas_call(
         spread_kernel,
-        out_shape=shape((seq_count * groups, CAP, columns), bf16),
+        out_shape=shape((seq_count * groups, CAP, part_width), bf16),
         compiler_params=params(8),
         name="spread",
     )(kept, other)
@@ -607,7 +616,16 @@
         split_axis=0,
         concat_axis=0,
         tiled=True,
-    ).reshape(seq_count, groups, CAP, columns)
+    ).reshape(seq_count, groups, CAP, part_width)
+
+    columns, _ = lax.optimization_barrier((columns, outgoing))
+    residual, gates = pl.pallas_call(
+        functools.partial(home_kernel, seq_count),
+        out_shape=(shape((rows, width), f32), shape((rows, slots), f32)),
+        scratch_shapes=[pltpu.VMEM((seq_count, rows, w_out.shape[0]), f32)],
+        compiler_params=params(8),
+        name="home",
+    )(*columns, moe_row, router.T, select, chosen)
 
     return pl.pallas_call(
         final_kernel,

time: 69.3 us -> 65.9 us (0.951)
  blocking collectives: 0 us -> 13.5 us
  waiting for transfers between devices: 24 us -> 13.8 us
  starting transfers between devices: 20.8 us -> 15.9 us
  Pallas kernels: 24 us -> 22.3 us
    all_to_all x0 -> x1, blocking collectives: none -> 13.5 us  [body(): lax.all_to_all(outgoing, ('seq', 'exp'), split_axis=0, concat_axis=0, til...]
    all_to_all x1, waiting for transfers between devices: 9.94 us -> 1.54 us  [body(): lax.all_to_all(outgoing, ('seq', 'exp'), split_axis=0, concat_axis=0, til...]
    ppermute x3 -> x0, waiting for transfers between devices: 5.32 us -> none  [body(): lax.ppermute(block, 'exp', [(i, i ^ k) for i in range(groups)])]
    ppermute x3 -> x0, starting transfers between devices: 4.45 us -> none  [body(): lax.ppermute(block, 'exp', [(i, i ^ k) for i in range(groups)])]
    ppermute x21, waiting for transfers between devices: 7.47 us -> 11 us  [exchange(): return lax.ppermute(value, 'seq', [(i, i ^ bits) for i in range(count)])]
    pallas_call x8 -> x5, Pallas kernels: 14 us -> 12.3 us  [the longest x1 5.54 us: fetch_window(): pl.pallas_call(fetch_window_kernel, in_specs=[vmem] + [hbm] * 4, out_shap...]
  transfers between devices with their start and end apart: 26 -> 23, of which waited for: 15 -> 15; matrix products, arithmetic and copies ran while one was open for 0% -> 0% of each run, Pallas kernels for 15% -> 10%
where the time goes in v5:
time: 65.9 us; the launch traced here: 65.6 us
  Pallas kernels  22.3 us (34%)
  starting transfers between devices  15.9 us (24%)
  waiting for transfers between devices  13.8 us (21%)
  blocking collectives  13.5 us (20%)
    all_to_all x1, blocking collectives, body(): lax.all_to_all(outgoing, ('seq', 'exp'), split_axis=0, concat_axis=0, til...  13.5 us
    ppermute x21, starting transfers between devices, exchange(): return lax.ppermute(value, 'seq', [(i, i ^ bits) for i in range(count)])  13.3 us
    ppermute x21, waiting for transfers between devices, exchange(): return lax.ppermute(value, 'seq', [(i, i ^ bits) for i in range(count)])  11 us
    pallas_call x1, Pallas kernels, body(): pl.pallas_call(attention_kernel, in_specs=[vmem] * (seq_count + 3) + [hbm...  6.61 us
    pallas_call x1, Pallas kernels, fetch_window(): pl.pallas_call(fetch_window_kernel, in_specs=[vmem] + [hbm] * 4, out_shap...  5.54 us
    pallas_call x1, Pallas kernels, body(): pl.pallas_call(expert_kernel, in_specs=[vmem, vmem, hbm, hbm], out_shape=...  4.39 us
    all_to_all x1, starting transfers between devices, body(): lax.all_to_all(outgoing, ('seq', 'exp'), split_axis=0, concat_axis=0, til...  2.58 us
    pallas_call x1, Pallas kernels, body(): pl.pallas_call(qkv_kernel, in_specs=[hbm] * 3, out_shape=shape((rows, sha...  1.63 us
  transfers between devices with their start and end apart: 23, of which 15 were waited for; matrix products, arithmetic and copies ran while one was open for 0% of the time, Pallas kernels for 10%

profile of v5, /device:TPU:0, one launch (start us, length us, event | category | flops | bytes accessed | tf_op | source)
XLA Modules:
  0.0 65.6 jit_solution(3934889996235278024)
XLA Ops:
  0.0 1.6 %qkv.1.sent_ref = bf16[48,384]{1,0:T(8,128)(2,1)S(1)} custom-call(bf16[12,4,1024]{2,1,0:T(4,128)(2,1)} %refs_11_.3, f32[1,1024]{1,0:T(1,128)} %bitcast.9, bf16[384,1024]{1,0:T(8,128)(2,1)} %weight_ref.1), custom_call_target="tpu_custom_call" | custom-call | tf_op jit(solution)/shard_map/qkv/pallas_call | solution.py:480
  1.6 4.0 %collective-permute-start.5 = (bf16[48,384]{1,0:T(8,128)(2,1)S(1)}, bf16[48,384]{1,0:T(8,128)(2,1)S(1)}, u32[]{:S(2)}, u32[]{:S(2)}) collective-permute-start(bf16[48,384]{1,0:T(8,128)(2,1)S(1)} %qkv.1.sent_ref), channel_id=1, source_target_pairs={{0,24},{4,28},{8,16},{12,20},{16,8},{20,12},{24,0},{28,4},{1,25},{... | collective-permute-start | bytes 110600 | tf_op jit(solution)/shard_map/ppermute | solution.py:436
  5.6 0.5 collective-permute-start.3
  6.1 0.1 collective-permute-start.1
  6.2 5.5 %fetch_window.1 = (bf16[48,384]{1,0:T(8,128)(2,1)S(1)}, bf16[12,512,1024]{2,1,0:T(8,128)(2,1)S(1)}, bf16[3,512,1024]{2,1,0:T(8,128)(2,1)S(1)}, s32[12,128]{1,0:T...) custom-call(bf16[48,384]{1,0:T(8,128)(2,1)S(1)} %qkv.1.sent_ref, ...), custom_call_target="tpu_custom_call" | custom-call | bytes 12582912 | tf_op jit(solution)/shard_map/fetch_window/pallas_call | solution.py:499
  11.8 0.1 collective-permute-start
  11.9 0.0 collective-permute-done.5.refs_6_
  11.9 0.5 collective-permute-start.6
  12.4 0.1 collective-permute-start.4
  12.5 0.4 collective-permute-start.2
  12.9 0.2 collective-permute-done.refs_1_
  13.1 0.2 collective-permute-done.6.refs_7_
  13.2 0.4 collective-permute-done.4.refs_5_
  13.6 0.2 collective-permute-done.2.refs_3_
  13.8 6.6 %attention.1.refs_0_ = bf16[48,1152]{1,0:T(8,128)(2,1)S(1)} custom-call(bf16[48,384]{1,0:T(8,128)(2,1)S(1)} %get-tuple-element.28.refs_0_, bf16[48,384]{1,0:T(8,128)(2,1)S(1)} %collective-permute-done.refs_1_, bf16[48,384]{1,0:T(8,128)(2,1)S(1)} %collective-permute-done.1.refs_2_, bf16[48,384]{1,0:T(8,128)(2,1)S(1)} %collective-permute-done.2.refs_3_, ...), custom_call_target="tpu_custom_call" | custom-call | tf_op jit(solution)/shard_map/attention/pallas_call | solution.py:534
  20.4 2.9 %collective-permute-start.12 = (bf16[48,1152]{1,0:T(8,128)(2,1)S(1)}, bf16[48,1152]{1,0:T(8,128)(2,1)S(1)}, u32[]{:S(2)}, u32[]{:S(2)}) collective-permute-start(bf16[48,1152]{1,0:T(8,128)(2,1)S(1)} %attention.1.refs_0_), channel_id=1, source_target_pairs={{0,24},{4,28},{8,16},{12,20},{16,8},{20,12},{24,0},{28,4},{1,25},{... | collective-permute-start | bytes 331784 | tf_op jit(solution)/shard_map/ppermute | solution.py:436
  23.3 0.5 collective-permute-start.10
  23.8 0.1 collective-permute-start.8
  23.9 3.0 %collective-permute-done.12.refs_6_ = bf16[48,1152]{1,0:T(8,128)(2,1)S(1)} collective-permute-done((bf16[48,1152]{1,0:T(8,128)(2,1)S(1)}, bf16[48,1152]{1,0:T(8,128)(2,1)S(1)}, u32[]{:S(2)}, u32[]{:S(2)}) %collective-permute-start.12) | collective-permute-done | bytes 110624 | tf_op jit(solution)/shard_map/ppermute | solution.py:436
  27.0 0.0 collective-permute-start.13
  27.0 2.3 %collective-permute-done.10.refs_4_ = bf16[48,1152]{1,0:T(8,128)(2,1)S(1)} collective-permute-done((bf16[48,1152]{1,0:T(8,128)(2,1)S(1)}, bf16[48,1152]{1,0:T(8,128)(2,1)S(1)}, u32[]{:S(2)}, u32[]{:S(2)}) %collective-permute-start.10) | collective-permute-done | bytes 110624 | tf_op jit(solution)/shard_map/ppermute | solution.py:436
  29.2 0.0 collective-permute-start.11
  29.3 0.2 collective-permute-done.8.refs_2_
  29.5 0.3 collective-permute-start.9
  29.8 0.9 %extra.1 = (f32[48,1024]{1,0:T(8,128)S(1)}, f32[48,128]{1,0:T(8,128)S(1)}) custom-call(bf16[48,384]{1,0:T(8,128)(2,1)S(1)} %get-tuple-element.28.refs_0_, bf16[48,384]{1,0:T(8,128)(2,1)S(1)} %collective-permute-done.refs_1_, bf16[48,384]{1,0:T(8,128)(2,1)S(1)} %collective-permute-done.1.refs_2_, bf16[48,384]{1,0:T(8,128)(2,1)S(1)} %collective-permute-done.2.refs_3_, ...), custom_call_target="tpu_custom_call" | custom-call | tf_op jit(solution)/shard_map/extra/pallas_call | solution.py:550
  30.7 0.0 copy-start.3
  30.7 0.0 collective-permute-done.7.refs_1_
  30.7 0.0 collective-permute-done.13.refs_7_
  30.7 0.1 collective-permute-done.9.refs_3_
  30.8 1.3 %project.1 = (f32[32,8,128]{2,1,0:T(8,128)S(1)}, f32[48,128]{1,0:T(8,128)S(1)}) custom-call(bf16[48,1152]{1,0:T(8,128)(2,1)S(1)} %attention.1.refs_0_, bf16[48,1152]{1,0:T(8,128)(2,1)S(1)} %collective-permute-done.7.refs_1_, bf16[48,1152]{1,0:T(8,128)(2,1)S(1)} %collective-permute-done.8.refs_2_, bf16[48,1152]{1,0:T(8,128)(2,1)S(1)} %collective-permute-done.9.refs_3_, ...), custom_call_target="tpu_custom_call" | custom-call | tf_op jit(solution)/shard_map/project/pallas_call | solution.py:563
  32.1 13.5 %all_to_all.10.received_ref = f32[32,8,128]{2,1,0:T(8,128)S(1)} all-to-all(f32[32,8,128]{2,1,0:T(8,128)S(1)} %get-tuple-element.36), channel_id=1, replica_groups=mesh['seq'=8,'exp'=4] {'seq','exp'}, dimensions={0} | all-to-all | bytes 262144 | tf_op jit(solution)/shard_map/all_to_all | solution.py:576
  45.6 4.4 %expert.1 = (f32[32,512]{1,0:T(8,128)S(1)}, f32[32,512]{1,0:T(8,128)S(1)}) custom-call(f32[32,8,128]{2,1,0:T(8,128)S(1)} %all_to_all.10.received_ref, f32[1,1024]{1,0:T(1,128)S(1)} %bitcast.7, bf16[2,1,1408,1024]{3,2,1,0:T(8,128)(2,1)} %in_ref.1, bf16[1,1408,1024]{2,1,0:T(8,128)(2,1)} %down_ref.1), custom_call_target="tpu_custom_call" | custom-call | tf_op jit(solution)/shard_map/expert/pallas_call | solution.py:581
  50.0 0.1 collective-permute-start.21
  50.0 1.2 %collective-permute-done.21.other_ref = f32[32,512]{1,0:T(8,128)S(1)} collective-permute-done((f32[32,512]{1,0:T(8,128)S(1)}, f32[32,512]{1,0:T(8,128)S(1)}, u32[]{:S(2)}, u32[]{:S(2)}) %collective-permute-start.21) | collective-permute-done | bytes 65568 | tf_op jit(solution)/shard_map/ppermute | solution.py:599
  51.3 0.7 %spread.1 = bf16[32,8,512]{2,1,0:T(8,128)(2,1)} custom-call(f32[32,512]{1,0:T(8,128)S(1)} %get-tuple-element.37.kept_ref, f32[32,512]{1,0:T(8,128)S(1)} %collective-permute-done.21.other_ref), custom_call_target="tpu_custom_call" | custom-call | tf_op jit(solution)/shard_map/spread/pallas_call | solution.py:607
  52.0 2.6 %all-to-all-start.1 = ((bf16[32,8,512]{2,1,0:T(8,128)(2,1)}), bf16[32,8,512]{2,1,0:T(8,128)(2,1)S(1)}, u32[]{:S(2)}, u32[]{:S(2)}) async-start(bf16[32,8,512]{2,1,0:T(8,128)(2,1)} %spread.1), calls=%async_computation.1 | async-start | bytes 524288 | tf_op jit(solution)/shard_map/all_to_all | solution.py:613
  54.6 2.6 %collective-permute-start.19 = (f32[48,128]{1,0:T(8,128)S(1)}, f32[48,128]{1,0:T(8,128)S(1)}, u32[]{:S(2)}, u32[]{:S(2)}) collective-permute-start(f32[48,128]{1,0:T(8,128)S(1)} %get-tuple-element.39.refs_0_), channel_id=1, source_target_pairs={{0,24},{4,28},{8,16},{12,20},{16,8},{20,12},{24,0},{28,4},{1,25},{... | collective-permute-start | bytes 73736 | tf_op jit(solution)/shard_map/ppermute | solution.py:436
  57.2 0.5 collective-permute-start.17
  57.8 0.4 collective-permute-start.15
  58.2 1.6 %collective-permute-done.19.refs_6_ = f32[48,128]{1,0:T(8,128)S(1)} collective-permute-done((f32[48,128]{1,0:T(8,128)S(1)}, f32[48,128]{1,0:T(8,128)S(1)}, u32[]{:S(2)}, u32[]{:S(2)}) %collective-permute-start.19) | collective-permute-done | bytes 24608 | tf_op jit(solution)/shard_map/ppermute | solution.py:436
  59.8 1.6 %collective-permute-done.17.refs_4_ = f32[48,128]{1,0:T(8,128)S(1)} collective-permute-done((f32[48,128]{1,0:T(8,128)S(1)}, f32[48,128]{1,0:T(8,128)S(1)}, u32[]{:S(2)}, u32[]{:S(2)}) %collective-permute-start.17) | collective-permute-done | bytes 24608 | tf_op jit(solution)/shard_map/ppermute | solution.py:436
  61.4 0.3 collective-permute-done.15.refs_2_
  61.7 0.2 collective-permute-start.16
  61.9 0.7 %collective-permute-done.18.refs_5_ = f32[48,128]{1,0:T(8,128)S(1)} collective-permute-done((f32[48,128]{1,0:T(8,128)S(1)}, f32[48,128]{1,0:T(8,128)S(1)}, u32[]{:S(2)}, u32[]{:S(2)}) %collective-permute-start.18) | collective-permute-done | bytes 24608 | tf_op jit(solution)/shard_map/ppermute | solution.py:436
  62.5 0.3 collective-permute-done.16.refs_3_
  62.9 0.4 home.1
  63.3 1.5 %all-to-all-done.1 = bf16[32,8,512]{2,1,0:T(8,128)(2,1)S(1)} async-done(((bf16[32,8,512]{2,1,0:T(8,128)(2,1)}), bf16[32,8,512]{2,1,0:T(8,128)(2,1)S(1)}, u32[]{:S(2)}, u32[]{:S(2)}) %all-to-all-start.1) | async-done | bytes 262176 | tf_op jit(solution)/shard_map/all_to_all | solution.py:613
  64.8 0.9 %final.1 = bf16[12,4,1024]{2,1,0:T(4,128)(2,1)} custom-call(f32[48,128]{1,0:T(8,128)S(1)} %get-tuple-element.49.gates_ref, bf16[8,4,8,512]{3,2,1,0:T(8,128)(2,1)S(1)} %bitcast.5, f32[48,1024]{1,0:T(8,128)S(1)} %get-tuple-element.50.residual_ref), custom_call_target="tpu_custom_call" | custom-call | tf_op jit(solution)/shard_map/final/pallas_call | solution.py:630
  (18 shorter events, 0.0 us)
Async XLA Ops:
  1.6 10.2 %collective-permute-start.5 = (bf16[48,384]{1,0:T(8,128)(2,1)S(1)}, bf16[48,384]{1,0:T(8,128)(2,1)S(1)}, u32[]{:S(2)}, u32[]{:S(2)}) collective-permute-start(bf16[48,384]{1,0:T(8,128)(2,1)S(1)} %qkv.1.sent_ref), channel_id=1, source_target_pairs={{0,24},{4,28},{8,16},{12,20},{16,8},{20,12},{24,0},{28,4},{1,25},{... | collective-permute-start | bytes 110600 | tf_op jit(solution)/shard_map/ppermute | solution.py:436
  5.6 6.8 %collective-permute-start.3 = (bf16[48,384]{1,0:T(8,128)(2,1)S(1)}, bf16[48,384]{1,0:T(8,128)(2,1)S(1)}, u32[]{:S(2)}, u32[]{:S(2)}) collective-permute-start(bf16[48,384]{1,0:T(8,128)(2,1)S(1)} %qkv.1.sent_ref), channel_id=1, source_target_pairs={{0,16},{4,20},{8,24},{12,28},{16,0},{20,4},{24,8},{28,12},{1,17},{... | collective-permute-start | bytes 110600 | tf_op jit(solution)/shard_map/ppermute | solution.py:436
  6.1 6.4 %collective-permute-start.1 = (bf16[48,384]{1,0:T(8,128)(2,1)S(1)}, bf16[48,384]{1,0:T(8,128)(2,1)S(1)}, u32[]{:S(2)}, u32[]{:S(2)}) collective-permute-start(bf16[48,384]{1,0:T(8,128)(2,1)S(1)} %qkv.1.sent_ref), channel_id=1, source_target_pairs={{0,8},{4,12},{8,0},{12,4},{16,24},{20,28},{24,16},{28,20},{1,9},{5... | collective-permute-start | bytes 110600 | tf_op jit(solution)/shard_map/ppermute | solution.py:436
  11.8 1.3 %collective-permute-start = (bf16[48,384]{1,0:T(8,128)(2,1)S(1)}, bf16[48,384]{1,0:T(8,128)(2,1)S(1)}, u32[]{:S(2)}, u32[]{:S(2)}) collective-permute-start(bf16[48,384]{1,0:T(8,128)(2,1)S(1)} %get-tuple-element.28.refs_0_), channel_id=1, source_target_pairs={{0,4},{4,0},{8,12},{12,8},{16,20},{20,16},{24,28},{28,24},{1,5},{5... | collective-permute-start | bytes 110600 | tf_op jit(solution)/shard_map/ppermute | solution.py:436
  11.9 1.4 %collective-permute-start.6 = (bf16[48,384]{1,0:T(8,128)(2,1)S(1)}, bf16[48,384]{1,0:T(8,128)(2,1)S(1)}, u32[]{:S(2)}, u32[]{:S(2)}) collective-permute-start(bf16[48,384]{1,0:T(8,128)(2,1)S(1)} %collective-permute-done.5.refs_6_), channel_id=1, source_target_pairs={{0,4},{4,0},{8,12},{12,8},{16,20},{20,16},{24,28},{28,24},{1,5},{5... | collective-permute-start | bytes 110600 | tf_op jit(solution)/shard_map/ppermute | solution.py:436
  12.4 1.2 %collective-permute-start.4 = (bf16[48,384]{1,0:T(8,128)(2,1)S(1)}, bf16[48,384]{1,0:T(8,128)(2,1)S(1)}, u32[]{:S(2)}, u32[]{:S(2)}) collective-permute-start(bf16[48,384]{1,0:T(8,128)(2,1)S(1)} %collective-permute-done.3.refs_4_), channel_id=1, source_target_pairs={{0,4},{4,0},{8,12},{12,8},{16,20},{20,16},{24,28},{28,24},{1,5},{5... | collective-permute-start | bytes 110600 | tf_op jit(solution)/shard_map/ppermute | solution.py:436
  12.5 1.3 %collective-permute-start.2 = (bf16[48,384]{1,0:T(8,128)(2,1)S(1)}, bf16[48,384]{1,0:T(8,128)(2,1)S(1)}, u32[]{:S(2)}, u32[]{:S(2)}) collective-permute-start(bf16[48,384]{1,0:T(8,128)(2,1)S(1)} %collective-permute-done.1.refs_2_), channel_id=1, source_target_pairs={{0,4},{4,0},{8,12},{12,8},{16,20},{20,16},{24,28},{28,24},{1,5},{5... | collective-permute-start | bytes 110600 | tf_op jit(solution)/shard_map/ppermute | solution.py:436
  13.8 16.0 %copy-start.2 = (bf16[2,12,4,1024]{3,2,1,0:T(4,128)(2,1)S(1)}, bf16[2,12,4,1024]{3,2,1,0:T(4,128)(2,1)}, u32[]{:S(2)}) copy-start(bf16[2,12,4,1024]{3,2,1,0:T(4,128)(2,1)} %refs_8_.1) | copy-start | bytes 589828
  13.8 17.1 %copy-start = (bf16[12,4,1024]{2,1,0:T(4,128)(2,1)S(1)}, bf16[12,4,1024]{2,1,0:T(4,128)(2,1)}, u32[]{:S(2)}) copy-start(bf16[12,4,1024]{2,1,0:T(4,128)(2,1)} %refs_11_.3) | copy-start | bytes 294916
  13.8 17.1 %copy-start.1 = (bf16[128,1024]{1,0:T(8,128)(2,1)S(1)}, bf16[128,1024]{1,0:T(8,128)(2,1)}, u32[]{:S(2)}) copy-start(bf16[128,1024]{1,0:T(8,128)(2,1)} %refs_10_.1) | copy-start | bytes 786436
  13.8 31.8 %copy-start.4 = (f32[1024]{0:T(1024)S(1)}, f32[1024]{0:T(1024)}, u32[]{:S(2)}) copy-start(f32[1024]{0:T(1024)} %param.20) | copy-start | bytes 12292
  20.4 6.6 %collective-permute-start.12 = (bf16[48,1152]{1,0:T(8,128)(2,1)S(1)}, bf16[48,1152]{1,0:T(8,128)(2,1)S(1)}, u32[]{:S(2)}, u32[]{:S(2)}) collective-permute-start(bf16[48,1152]{1,0:T(8,128)(2,1)S(1)} %attention.1.refs_0_), channel_id=1, source_target_pairs={{0,24},{4,28},{8,16},{12,20},{16,8},{20,12},{24,0},{28,4},{1,25},{... | collective-permute-start | bytes 331784 | tf_op jit(solution)/shard_map/ppermute | solution.py:436
  23.3 5.9 %collective-permute-start.10 = (bf16[48,1152]{1,0:T(8,128)(2,1)S(1)}, bf16[48,1152]{1,0:T(8,128)(2,1)S(1)}, u32[]{:S(2)}, u32[]{:S(2)}) collective-permute-start(bf16[48,1152]{1,0:T(8,128)(2,1)S(1)} %attention.1.refs_0_), channel_id=1, source_target_pairs={{0,16},{4,20},{8,24},{12,28},{16,0},{20,4},{24,8},{28,12},{1,17},{... | collective-permute-start | bytes 331784 | tf_op jit(solution)/shard_map/ppermute | solution.py:436
  23.8 5.7 %collective-permute-start.8 = (bf16[48,1152]{1,0:T(8,128)(2,1)S(1)}, bf16[48,1152]{1,0:T(8,128)(2,1)S(1)}, u32[]{:S(2)}, u32[]{:S(2)}) collective-permute-start(bf16[48,1152]{1,0:T(8,128)(2,1)S(1)} %attention.1.refs_0_), channel_id=1, source_target_pairs={{0,8},{4,12},{8,0},{12,4},{16,24},{20,28},{24,16},{28,20},{1,9},{5... | collective-permute-start | bytes 331784 | tf_op jit(solution)/shard_map/ppermute | solution.py:436
  23.9 6.8 %collective-permute-start.7 = (bf16[48,1152]{1,0:T(8,128)(2,1)S(1)}, bf16[48,1152]{1,0:T(8,128)(2,1)S(1)}, u32[]{:S(2)}, u32[]{:S(2)}) collective-permute-start(bf16[48,1152]{1,0:T(8,128)(2,1)S(1)} %attention.1.refs_0_), channel_id=1, source_target_pairs={{0,4},{4,0},{8,12},{12,8},{16,20},{20,16},{24,28},{28,24},{1,5},{5... | collective-permute-start | bytes 331784 | tf_op jit(solution)/shard_map/ppermute | solution.py:436
  27.0 3.7 %collective-permute-start.13 = (bf16[48,1152]{1,0:T(8,128)(2,1)S(1)}, bf16[48,1152]{1,0:T(8,128)(2,1)S(1)}, u32[]{:S(2)}, u32[]{:S(2)}) collective-permute-start(bf16[48,1152]{1,0:T(8,128)(2,1)S(1)} %collective-permute-done.12.refs_6_), channel_id=1, source_target_pairs={{0,4},{4,0},{8,12},{12,8},{16,20},{20,16},{24,28},{28,24},{1,5},{5... | collective-permute-start | bytes 331784 | tf_op jit(solution)/shard_map/ppermute | solution.py:436
  29.2 1.5 %collective-permute-start.11 = (bf16[48,1152]{1,0:T(8,128)(2,1)S(1)}, bf16[48,1152]{1,0:T(8,128)(2,1)S(1)}, u32[]{:S(2)}, u32[]{:S(2)}) collective-permute-start(bf16[48,1152]{1,0:T(8,128)(2,1)S(1)} %collective-permute-done.10.refs_4_), channel_id=1, source_target_pairs={{0,4},{4,0},{8,12},{12,8},{16,20},{20,16},{24,28},{28,24},{1,5},{5... | collective-permute-start | bytes 331784 | tf_op jit(solution)/shard_map/ppermute | solution.py:436
  29.5 1.3 %collective-permute-start.9 = (bf16[48,1152]{1,0:T(8,128)(2,1)S(1)}, bf16[48,1152]{1,0:T(8,128)(2,1)S(1)}, u32[]{:S(2)}, u32[]{:S(2)}) collective-permute-start(bf16[48,1152]{1,0:T(8,128)(2,1)S(1)} %collective-permute-done.8.refs_2_), channel_id=1, source_target_pairs={{0,4},{4,0},{8,12},{12,8},{16,20},{20,16},{24,28},{28,24},{1,5},{5... | collective-permute-start | bytes 331784 | tf_op jit(solution)/shard_map/ppermute | solution.py:436
  30.7 32.2 %copy-start.3 = (bf16[1024,16]{0,1:T(8,128)(2,1)S(1)}, bf16[1024,16]{0,1:T(8,128)(2,1)}, u32[]{:S(2)}) copy-start(bf16[1024,16]{0,1:T(8,128)(2,1)} %param.21) | copy-start | bytes 98308
  50.0 1.3 %collective-permute-start.21 = (f32[32,512]{1,0:T(8,128)S(1)}, f32[32,512]{1,0:T(8,128)S(1)}, u32[]{:S(2)}, u32[]{:S(2)}) collective-permute-start(f32[32,512]{1,0:T(8,128)S(1)} %get-tuple-element.38), channel_id=1, source_target_pairs={{0,4},{4,0},{8,12},{12,8},{16,20},{20,16},{24,28},{28,24},{1,5},{5... | collective-permute-start | bytes 196616 | tf_op jit(solution)/shard_map/ppermute | solution.py:599
  52.0 12.8 %all-to-all-start.1 = ((bf16[32,8,512]{2,1,0:T(8,128)(2,1)}), bf16[32,8,512]{2,1,0:T(8,128)(2,1)S(1)}, u32[]{:S(2)}, u32[]{:S(2)}) async-start(bf16[32,8,512]{2,1,0:T(8,128)(2,1)} %spread.1), calls=%async_computation.1 | async-start | bytes 524288 | tf_op jit(solution)/shard_map/all_to_all | solution.py:613
  54.6 5.2 %collective-permute-start.19 = (f32[48,128]{1,0:T(8,128)S(1)}, f32[48,128]{1,0:T(8,128)S(1)}, u32[]{:S(2)}, u32[]{:S(2)}) collective-permute-start(f32[48,128]{1,0:T(8,128)S(1)} %get-tuple-element.39.refs_0_), channel_id=1, source_target_pairs={{0,24},{4,28},{8,16},{12,20},{16,8},{20,12},{24,0},{28,4},{1,25},{... | collective-permute-start | bytes 73736 | tf_op jit(solution)/shard_map/ppermute | solution.py:436
  57.2 4.1 %collective-permute-start.17 = (f32[48,128]{1,0:T(8,128)S(1)}, f32[48,128]{1,0:T(8,128)S(1)}, u32[]{:S(2)}, u32[]{:S(2)}) collective-permute-start(f32[48,128]{1,0:T(8,128)S(1)} %get-tuple-element.39.refs_0_), channel_id=1, source_target_pairs={{0,16},{4,20},{8,24},{12,28},{16,0},{20,4},{24,8},{28,12},{1,17},{... | collective-permute-start | bytes 73736 | tf_op jit(solution)/shard_map/ppermute | solution.py:436
  57.8 3.9 %collective-permute-start.15 = (f32[48,128]{1,0:T(8,128)S(1)}, f32[48,128]{1,0:T(8,128)S(1)}, u32[]{:S(2)}, u32[]{:S(2)}) collective-permute-start(f32[48,128]{1,0:T(8,128)S(1)} %get-tuple-element.39.refs_0_), channel_id=1, source_target_pairs={{0,8},{4,12},{8,0},{12,4},{16,24},{20,28},{24,16},{28,20},{1,9},{5... | collective-permute-start | bytes 73736 | tf_op jit(solution)/shard_map/ppermute | solution.py:436
  58.1 3.7 %collective-permute-start.14 = (f32[48,128]{1,0:T(8,128)S(1)}, f32[48,128]{1,0:T(8,128)S(1)}, u32[]{:S(2)}, u32[]{:S(2)}) collective-permute-start(f32[48,128]{1,0:T(8,128)S(1)} %get-tuple-element.39.refs_0_), channel_id=1, source_target_pairs={{0,4},{4,0},{8,12},{12,8},{16,20},{20,16},{24,28},{28,24},{1,5},{5... | collective-permute-start | bytes 73736 | tf_op jit(solution)/shard_map/ppermute | solution.py:436
  59.8 2.1 %collective-permute-start.20 = (f32[48,128]{1,0:T(8,128)S(1)}, f32[48,128]{1,0:T(8,128)S(1)}, u32[]{:S(2)}, u32[]{:S(2)}) collective-permute-start(f32[48,128]{1,0:T(8,128)S(1)} %collective-permute-done.19.refs_6_), channel_id=1, source_target_pairs={{0,4},{4,0},{8,12},{12,8},{16,20},{20,16},{24,28},{28,24},{1,5},{5... | collective-permute-start | bytes 73736 | tf_op jit(solution)/shard_map/ppermute | solution.py:436
  61.4 1.2 %collective-permute-start.18 = (f32[48,128]{1,0:T(8,128)S(1)}, f32[48,128]{1,0:T(8,128)S(1)}, u32[]{:S(2)}, u32[]{:S(2)}) collective-permute-start(f32[48,128]{1,0:T(8,128)S(1)} %collective-permute-done.17.refs_4_), channel_id=1, source_target_pairs={{0,4},{4,0},{8,12},{12,8},{16,20},{20,16},{24,28},{28,24},{1,5},{5... | collective-permute-start | bytes 73736 | tf_op jit(solution)/shard_map/ppermute | solution.py:436
  61.7 1.2 %collective-permute-start.16 = (f32[48,128]{1,0:T(8,128)S(1)}, f32[48,128]{1,0:T(8,128)S(1)}, u32[]{:S(2)}, u32[]{:S(2)}) collective-permute-start(f32[48,128]{1,0:T(8,128)S(1)} %collective-permute-done.15.refs_2_), channel_id=1, source_target_pairs={{0,4},{4,0},{8,12},{12,8},{16,20},{20,16},{24,28},{28,24},{1,5},{5... | collective-permute-start | bytes 73736 | tf_op jit(solution)/shard_map/ppermute | solution.py:436

commit v6 on v5

--- a/solution.py
+++ b/solution.py
@@ -16,7 +16,9 @@
 CAP = 8
 LANES = 128
 PIECES = 3
-EARLY = 3
+FIRST_KEYS = 2
+SECOND_KEYS = 8
+SECOND_VALUES = 3
 PIECE = 512
 BLOCK = 256
 BLOCK_HEADS = BLOCK // HD
@@ -106,15 +108,34 @@
     return jnp.transpose(both)
 
 
-def qkv_kernel(tokens_ref, gain_ref, weight_ref, out_ref, token_buf, gain_buf, weight_buf, rows_ref, sems):
+def qkv_kernel(
+    tokens_ref,
+    gain_ref,
+    weight_ref,
+    window_ref,
+    out_ref,
+    keys_ref,
+    token_buf,
+    gain_buf,
+    weight_buf,
+    rows_ref,
+    sems,
+):
     copies = started(
-        ((tokens_ref, token_buf), (gain_ref, gain_buf), (weight_ref, weight_buf)), sems
+        (
+            (tokens_ref, token_buf),
+            (gain_ref, gain_buf),
+            (weight_ref, weight_buf),
+            (window_ref.at[0, pl.ds(0, keys_ref.shape[0])], keys_ref),
+        ),
+        sems,
     )
-    for copy in copies:
+    for copy in copies[:3]:
         copy.wait()
     copy_rows(token_buf, rows_ref)
     normed = rms_rows(rows_ref[...], gain_buf[...])
     out_ref[...] = dot(normed, weight_buf[...], ROWS_BY_ROWS).astype(jnp.bfloat16)
+    copies[3].wait()
 
 
 def in_order(sent_refs, ordered_ref):
@@ -130,6 +151,7 @@
 
 
 def fetch_window_kernel(
+    first,
     sent_ref,
     window_ref,
     lengths_ref,
@@ -152,7 +174,7 @@
             (ids_ref, ids_buf),
             (order_ref, order_buf),
             (lengths_ref, numbers_ref),
-            (window_ref.at[0], keys_ref),
+            (window_ref.at[0, pl.ds(first, keys_ref.shape[0])], keys_ref),
             (window_ref.at[1, pl.ds(0, values_ref.shape[0])], values_ref),
         ),
         sems,
@@ -167,18 +189,33 @@
         copy.wait()
 
 
+def fetch_expert_kernel(sent_ref, in_ref, held_ref, piece_ref, sems):
+    copies = started([(in_ref.at[p, 0, pl.ds(0, piece_ref.shape[1])], piece_ref.at[p]) for p in range(2)], sems)
+    held_ref[...] = sent_ref[...]
+    for copy in copies:
+        copy.wait()
+
+
 def attention_kernel(*refs):
-    *mixed_refs, spans_ref, keys_ref, values_ref, window_ref = refs[:-6]
+    *mixed_refs, spans_ref, first_ref, keys_ref, values_ref, window_ref = refs[:-6]
     out_ref, ordered_ref, flat_ref, query_ref, late_ref, sems = refs[-6:]
     devices, rows, share = ordered_ref.shape
-    requests, span, width = keys_ref.shape
-    early = values_ref.shape[0]
-    late = [
-        pltpu.make_async_copy(window_ref.at[1, r], late_ref.at[r - early], sems.at[r - early])
-        for r in range(early, requests)
-    ]
-    for copy in late:
-        copy.start()
+    _, requests, span, width = window_ref.shape
+    held = {(0, r): first_ref.at[r] for r in range(first_ref.shape[0])}
+    held |= {(0, r + first_ref.shape[0]): keys_ref.at[r] for r in range(keys_ref.shape[0])}
+    held |= {(1, r): values_ref.at[r] for r in range(values_ref.shape[0])}
+    needed = [(p, r) for i in range(requests + 1) for p, r in ((0, i), (1, i - 1))]
+    needed = [at for at in needed if 0 <= at[1] < requests and at not in held]
+    late = {at: late_ref.at[i] for i, at in enumerate(needed)}
+    copies = started([(window_ref.at[p, r], late[p, r]) for p, r in needed], sems)
+    waits = dict(zip(needed, copies))
+
+    def window(p, r):
+        if (p, r) in held:
+            return held[p, r]
+        waits[p, r].wait()
+        return late[p, r]
+
     steps = rows // requests
     block_rows = BLOCK_HEADS * steps
     place = lax.axis_index("seq")
@@ -203,8 +240,9 @@
     cols = [slice(c, c + BLOCK) for c in range(0, width, BLOCK)]
 
     def score(r):
+        keys = window(0, r)
         return jnp.concatenate(
-            [dot(query_ref[r, :, c], keys_ref[r, :, c], ROWS_BY_ROWS) for c in cols], axis=0
+            [dot(query_ref[r, :, c], keys[:, c], ROWS_BY_ROWS) for c in cols], axis=0
         )
 
     scores = score(0)
@@ -218,9 +256,7 @@
         weight = jnp.where(live, jnp.exp(scores - peak), 0.0)
         total = jnp.sum(weight, axis=-1, keepdims=True)
         weight = weight.reshape(HEADS * steps, span).astype(jnp.bfloat16)
-        if r >= early:
-            late[r - early].wait()
-        values = values_ref.at[r] if r < early else late_ref.at[r - early]
+        values = window(1, r)
         outs = []
         for b, c in enumerate(cols):
             own = slice(b * block_rows, (b + 1) * block_rows)
@@ -320,12 +356,12 @@
     head_of_col = lax.broadcasted_iota(jnp.int32, (HEADS, width), 1) // HD
     expand = (head_of_row == head_of_col).astype(jnp.bfloat16)
 
-    def spread(factor):
-        return sum(dot(part, expand) for part in split(factor * inverse, 2))
-
-    attended = spread(factors[-1]) * extra_ref[...]
+    spread = jnp.concatenate([factor * inverse for factor in factors], axis=0)
+    spread = sum(dot(part, expand) for part in split(spread, 2))
+    attended = spread[devices * rows :] * extra_ref[...]
     for d in range(devices):
-        attended = attended + spread(factors[d]) * ordered_ref[d][:, :width].astype(jnp.float32)
+        share = spread[d * rows : (d + 1) * rows]
+        attended = attended + share * ordered_ref[d][:, :width].astype(jnp.float32)
     projected = dot(attended.astype(jnp.bfloat16), weight_ref[...], ROWS_BY_ROWS).astype(jnp.bfloat16)
     copy_rows(tokens_ref, rows_ref)
     share = weight_ref.shape[0]
@@ -360,16 +396,17 @@
 
 
 def expert_kernel(
-    received_ref, gain_ref, in_ref, down_ref, keep_ref, send_ref, in_buf, down_buf, sems
+    received_ref, gain_ref, piece_ref, in_ref, down_ref, keep_ref, send_ref, in_buf, down_buf, sems
 ):
     hidden_units, width = down_buf.shape
-    pieces = [
-        slice(at, min(at + PIECE, hidden_units)) for at in range(0, hidden_units, PIECE)
-    ]
+    held = piece_ref.shape[1]
+    pieces = [(at, min(PIECE, hidden_units - at)) for at in range(held, hidden_units, PIECE)]
     pairs = []
-    for piece in pieces:
-        rows = pl.ds(piece.start, piece.stop - piece.start)
-        pairs += [(in_ref.at[p, 0, rows], in_buf.at[p, rows]) for p in range(2)]
+    for at, count in pieces:
+        for p in range(2):
+            pairs.append(
+                (in_ref.at[p, 0, pl.ds(at, count)], in_buf.at[p, pl.ds(at - held, count)])
+            )
     copies = started(pairs + [(down_ref.at[0], down_buf)], sems)
     devices = lax.axis_size("seq")
     groups = lax.axis_size("exp")
@@ -379,13 +416,18 @@
             jnp.concatenate([received_ref[s * groups + g] for g in range(groups)], axis=0)
         )
     rows = rms_rows(jnp.concatenate(columns, axis=1), gain_ref[...])
-    hidden = []
-    for i, piece in enumerate(pieces):
+
+    def layer(gate_weight, up_weight):
+        gate = dot(rows, gate_weight, ROWS_BY_ROWS)
+        up = dot(rows, up_weight, ROWS_BY_ROWS)
+        return (jax.nn.gelu(gate, approximate=True) * up).astype(jnp.bfloat16)
+
+    hidden = [layer(piece_ref[0], piece_ref[1])]
+    for i, (at, count) in enumerate(pieces):
         copies[2 * i].wait()
-        gate = dot(rows, in_buf[0, piece], ROWS_BY_ROWS)
         copies[2 * i + 1].wait()
-        up = dot(rows, in_buf[1, piece], ROWS_BY_ROWS)
-        hidden.append((jax.nn.gelu(gate, approximate=True) * up).astype(jnp.bfloat16))
+        own = slice(at - held, at - held + count)
+        hidden.append(layer(in_buf[0, own], in_buf[1, own]))
     copies[-1].wait()
     outputs = dot(jnp.concatenate(hidden, axis=1), down_buf[...])
     half = width // 2
@@ -477,32 +519,35 @@
     hbm = pl.BlockSpec(memory_space=pltpu.HBM)
 
     gain_row = attn_gain.reshape(1, width)
-    local_mix = pl.pallas_call(
+    first_keys = min(FIRST_KEYS, requests)
+    second_keys = min(SECOND_KEYS, requests - first_keys)
+    second_values = min(SECOND_VALUES, requests)
+    late = 2 * requests - first_keys - second_keys - second_values
+    local_mix, first = pl.pallas_call(
         qkv_kernel,
-        in_specs=[hbm] * 3,
-        out_shape=shape((rows, share), bf16),
+        in_specs=[hbm] * 4,
+        out_shape=(shape((rows, share), bf16), shape((first_keys, span, width), bf16)),
         scratch_shapes=[
             pltpu.VMEM(tokens.shape, bf16),
             pltpu.VMEM(gain_row.shape, f32),
             pltpu.VMEM(w_qkv.shape, bf16),
             pltpu.VMEM((rows, width), f32),
-            pltpu.SemaphoreType.DMA((3,)),
+            pltpu.SemaphoreType.DMA((4,)),
         ],
         compiler_params=params(4),
         name="qkv",
-    )(in_hbm(tokens), in_hbm(gain_row), in_hbm(w_qkv))
-    early = min(EARLY, requests - 1)
+    )(in_hbm(tokens), in_hbm(gain_row), in_hbm(w_qkv), in_hbm(window_cache))
 
     fetched = []
 
     def fetch_window(values):
         held, *outputs = pl.pallas_call(
-            fetch_window_kernel,
+            functools.partial(fetch_window_kernel, first_keys),
             in_specs=[vmem] + [hbm] * 4,
             out_shape=(
                 shape(values.shape, bf16),
-                shape((requests, span, width), bf16),
-                shape((early, span, width), bf16),
+                shape((second_keys, span, width), bf16),
+                shape((second_values, span, width), bf16),
                 shape((requests, LANES), jnp.int32),
                 shape((TOPK, rows, slots), f32),
                 shape((TOPK, rows, LANES), f32),
@@ -533,19 +578,37 @@
     padded = width + LANES
     part = pl.pallas_call(
         attention_kernel,
-        in_specs=[vmem] * (seq_count + 3) + [hbm],
+        in_specs=[vmem] * (seq_count + 4) + [hbm],
         out_shape=shape((rows, padded), bf16),
         scratch_shapes=[
             pltpu.VMEM((seq_count, rows, share), bf16),
             pltpu.VMEM((rows, padded), f32),
             pltpu.VMEM((requests, BLOCK_HEADS * steps, width), bf16),
-            pltpu.VMEM((requests - early, span, width), bf16),
-            pltpu.SemaphoreType.DMA((requests - early,)),
+            pltpu.VMEM((late, span, width), bf16),
+            pltpu.SemaphoreType.DMA((late,)),
         ],
-        compiler_params=params(20),
+        compiler_params=params(24),
         name="attention",
-    )(*mixed, spans, keys, values, in_hbm(window_cache))
-    parts = gather_seq(part)
+    )(*mixed, spans, first, keys, values, in_hbm(window_cache))
+    hidden_units = expert_down.shape[1]
+    held_units = min(PIECE, hidden_units)
+    late_units = max(hidden_units - held_units, 16)
+
+    def fetch_expert(values):
+        held, piece = pl.pallas_call(
+            fetch_expert_kernel,
+            in_specs=[vmem, hbm],
+            out_shape=(shape(values.shape, bf16), shape((2, held_units, width), bf16)),
+            scratch_shapes=[pltpu.SemaphoreType.DMA((2,))],
+            compiler_params=params(8),
+            cost_estimate=moving(4 * held_units * width),
+            name="fetch_expert",
+        )(values, in_hbm(expert_in))
+        fetched.append(piece)
+        return held
+
+    parts = gather_seq(part, fetch_expert)
+    piece = fetched[-1]
 
     extra, extra_stats = pl.pallas_call(
         extra_kernel,
@@ -570,29 +633,28 @@
             pltpu.VMEM((seq_count, rows, padded), bf16),
             pltpu.VMEM((rows, width), f32),
         ],
-        compiler_params=params(8),
+        compiler_params=params(16),
         name="project",
     )(*parts, extra, extra_stats, w_out, tokens, turned)
     received = lax.all_to_all(outgoing, ("seq", "exp"), split_axis=0, concat_axis=0, tiled=True)
     columns = gather_seq(residual_columns)
 
     moe_row = moe_gain.reshape(1, width)
-    hidden_units = expert_down.shape[1]
     kept, sent = pl.pallas_call(
         expert_kernel,
-        in_specs=[vmem, vmem, hbm, hbm],
+        in_specs=[vmem, vmem, vmem, hbm, hbm],
         out_shape=(
             shape((groups * CAP, width // 2), f32),
             shape((groups * CAP, width // 2), f32),
         ),
         scratch_shapes=[
-            pltpu.VMEM((2, hidden_units, width), bf16),
+            pltpu.VMEM((2, late_units, width), bf16),
             pltpu.VMEM((hidden_units, width), bf16),
             pltpu.SemaphoreType.DMA((2 * pl.cdiv(hidden_units, PIECE) + 1,)),
         ],
         compiler_params=params(20),
         name="expert",
-    )(received, moe_row, in_hbm(expert_in), in_hbm(expert_down))
+    )(received, moe_row, piece, in_hbm(expert_in), in_hbm(expert_down))
 
     reach = 1
     while True:

time: 65.9 us -> 64.6 us (0.980)
  waiting for transfers between devices: 13.8 us -> 12.2 us
    ppermute x21, waiting for transfers between devices: 11 us -> 9.41 us  [exchange(): return lax.ppermute(value, 'seq', [(i, i ^ bits) for i in range(count)])]
    pallas_call x4 -> x5, Pallas kernels: 18.2 us -> 18.3 us  [the longest x1 6.85 us: body(): pl.pallas_call(attention_kernel, in_specs=[vmem] * (seq_count + 4) + [hbm...]
  transfers between devices with their start and end apart: 23 -> 23, of which waited for: 15 -> 15; matrix products, arithmetic and copies ran while one was open for 0% -> 0% of each run, Pallas kernels for 10% -> 11%
where the time goes in v6:
time: 64.6 us; the launch traced here: 64.4 us
  Pallas kernels  22.5 us (35%)
  starting transfers between devices  16 us (25%)
  blocking collectives  13.5 us (21%)
  waiting for transfers between devices  12.2 us (19%)
    all_to_all x1, blocking collectives, body(): lax.all_to_all(outgoing, ('seq', 'exp'), split_axis=0, concat_axis=0, til...  13.5 us
    ppermute x21, starting transfers between devices, exchange(): return lax.ppermute(value, 'seq', [(i, i ^ bits) for i in range(count)])  13.3 us
    ppermute x21, waiting for transfers between devices, exchange(): return lax.ppermute(value, 'seq', [(i, i ^ bits) for i in range(count)])  9.41 us
    pallas_call x1, Pallas kernels, body(): pl.pallas_call(attention_kernel, in_specs=[vmem] * (seq_count + 4) + [hbm...  6.85 us
    pallas_call x1, Pallas kernels, fetch_window(): pl.pallas_call(functools.partial(fetch_window_kernel, first_keys), in_spe...  4.35 us
    pallas_call x1, Pallas kernels, body(): pl.pallas_call(expert_kernel, in_specs=[vmem, vmem, vmem, hbm, hbm], out_...  3.65 us
    all_to_all x1, starting transfers between devices, body(): lax.all_to_all(outgoing, ('seq', 'exp'), split_axis=0, concat_axis=0, til...  2.58 us
    pallas_call x1, Pallas kernels, body(): pl.pallas_call(qkv_kernel, in_specs=[hbm] * 4, out_shape=(shape((rows, sh...  1.94 us
  transfers between devices with their start and end apart: 23, of which 15 were waited for; matrix products, arithmetic and copies ran while one was open for 0% of the time, Pallas kernels for 11%

profile of v6, /device:TPU:0, one launch (start us, length us, event | category | flops | bytes accessed | tf_op | source)
XLA Modules:
  0.0 64.4 jit_solution(707737249507255105)
XLA Ops:
  0.0 1.9 %qkv.1 = (bf16[48,384]{1,0:T(8,128)(2,1)S(1)}, bf16[2,512,1024]{2,1,0:T(8,128)(2,1)S(1)}) custom-call(bf16[12,4,1024]{2,1,0:T(4,128)(2,1)} %refs_11_.1, f32[1,1024]{1,0:T(1,128)} %bitcast.10, bf16[384,1024]{1,0:T(8,128)(2,1)} %weight_ref.1, bf16[2,12,512,1024]{3,2,1,0:T(8,128)(2,1)} %refs_12_.1), custom_call_target="tpu_custom_call" | custom-call | tf_op jit(solution)/shard_map/qkv/pallas_call | solution.py:526
  1.9 4.0 %collective-permute-start.5 = (bf16[48,384]{1,0:T(8,128)(2,1)S(1)}, bf16[48,384]{1,0:T(8,128)(2,1)S(1)}, u32[]{:S(2)}, u32[]{:S(2)}) collective-permute-start(bf16[48,384]{1,0:T(8,128)(2,1)S(1)} %get-tuple-element.32.sent_ref), channel_id=1, source_target_pairs={{0,24},{4,28},{8,16},{12,20},{16,8},{20,12},{24,0},{28,4},{1,25},{... | collective-permute-start | bytes 110600 | tf_op jit(solution)/shard_map/ppermute | solution.py:478
  5.9 0.5 collective-permute-start.3
  6.4 0.1 collective-permute-start.1
  6.5 4.4 %fetch_window.1 = (bf16[48,384]{1,0:T(8,128)(2,1)S(1)}, bf16[8,512,1024]{2,1,0:T(8,128)(2,1)S(1)}, bf16[3,512,1024]{2,1,0:T(8,128)(2,1)S(1)}, s32[12,128]{1,0:T(...) custom-call(bf16[48,384]{1,0:T(8,128)(2,1)S(1)} %get-tuple-element.32.sent_ref, ...), custom_call_target="tpu_custom_call" | custom-call | bytes 12582912 | tf_op jit(solution)/shard_map/fetch_window/pallas_call | solution.py:544
  10.9 0.1 collective-permute-start
  11.0 0.5 collective-permute-start.6
  11.5 0.1 collective-permute-start.4
  11.6 0.4 collective-permute-start.2
  12.0 0.2 collective-permute-done.refs_1_
  12.2 0.2 collective-permute-done.6.refs_7_
  12.4 0.4 collective-permute-done.4.refs_5_
  12.7 0.2 collective-permute-done.2.refs_3_
  12.9 6.9 %attention.1.sent_ref = bf16[48,1152]{1,0:T(8,128)(2,1)S(1)} custom-call(bf16[48,384]{1,0:T(8,128)(2,1)S(1)} %get-tuple-element.33.refs_0_, bf16[48,384]{1,0:T(8,128)(2,1)S(1)} %collective-permute-done.refs_1_, bf16[48,384]{1,0:T(8,128)(2,1)S(1)} %collective-permute-done.1.refs_2_, bf16[48,384]{1,0:T(8,128)(2,1)S(1)} %collective-permute-done.2.refs_3_, ...), custom_call_target="tpu_custom_call" | custom-call | tf_op jit(solution)/shard_map/attention/pallas_call | solution.py:579
  19.7 0.0 copy-start.2
  19.7 0.0 copy-start
  19.8 0.0 copy-start.1
  19.8 2.9 %collective-permute-start.12 = (bf16[48,1152]{1,0:T(8,128)(2,1)S(1)}, bf16[48,1152]{1,0:T(8,128)(2,1)S(1)}, u32[]{:S(2)}, u32[]{:S(2)}) collective-permute-start(bf16[48,1152]{1,0:T(8,128)(2,1)S(1)} %attention.1.sent_ref), channel_id=1, source_target_pairs={{0,24},{4,28},{8,16},{12,20},{16,8},{20,12},{24,0},{28,4},{1,25},{... | collective-permute-start | bytes 331784 | tf_op jit(solution)/shard_map/ppermute | solution.py:478
  22.7 0.5 collective-permute-start.10
  23.2 0.1 collective-permute-start.8
  23.3 1.6 %fetch_expert.1 = (bf16[48,1152]{1,0:T(8,128)(2,1)S(1)}, bf16[2,512,1024]{2,1,0:T(8,128)(2,1)S(1)}) custom-call(bf16[48,1152]{1,0:T(8,128)(2,1)S(1)} %attention.1.sent_ref, bf16[2,1,1408,1024]{3,2,1,0:T(8,128)(2,1)} %in_ref.3), custom_call_target="tpu_custom_call" | custom-call | bytes 2097152 | tf_op jit(solution)/shard_map/fetch_expert/pallas_call | solution.py:598
  24.9 0.1 collective-permute-start.7
  25.0 1.4 %collective-permute-done.12.refs_6_ = bf16[48,1152]{1,0:T(8,128)(2,1)S(1)} collective-permute-done((bf16[48,1152]{1,0:T(8,128)(2,1)S(1)}, bf16[48,1152]{1,0:T(8,128)(2,1)S(1)}, u32[]{:S(2)}, u32[]{:S(2)}) %collective-permute-start.12) | collective-permute-done | bytes 110624 | tf_op jit(solution)/shard_map/ppermute | solution.py:478
  26.4 2.3 %collective-permute-done.10.refs_4_ = bf16[48,1152]{1,0:T(8,128)(2,1)S(1)} collective-permute-done((bf16[48,1152]{1,0:T(8,128)(2,1)S(1)}, bf16[48,1152]{1,0:T(8,128)(2,1)S(1)}, u32[]{:S(2)}, u32[]{:S(2)}) %collective-permute-start.10) | collective-permute-done | bytes 110624 | tf_op jit(solution)/shard_map/ppermute | solution.py:478
  28.6 0.0 collective-permute-start.11
  28.7 0.2 collective-permute-done.8.refs_2_
  28.9 0.3 collective-permute-start.9
  29.2 0.9 %extra.1 = (f32[48,1024]{1,0:T(8,128)S(1)}, f32[48,128]{1,0:T(8,128)S(1)}) custom-call(bf16[48,384]{1,0:T(8,128)(2,1)S(1)} %get-tuple-element.33.refs_0_, bf16[48,384]{1,0:T(8,128)(2,1)S(1)} %collective-permute-done.refs_1_, bf16[48,384]{1,0:T(8,128)(2,1)S(1)} %collective-permute-done.1.refs_2_, bf16[48,384]{1,0:T(8,128)(2,1)S(1)} %collective-permute-done.2.refs_3_, ...), custom_call_target="tpu_custom_call" | custom-call | tf_op jit(solution)/shard_map/extra/pallas_call | solution.py:613
  30.1 0.1 collective-permute-done.9.refs_3_
  30.2 1.3 %project.1 = (f32[32,8,128]{2,1,0:T(8,128)S(1)}, f32[48,128]{1,0:T(8,128)S(1)}) custom-call(bf16[48,1152]{1,0:T(8,128)(2,1)S(1)} %get-tuple-element.38.refs_0_, bf16[48,1152]{1,0:T(8,128)(2,1)S(1)} %collective-permute-done.7.refs_1_, bf16[48,1152]{1,0:T(8,128)(2,1)S(1)} %collective-permute-done.8.refs_2_, ...), custom_call_target="tpu_custom_call" | custom-call | tf_op jit(solution)/shard_map/project/pallas_call | solution.py:626
  31.6 13.5 %all_to_all.10.received_ref = f32[32,8,128]{2,1,0:T(8,128)S(1)} all-to-all(f32[32,8,128]{2,1,0:T(8,128)S(1)} %get-tuple-element.43), channel_id=1, replica_groups=mesh['seq'=8,'exp'=4] {'seq','exp'}, dimensions={0} | all-to-all | bytes 262144 | tf_op jit(solution)/shard_map/all_to_all | solution.py:639
  45.0 3.6 %expert.1 = (f32[32,512]{1,0:T(8,128)S(1)}, f32[32,512]{1,0:T(8,128)S(1)}) custom-call(f32[32,8,128]{2,1,0:T(8,128)S(1)} %all_to_all.10.received_ref, f32[1,1024]{1,0:T(1,128)S(1)} %bitcast.7, bf16[2,512,1024]{2,1,0:T(8,128)(2,1)S(1)} %get-tuple-element.44.piece_ref, bf16[2,1,1408,1024]{3,2,1,0:T(8,128)(2,1)} %in_ref.3, bf16[1,1408,1024]{2,1,0:T(8,128)(2,1)} %down_ref.1), custom_call_target="tpu_custom_call" | custom-call | tf_op jit(solution)/shard_map/expert/pallas_call | solution.py:643
  48.7 0.1 collective-permute-start.21
  48.8 1.2 %collective-permute-done.21.other_ref = f32[32,512]{1,0:T(8,128)S(1)} collective-permute-done((f32[32,512]{1,0:T(8,128)S(1)}, f32[32,512]{1,0:T(8,128)S(1)}, u32[]{:S(2)}, u32[]{:S(2)}) %collective-permute-start.21) | collective-permute-done | bytes 65568 | tf_op jit(solution)/shard_map/ppermute | solution.py:661
  50.0 0.7 %spread.1 = bf16[32,8,512]{2,1,0:T(8,128)(2,1)} custom-call(f32[32,512]{1,0:T(8,128)S(1)} %get-tuple-element.45.kept_ref, f32[32,512]{1,0:T(8,128)S(1)} %collective-permute-done.21.other_ref), custom_call_target="tpu_custom_call" | custom-call | tf_op jit(solution)/shard_map/spread/pallas_call | solution.py:669
  50.7 2.6 %all-to-all-start.1 = ((bf16[32,8,512]{2,1,0:T(8,128)(2,1)}), bf16[32,8,512]{2,1,0:T(8,128)(2,1)S(1)}, u32[]{:S(2)}, u32[]{:S(2)}) async-start(bf16[32,8,512]{2,1,0:T(8,128)(2,1)} %spread.1), calls=%async_computation.1 | async-start | bytes 524288 | tf_op jit(solution)/shard_map/all_to_all | solution.py:675
  53.3 2.6 %collective-permute-start.19 = (f32[48,128]{1,0:T(8,128)S(1)}, f32[48,128]{1,0:T(8,128)S(1)}, u32[]{:S(2)}, u32[]{:S(2)}) collective-permute-start(f32[48,128]{1,0:T(8,128)S(1)} %get-tuple-element.47.refs_0_), channel_id=1, source_target_pairs={{0,24},{4,28},{8,16},{12,20},{16,8},{20,12},{24,0},{28,4},{1,25},{... | collective-permute-start | bytes 73736 | tf_op jit(solution)/shard_map/ppermute | solution.py:478
  56.0 0.5 collective-permute-start.17
  56.5 0.4 collective-permute-start.15
  56.9 1.6 %collective-permute-done.19.refs_6_ = f32[48,128]{1,0:T(8,128)S(1)} collective-permute-done((f32[48,128]{1,0:T(8,128)S(1)}, f32[48,128]{1,0:T(8,128)S(1)}, u32[]{:S(2)}, u32[]{:S(2)}) %collective-permute-start.19) | collective-permute-done | bytes 24608 | tf_op jit(solution)/shard_map/ppermute | solution.py:478
  58.5 1.6 %collective-permute-done.17.refs_4_ = f32[48,128]{1,0:T(8,128)S(1)} collective-permute-done((f32[48,128]{1,0:T(8,128)S(1)}, f32[48,128]{1,0:T(8,128)S(1)}, u32[]{:S(2)}, u32[]{:S(2)}) %collective-permute-start.17) | collective-permute-done | bytes 24608 | tf_op jit(solution)/shard_map/ppermute | solution.py:478
  60.1 0.3 collective-permute-done.15.refs_2_
  60.4 0.2 collective-permute-start.16
  60.6 0.7 %collective-permute-done.18.refs_5_ = f32[48,128]{1,0:T(8,128)S(1)} collective-permute-done((f32[48,128]{1,0:T(8,128)S(1)}, f32[48,128]{1,0:T(8,128)S(1)}, u32[]{:S(2)}, u32[]{:S(2)}) %collective-permute-start.18) | collective-permute-done | bytes 24608 | tf_op jit(solution)/shard_map/ppermute | solution.py:478
  61.3 0.3 collective-permute-done.16.refs_3_
  61.6 0.4 home.1
  62.0 1.5 %all-to-all-done.1 = bf16[32,8,512]{2,1,0:T(8,128)(2,1)S(1)} async-done(((bf16[32,8,512]{2,1,0:T(8,128)(2,1)}), bf16[32,8,512]{2,1,0:T(8,128)(2,1)S(1)}, u32[]{:S(2)}, u32[]{:S(2)}) %all-to-all-start.1) | async-done | bytes 262176 | tf_op jit(solution)/shard_map/all_to_all | solution.py:675
  63.5 0.9 %final.1 = bf16[12,4,1024]{2,1,0:T(4,128)(2,1)} custom-call(f32[48,128]{1,0:T(8,128)S(1)} %get-tuple-element.57.gates_ref, bf16[8,4,8,512]{3,2,1,0:T(8,128)(2,1)S(1)} %bitcast.5, f32[48,1024]{1,0:T(8,128)S(1)} %get-tuple-element.58.residual_ref), custom_call_target="tpu_custom_call" | custom-call | tf_op jit(solution)/shard_map/final/pallas_call | solution.py:692
  (19 shorter events, 0.0 us)
Async XLA Ops:
  1.9 9.0 %collective-permute-start.5 = (bf16[48,384]{1,0:T(8,128)(2,1)S(1)}, bf16[48,384]{1,0:T(8,128)(2,1)S(1)}, u32[]{:S(2)}, u32[]{:S(2)}) collective-permute-start(bf16[48,384]{1,0:T(8,128)(2,1)S(1)} %get-tuple-element.32.sent_ref), channel_id=1, source_target_pairs={{0,24},{4,28},{8,16},{12,20},{16,8},{20,12},{24,0},{28,4},{1,25},{... | collective-permute-start | bytes 110600 | tf_op jit(solution)/shard_map/ppermute | solution.py:478
  5.9 5.6 %collective-permute-start.3 = (bf16[48,384]{1,0:T(8,128)(2,1)S(1)}, bf16[48,384]{1,0:T(8,128)(2,1)S(1)}, u32[]{:S(2)}, u32[]{:S(2)}) collective-permute-start(bf16[48,384]{1,0:T(8,128)(2,1)S(1)} %get-tuple-element.32.sent_ref), channel_id=1, source_target_pairs={{0,16},{4,20},{8,24},{12,28},{16,0},{20,4},{24,8},{28,12},{1,17},{... | collective-permute-start | bytes 110600 | tf_op jit(solution)/shard_map/ppermute | solution.py:478
  6.4 5.2 %collective-permute-start.1 = (bf16[48,384]{1,0:T(8,128)(2,1)S(1)}, bf16[48,384]{1,0:T(8,128)(2,1)S(1)}, u32[]{:S(2)}, u32[]{:S(2)}) collective-permute-start(bf16[48,384]{1,0:T(8,128)(2,1)S(1)} %get-tuple-element.32.sent_ref), channel_id=1, source_target_pairs={{0,8},{4,12},{8,0},{12,4},{16,24},{20,28},{24,16},{28,20},{1,9},{5... | collective-permute-start | bytes 110600 | tf_op jit(solution)/shard_map/ppermute | solution.py:478
  10.9 1.3 %collective-permute-start = (bf16[48,384]{1,0:T(8,128)(2,1)S(1)}, bf16[48,384]{1,0:T(8,128)(2,1)S(1)}, u32[]{:S(2)}, u32[]{:S(2)}) collective-permute-start(bf16[48,384]{1,0:T(8,128)(2,1)S(1)} %get-tuple-element.33.refs_0_), channel_id=1, source_target_pairs={{0,4},{4,0},{8,12},{12,8},{16,20},{20,16},{24,28},{28,24},{1,5},{5... | collective-permute-start | bytes 110600 | tf_op jit(solution)/shard_map/ppermute | solution.py:478
  11.0 1.4 %collective-permute-start.6 = (bf16[48,384]{1,0:T(8,128)(2,1)S(1)}, bf16[48,384]{1,0:T(8,128)(2,1)S(1)}, u32[]{:S(2)}, u32[]{:S(2)}) collective-permute-start(bf16[48,384]{1,0:T(8,128)(2,1)S(1)} %collective-permute-done.5.refs_6_), channel_id=1, source_target_pairs={{0,4},{4,0},{8,12},{12,8},{16,20},{20,16},{24,28},{28,24},{1,5},{5... | collective-permute-start | bytes 110600 | tf_op jit(solution)/shard_map/ppermute | solution.py:478
  11.5 1.2 %collective-permute-start.4 = (bf16[48,384]{1,0:T(8,128)(2,1)S(1)}, bf16[48,384]{1,0:T(8,128)(2,1)S(1)}, u32[]{:S(2)}, u32[]{:S(2)}) collective-permute-start(bf16[48,384]{1,0:T(8,128)(2,1)S(1)} %collective-permute-done.3.refs_4_), channel_id=1, source_target_pairs={{0,4},{4,0},{8,12},{12,8},{16,20},{20,16},{24,28},{28,24},{1,5},{5... | collective-permute-start | bytes 110600 | tf_op jit(solution)/shard_map/ppermute | solution.py:478
  11.6 1.3 %collective-permute-start.2 = (bf16[48,384]{1,0:T(8,128)(2,1)S(1)}, bf16[48,384]{1,0:T(8,128)(2,1)S(1)}, u32[]{:S(2)}, u32[]{:S(2)}) collective-permute-start(bf16[48,384]{1,0:T(8,128)(2,1)S(1)} %collective-permute-done.1.refs_2_), channel_id=1, source_target_pairs={{0,4},{4,0},{8,12},{12,8},{16,20},{20,16},{24,28},{28,24},{1,5},{5... | collective-permute-start | bytes 110600 | tf_op jit(solution)/shard_map/ppermute | solution.py:478
  19.7 9.4 %copy-start.2 = (bf16[2,12,4,1024]{3,2,1,0:T(4,128)(2,1)S(1)}, bf16[2,12,4,1024]{3,2,1,0:T(4,128)(2,1)}, u32[]{:S(2)}) copy-start(bf16[2,12,4,1024]{3,2,1,0:T(4,128)(2,1)} %refs_8_.1) | copy-start | bytes 589828
  19.7 10.5 %copy-start = (bf16[12,4,1024]{2,1,0:T(4,128)(2,1)S(1)}, bf16[12,4,1024]{2,1,0:T(4,128)(2,1)}, u32[]{:S(2)}) copy-start(bf16[12,4,1024]{2,1,0:T(4,128)(2,1)} %refs_11_.1) | copy-start | bytes 294916
  19.8 10.5 %copy-start.1 = (bf16[128,1024]{1,0:T(8,128)(2,1)S(1)}, bf16[128,1024]{1,0:T(8,128)(2,1)}, u32[]{:S(2)}) copy-start(bf16[128,1024]{1,0:T(8,128)(2,1)} %refs_10_.1) | copy-start | bytes 786436
  19.8 25.3 %copy-start.4 = (f32[1024]{0:T(1024)S(1)}, f32[1024]{0:T(1024)}, u32[]{:S(2)}) copy-start(f32[1024]{0:T(1024)} %param.20) | copy-start | bytes 12292
  19.8 6.6 %collective-permute-start.12 = (bf16[48,1152]{1,0:T(8,128)(2,1)S(1)}, bf16[48,1152]{1,0:T(8,128)(2,1)S(1)}, u32[]{:S(2)}, u32[]{:S(2)}) collective-permute-start(bf16[48,1152]{1,0:T(8,128)(2,1)S(1)} %attention.1.sent_ref), channel_id=1, source_target_pairs={{0,24},{4,28},{8,16},{12,20},{16,8},{20,12},{24,0},{28,4},{1,25},{... | collective-permute-start | bytes 331784 | tf_op jit(solution)/shard_map/ppermute | solution.py:478
  22.7 5.9 %collective-permute-start.10 = (bf16[48,1152]{1,0:T(8,128)(2,1)S(1)}, bf16[48,1152]{1,0:T(8,128)(2,1)S(1)}, u32[]{:S(2)}, u32[]{:S(2)}) collective-permute-start(bf16[48,1152]{1,0:T(8,128)(2,1)S(1)} %attention.1.sent_ref), channel_id=1, source_target_pairs={{0,16},{4,20},{8,24},{12,28},{16,0},{20,4},{24,8},{28,12},{1,17},{... | collective-permute-start | bytes 331784 | tf_op jit(solution)/shard_map/ppermute | solution.py:478
  23.2 5.7 %collective-permute-start.8 = (bf16[48,1152]{1,0:T(8,128)(2,1)S(1)}, bf16[48,1152]{1,0:T(8,128)(2,1)S(1)}, u32[]{:S(2)}, u32[]{:S(2)}) collective-permute-start(bf16[48,1152]{1,0:T(8,128)(2,1)S(1)} %attention.1.sent_ref), channel_id=1, source_target_pairs={{0,8},{4,12},{8,0},{12,4},{16,24},{20,28},{24,16},{28,20},{1,9},{5... | collective-permute-start | bytes 331784 | tf_op jit(solution)/shard_map/ppermute | solution.py:478
  24.9 5.2 %collective-permute-start.7 = (bf16[48,1152]{1,0:T(8,128)(2,1)S(1)}, bf16[48,1152]{1,0:T(8,128)(2,1)S(1)}, u32[]{:S(2)}, u32[]{:S(2)}) collective-permute-start(bf16[48,1152]{1,0:T(8,128)(2,1)S(1)} %get-tuple-element.38.refs_0_), channel_id=1, source_target_pairs={{0,4},{4,0},{8,12},{12,8},{16,20},{20,16},{24,28},{28,24},{1,5},{5... | collective-permute-start | bytes 331784 | tf_op jit(solution)/shard_map/ppermute | solution.py:478
  26.4 3.7 %collective-permute-start.13 = (bf16[48,1152]{1,0:T(8,128)(2,1)S(1)}, bf16[48,1152]{1,0:T(8,128)(2,1)S(1)}, u32[]{:S(2)}, u32[]{:S(2)}) collective-permute-start(bf16[48,1152]{1,0:T(8,128)(2,1)S(1)} %collective-permute-done.12.refs_6_), channel_id=1, source_target_pairs={{0,4},{4,0},{8,12},{12,8},{16,20},{20,16},{24,28},{28,24},{1,5},{5... | collective-permute-start | bytes 331784 | tf_op jit(solution)/shard_map/ppermute | solution.py:478
  28.6 1.5 %collective-permute-start.11 = (bf16[48,1152]{1,0:T(8,128)(2,1)S(1)}, bf16[48,1152]{1,0:T(8,128)(2,1)S(1)}, u32[]{:S(2)}, u32[]{:S(2)}) collective-permute-start(bf16[48,1152]{1,0:T(8,128)(2,1)S(1)} %collective-permute-done.10.refs_4_), channel_id=1, source_target_pairs={{0,4},{4,0},{8,12},{12,8},{16,20},{20,16},{24,28},{28,24},{1,5},{5... | collective-permute-start | bytes 331784 | tf_op jit(solution)/shard_map/ppermute | solution.py:478
  28.9 1.3 %collective-permute-start.9 = (bf16[48,1152]{1,0:T(8,128)(2,1)S(1)}, bf16[48,1152]{1,0:T(8,128)(2,1)S(1)}, u32[]{:S(2)}, u32[]{:S(2)}) collective-permute-start(bf16[48,1152]{1,0:T(8,128)(2,1)S(1)} %collective-permute-done.8.refs_2_), channel_id=1, source_target_pairs={{0,4},{4,0},{8,12},{12,8},{16,20},{20,16},{24,28},{28,24},{1,5},{5... | collective-permute-start | bytes 331784 | tf_op jit(solution)/shard_map/ppermute | solution.py:478
  45.0 16.6 %copy-start.3 = (bf16[1024,16]{0,1:T(8,128)(2,1)S(1)}, bf16[1024,16]{0,1:T(8,128)(2,1)}, u32[]{:S(2)}) copy-start(bf16[1024,16]{0,1:T(8,128)(2,1)} %param.21) | copy-start | bytes 98308
  48.7 1.3 %collective-permute-start.21 = (f32[32,512]{1,0:T(8,128)S(1)}, f32[32,512]{1,0:T(8,128)S(1)}, u32[]{:S(2)}, u32[]{:S(2)}) collective-permute-start(f32[32,512]{1,0:T(8,128)S(1)} %get-tuple-element.46), channel_id=1, source_target_pairs={{0,4},{4,0},{8,12},{12,8},{16,20},{20,16},{24,28},{28,24},{1,5},{5... | collective-permute-start | bytes 196616 | tf_op jit(solution)/shard_map/ppermute | solution.py:661
  50.7 12.8 %all-to-all-start.1 = ((bf16[32,8,512]{2,1,0:T(8,128)(2,1)}), bf16[32,8,512]{2,1,0:T(8,128)(2,1)S(1)}, u32[]{:S(2)}, u32[]{:S(2)}) async-start(bf16[32,8,512]{2,1,0:T(8,128)(2,1)} %spread.1), calls=%async_computation.1 | async-start | bytes 524288 | tf_op jit(solution)/shard_map/all_to_all | solution.py:675
  53.3 5.2 %collective-permute-start.19 = (f32[48,128]{1,0:T(8,128)S(1)}, f32[48,128]{1,0:T(8,128)S(1)}, u32[]{:S(2)}, u32[]{:S(2)}) collective-permute-start(f32[48,128]{1,0:T(8,128)S(1)} %get-tuple-element.47.refs_0_), channel_id=1, source_target_pairs={{0,24},{4,28},{8,16},{12,20},{16,8},{20,12},{24,0},{28,4},{1,25},{... | collective-permute-start | bytes 73736 | tf_op jit(solution)/shard_map/ppermute | solution.py:478
  56.0 4.1 %collective-permute-start.17 = (f32[48,128]{1,0:T(8,128)S(1)}, f32[48,128]{1,0:T(8,128)S(1)}, u32[]{:S(2)}, u32[]{:S(2)}) collective-permute-start(f32[48,128]{1,0:T(8,128)S(1)} %get-tuple-element.47.refs_0_), channel_id=1, source_target_pairs={{0,16},{4,20},{8,24},{12,28},{16,0},{20,4},{24,8},{28,12},{1,17},{... | collective-permute-start | bytes 73736 | tf_op jit(solution)/shard_map/ppermute | solution.py:478
  56.5 3.9 %collective-permute-start.15 = (f32[48,128]{1,0:T(8,128)S(1)}, f32[48,128]{1,0:T(8,128)S(1)}, u32[]{:S(2)}, u32[]{:S(2)}) collective-permute-start(f32[48,128]{1,0:T(8,128)S(1)} %get-tuple-element.47.refs_0_), channel_id=1, source_target_pairs={{0,8},{4,12},{8,0},{12,4},{16,24},{20,28},{24,16},{28,20},{1,9},{5... | collective-permute-start | bytes 73736 | tf_op jit(solution)/shard_map/ppermute | solution.py:478
  56.9 3.7 %collective-permute-start.14 = (f32[48,128]{1,0:T(8,128)S(1)}, f32[48,128]{1,0:T(8,128)S(1)}, u32[]{:S(2)}, u32[]{:S(2)}) collective-permute-start(f32[48,128]{1,0:T(8,128)S(1)} %get-tuple-element.47.refs_0_), channel_id=1, source_target_pairs={{0,4},{4,0},{8,12},{12,8},{16,20},{20,16},{24,28},{28,24},{1,5},{5... | collective-permute-start | bytes 73736 | tf_op jit(solution)/shard_map/ppermute | solution.py:478
  58.5 2.1 %collective-permute-start.20 = (f32[48,128]{1,0:T(8,128)S(1)}, f32[48,128]{1,0:T(8,128)S(1)}, u32[]{:S(2)}, u32[]{:S(2)}) collective-permute-start(f32[48,128]{1,0:T(8,128)S(1)} %collective-permute-done.19.refs_6_), channel_id=1, source_target_pairs={{0,4},{4,0},{8,12},{12,8},{16,20},{20,16},{24,28},{28,24},{1,5},{5... | collective-permute-start | bytes 73736 | tf_op jit(solution)/shard_map/ppermute | solution.py:478
  60.1 1.2 %collective-permute-start.18 = (f32[48,128]{1,0:T(8,128)S(1)}, f32[48,128]{1,0:T(8,128)S(1)}, u32[]{:S(2)}, u32[]{:S(2)}) collective-permute-start(f32[48,128]{1,0:T(8,128)S(1)} %collective-permute-done.17.refs_4_), channel_id=1, source_target_pairs={{0,4},{4,0},{8,12},{12,8},{16,20},{20,16},{24,28},{28,24},{1,5},{5... | collective-permute-start | bytes 73736 | tf_op jit(solution)/shard_map/ppermute | solution.py:478
  60.4 1.2 %collective-permute-start.16 = (f32[48,128]{1,0:T(8,128)S(1)}, f32[48,128]{1,0:T(8,128)S(1)}, u32[]{:S(2)}, u32[]{:S(2)}) collective-permute-start(f32[48,128]{1,0:T(8,128)S(1)} %collective-permute-done.15.refs_2_), channel_id=1, source_target_pairs={{0,4},{4,0},{8,12},{12,8},{16,20},{20,16},{24,28},{28,24},{1,5},{5... | collective-permute-start | bytes 73736 | tf_op jit(solution)/shard_map/ppermute | solution.py:478

commit v7 on v6

--- a/solution.py
+++ b/solution.py
@@ -114,7 +114,6 @@
     weight_ref,
     window_ref,
     out_ref,
-    keys_ref,
     token_buf,
     gain_buf,
     weight_buf,
@@ -126,16 +125,14 @@
             (tokens_ref, token_buf),
             (gain_ref, gain_buf),
             (weight_ref, weight_buf),
-            (window_ref.at[0, pl.ds(0, keys_ref.shape[0])], keys_ref),
         ),
         sems,
     )
-    for copy in copies[:3]:
+    for copy in copies:
         copy.wait()
     copy_rows(token_buf, rows_ref)
     normed = rms_rows(rows_ref[...], gain_buf[...])
     out_ref[...] = dot(normed, weight_buf[...], ROWS_BY_ROWS).astype(jnp.bfloat16)
-    copies[3].wait()
 
 
 def in_order(sent_refs, ordered_ref):
@@ -150,16 +147,12 @@
     return (row_head == col_head).astype(jnp.float32)
 
 
-def fetch_window_kernel(
-    first,
+def routing_kernel(
     sent_ref,
-    window_ref,
     lengths_ref,
     ids_ref,
     order_ref,
     held_ref,
-    keys_ref,
-    values_ref,
     spans_ref,
     select_ref,
     chosen_ref,
@@ -174,19 +167,15 @@
             (ids_ref, ids_buf),
             (order_ref, order_buf),
             (lengths_ref, numbers_ref),
-            (window_ref.at[0, pl.ds(first, keys_ref.shape[0])], keys_ref),
-            (window_ref.at[1, pl.ds(0, values_ref.shape[0])], values_ref),
         ),
         sems,
     )
     held_ref[...] = sent_ref[...]
-    for copy in copies[:3]:
+    for copy in copies:
         copy.wait()
     turned_ref[...] = route(ids_buf, order_buf, select_ref, chosen_ref)
     for r in range(spans_ref.shape[0]):
         spans_ref[r : r + 1, :] = jnp.full((1, LANES), numbers_ref[r], jnp.int32)
-    for copy in copies[3:]:
-        copy.wait()
 
 
 def fetch_expert_kernel(sent_ref, in_ref, held_ref, piece_ref, sems):
@@ -197,25 +186,10 @@
 
 
 def attention_kernel(*refs):
-    *mixed_refs, spans_ref, first_ref, keys_ref, values_ref, window_ref = refs[:-6]
-    out_ref, ordered_ref, flat_ref, query_ref, late_ref, sems = refs[-6:]
+    *mixed_refs, spans_ref, window_ref = refs[:-4]
+    out_ref, ordered_ref, flat_ref, query_ref = refs[-4:]
     devices, rows, share = ordered_ref.shape
     _, requests, span, width = window_ref.shape
-    held = {(0, r): first_ref.at[r] for r in range(first_ref.shape[0])}
-    held |= {(0, r + first_ref.shape[0]): keys_ref.at[r] for r in range(keys_ref.shape[0])}
-    held |= {(1, r): values_ref.at[r] for r in range(values_ref.shape[0])}
-    needed = [(p, r) for i in range(requests + 1) for p, r in ((0, i), (1, i - 1))]
-    needed = [at for at in needed if 0 <= at[1] < requests and at not in held]
-    late = {at: late_ref.at[i] for i, at in enumerate(needed)}
-    copies = started([(window_ref.at[p, r], late[p, r]) for p, r in needed], sems)
-    waits = dict(zip(needed, copies))
-
-    def window(p, r):
-        if (p, r) in held:
-            return held[p, r]
-        waits[p, r].wait()
-        return late[p, r]
-
     steps = rows // requests
     block_rows = BLOCK_HEADS * steps
     place = lax.axis_index("seq")
@@ -240,7 +214,7 @@
     cols = [slice(c, c + BLOCK) for c in range(0, width, BLOCK)]
 
     def score(r):
-        keys = window(0, r)
+        keys = window_ref.at[0, r]
         return jnp.concatenate(
             [dot(query_ref[r, :, c], keys[:, c], ROWS_BY_ROWS) for c in cols], axis=0
         )
@@ -256,7 +230,7 @@
         weight = jnp.where(live, jnp.exp(scores - peak), 0.0)
         total = jnp.sum(weight, axis=-1, keepdims=True)
         weight = weight.reshape(HEADS * steps, span).astype(jnp.bfloat16)
-        values = window(1, r)
+        values = window_ref.at[1, r]
         outs = []
         for b, c in enumerate(cols):
             own = slice(b * block_rows, (b + 1) * block_rows)
@@ -519,14 +493,10 @@
     hbm = pl.BlockSpec(memory_space=pltpu.HBM)
 
     gain_row = attn_gain.reshape(1, width)
-    first_keys = min(FIRST_KEYS, requests)
-    second_keys = min(SECOND_KEYS, requests - first_keys)
-    second_values = min(SECOND_VALUES, requests)
-    late = 2 * requests - first_keys - second_keys - second_values
-    local_mix, first = pl.pallas_call(
+    local_mix = pl.pallas_call(
         qkv_kernel,
         in_specs=[hbm] * 4,
-        out_shape=(shape((rows, share), bf16), shape((first_keys, span, width), bf16)),
+        out_shape=shape((rows, share), bf16),
         scratch_shapes=[
             pltpu.VMEM(tokens.shape, bf16),
             pltpu.VMEM(gain_row.shape, f32),
@@ -540,14 +510,12 @@
 
     fetched = []
 
-    def fetch_window(values):
+    def routing(values):
         held, *outputs = pl.pallas_call(
-            functools.partial(fetch_window_kernel, first_keys),
-            in_specs=[vmem] + [hbm] * 4,
+            routing_kernel,
+            in_specs=[vmem] + [hbm] * 3,
             out_shape=(
                 shape(values.shape, bf16),
-                shape((second_keys, span, width), bf16),
-                shape((second_values, span, width), bf16),
                 shape((requests, LANES), jnp.int32),
                 shape((TOPK, rows, slots), f32),
                 shape((TOPK, rows, LANES), f32),
@@ -557,14 +525,12 @@
                 pltpu.SMEM((requests,), jnp.int32),
                 pltpu.VMEM((steps, TOPK, requests), jnp.int32),
                 pltpu.VMEM(slot_order.shape, jnp.int32),
-                pltpu.SemaphoreType.DMA((5,)),
+                pltpu.SemaphoreType.DMA((3,)),
             ],
             compiler_params=params(8),
-            cost_estimate=moving(window_cache.size),
-            name="fetch_window",
+            name="routing",
         )(
             values,
-            in_hbm(window_cache),
             in_hbm(lengths),
             in_hbm(expert_ids.transpose(1, 2, 0)),
             in_hbm(slot_order),
@@ -572,24 +538,22 @@
         fetched.extend(outputs)
         return held
 
-    mixed = gather_seq(local_mix, fetch_window)
-    keys, values, spans, select, chosen, turned = fetched
+    mixed = gather_seq(local_mix, routing)
+    spans, select, chosen, turned = fetched
 
     padded = width + LANES
     part = pl.pallas_call(
         attention_kernel,
-        in_specs=[vmem] * (seq_count + 4) + [hbm],
+        in_specs=[vmem] * (seq_count + 2),
         out_shape=shape((rows, padded), bf16),
         scratch_shapes=[
             pltpu.VMEM((seq_count, rows, share), bf16),
             pltpu.VMEM((rows, padded), f32),
             pltpu.VMEM((requests, BLOCK_HEADS * steps, width), bf16),
-            pltpu.VMEM((late, span, width), bf16),
-            pltpu.SemaphoreType.DMA((late,)),
         ],
-        compiler_params=params(24),
+        compiler_params=params(8),
         name="attention",
-    )(*mixed, spans, first, keys, values, in_hbm(window_cache))
+    )(*mixed, spans, window_cache)
     hidden_units = expert_down.shape[1]
     held_units = min(PIECE, hidden_units)
     late_units = max(hidden_units - held_units, 16)

time: 64.6 us -> 61.1 us (0.946)
  Pallas kernels: 22.5 us -> 18.4 us
  waiting for transfers between devices: 12.2 us -> 13.2 us
    pallas_call x3, Pallas kernels: 13.1 us -> 9 us  [the longest x1 5.35 us: body(): pl.pallas_call(attention_kernel, in_specs=[vmem] * (seq_count + 2), out_s...]
    ppermute x21, waiting for transfers between devices: 9.41 us -> 10.5 us  [exchange(): return lax.ppermute(value, 'seq', [(i, i ^ bits) for i in range(count)])]
  transfers between devices with their start and end apart: 23 -> 23, of which waited for: 15 -> 14; matrix products, arithmetic and copies ran while one was open for 0% -> 0% of each run, Pallas kernels for 11% -> 8%
where the time goes in v7:
time: 61.1 us; the launch traced here: 60.8 us
  Pallas kernels  18.4 us (30%)
  starting transfers between devices  15.6 us (26%)
  blocking collectives  13.4 us (22%)
  waiting for transfers between devices  13.2 us (22%)
    all_to_all x1, blocking collectives, body(): lax.all_to_all(outgoing, ('seq', 'exp'), split_axis=0, concat_axis=0, til...  13.4 us
    ppermute x21, starting transfers between devices, exchange(): return lax.ppermute(value, 'seq', [(i, i ^ bits) for i in range(count)])  13 us
    ppermute x21, waiting for transfers between devices, exchange(): return lax.ppermute(value, 'seq', [(i, i ^ bits) for i in range(count)])  10.5 us
    pallas_call x1, Pallas kernels, body(): pl.pallas_call(attention_kernel, in_specs=[vmem] * (seq_count + 2), out_s...  5.35 us
    pallas_call x1, Pallas kernels, body(): pl.pallas_call(expert_kernel, in_specs=[vmem, vmem, vmem, hbm, hbm], out_...  3.65 us
    all_to_all x1, starting transfers between devices, body(): lax.all_to_all(outgoing, ('seq', 'exp'), split_axis=0, concat_axis=0, til...  2.58 us
    pallas_call x1, Pallas kernels, routing(): pl.pallas_call(routing_kernel, in_specs=[vmem] + [hbm] * 3, out_shape=(sh...  1.88 us
    pallas_call x1, Pallas kernels, body(): pl.pallas_call(qkv_kernel, in_specs=[hbm] * 4, out_shape=shape((rows, sha...  1.77 us
  transfers between devices with their start and end apart: 23, of which 14 were waited for; matrix products, arithmetic and copies ran while one was open for 0% of the time, Pallas kernels for 8%

profile of v7, /device:TPU:0, one launch (start us, length us, event | category | flops | bytes accessed | tf_op | source)
XLA Modules:
  0.0 60.8 jit_solution(2606579891634382301)
XLA Ops:
  0.0 1.8 %qkv.1.sent_ref = bf16[48,384]{1,0:T(8,128)(2,1)S(1)} custom-call(bf16[12,4,1024]{2,1,0:T(4,128)(2,1)} %refs_11_.1, f32[1,1024]{1,0:T(1,128)} %bitcast.9, bf16[384,1024]{1,0:T(8,128)(2,1)} %weight_ref.1, bf16[2,12,512,1024]{3,2,1,0:T(8,128)(2,1)} %refs_9_.1), custom_call_target="tpu_custom_call" | custom-call | tf_op jit(solution)/shard_map/qkv/pallas_call | solution.py:496
  1.8 4.0 %collective-permute-start.5 = (bf16[48,384]{1,0:T(8,128)(2,1)S(1)}, bf16[48,384]{1,0:T(8,128)(2,1)S(1)}, u32[]{:S(2)}, u32[]{:S(2)}) collective-permute-start(bf16[48,384]{1,0:T(8,128)(2,1)S(1)} %qkv.1.sent_ref), channel_id=1, source_target_pairs={{0,24},{4,28},{8,16},{12,20},{16,8},{20,12},{24,0},{28,4},{1,25},{... | collective-permute-start | bytes 110600 | tf_op jit(solution)/shard_map/ppermute | solution.py:452
  5.7 0.5 collective-permute-start.3
  6.3 0.1 collective-permute-start.1
  6.4 1.9 %routing.1 = (bf16[48,384]{1,0:T(8,128)(2,1)S(1)}, s32[12,128]{1,0:T(8,128)S(1)}, f32[2,48,128]{2,1,0:T(8,128)S(1)}, f32[2,48,128]{2,1,0:T(8,128)S(1)}, f32[128,48]{1,0:T(8,128)S(1)}) custom-call(bf16[48,384]{1,0:T(8,128)(2,1)S(1)} %qkv.1.sent_ref, s32[12]{0:T(128)} %lengths_ref.1, s32[4,2,12]{2,1,0:T(2,128)} %bitcast.10, s32[1,48]{1,0:T(1,128)} %order_ref.1), custom_call_target="tpu_custom_call" | custom-call | tf_op jit(solution)/shard_map/routing/pallas_call | solution.py:514
  8.3 0.1 collective-permute-start
  8.4 0.5 collective-permute-start.6
  8.9 0.8 %collective-permute-done.3.refs_4_ = bf16[48,384]{1,0:T(8,128)(2,1)S(1)} collective-permute-done((bf16[48,384]{1,0:T(8,128)(2,1)S(1)}, bf16[48,384]{1,0:T(8,128)(2,1)S(1)}, u32[]{:S(2)}, u32[]{:S(2)}) %collective-permute-start.3) | collective-permute-done | bytes 36896 | tf_op jit(solution)/shard_map/ppermute | solution.py:452
  9.7 0.5 collective-permute-done.1.refs_2_
  10.2 0.0 collective-permute-start.2
  10.2 0.7 %collective-permute-done.4.refs_5_ = bf16[48,384]{1,0:T(8,128)(2,1)S(1)} collective-permute-done((bf16[48,384]{1,0:T(8,128)(2,1)S(1)}, bf16[48,384]{1,0:T(8,128)(2,1)S(1)}, u32[]{:S(2)}, u32[]{:S(2)}) %collective-permute-start.4) | collective-permute-done | bytes 36896 | tf_op jit(solution)/shard_map/ppermute | solution.py:452
  10.9 0.5 collective-permute-done.2.refs_3_
  11.4 5.3 %attention.1.sent_ref = bf16[48,1152]{1,0:T(8,128)(2,1)S(1)} custom-call(bf16[48,384]{1,0:T(8,128)(2,1)S(1)} %get-tuple-element.28.refs_0_, bf16[48,384]{1,0:T(8,128)(2,1)S(1)} %collective-permute-done.refs_1_, bf16[48,384]{1,0:T(8,128)(2,1)S(1)} %collective-permute-done.1.refs_2_, bf16[48,384]{1,0:T(8,128)(2,1)S(1)} %collective-permute-done.2.refs_3_, ...), custom_call_target="tpu_custom_call" | custom-call | tf_op jit(solution)/shard_map/attention/pallas_call | solution.py:545
  16.8 0.0 copy-start.3
  16.8 0.0 copy-start.1
  16.8 0.0 copy-start.2
  16.8 0.0 copy-start.5
  16.8 1.7 %collective-permute-start.12 = (bf16[48,1152]{1,0:T(8,128)(2,1)S(1)}, bf16[48,1152]{1,0:T(8,128)(2,1)S(1)}, u32[]{:S(2)}, u32[]{:S(2)}) collective-permute-start(bf16[48,1152]{1,0:T(8,128)(2,1)S(1)} %attention.1.sent_ref), channel_id=1, source_target_pairs={{0,24},{4,28},{8,16},{12,20},{16,8},{20,12},{24,0},{28,4},{1,25},{... | collective-permute-start | bytes 331784 | tf_op jit(solution)/shard_map/ppermute | solution.py:452
  18.5 0.5 collective-permute-start.10
  19.1 1.3 %collective-permute-start.8 = (bf16[48,1152]{1,0:T(8,128)(2,1)S(1)}, bf16[48,1152]{1,0:T(8,128)(2,1)S(1)}, u32[]{:S(2)}, u32[]{:S(2)}) collective-permute-start(bf16[48,1152]{1,0:T(8,128)(2,1)S(1)} %attention.1.sent_ref), channel_id=1, source_target_pairs={{0,8},{4,12},{8,0},{12,4},{16,24},{20,28},{24,16},{28,20},{1,9},{5... | collective-permute-start | bytes 331784 | tf_op jit(solution)/shard_map/ppermute | solution.py:452
  20.4 1.6 %fetch_expert.1 = (bf16[48,1152]{1,0:T(8,128)(2,1)S(1)}, bf16[2,512,1024]{2,1,0:T(8,128)(2,1)S(1)}) custom-call(bf16[48,1152]{1,0:T(8,128)(2,1)S(1)} %attention.1.sent_ref, bf16[2,1,1408,1024]{3,2,1,0:T(8,128)(2,1)} %in_ref.3), custom_call_target="tpu_custom_call" | custom-call | bytes 2097152 | tf_op jit(solution)/shard_map/fetch_expert/pallas_call | solution.py:562
  21.9 0.1 collective-permute-start.7
  22.0 1.4 %collective-permute-done.12.refs_6_ = bf16[48,1152]{1,0:T(8,128)(2,1)S(1)} collective-permute-done((bf16[48,1152]{1,0:T(8,128)(2,1)S(1)}, bf16[48,1152]{1,0:T(8,128)(2,1)S(1)}, u32[]{:S(2)}, u32[]{:S(2)}) %collective-permute-start.12) | collective-permute-done | bytes 110624 | tf_op jit(solution)/shard_map/ppermute | solution.py:452
  23.4 1.9 %collective-permute-done.10.refs_4_ = bf16[48,1152]{1,0:T(8,128)(2,1)S(1)} collective-permute-done((bf16[48,1152]{1,0:T(8,128)(2,1)S(1)}, bf16[48,1152]{1,0:T(8,128)(2,1)S(1)}, u32[]{:S(2)}, u32[]{:S(2)}) %collective-permute-start.10) | collective-permute-done | bytes 110624 | tf_op jit(solution)/shard_map/ppermute | solution.py:452
  25.3 0.0 collective-permute-start.11
  25.3 0.1 collective-permute-done.8.refs_2_
  25.4 0.4 collective-permute-start.9
  25.8 0.9 %extra.1 = (f32[48,1024]{1,0:T(8,128)S(1)}, f32[48,128]{1,0:T(8,128)S(1)}) custom-call(bf16[48,384]{1,0:T(8,128)(2,1)S(1)} %get-tuple-element.28.refs_0_, bf16[48,384]{1,0:T(8,128)(2,1)S(1)} %collective-permute-done.refs_1_, bf16[48,384]{1,0:T(8,128)(2,1)S(1)} %collective-permute-done.1.refs_2_, bf16[48,384]{1,0:T(8,128)(2,1)S(1)} %collective-permute-done.2.refs_3_, ...), custom_call_target="tpu_custom_call" | custom-call | tf_op jit(solution)/shard_map/extra/pallas_call | solution.py:577
  26.8 0.0 collective-permute-done.9.refs_3_
  26.8 1.3 %project.1 = (f32[32,8,128]{2,1,0:T(8,128)S(1)}, f32[48,128]{1,0:T(8,128)S(1)}) custom-call(bf16[48,1152]{1,0:T(8,128)(2,1)S(1)} %get-tuple-element.30.refs_0_, bf16[48,1152]{1,0:T(8,128)(2,1)S(1)} %collective-permute-done.7.refs_1_, bf16[48,1152]{1,0:T(8,128)(2,1)S(1)} %collective-permute-done.8.refs_2_, ...), custom_call_target="tpu_custom_call" | custom-call | tf_op jit(solution)/shard_map/project/pallas_call | solution.py:590
  28.1 13.4 %all_to_all.10.received_ref = f32[32,8,128]{2,1,0:T(8,128)S(1)} all-to-all(f32[32,8,128]{2,1,0:T(8,128)S(1)} %get-tuple-element.35), channel_id=1, replica_groups=mesh['seq'=8,'exp'=4] {'seq','exp'}, dimensions={0} | all-to-all | bytes 262144 | tf_op jit(solution)/shard_map/all_to_all | solution.py:603
  41.5 3.6 %expert.1 = (f32[32,512]{1,0:T(8,128)S(1)}, f32[32,512]{1,0:T(8,128)S(1)}) custom-call(f32[32,8,128]{2,1,0:T(8,128)S(1)} %all_to_all.10.received_ref, f32[1,1024]{1,0:T(1,128)S(1)} %bitcast.7, bf16[2,512,1024]{2,1,0:T(8,128)(2,1)S(1)} %get-tuple-element.36.piece_ref, bf16[2,1,1408,1024]{3,2,1,0:T(8,128)(2,1)} %in_ref.3, bf16[1,1408,1024]{2,1,0:T(8,128)(2,1)} %down_ref.1), custom_call_target="tpu_custom_call" | custom-call | tf_op jit(solution)/shard_map/expert/pallas_call | solution.py:607
  45.2 0.1 collective-permute-start.21
  45.2 1.2 %collective-permute-done.21.other_ref = f32[32,512]{1,0:T(8,128)S(1)} collective-permute-done((f32[32,512]{1,0:T(8,128)S(1)}, f32[32,512]{1,0:T(8,128)S(1)}, u32[]{:S(2)}, u32[]{:S(2)}) %collective-permute-start.21) | collective-permute-done | bytes 65568 | tf_op jit(solution)/shard_map/ppermute | solution.py:625
  46.5 0.7 %spread.1 = bf16[32,8,512]{2,1,0:T(8,128)(2,1)} custom-call(f32[32,512]{1,0:T(8,128)S(1)} %get-tuple-element.37.kept_ref, f32[32,512]{1,0:T(8,128)S(1)} %collective-permute-done.21.other_ref), custom_call_target="tpu_custom_call" | custom-call | tf_op jit(solution)/shard_map/spread/pallas_call | solution.py:633
  47.2 2.6 %all-to-all-start.1 = ((bf16[32,8,512]{2,1,0:T(8,128)(2,1)}), bf16[32,8,512]{2,1,0:T(8,128)(2,1)S(1)}, u32[]{:S(2)}, u32[]{:S(2)}) async-start(bf16[32,8,512]{2,1,0:T(8,128)(2,1)} %spread.1), calls=%async_computation.1 | async-start | bytes 524288 | tf_op jit(solution)/shard_map/all_to_all | solution.py:639
  49.8 2.6 %collective-permute-start.19 = (f32[48,128]{1,0:T(8,128)S(1)}, f32[48,128]{1,0:T(8,128)S(1)}, u32[]{:S(2)}, u32[]{:S(2)}) collective-permute-start(f32[48,128]{1,0:T(8,128)S(1)} %get-tuple-element.39.refs_0_), channel_id=1, source_target_pairs={{0,24},{4,28},{8,16},{12,20},{16,8},{20,12},{24,0},{28,4},{1,25},{... | collective-permute-start | bytes 73736 | tf_op jit(solution)/shard_map/ppermute | solution.py:452
  52.4 0.5 collective-permute-start.17
  52.9 0.4 collective-permute-start.15
  53.3 1.6 %collective-permute-done.19.refs_6_ = f32[48,128]{1,0:T(8,128)S(1)} collective-permute-done((f32[48,128]{1,0:T(8,128)S(1)}, f32[48,128]{1,0:T(8,128)S(1)}, u32[]{:S(2)}, u32[]{:S(2)}) %collective-permute-start.19) | collective-permute-done | bytes 24608 | tf_op jit(solution)/shard_map/ppermute | solution.py:452
  55.0 1.6 %collective-permute-done.17.refs_4_ = f32[48,128]{1,0:T(8,128)S(1)} collective-permute-done((f32[48,128]{1,0:T(8,128)S(1)}, f32[48,128]{1,0:T(8,128)S(1)}, u32[]{:S(2)}, u32[]{:S(2)}) %collective-permute-start.17) | collective-permute-done | bytes 24608 | tf_op jit(solution)/shard_map/ppermute | solution.py:452
  56.5 0.3 collective-permute-done.15.refs_2_
  56.9 0.2 collective-permute-start.16
  57.1 0.7 %collective-permute-done.18.refs_5_ = f32[48,128]{1,0:T(8,128)S(1)} collective-permute-done((f32[48,128]{1,0:T(8,128)S(1)}, f32[48,128]{1,0:T(8,128)S(1)}, u32[]{:S(2)}, u32[]{:S(2)}) %collective-permute-start.18) | collective-permute-done | bytes 24608 | tf_op jit(solution)/shard_map/ppermute | solution.py:452
  57.7 0.3 collective-permute-done.16.refs_3_
  58.1 0.4 home.1
  58.4 1.5 %all-to-all-done.1 = bf16[32,8,512]{2,1,0:T(8,128)(2,1)S(1)} async-done(((bf16[32,8,512]{2,1,0:T(8,128)(2,1)}), bf16[32,8,512]{2,1,0:T(8,128)(2,1)S(1)}, u32[]{:S(2)}, u32[]{:S(2)}) %all-to-all-start.1) | async-done | bytes 262176 | tf_op jit(solution)/shard_map/all_to_all | solution.py:639
  60.0 0.9 %final.1 = bf16[12,4,1024]{2,1,0:T(4,128)(2,1)} custom-call(f32[48,128]{1,0:T(8,128)S(1)} %get-tuple-element.49.gates_ref, bf16[8,4,8,512]{3,2,1,0:T(8,128)(2,1)S(1)} %bitcast.5, f32[48,1024]{1,0:T(8,128)S(1)} %get-tuple-element.50.residual_ref), custom_call_target="tpu_custom_call" | custom-call | tf_op jit(solution)/shard_map/final/pallas_call | solution.py:656
  (21 shorter events, 0.1 us)
Async XLA Ops:
  0.0 11.4 %copy-start = (bf16[2,12,512,1024]{3,2,1,0:T(8,128)(2,1)S(1)}, bf16[2,12,512,1024]{3,2,1,0:T(8,128)(2,1)}, u32[]{:S(2)}) copy-start(bf16[2,12,512,1024]{3,2,1,0:T(8,128)(2,1)} %refs_9_.1) | copy-start | bytes 75497472
  1.8 6.6 %collective-permute-start.5 = (bf16[48,384]{1,0:T(8,128)(2,1)S(1)}, bf16[48,384]{1,0:T(8,128)(2,1)S(1)}, u32[]{:S(2)}, u32[]{:S(2)}) collective-permute-start(bf16[48,384]{1,0:T(8,128)(2,1)S(1)} %qkv.1.sent_ref), channel_id=1, source_target_pairs={{0,24},{4,28},{8,16},{12,20},{16,8},{20,12},{24,0},{28,4},{1,25},{... | collective-permute-start | bytes 110600 | tf_op jit(solution)/shard_map/ppermute | solution.py:452
  5.7 4.0 %collective-permute-start.3 = (bf16[48,384]{1,0:T(8,128)(2,1)S(1)}, bf16[48,384]{1,0:T(8,128)(2,1)S(1)}, u32[]{:S(2)}, u32[]{:S(2)}) collective-permute-start(bf16[48,384]{1,0:T(8,128)(2,1)S(1)} %qkv.1.sent_ref), channel_id=1, source_target_pairs={{0,16},{4,20},{8,24},{12,28},{16,0},{20,4},{24,8},{28,12},{1,17},{... | collective-permute-start | bytes 110600 | tf_op jit(solution)/shard_map/ppermute | solution.py:452
  6.3 4.0 %collective-permute-start.1 = (bf16[48,384]{1,0:T(8,128)(2,1)S(1)}, bf16[48,384]{1,0:T(8,128)(2,1)S(1)}, u32[]{:S(2)}, u32[]{:S(2)}) collective-permute-start(bf16[48,384]{1,0:T(8,128)(2,1)S(1)} %qkv.1.sent_ref), channel_id=1, source_target_pairs={{0,8},{4,12},{8,0},{12,4},{16,24},{20,28},{24,16},{28,20},{1,9},{5... | collective-permute-start | bytes 110600 | tf_op jit(solution)/shard_map/ppermute | solution.py:452
  8.3 1.9 %collective-permute-start = (bf16[48,384]{1,0:T(8,128)(2,1)S(1)}, bf16[48,384]{1,0:T(8,128)(2,1)S(1)}, u32[]{:S(2)}, u32[]{:S(2)}) collective-permute-start(bf16[48,384]{1,0:T(8,128)(2,1)S(1)} %get-tuple-element.28.refs_0_), channel_id=1, source_target_pairs={{0,4},{4,0},{8,12},{12,8},{16,20},{20,16},{24,28},{28,24},{1,5},{5... | collective-permute-start | bytes 110600 | tf_op jit(solution)/shard_map/ppermute | solution.py:452
  8.4 1.9 %collective-permute-start.6 = (bf16[48,384]{1,0:T(8,128)(2,1)S(1)}, bf16[48,384]{1,0:T(8,128)(2,1)S(1)}, u32[]{:S(2)}, u32[]{:S(2)}) collective-permute-start(bf16[48,384]{1,0:T(8,128)(2,1)S(1)} %collective-permute-done.5.refs_6_), channel_id=1, source_target_pairs={{0,4},{4,0},{8,12},{12,8},{16,20},{20,16},{24,28},{28,24},{1,5},{5... | collective-permute-start | bytes 110600 | tf_op jit(solution)/shard_map/ppermute | solution.py:452
  9.7 1.2 %collective-permute-start.4 = (bf16[48,384]{1,0:T(8,128)(2,1)S(1)}, bf16[48,384]{1,0:T(8,128)(2,1)S(1)}, u32[]{:S(2)}, u32[]{:S(2)}) collective-permute-start(bf16[48,384]{1,0:T(8,128)(2,1)S(1)} %collective-permute-done.3.refs_4_), channel_id=1, source_target_pairs={{0,4},{4,0},{8,12},{12,8},{16,20},{20,16},{24,28},{28,24},{1,5},{5... | collective-permute-start | bytes 110600 | tf_op jit(solution)/shard_map/ppermute | solution.py:452
  10.2 1.2 %collective-permute-start.2 = (bf16[48,384]{1,0:T(8,128)(2,1)S(1)}, bf16[48,384]{1,0:T(8,128)(2,1)S(1)}, u32[]{:S(2)}, u32[]{:S(2)}) collective-permute-start(bf16[48,384]{1,0:T(8,128)(2,1)S(1)} %collective-permute-done.1.refs_2_), channel_id=1, source_target_pairs={{0,4},{4,0},{8,12},{12,8},{16,20},{20,16},{24,28},{28,24},{1,5},{5... | collective-permute-start | bytes 110600 | tf_op jit(solution)/shard_map/ppermute | solution.py:452
  16.8 9.0 %copy-start.3 = (bf16[2,12,4,1024]{3,2,1,0:T(4,128)(2,1)S(1)}, bf16[2,12,4,1024]{3,2,1,0:T(4,128)(2,1)}, u32[]{:S(2)}) copy-start(bf16[2,12,4,1024]{3,2,1,0:T(4,128)(2,1)} %refs_8_.1) | copy-start | bytes 589828
  16.8 10.0 %copy-start.1 = (bf16[12,4,1024]{2,1,0:T(4,128)(2,1)S(1)}, bf16[12,4,1024]{2,1,0:T(4,128)(2,1)}, u32[]{:S(2)}) copy-start(bf16[12,4,1024]{2,1,0:T(4,128)(2,1)} %refs_11_.1) | copy-start | bytes 294916
  16.8 10.0 %copy-start.2 = (bf16[128,1024]{1,0:T(8,128)(2,1)S(1)}, bf16[128,1024]{1,0:T(8,128)(2,1)}, u32[]{:S(2)}) copy-start(bf16[128,1024]{1,0:T(8,128)(2,1)} %refs_10_.1) | copy-start | bytes 786436
  16.8 24.7 %copy-start.5 = (f32[1024]{0:T(1024)S(1)}, f32[1024]{0:T(1024)}, u32[]{:S(2)}) copy-start(f32[1024]{0:T(1024)} %param.20) | copy-start | bytes 12292
  16.8 6.6 %collective-permute-start.12 = (bf16[48,1152]{1,0:T(8,128)(2,1)S(1)}, bf16[48,1152]{1,0:T(8,128)(2,1)S(1)}, u32[]{:S(2)}, u32[]{:S(2)}) collective-permute-start(bf16[48,1152]{1,0:T(8,128)(2,1)S(1)} %attention.1.sent_ref), channel_id=1, source_target_pairs={{0,24},{4,28},{8,16},{12,20},{16,8},{20,12},{24,0},{28,4},{1,25},{... | collective-permute-start | bytes 331784 | tf_op jit(solution)/shard_map/ppermute | solution.py:452
  18.5 6.7 %collective-permute-start.10 = (bf16[48,1152]{1,0:T(8,128)(2,1)S(1)}, bf16[48,1152]{1,0:T(8,128)(2,1)S(1)}, u32[]{:S(2)}, u32[]{:S(2)}) collective-permute-start(bf16[48,1152]{1,0:T(8,128)(2,1)S(1)} %attention.1.sent_ref), channel_id=1, source_target_pairs={{0,16},{4,20},{8,24},{12,28},{16,0},{20,4},{24,8},{28,12},{1,17},{... | collective-permute-start | bytes 331784 | tf_op jit(solution)/shard_map/ppermute | solution.py:452
  19.1 6.3 %collective-permute-start.8 = (bf16[48,1152]{1,0:T(8,128)(2,1)S(1)}, bf16[48,1152]{1,0:T(8,128)(2,1)S(1)}, u32[]{:S(2)}, u32[]{:S(2)}) collective-permute-start(bf16[48,1152]{1,0:T(8,128)(2,1)S(1)} %attention.1.sent_ref), channel_id=1, source_target_pairs={{0,8},{4,12},{8,0},{12,4},{16,24},{20,28},{24,16},{28,20},{1,9},{5... | collective-permute-start | bytes 331784 | tf_op jit(solution)/shard_map/ppermute | solution.py:452
  21.9 4.8 %collective-permute-start.7 = (bf16[48,1152]{1,0:T(8,128)(2,1)S(1)}, bf16[48,1152]{1,0:T(8,128)(2,1)S(1)}, u32[]{:S(2)}, u32[]{:S(2)}) collective-permute-start(bf16[48,1152]{1,0:T(8,128)(2,1)S(1)} %get-tuple-element.30.refs_0_), channel_id=1, source_target_pairs={{0,4},{4,0},{8,12},{12,8},{16,20},{20,16},{24,28},{28,24},{1,5},{5... | collective-permute-start | bytes 331784 | tf_op jit(solution)/shard_map/ppermute | solution.py:452
  23.4 3.3 %collective-permute-start.13 = (bf16[48,1152]{1,0:T(8,128)(2,1)S(1)}, bf16[48,1152]{1,0:T(8,128)(2,1)S(1)}, u32[]{:S(2)}, u32[]{:S(2)}) collective-permute-start(bf16[48,1152]{1,0:T(8,128)(2,1)S(1)} %collective-permute-done.12.refs_6_), channel_id=1, source_target_pairs={{0,4},{4,0},{8,12},{12,8},{16,20},{20,16},{24,28},{28,24},{1,5},{5... | collective-permute-start | bytes 331784 | tf_op jit(solution)/shard_map/ppermute | solution.py:452
  25.3 1.5 %collective-permute-start.11 = (bf16[48,1152]{1,0:T(8,128)(2,1)S(1)}, bf16[48,1152]{1,0:T(8,128)(2,1)S(1)}, u32[]{:S(2)}, u32[]{:S(2)}) collective-permute-start(bf16[48,1152]{1,0:T(8,128)(2,1)S(1)} %collective-permute-done.10.refs_4_), channel_id=1, source_target_pairs={{0,4},{4,0},{8,12},{12,8},{16,20},{20,16},{24,28},{28,24},{1,5},{5... | collective-permute-start | bytes 331784 | tf_op jit(solution)/shard_map/ppermute | solution.py:452
  25.4 1.4 %collective-permute-start.9 = (bf16[48,1152]{1,0:T(8,128)(2,1)S(1)}, bf16[48,1152]{1,0:T(8,128)(2,1)S(1)}, u32[]{:S(2)}, u32[]{:S(2)}) collective-permute-start(bf16[48,1152]{1,0:T(8,128)(2,1)S(1)} %collective-permute-done.8.refs_2_), channel_id=1, source_target_pairs={{0,4},{4,0},{8,12},{12,8},{16,20},{20,16},{24,28},{28,24},{1,5},{5... | collective-permute-start | bytes 331784 | tf_op jit(solution)/shard_map/ppermute | solution.py:452
  41.5 16.6 %copy-start.4 = (bf16[1024,16]{0,1:T(8,128)(2,1)S(1)}, bf16[1024,16]{0,1:T(8,128)(2,1)}, u32[]{:S(2)}) copy-start(bf16[1024,16]{0,1:T(8,128)(2,1)} %param.21) | copy-start | bytes 98308
  45.2 1.3 %collective-permute-start.21 = (f32[32,512]{1,0:T(8,128)S(1)}, f32[32,512]{1,0:T(8,128)S(1)}, u32[]{:S(2)}, u32[]{:S(2)}) collective-permute-start(f32[32,512]{1,0:T(8,128)S(1)} %get-tuple-element.38), channel_id=1, source_target_pairs={{0,4},{4,0},{8,12},{12,8},{16,20},{20,16},{24,28},{28,24},{1,5},{5... | collective-permute-start | bytes 196616 | tf_op jit(solution)/shard_map/ppermute | solution.py:625
  47.2 12.8 %all-to-all-start.1 = ((bf16[32,8,512]{2,1,0:T(8,128)(2,1)}), bf16[32,8,512]{2,1,0:T(8,128)(2,1)S(1)}, u32[]{:S(2)}, u32[]{:S(2)}) async-start(bf16[32,8,512]{2,1,0:T(8,128)(2,1)} %spread.1), calls=%async_computation.1 | async-start | bytes 524288 | tf_op jit(solution)/shard_map/all_to_all | solution.py:639
  49.8 5.2 %collective-permute-start.19 = (f32[48,128]{1,0:T(8,128)S(1)}, f32[48,128]{1,0:T(8,128)S(1)}, u32[]{:S(2)}, u32[]{:S(2)}) collective-permute-start(f32[48,128]{1,0:T(8,128)S(1)} %get-tuple-element.39.refs_0_), channel_id=1, source_target_pairs={{0,24},{4,28},{8,16},{12,20},{16,8},{20,12},{24,0},{28,4},{1,25},{... | collective-permute-start | bytes 73736 | tf_op jit(solution)/shard_map/ppermute | solution.py:452
  52.4 4.1 %collective-permute-start.17 = (f32[48,128]{1,0:T(8,128)S(1)}, f32[48,128]{1,0:T(8,128)S(1)}, u32[]{:S(2)}, u32[]{:S(2)}) collective-permute-start(f32[48,128]{1,0:T(8,128)S(1)} %get-tuple-element.39.refs_0_), channel_id=1, source_target_pairs={{0,16},{4,20},{8,24},{12,28},{16,0},{20,4},{24,8},{28,12},{1,17},{... | collective-permute-start | bytes 73736 | tf_op jit(solution)/shard_map/ppermute | solution.py:452
  52.9 3.9 %collective-permute-start.15 = (f32[48,128]{1,0:T(8,128)S(1)}, f32[48,128]{1,0:T(8,128)S(1)}, u32[]{:S(2)}, u32[]{:S(2)}) collective-permute-start(f32[48,128]{1,0:T(8,128)S(1)} %get-tuple-element.39.refs_0_), channel_id=1, source_target_pairs={{0,8},{4,12},{8,0},{12,4},{16,24},{20,28},{24,16},{28,20},{1,9},{5... | collective-permute-start | bytes 73736 | tf_op jit(solution)/shard_map/ppermute | solution.py:452
  53.3 3.7 %collective-permute-start.14 = (f32[48,128]{1,0:T(8,128)S(1)}, f32[48,128]{1,0:T(8,128)S(1)}, u32[]{:S(2)}, u32[]{:S(2)}) collective-permute-start(f32[48,128]{1,0:T(8,128)S(1)} %get-tuple-element.39.refs_0_), channel_id=1, source_target_pairs={{0,4},{4,0},{8,12},{12,8},{16,20},{20,16},{24,28},{28,24},{1,5},{5... | collective-permute-start | bytes 73736 | tf_op jit(solution)/shard_map/ppermute | solution.py:452
  55.0 2.1 %collective-permute-start.20 = (f32[48,128]{1,0:T(8,128)S(1)}, f32[48,128]{1,0:T(8,128)S(1)}, u32[]{:S(2)}, u32[]{:S(2)}) collective-permute-start(f32[48,128]{1,0:T(8,128)S(1)} %collective-permute-done.19.refs_6_), channel_id=1, source_target_pairs={{0,4},{4,0},{8,12},{12,8},{16,20},{20,16},{24,28},{28,24},{1,5},{5... | collective-permute-start | bytes 73736 | tf_op jit(solution)/shard_map/ppermute | solution.py:452
  56.5 1.2 %collective-permute-start.18 = (f32[48,128]{1,0:T(8,128)S(1)}, f32[48,128]{1,0:T(8,128)S(1)}, u32[]{:S(2)}, u32[]{:S(2)}) collective-permute-start(f32[48,128]{1,0:T(8,128)S(1)} %collective-permute-done.17.refs_4_), channel_id=1, source_target_pairs={{0,4},{4,0},{8,12},{12,8},{16,20},{20,16},{24,28},{28,24},{1,5},{5... | collective-permute-start | bytes 73736 | tf_op jit(solution)/shard_map/ppermute | solution.py:452
  56.9 1.2 %collective-permute-start.16 = (f32[48,128]{1,0:T(8,128)S(1)}, f32[48,128]{1,0:T(8,128)S(1)}, u32[]{:S(2)}, u32[]{:S(2)}) collective-permute-start(f32[48,128]{1,0:T(8,128)S(1)} %collective-permute-done.15.refs_2_), channel_id=1, source_target_pairs={{0,4},{4,0},{8,12},{12,8},{16,20},{20,16},{24,28},{28,24},{1,5},{5... | collective-permute-start | bytes 73736 | tf_op jit(solution)/shard_map/ppermute | solution.py:452

commit v8 on v7

--- a/solution.py
+++ b/solution.py
@@ -19,7 +19,9 @@
 FIRST_KEYS = 2
 SECOND_KEYS = 8
 SECOND_VALUES = 3
-PIECE = 512
+HELD = 768
+PIECE = 320
+AHEAD = 10
 BLOCK = 256
 BLOCK_HEADS = BLOCK // HD
 
@@ -55,6 +57,12 @@
     return parts
 
 
+def exact_dot(values, table):
+    high, low = split(values, 2)
+    both = dot(jnp.concatenate([high, low], axis=0), table)
+    return both[: values.shape[0]] + both[values.shape[0] :]
+
+
 def rms_rows(widened, gain_row):
     inverse = lax.rsqrt(jnp.mean(widened * widened, axis=-1, keepdims=True) + EPSILON)
     return (widened * inverse * gain_row).astype(jnp.bfloat16)
@@ -66,8 +74,12 @@
         rows_ref[r * steps : (r + 1) * steps, :] = source_ref[r].astype(rows_ref.dtype)
 
 
+def each(sems):
+    return [sems.at[i] for i in range(sems.shape[0])]
+
+
 def started(pairs, sems):
-    copies = [pltpu.make_async_copy(*pair, sems.at[i]) for i, pair in enumerate(pairs)]
+    copies = [pltpu.make_async_copy(*pair, sem) for pair, sem in zip(pairs, sems)]
     for copy in copies:
         copy.start()
     return copies
@@ -126,12 +138,13 @@
             (gain_ref, gain_buf),
             (weight_ref, weight_buf),
         ),
-        sems,
+        each(sems),
     )
-    for copy in copies:
+    for copy in copies[:2]:
         copy.wait()
     copy_rows(token_buf, rows_ref)
     normed = rms_rows(rows_ref[...], gain_buf[...])
+    copies[2].wait()
     out_ref[...] = dot(normed, weight_buf[...], ROWS_BY_ROWS).astype(jnp.bfloat16)
 
 
@@ -152,14 +165,18 @@
     lengths_ref,
     ids_ref,
     order_ref,
+    tokens_ref,
     held_ref,
     spans_ref,
     select_ref,
     chosen_ref,
     turned_ref,
+    columns_ref,
     numbers_ref,
     ids_buf,
     order_buf,
+    tokens_buf,
+    rows_ref,
     sems,
 ):
     copies = started(
@@ -167,8 +184,9 @@
             (ids_ref, ids_buf),
             (order_ref, order_buf),
             (lengths_ref, numbers_ref),
+            (tokens_ref, tokens_buf),
         ),
-        sems,
+        each(sems),
     )
     held_ref[...] = sent_ref[...]
     for copy in copies:
@@ -176,10 +194,16 @@
     turned_ref[...] = route(ids_buf, order_buf, select_ref, chosen_ref)
     for r in range(spans_ref.shape[0]):
         spans_ref[r : r + 1, :] = jnp.full((1, LANES), numbers_ref[r], jnp.int32)
+    copy_rows(tokens_buf, rows_ref)
+    width, share = rows_ref.shape[1], columns_ref.shape[1]
+    feature = lax.broadcasted_iota(jnp.int32, (width, share), 0)
+    column = lax.broadcasted_iota(jnp.int32, (width, share), 1)
+    own = (feature == column + lax.axis_index("seq") * share).astype(jnp.bfloat16)
+    columns_ref[...] = dot(rows_ref[...].astype(jnp.bfloat16), own)
 
 
 def fetch_expert_kernel(sent_ref, in_ref, held_ref, piece_ref, sems):
-    copies = started([(in_ref.at[p, 0, pl.ds(0, piece_ref.shape[1])], piece_ref.at[p]) for p in range(2)], sems)
+    copies = started([(in_ref.at[p, 0, pl.ds(0, piece_ref.shape[1])], piece_ref.at[p]) for p in range(2)], each(sems))
     held_ref[...] = sent_ref[...]
     for copy in copies:
         copy.wait()
@@ -237,18 +261,19 @@
             mixed = dot(weight[own], values[:, c]) * own_head[:, c]
             mixed = sum(mixed[i : i + pair] for i in range(0, block_rows, pair))
             outs.append(mixed[:steps] + mixed[steps:])
-        stats = jnp.zeros((HEADS * steps, LANES), jnp.float32)
-        parts = split(peak.reshape(HEADS * steps, 1), PIECES)
-        parts = parts + split(total.reshape(HEADS * steps, 1), PIECES)
-        for i, part in enumerate(parts):
-            stats = jnp.where(
-                stat_lane == stat_head + i * HEADS, part.astype(jnp.float32), stats
-            )
+        stats = jnp.where(stat_lane == stat_head, peak.reshape(HEADS * steps, 1), 0.0)
+        stats = jnp.where(stat_lane == stat_head + HEADS, total.reshape(HEADS * steps, 1), stats)
         stats = jnp.sum(stats.reshape(tiles, pair, LANES), axis=0)
         outs.append(stats[:steps] + stats[steps:])
         flat_ref[r * steps : (r + 1) * steps, :] = jnp.concatenate(outs, axis=1)
         scores = following
-    out_ref[...] = flat_ref[...].astype(jnp.bfloat16)
+    out_ref[:, :width] = flat_ref[:, :width].astype(jnp.bfloat16)
+    parts = []
+    for first in (0, HEADS):
+        parts += split(flat_ref[:, width + first : width + first + HEADS], PIECES)
+    blank = jnp.zeros((rows, LANES - 2 * PIECES * HEADS), jnp.float32)
+    parts = [part.astype(jnp.float32) for part in parts] + [blank]
+    out_ref[:, width:] = jnp.concatenate(parts, axis=1).astype(jnp.bfloat16)
 
 
 def extra_kernel(*refs):
@@ -308,12 +333,11 @@
 
 
 def project_kernel(*refs):
-    *part_refs, extra_ref, extra_stats_ref, weight_ref, tokens_ref, turned_ref = refs[:-4]
-    out_ref, residual_ref, ordered_ref, rows_ref = refs[-4:]
-    devices, rows, padded = ordered_ref.shape
-    width = padded - LANES
-    in_order(part_refs, ordered_ref)
-    stats = [ordered_ref[d][:, width:].astype(jnp.float32) for d in range(devices)]
+    *part_refs, extra_ref, extra_stats_ref, weight_ref, columns_ref, turned_ref = refs[:-2]
+    out_ref, residual_ref = refs[-2:]
+    devices = len(part_refs)
+    rows, width = extra_ref.shape
+    stats = [part_ref[:, width:].astype(jnp.float32) for part_ref in part_refs]
 
     def joined(stat, first):
         return sum(
@@ -331,27 +355,21 @@
     expand = (head_of_row == head_of_col).astype(jnp.bfloat16)
 
     spread = jnp.concatenate([factor * inverse for factor in factors], axis=0)
-    spread = sum(dot(part, expand) for part in split(spread, 2))
+    spread = exact_dot(spread, expand)
     attended = spread[devices * rows :] * extra_ref[...]
     for d in range(devices):
         share = spread[d * rows : (d + 1) * rows]
-        attended = attended + share * ordered_ref[d][:, :width].astype(jnp.float32)
+        attended = attended + share * part_refs[d][:, :width].astype(jnp.float32)
     projected = dot(attended.astype(jnp.bfloat16), weight_ref[...], ROWS_BY_ROWS).astype(jnp.bfloat16)
-    copy_rows(tokens_ref, rows_ref)
-    share = weight_ref.shape[0]
-    feature = lax.broadcasted_iota(jnp.int32, (width, share), 0)
-    column = lax.broadcasted_iota(jnp.int32, (width, share), 1)
-    own = (feature == column + lax.axis_index("seq") * share).astype(jnp.bfloat16)
-    residual = dot(rows_ref[...].astype(jnp.bfloat16), own) + projected.astype(jnp.float32)
+    residual = columns_ref[...] + projected.astype(jnp.float32)
     residual_ref[...] = residual
-    turned = turned_ref[...].astype(jnp.bfloat16)
-    table = sum(dot(turned, part) for part in split(residual, PIECES))
+    table = dot(turned_ref[...].astype(jnp.bfloat16), residual.astype(jnp.bfloat16))
     groups = lax.axis_size("exp")
     local_experts = EXPERTS // groups
     for s in range(devices):
         for x in range(groups):
             row = (x * local_experts + s // (devices // local_experts)) * CAP
-            out_ref[s * groups + x] = table[row : row + CAP]
+            out_ref[s * groups + x] = table[row : row + CAP].astype(jnp.bfloat16)
 
 
 def home_kernel(devices, *refs):
@@ -375,19 +393,39 @@
     hidden_units, width = down_buf.shape
     held = piece_ref.shape[1]
     pieces = [(at, min(PIECE, hidden_units - at)) for at in range(held, hidden_units, PIECE)]
-    pairs = []
+    downs = [(0, held)] + pieces
+    stages = []
     for at, count in pieces:
-        for p in range(2):
-            pairs.append(
+        stages.append(
+            [
                 (in_ref.at[p, 0, pl.ds(at, count)], in_buf.at[p, pl.ds(at - held, count)])
-            )
-    copies = started(pairs + [(down_ref.at[0], down_buf)], sems)
+                for p in range(2)
+            ]
+        )
+    for at, count in downs:
+        stages.append([(down_ref.at[0, pl.ds(at, count)], down_buf.at[pl.ds(at, count)])])
+    flying = []
+
+    def start_next():
+        if len(flying) < len(stages):
+            first = sum(len(stage) for stage in stages[: len(flying)])
+            flying.append(started(stages[len(flying)], [sems.at[first + i] for i in range(len(stages[len(flying)]))]))
+
+    def wait_for(stage):
+        for copy in flying[stage]:
+            copy.wait()
+        start_next()
+
+    for _ in range(AHEAD):
+        start_next()
     devices = lax.axis_size("seq")
     groups = lax.axis_size("exp")
     columns = []
     for s in range(devices):
         columns.append(
-            jnp.concatenate([received_ref[s * groups + g] for g in range(groups)], axis=0)
+            jnp.concatenate(
+                [received_ref[s * groups + g].astype(jnp.float32) for g in range(groups)], axis=0
+            )
         )
     rows = rms_rows(jnp.concatenate(columns, axis=1), gain_ref[...])
 
@@ -398,12 +436,13 @@
 
     hidden = [layer(piece_ref[0], piece_ref[1])]
     for i, (at, count) in enumerate(pieces):
-        copies[2 * i].wait()
-        copies[2 * i + 1].wait()
+        wait_for(i)
         own = slice(at - held, at - held + count)
         hidden.append(layer(in_buf[0, own], in_buf[1, own]))
-    copies[-1].wait()
-    outputs = dot(jnp.concatenate(hidden, axis=1), down_buf[...])
+    outputs = jnp.zeros((groups * CAP, width), jnp.float32)
+    for i, (at, count) in enumerate(downs):
+        wait_for(len(pieces) + i)
+        outputs = outputs + dot(hidden[i], down_buf[at : at + count])
     half = width // 2
     odd = lax.axis_index("seq") % 2 == 1
     keep_ref[...] = jnp.where(odd, outputs[:, half:], outputs[:, :half])
@@ -439,7 +478,7 @@
             row = (x * local_experts + s // sharers) * slots
             table_ref[row : row + slots, first : first + part] = returned_ref[s, x].astype(jnp.float32)
     table = table_ref[...].astype(jnp.bfloat16)
-    moe = sum(dot(part, table) for part in split(gates_ref[...], 2))
+    moe = exact_dot(gates_ref[...], table)
     total = residual_ref[...] + moe
     for r in range(requests):
         out_ref[r] = total[r * steps : (r + 1) * steps].astype(jnp.bfloat16)
@@ -513,19 +552,22 @@
     def routing(values):
         held, *outputs = pl.pallas_call(
             routing_kernel,
-            in_specs=[vmem] + [hbm] * 3,
+            in_specs=[vmem] + [hbm] * 4,
             out_shape=(
                 shape(values.shape, bf16),
                 shape((requests, LANES), jnp.int32),
                 shape((TOPK, rows, slots), f32),
                 shape((TOPK, rows, LANES), f32),
                 shape((slots, rows), f32),
+                shape((rows, w_out.shape[0]), f32),
             ),
             scratch_shapes=[
                 pltpu.SMEM((requests,), jnp.int32),
                 pltpu.VMEM((steps, TOPK, requests), jnp.int32),
                 pltpu.VMEM(slot_order.shape, jnp.int32),
-                pltpu.SemaphoreType.DMA((3,)),
+                pltpu.VMEM(tokens.shape, bf16),
+                pltpu.VMEM((rows, width), f32),
+                pltpu.SemaphoreType.DMA((4,)),
             ],
             compiler_params=params(8),
             name="routing",
@@ -534,12 +576,13 @@
             in_hbm(lengths),
             in_hbm(expert_ids.transpose(1, 2, 0)),
             in_hbm(slot_order),
+            in_hbm(tokens),
         )
         fetched.extend(outputs)
         return held
 
     mixed = gather_seq(local_mix, routing)
-    spans, select, chosen, turned = fetched
+    spans, select, chosen, turned, token_columns = fetched
 
     padded = width + LANES
     part = pl.pallas_call(
@@ -555,7 +598,7 @@
         name="attention",
     )(*mixed, spans, window_cache)
     hidden_units = expert_down.shape[1]
-    held_units = min(PIECE, hidden_units)
+    held_units = min(HELD, hidden_units)
     late_units = max(hidden_units - held_units, 16)
 
     def fetch_expert(values):
@@ -590,16 +633,12 @@
     outgoing, residual_columns = pl.pallas_call(
         project_kernel,
         out_shape=(
-            shape((seq_count * groups, CAP, w_out.shape[0]), f32),
+            shape((seq_count * groups, CAP, w_out.shape[0]), bf16),
             shape((rows, w_out.shape[0]), f32),
         ),
-        scratch_shapes=[
-            pltpu.VMEM((seq_count, rows, padded), bf16),
-            pltpu.VMEM((rows, width), f32),
-        ],
         compiler_params=params(16),
         name="project",
-    )(*parts, extra, extra_stats, w_out, tokens, turned)
+    )(*parts, extra, extra_stats, w_out, token_columns, turned)
     received = lax.all_to_all(outgoing, ("seq", "exp"), split_axis=0, concat_axis=0, tiled=True)
     columns = gather_seq(residual_columns)
 
@@ -614,7 +653,7 @@
         scratch_shapes=[
             pltpu.VMEM((2, late_units, width), bf16),
             pltpu.VMEM((hidden_units, width), bf16),
-            pltpu.SemaphoreType.DMA((2 * pl.cdiv(hidden_units, PIECE) + 1,)),
+            pltpu.SemaphoreType.DMA((3 * pl.cdiv(late_units, PIECE) + 1,)),
         ],
         compiler_params=params(20),
         name="expert",

time: 61.1 us -> 59.2 us (0.969)
  blocking collectives: 13.4 us -> 12.5 us
    all_to_all x1, blocking collectives: 13.4 us -> 12.5 us  [body(): lax.all_to_all(outgoing, ('seq', 'exp'), split_axis=0, concat_axis=0, til...]
  transfers between devices with their start and end apart: 23 -> 23, of which waited for: 14 -> 14; matrix products, arithmetic and copies ran while one was open for 0% -> 0% of each run, Pallas kernels for 8% -> 9%
where the time goes in v8:
time: 59.2 us; the launch traced here: 58.9 us
  Pallas kernels  18 us (30%)
  starting transfers between devices  15.6 us (26%)
  waiting for transfers between devices  12.7 us (21%)
  blocking collectives  12.5 us (21%)
    ppermute x21, starting transfers between devices, exchange(): return lax.ppermute(value, 'seq', [(i, i ^ bits) for i in range(count)])  13 us
    all_to_all x1, blocking collectives, body(): lax.all_to_all(outgoing, ('seq', 'exp'), split_axis=0, concat_axis=0, til...  12.5 us
    ppermute x21, waiting for transfers between devices, exchange(): return lax.ppermute(value, 'seq', [(i, i ^ bits) for i in range(count)])  9.88 us
    pallas_call x1, Pallas kernels, body(): pl.pallas_call(attention_kernel, in_specs=[vmem] * (seq_count + 2), out_s...  5.22 us
    pallas_call x1, Pallas kernels, body(): pl.pallas_call(expert_kernel, in_specs=[vmem, vmem, vmem, hbm, hbm], out_...  3.07 us
    all_to_all x1, starting transfers between devices, body(): lax.all_to_all(outgoing, ('seq', 'exp'), split_axis=0, concat_axis=0, til...  2.58 us
    pallas_call x1, Pallas kernels, routing(): pl.pallas_call(routing_kernel, in_specs=[vmem] + [hbm] * 4, out_shape=(sh...  2.11 us
    pallas_call x1, Pallas kernels, fetch_expert(): pl.pallas_call(fetch_expert_kernel, in_specs=[vmem, hbm], out_shape=(shap...  1.9 us
  transfers between devices with their start and end apart: 23, of which 14 were waited for; matrix products, arithmetic and copies ran while one was open for 0% of the time, Pallas kernels for 9%

profile of v8, /device:TPU:0, one launch (start us, length us, event | category | flops | bytes accessed | tf_op | source)
XLA Modules:
  0.0 58.9 jit_solution(15314879755973288716)
XLA Ops:
  0.0 1.7 %qkv.1.sent_ref = bf16[48,384]{1,0:T(8,128)(2,1)S(1)} custom-call(bf16[12,4,1024]{2,1,0:T(4,128)(2,1)} %tokens_ref.3, f32[1,1024]{1,0:T(1,128)} %bitcast.9, bf16[384,1024]{1,0:T(8,128)(2,1)} %weight_ref.1, bf16[2,12,512,1024]{3,2,1,0:T(8,128)(2,1)} %refs_9_.1), custom_call_target="tpu_custom_call" | custom-call | tf_op jit(solution)/shard_map/qkv/pallas_call | solution.py:535
  1.7 4.0 %collective-permute-start.5 = (bf16[48,384]{1,0:T(8,128)(2,1)S(1)}, bf16[48,384]{1,0:T(8,128)(2,1)S(1)}, u32[]{:S(2)}, u32[]{:S(2)}) collective-permute-start(bf16[48,384]{1,0:T(8,128)(2,1)S(1)} %qkv.1.sent_ref), channel_id=1, source_target_pairs={{0,24},{4,28},{8,16},{12,20},{16,8},{20,12},{24,0},{28,4},{1,25},{... | collective-permute-start | bytes 110600 | tf_op jit(solution)/shard_map/ppermute | solution.py:491
  5.7 0.5 collective-permute-start.3
  6.2 0.1 collective-permute-start.1
  6.3 2.1 %routing.1 = (bf16[48,384]{1,0:T(8,128)(2,1)S(1)}, s32[12,128]{1,0:T(8,128)S(1)}, f32[2,48,128]{2,1,0:T(8,128)S(1)}, f32[2,48,128]{2,1,0:T(8,128)S(1)}, f32[128,48]{1,0:T(8,128)S(1)}, /*index=5*/f32[48,128]{1,0:T(8,128)S(1)}) custom-call(bf16[48,384]{1,0:T(8,128)(2,1)S(1)} %qkv.1.sent_ref, s32[12]{0:T(128)} %lengths_ref.1, s32[4,2,12]{2,1,0:T(2,128)} %bitcast.10, ...), custom_call_target="tpu_custom_call" | custom-call | tf_op jit(solution)/shard_map/routing/pallas_call | solution.py:553
  8.5 0.1 collective-permute-start
  8.6 0.5 collective-permute-start.6
  9.0 0.6 %collective-permute-done.3.refs_4_ = bf16[48,384]{1,0:T(8,128)(2,1)S(1)} collective-permute-done((bf16[48,384]{1,0:T(8,128)(2,1)S(1)}, bf16[48,384]{1,0:T(8,128)(2,1)S(1)}, u32[]{:S(2)}, u32[]{:S(2)}) %collective-permute-start.3) | collective-permute-done | bytes 36896 | tf_op jit(solution)/shard_map/ppermute | solution.py:491
  9.7 0.5 collective-permute-done.1.refs_2_
  10.2 0.0 collective-permute-start.2
  10.2 0.7 %collective-permute-done.4.refs_5_ = bf16[48,384]{1,0:T(8,128)(2,1)S(1)} collective-permute-done((bf16[48,384]{1,0:T(8,128)(2,1)S(1)}, bf16[48,384]{1,0:T(8,128)(2,1)S(1)}, u32[]{:S(2)}, u32[]{:S(2)}) %collective-permute-start.4) | collective-permute-done | bytes 36896 | tf_op jit(solution)/shard_map/ppermute | solution.py:491
  10.9 0.5 collective-permute-done.2.refs_3_
  11.4 5.2 %attention.1.sent_ref = bf16[48,1152]{1,0:T(8,128)(2,1)S(1)} custom-call(bf16[48,384]{1,0:T(8,128)(2,1)S(1)} %get-tuple-element.29.refs_0_, bf16[48,384]{1,0:T(8,128)(2,1)S(1)} %collective-permute-done.refs_1_, bf16[48,384]{1,0:T(8,128)(2,1)S(1)} %collective-permute-done.1.refs_2_, bf16[48,384]{1,0:T(8,128)(2,1)S(1)} %collective-permute-done.2.refs_3_, ...), custom_call_target="tpu_custom_call" | custom-call | tf_op jit(solution)/shard_map/attention/pallas_call | solution.py:588
  16.6 0.0 copy-start.2
  16.6 0.0 copy-start.1
  16.6 0.0 copy-start.4
  16.6 2.0 %collective-permute-start.12 = (bf16[48,1152]{1,0:T(8,128)(2,1)S(1)}, bf16[48,1152]{1,0:T(8,128)(2,1)S(1)}, u32[]{:S(2)}, u32[]{:S(2)}) collective-permute-start(bf16[48,1152]{1,0:T(8,128)(2,1)S(1)} %attention.1.sent_ref), channel_id=1, source_target_pairs={{0,24},{4,28},{8,16},{12,20},{16,8},{20,12},{24,0},{28,4},{1,25},{... | collective-permute-start | bytes 331784 | tf_op jit(solution)/shard_map/ppermute | solution.py:491
  18.6 0.5 collective-permute-start.10
  19.1 1.1 %collective-permute-start.8 = (bf16[48,1152]{1,0:T(8,128)(2,1)S(1)}, bf16[48,1152]{1,0:T(8,128)(2,1)S(1)}, u32[]{:S(2)}, u32[]{:S(2)}) collective-permute-start(bf16[48,1152]{1,0:T(8,128)(2,1)S(1)} %attention.1.sent_ref), channel_id=1, source_target_pairs={{0,8},{4,12},{8,0},{12,4},{16,24},{20,28},{24,16},{28,20},{1,9},{5... | collective-permute-start | bytes 331784 | tf_op jit(solution)/shard_map/ppermute | solution.py:491
  20.2 1.9 %fetch_expert.1 = (bf16[48,1152]{1,0:T(8,128)(2,1)S(1)}, bf16[2,768,1024]{2,1,0:T(8,128)(2,1)S(1)}) custom-call(bf16[48,1152]{1,0:T(8,128)(2,1)S(1)} %attention.1.sent_ref, bf16[2,1,1408,1024]{3,2,1,0:T(8,128)(2,1)} %in_ref.3), custom_call_target="tpu_custom_call" | custom-call | bytes 3145728 | tf_op jit(solution)/shard_map/fetch_expert/pallas_call | solution.py:605
  22.1 0.1 collective-permute-start.7
  22.2 0.8 %collective-permute-done.12.refs_6_ = bf16[48,1152]{1,0:T(8,128)(2,1)S(1)} collective-permute-done((bf16[48,1152]{1,0:T(8,128)(2,1)S(1)}, bf16[48,1152]{1,0:T(8,128)(2,1)S(1)}, u32[]{:S(2)}, u32[]{:S(2)}) %collective-permute-start.12) | collective-permute-done | bytes 110624 | tf_op jit(solution)/shard_map/ppermute | solution.py:491
  23.0 0.0 collective-permute-start.13
  23.0 2.1 %collective-permute-done.10.refs_4_ = bf16[48,1152]{1,0:T(8,128)(2,1)S(1)} collective-permute-done((bf16[48,1152]{1,0:T(8,128)(2,1)S(1)}, bf16[48,1152]{1,0:T(8,128)(2,1)S(1)}, u32[]{:S(2)}, u32[]{:S(2)}) %collective-permute-start.10) | collective-permute-done | bytes 110624 | tf_op jit(solution)/shard_map/ppermute | solution.py:491
  25.1 0.0 collective-permute-start.11
  25.1 0.1 collective-permute-done.8.refs_2_
  25.2 0.4 collective-permute-start.9
  25.6 0.9 %extra.1 = (f32[48,1024]{1,0:T(8,128)S(1)}, f32[48,128]{1,0:T(8,128)S(1)}) custom-call(bf16[48,384]{1,0:T(8,128)(2,1)S(1)} %get-tuple-element.29.refs_0_, bf16[48,384]{1,0:T(8,128)(2,1)S(1)} %collective-permute-done.refs_1_, bf16[48,384]{1,0:T(8,128)(2,1)S(1)} %collective-permute-done.1.refs_2_, bf16[48,384]{1,0:T(8,128)(2,1)S(1)} %collective-permute-done.2.refs_3_, ...), custom_call_target="tpu_custom_call" | custom-call | tf_op jit(solution)/shard_map/extra/pallas_call | solution.py:620
  26.6 0.0 collective-permute-done.9.refs_3_
  26.6 1.1 %project.1 = (bf16[32,8,128]{2,1,0:T(8,128)(2,1)S(1)}, f32[48,128]{1,0:T(8,128)S(1)}) custom-call(bf16[48,1152]{1,0:T(8,128)(2,1)S(1)} %get-tuple-element.31.refs_0_, bf16[48,1152]{1,0:T(8,128)(2,1)S(1)} %collective-permute-done.7.refs_1_, bf16[48,1152]{1,0:T(8,128)(2,1)S(1)} %collective-permute-done.8.refs_2_, ...), custom_call_target="tpu_custom_call" | custom-call | tf_op jit(solution)/shard_map/project/pallas_call | solution.py:633
  27.7 12.5 %all_to_all.10.received_ref = bf16[32,8,128]{2,1,0:T(8,128)(2,1)S(1)} all-to-all(bf16[32,8,128]{2,1,0:T(8,128)(2,1)S(1)} %get-tuple-element.37), channel_id=1, replica_groups=mesh['seq'=8,'exp'=4] {'seq','exp'}, dimensions={0} | all-to-all | bytes 131072 | tf_op jit(solution)/shard_map/all_to_all | solution.py:642
  40.2 3.1 %expert.1 = (f32[32,512]{1,0:T(8,128)S(1)}, f32[32,512]{1,0:T(8,128)S(1)}) custom-call(bf16[32,8,128]{2,1,0:T(8,128)(2,1)S(1)} %all_to_all.10.received_ref, f32[1,1024]{1,0:T(1,128)S(1)} %bitcast.7, bf16[2,768,1024]{2,1,0:T(8,128)(2,1)S(1)} %get-tuple-element.38.piece_ref, bf16[2,1,1408,1024]{3,2,1,0:T(8,128)(2,1)} %in_ref.3, bf16[1,1408,1024]{2,1,0:T(8,128)(2,1)} %down_ref.1), custom_call_target="tpu_custom_call" | custom-call | tf_op jit(solution)/shard_map/expert/pallas_call | solution.py:646
  43.3 0.1 collective-permute-start.21
  43.3 1.2 %collective-permute-done.21.other_ref = f32[32,512]{1,0:T(8,128)S(1)} collective-permute-done((f32[32,512]{1,0:T(8,128)S(1)}, f32[32,512]{1,0:T(8,128)S(1)}, u32[]{:S(2)}, u32[]{:S(2)}) %collective-permute-start.21) | collective-permute-done | bytes 65568 | tf_op jit(solution)/shard_map/ppermute | solution.py:664
  44.6 0.7 %spread.1 = bf16[32,8,512]{2,1,0:T(8,128)(2,1)} custom-call(f32[32,512]{1,0:T(8,128)S(1)} %get-tuple-element.39.kept_ref, f32[32,512]{1,0:T(8,128)S(1)} %collective-permute-done.21.other_ref), custom_call_target="tpu_custom_call" | custom-call | tf_op jit(solution)/shard_map/spread/pallas_call | solution.py:672
  45.3 2.6 %all-to-all-start.1 = ((bf16[32,8,512]{2,1,0:T(8,128)(2,1)}), bf16[32,8,512]{2,1,0:T(8,128)(2,1)S(1)}, u32[]{:S(2)}, u32[]{:S(2)}) async-start(bf16[32,8,512]{2,1,0:T(8,128)(2,1)} %spread.1), calls=%async_computation.1 | async-start | bytes 524288 | tf_op jit(solution)/shard_map/all_to_all | solution.py:678
  47.9 2.6 %collective-permute-start.19 = (f32[48,128]{1,0:T(8,128)S(1)}, f32[48,128]{1,0:T(8,128)S(1)}, u32[]{:S(2)}, u32[]{:S(2)}) collective-permute-start(f32[48,128]{1,0:T(8,128)S(1)} %get-tuple-element.41.refs_0_), channel_id=1, source_target_pairs={{0,24},{4,28},{8,16},{12,20},{16,8},{20,12},{24,0},{28,4},{1,25},{... | collective-permute-start | bytes 73736 | tf_op jit(solution)/shard_map/ppermute | solution.py:491
  50.5 0.5 collective-permute-start.17
  51.1 0.4 collective-permute-start.15
  51.4 1.6 %collective-permute-done.19.refs_6_ = f32[48,128]{1,0:T(8,128)S(1)} collective-permute-done((f32[48,128]{1,0:T(8,128)S(1)}, f32[48,128]{1,0:T(8,128)S(1)}, u32[]{:S(2)}, u32[]{:S(2)}) %collective-permute-start.19) | collective-permute-done | bytes 24608 | tf_op jit(solution)/shard_map/ppermute | solution.py:491
  53.1 1.6 %collective-permute-done.17.refs_4_ = f32[48,128]{1,0:T(8,128)S(1)} collective-permute-done((f32[48,128]{1,0:T(8,128)S(1)}, f32[48,128]{1,0:T(8,128)S(1)}, u32[]{:S(2)}, u32[]{:S(2)}) %collective-permute-start.17) | collective-permute-done | bytes 24608 | tf_op jit(solution)/shard_map/ppermute | solution.py:491
  54.7 0.3 collective-permute-done.15.refs_2_
  55.0 0.2 collective-permute-start.16
  55.2 0.7 %collective-permute-done.18.refs_5_ = f32[48,128]{1,0:T(8,128)S(1)} collective-permute-done((f32[48,128]{1,0:T(8,128)S(1)}, f32[48,128]{1,0:T(8,128)S(1)}, u32[]{:S(2)}, u32[]{:S(2)}) %collective-permute-start.18) | collective-permute-done | bytes 24608 | tf_op jit(solution)/shard_map/ppermute | solution.py:491
  55.8 0.3 collective-permute-done.16.refs_3_
  56.2 0.4 home.1
  56.6 1.5 %all-to-all-done.1 = bf16[32,8,512]{2,1,0:T(8,128)(2,1)S(1)} async-done(((bf16[32,8,512]{2,1,0:T(8,128)(2,1)}), bf16[32,8,512]{2,1,0:T(8,128)(2,1)S(1)}, u32[]{:S(2)}, u32[]{:S(2)}) %all-to-all-start.1) | async-done | bytes 262176 | tf_op jit(solution)/shard_map/all_to_all | solution.py:678
  58.1 0.8 %final.1 = bf16[12,4,1024]{2,1,0:T(4,128)(2,1)} custom-call(f32[48,128]{1,0:T(8,128)S(1)} %get-tuple-element.51.gates_ref, bf16[8,4,8,512]{3,2,1,0:T(8,128)(2,1)S(1)} %bitcast.5, f32[48,1024]{1,0:T(8,128)S(1)} %get-tuple-element.52.residual_ref), custom_call_target="tpu_custom_call" | custom-call | tf_op jit(solution)/shard_map/final/pallas_call | solution.py:695
  (19 shorter events, 0.0 us)
Async XLA Ops:
  0.0 11.4 %copy-start = (bf16[2,12,512,1024]{3,2,1,0:T(8,128)(2,1)S(1)}, bf16[2,12,512,1024]{3,2,1,0:T(8,128)(2,1)}, u32[]{:S(2)}) copy-start(bf16[2,12,512,1024]{3,2,1,0:T(8,128)(2,1)} %refs_9_.1) | copy-start | bytes 75497472
  1.7 6.8 %collective-permute-start.5 = (bf16[48,384]{1,0:T(8,128)(2,1)S(1)}, bf16[48,384]{1,0:T(8,128)(2,1)S(1)}, u32[]{:S(2)}, u32[]{:S(2)}) collective-permute-start(bf16[48,384]{1,0:T(8,128)(2,1)S(1)} %qkv.1.sent_ref), channel_id=1, source_target_pairs={{0,24},{4,28},{8,16},{12,20},{16,8},{20,12},{24,0},{28,4},{1,25},{... | collective-permute-start | bytes 110600 | tf_op jit(solution)/shard_map/ppermute | solution.py:491
  5.7 4.0 %collective-permute-start.3 = (bf16[48,384]{1,0:T(8,128)(2,1)S(1)}, bf16[48,384]{1,0:T(8,128)(2,1)S(1)}, u32[]{:S(2)}, u32[]{:S(2)}) collective-permute-start(bf16[48,384]{1,0:T(8,128)(2,1)S(1)} %qkv.1.sent_ref), channel_id=1, source_target_pairs={{0,16},{4,20},{8,24},{12,28},{16,0},{20,4},{24,8},{28,12},{1,17},{... | collective-permute-start | bytes 110600 | tf_op jit(solution)/shard_map/ppermute | solution.py:491
  6.2 4.0 %collective-permute-start.1 = (bf16[48,384]{1,0:T(8,128)(2,1)S(1)}, bf16[48,384]{1,0:T(8,128)(2,1)S(1)}, u32[]{:S(2)}, u32[]{:S(2)}) collective-permute-start(bf16[48,384]{1,0:T(8,128)(2,1)S(1)} %qkv.1.sent_ref), channel_id=1, source_target_pairs={{0,8},{4,12},{8,0},{12,4},{16,24},{20,28},{24,16},{28,20},{1,9},{5... | collective-permute-start | bytes 110600 | tf_op jit(solution)/shard_map/ppermute | solution.py:491
  8.5 1.7 %collective-permute-start = (bf16[48,384]{1,0:T(8,128)(2,1)S(1)}, bf16[48,384]{1,0:T(8,128)(2,1)S(1)}, u32[]{:S(2)}, u32[]{:S(2)}) collective-permute-start(bf16[48,384]{1,0:T(8,128)(2,1)S(1)} %get-tuple-element.29.refs_0_), channel_id=1, source_target_pairs={{0,4},{4,0},{8,12},{12,8},{16,20},{20,16},{24,28},{28,24},{1,5},{5... | collective-permute-start | bytes 110600 | tf_op jit(solution)/shard_map/ppermute | solution.py:491
  8.6 1.6 %collective-permute-start.6 = (bf16[48,384]{1,0:T(8,128)(2,1)S(1)}, bf16[48,384]{1,0:T(8,128)(2,1)S(1)}, u32[]{:S(2)}, u32[]{:S(2)}) collective-permute-start(bf16[48,384]{1,0:T(8,128)(2,1)S(1)} %collective-permute-done.5.refs_6_), channel_id=1, source_target_pairs={{0,4},{4,0},{8,12},{12,8},{16,20},{20,16},{24,28},{28,24},{1,5},{5... | collective-permute-start | bytes 110600 | tf_op jit(solution)/shard_map/ppermute | solution.py:491
  9.7 1.2 %collective-permute-start.4 = (bf16[48,384]{1,0:T(8,128)(2,1)S(1)}, bf16[48,384]{1,0:T(8,128)(2,1)S(1)}, u32[]{:S(2)}, u32[]{:S(2)}) collective-permute-start(bf16[48,384]{1,0:T(8,128)(2,1)S(1)} %collective-permute-done.3.refs_4_), channel_id=1, source_target_pairs={{0,4},{4,0},{8,12},{12,8},{16,20},{20,16},{24,28},{28,24},{1,5},{5... | collective-permute-start | bytes 110600 | tf_op jit(solution)/shard_map/ppermute | solution.py:491
  10.2 1.2 %collective-permute-start.2 = (bf16[48,384]{1,0:T(8,128)(2,1)S(1)}, bf16[48,384]{1,0:T(8,128)(2,1)S(1)}, u32[]{:S(2)}, u32[]{:S(2)}) collective-permute-start(bf16[48,384]{1,0:T(8,128)(2,1)S(1)} %collective-permute-done.1.refs_2_), channel_id=1, source_target_pairs={{0,4},{4,0},{8,12},{12,8},{16,20},{20,16},{24,28},{28,24},{1,5},{5... | collective-permute-start | bytes 110600 | tf_op jit(solution)/shard_map/ppermute | solution.py:491
  16.6 9.0 %copy-start.2 = (bf16[2,12,4,1024]{3,2,1,0:T(4,128)(2,1)S(1)}, bf16[2,12,4,1024]{3,2,1,0:T(4,128)(2,1)}, u32[]{:S(2)}) copy-start(bf16[2,12,4,1024]{3,2,1,0:T(4,128)(2,1)} %refs_8_.1) | copy-start | bytes 589828
  16.6 10.0 %copy-start.1 = (bf16[128,1024]{1,0:T(8,128)(2,1)S(1)}, bf16[128,1024]{1,0:T(8,128)(2,1)}, u32[]{:S(2)}) copy-start(bf16[128,1024]{1,0:T(8,128)(2,1)} %refs_10_.1) | copy-start | bytes 786436
  16.6 23.5 %copy-start.4 = (f32[1024]{0:T(1024)S(1)}, f32[1024]{0:T(1024)}, u32[]{:S(2)}) copy-start(f32[1024]{0:T(1024)} %param.20) | copy-start | bytes 12292
  16.6 6.3 %collective-permute-start.12 = (bf16[48,1152]{1,0:T(8,128)(2,1)S(1)}, bf16[48,1152]{1,0:T(8,128)(2,1)S(1)}, u32[]{:S(2)}, u32[]{:S(2)}) collective-permute-start(bf16[48,1152]{1,0:T(8,128)(2,1)S(1)} %attention.1.sent_ref), channel_id=1, source_target_pairs={{0,24},{4,28},{8,16},{12,20},{16,8},{20,12},{24,0},{28,4},{1,25},{... | collective-permute-start | bytes 331784 | tf_op jit(solution)/shard_map/ppermute | solution.py:491
  18.6 6.5 %collective-permute-start.10 = (bf16[48,1152]{1,0:T(8,128)(2,1)S(1)}, bf16[48,1152]{1,0:T(8,128)(2,1)S(1)}, u32[]{:S(2)}, u32[]{:S(2)}) collective-permute-start(bf16[48,1152]{1,0:T(8,128)(2,1)S(1)} %attention.1.sent_ref), channel_id=1, source_target_pairs={{0,16},{4,20},{8,24},{12,28},{16,0},{20,4},{24,8},{28,12},{1,17},{... | collective-permute-start | bytes 331784 | tf_op jit(solution)/shard_map/ppermute | solution.py:491
  19.1 6.1 %collective-permute-start.8 = (bf16[48,1152]{1,0:T(8,128)(2,1)S(1)}, bf16[48,1152]{1,0:T(8,128)(2,1)S(1)}, u32[]{:S(2)}, u32[]{:S(2)}) collective-permute-start(bf16[48,1152]{1,0:T(8,128)(2,1)S(1)} %attention.1.sent_ref), channel_id=1, source_target_pairs={{0,8},{4,12},{8,0},{12,4},{16,24},{20,28},{24,16},{28,20},{1,9},{5... | collective-permute-start | bytes 331784 | tf_op jit(solution)/shard_map/ppermute | solution.py:491
  22.1 4.4 %collective-permute-start.7 = (bf16[48,1152]{1,0:T(8,128)(2,1)S(1)}, bf16[48,1152]{1,0:T(8,128)(2,1)S(1)}, u32[]{:S(2)}, u32[]{:S(2)}) collective-permute-start(bf16[48,1152]{1,0:T(8,128)(2,1)S(1)} %get-tuple-element.31.refs_0_), channel_id=1, source_target_pairs={{0,4},{4,0},{8,12},{12,8},{16,20},{20,16},{24,28},{28,24},{1,5},{5... | collective-permute-start | bytes 331784 | tf_op jit(solution)/shard_map/ppermute | solution.py:491
  23.0 3.6 %collective-permute-start.13 = (bf16[48,1152]{1,0:T(8,128)(2,1)S(1)}, bf16[48,1152]{1,0:T(8,128)(2,1)S(1)}, u32[]{:S(2)}, u32[]{:S(2)}) collective-permute-start(bf16[48,1152]{1,0:T(8,128)(2,1)S(1)} %collective-permute-done.12.refs_6_), channel_id=1, source_target_pairs={{0,4},{4,0},{8,12},{12,8},{16,20},{20,16},{24,28},{28,24},{1,5},{5... | collective-permute-start | bytes 331784 | tf_op jit(solution)/shard_map/ppermute | solution.py:491
  25.1 1.5 %collective-permute-start.11 = (bf16[48,1152]{1,0:T(8,128)(2,1)S(1)}, bf16[48,1152]{1,0:T(8,128)(2,1)S(1)}, u32[]{:S(2)}, u32[]{:S(2)}) collective-permute-start(bf16[48,1152]{1,0:T(8,128)(2,1)S(1)} %collective-permute-done.10.refs_4_), channel_id=1, source_target_pairs={{0,4},{4,0},{8,12},{12,8},{16,20},{20,16},{24,28},{28,24},{1,5},{5... | collective-permute-start | bytes 331784 | tf_op jit(solution)/shard_map/ppermute | solution.py:491
  25.2 1.4 %collective-permute-start.9 = (bf16[48,1152]{1,0:T(8,128)(2,1)S(1)}, bf16[48,1152]{1,0:T(8,128)(2,1)S(1)}, u32[]{:S(2)}, u32[]{:S(2)}) collective-permute-start(bf16[48,1152]{1,0:T(8,128)(2,1)S(1)} %collective-permute-done.8.refs_2_), channel_id=1, source_target_pairs={{0,4},{4,0},{8,12},{12,8},{16,20},{20,16},{24,28},{28,24},{1,5},{5... | collective-permute-start | bytes 331784 | tf_op jit(solution)/shard_map/ppermute | solution.py:491
  40.2 16.0 %copy-start.3 = (bf16[1024,16]{0,1:T(8,128)(2,1)S(1)}, bf16[1024,16]{0,1:T(8,128)(2,1)}, u32[]{:S(2)}) copy-start(bf16[1024,16]{0,1:T(8,128)(2,1)} %param.21) | copy-start | bytes 98308
  43.3 1.3 %collective-permute-start.21 = (f32[32,512]{1,0:T(8,128)S(1)}, f32[32,512]{1,0:T(8,128)S(1)}, u32[]{:S(2)}, u32[]{:S(2)}) collective-permute-start(f32[32,512]{1,0:T(8,128)S(1)} %get-tuple-element.40), channel_id=1, source_target_pairs={{0,4},{4,0},{8,12},{12,8},{16,20},{20,16},{24,28},{28,24},{1,5},{5... | collective-permute-start | bytes 196616 | tf_op jit(solution)/shard_map/ppermute | solution.py:664
  45.3 12.8 %all-to-all-start.1 = ((bf16[32,8,512]{2,1,0:T(8,128)(2,1)}), bf16[32,8,512]{2,1,0:T(8,128)(2,1)S(1)}, u32[]{:S(2)}, u32[]{:S(2)}) async-start(bf16[32,8,512]{2,1,0:T(8,128)(2,1)} %spread.1), calls=%async_computation.1 | async-start | bytes 524288 | tf_op jit(solution)/shard_map/all_to_all | solution.py:678
  47.9 5.2 %collective-permute-start.19 = (f32[48,128]{1,0:T(8,128)S(1)}, f32[48,128]{1,0:T(8,128)S(1)}, u32[]{:S(2)}, u32[]{:S(2)}) collective-permute-start(f32[48,128]{1,0:T(8,128)S(1)} %get-tuple-element.41.refs_0_), channel_id=1, source_target_pairs={{0,24},{4,28},{8,16},{12,20},{16,8},{20,12},{24,0},{28,4},{1,25},{... | collective-permute-start | bytes 73736 | tf_op jit(solution)/shard_map/ppermute | solution.py:491
  50.5 4.1 %collective-permute-start.17 = (f32[48,128]{1,0:T(8,128)S(1)}, f32[48,128]{1,0:T(8,128)S(1)}, u32[]{:S(2)}, u32[]{:S(2)}) collective-permute-start(f32[48,128]{1,0:T(8,128)S(1)} %get-tuple-element.41.refs_0_), channel_id=1, source_target_pairs={{0,16},{4,20},{8,24},{12,28},{16,0},{20,4},{24,8},{28,12},{1,17},{... | collective-permute-start | bytes 73736 | tf_op jit(solution)/shard_map/ppermute | solution.py:491
  51.1 3.9 %collective-permute-start.15 = (f32[48,128]{1,0:T(8,128)S(1)}, f32[48,128]{1,0:T(8,128)S(1)}, u32[]{:S(2)}, u32[]{:S(2)}) collective-permute-start(f32[48,128]{1,0:T(8,128)S(1)} %get-tuple-element.41.refs_0_), channel_id=1, source_target_pairs={{0,8},{4,12},{8,0},{12,4},{16,24},{20,28},{24,16},{28,20},{1,9},{5... | collective-permute-start | bytes 73736 | tf_op jit(solution)/shard_map/ppermute | solution.py:491
  51.4 3.7 %collective-permute-start.14 = (f32[48,128]{1,0:T(8,128)S(1)}, f32[48,128]{1,0:T(8,128)S(1)}, u32[]{:S(2)}, u32[]{:S(2)}) collective-permute-start(f32[48,128]{1,0:T(8,128)S(1)} %get-tuple-element.41.refs_0_), channel_id=1, source_target_pairs={{0,4},{4,0},{8,12},{12,8},{16,20},{20,16},{24,28},{28,24},{1,5},{5... | collective-permute-start | bytes 73736 | tf_op jit(solution)/shard_map/ppermute | solution.py:491
  53.1 2.1 %collective-permute-start.20 = (f32[48,128]{1,0:T(8,128)S(1)}, f32[48,128]{1,0:T(8,128)S(1)}, u32[]{:S(2)}, u32[]{:S(2)}) collective-permute-start(f32[48,128]{1,0:T(8,128)S(1)} %collective-permute-done.19.refs_6_), channel_id=1, source_target_pairs={{0,4},{4,0},{8,12},{12,8},{16,20},{20,16},{24,28},{28,24},{1,5},{5... | collective-permute-start | bytes 73736 | tf_op jit(solution)/shard_map/ppermute | solution.py:491
  54.6 1.2 %collective-permute-start.18 = (f32[48,128]{1,0:T(8,128)S(1)}, f32[48,128]{1,0:T(8,128)S(1)}, u32[]{:S(2)}, u32[]{:S(2)}) collective-permute-start(f32[48,128]{1,0:T(8,128)S(1)} %collective-permute-done.17.refs_4_), channel_id=1, source_target_pairs={{0,4},{4,0},{8,12},{12,8},{16,20},{20,16},{24,28},{28,24},{1,5},{5... | collective-permute-start | bytes 73736 | tf_op jit(solution)/shard_map/ppermute | solution.py:491
  55.0 1.2 %collective-permute-start.16 = (f32[48,128]{1,0:T(8,128)S(1)}, f32[48,128]{1,0:T(8,128)S(1)}, u32[]{:S(2)}, u32[]{:S(2)}) collective-permute-start(f32[48,128]{1,0:T(8,128)S(1)} %collective-permute-done.15.refs_2_), channel_id=1, source_target_pairs={{0,4},{4,0},{8,12},{12,8},{16,20},{20,16},{24,28},{28,24},{1,5},{5... | collective-permute-start | bytes 73736 | tf_op jit(solution)/shard_map/ppermute | solution.py:491

commit v9 on v8

--- a/solution.py
+++ b/solution.py
@@ -19,6 +19,10 @@
 FIRST_KEYS = 2
 SECOND_KEYS = 8
 SECOND_VALUES = 3
+CORES = 2
+HALF_HEADS = HEADS // CORES
+HALF = HALF_HEADS * HD
+PACKED = HALF + LANES
 HELD = 768
 PIECE = 320
 AHEAD = 10
@@ -78,11 +82,55 @@
     return [sems.at[i] for i in range(sems.shape[0])]
 
 
+def each(sems):
+    return [sems.at[i] for i in range(sems.shape[0])]
+
+
 def started(pairs, sems):
     copies = [pltpu.make_async_copy(*pair, sem) for pair, sem in zip(pairs, sems)]
     for copy in copies:
         copy.start()
     return copies
+
+
+def unpack(packed):
+    stats = packed[:, HALF:].astype(jnp.float32)
+
+    def joined(first):
+        return sum(
+            stats[:, (first + i) * HALF_HEADS : (first + i + 1) * HALF_HEADS] for i in range(PIECES)
+        )
+
+    return joined(0), joined(PIECES), packed[:, :HALF].astype(jnp.float32)
+
+
+def pack(peak, total, mixed):
+    parts = [part.astype(jnp.float32) for part in split(peak, PIECES) + split(total, PIECES)]
+    blank = jnp.zeros((peak.shape[0], LANES - 2 * PIECES * HALF_HEADS), jnp.float32)
+    return jnp.concatenate([mixed] + parts + [blank], axis=1).astype(jnp.bfloat16)
+
+
+def over_heads(factor):
+    row = lax.broadcasted_iota(jnp.int32, (HALF_HEADS, HALF), 0)
+    col = lax.broadcasted_iota(jnp.int32, (HALF_HEADS, HALF), 1) // HD
+    expand = (row == col).astype(jnp.bfloat16)
+    return sum(dot(part, expand) for part in split(factor, 2))
+
+
+def merge(parts):
+    overall = functools.reduce(jnp.maximum, [peak for peak, _, _ in parts])
+    factors = [jnp.exp(peak - overall) for peak, _, _ in parts]
+    total = sum(factor * part[1] for factor, part in zip(factors, parts))
+    mixed = sum(over_heads(factor) * part[2] for factor, part in zip(factors, parts))
+    return overall, total, mixed
+
+
+def attend(parts):
+    overall = functools.reduce(jnp.maximum, [peak for peak, _, _ in parts])
+    factors = [jnp.exp(peak - overall) for peak, _, _ in parts]
+    total = sum(factor * part[1] for factor, part in zip(factors, parts))
+    inverse = jnp.where(total > 0, 1.0 / jnp.where(total > 0, total, 1.0), 0.0)
+    return sum(over_heads(factor * inverse) * part[2] for factor, part in zip(factors, parts))
 
 
 def route(ids_ref, order_ref, select_ref, chosen_ref):
@@ -125,26 +173,32 @@
     gain_ref,
     weight_ref,
     window_ref,
+    lengths_ref,
     out_ref,
+    spans_ref,
     token_buf,
     gain_buf,
     weight_buf,
     rows_ref,
+    numbers_ref,
     sems,
 ):
     copies = started(
         (
             (tokens_ref, token_buf),
             (gain_ref, gain_buf),
+            (lengths_ref, numbers_ref),
             (weight_ref, weight_buf),
         ),
         each(sems),
     )
-    for copy in copies[:2]:
+    for copy in copies[:3]:
         copy.wait()
     copy_rows(token_buf, rows_ref)
     normed = rms_rows(rows_ref[...], gain_buf[...])
-    copies[2].wait()
+    for r in range(spans_ref.shape[0]):
+        spans_ref[r : r + 1, :] = jnp.full((1, LANES), numbers_ref[r], jnp.int32)
+    copies[3].wait()
     out_ref[...] = dot(normed, weight_buf[...], ROWS_BY_ROWS).astype(jnp.bfloat16)
 
 
@@ -160,58 +214,46 @@
     return (row_head == col_head).astype(jnp.float32)
 
 
-def routing_kernel(
+def fetch_expert_kernel(
     sent_ref,
-    lengths_ref,
+    in_ref,
     ids_ref,
     order_ref,
     tokens_ref,
     held_ref,
-    spans_ref,
+    piece_ref,
     select_ref,
     chosen_ref,
     turned_ref,
     columns_ref,
-    numbers_ref,
     ids_buf,
     order_buf,
     tokens_buf,
     rows_ref,
     sems,
 ):
-    copies = started(
-        (
-            (ids_ref, ids_buf),
-            (order_ref, order_buf),
-            (lengths_ref, numbers_ref),
-            (tokens_ref, tokens_buf),
-        ),
-        each(sems),
-    )
+    pairs = [(ids_ref, ids_buf), (order_ref, order_buf), (tokens_ref, tokens_buf)]
+    pairs += [
+        (in_ref.at[p, 0, pl.ds(0, piece_ref.shape[1])], piece_ref.at[p]) for p in range(2)
+    ]
+    copies = started(pairs, each(sems))
     held_ref[...] = sent_ref[...]
-    for copy in copies:
+    for copy in copies[:3]:
         copy.wait()
     turned_ref[...] = route(ids_buf, order_buf, select_ref, chosen_ref)
-    for r in range(spans_ref.shape[0]):
-        spans_ref[r : r + 1, :] = jnp.full((1, LANES), numbers_ref[r], jnp.int32)
     copy_rows(tokens_buf, rows_ref)
     width, share = rows_ref.shape[1], columns_ref.shape[1]
     feature = lax.broadcasted_iota(jnp.int32, (width, share), 0)
     column = lax.broadcasted_iota(jnp.int32, (width, share), 1)
     own = (feature == column + lax.axis_index("seq") * share).astype(jnp.bfloat16)
     columns_ref[...] = dot(rows_ref[...].astype(jnp.bfloat16), own)
-
-
-def fetch_expert_kernel(sent_ref, in_ref, held_ref, piece_ref, sems):
-    copies = started([(in_ref.at[p, 0, pl.ds(0, piece_ref.shape[1])], piece_ref.at[p]) for p in range(2)], each(sems))
-    held_ref[...] = sent_ref[...]
-    for copy in copies:
+    for copy in copies[3:]:
         copy.wait()
 
 
 def attention_kernel(*refs):
-    *mixed_refs, spans_ref, window_ref = refs[:-4]
-    out_ref, ordered_ref, flat_ref, query_ref = refs[-4:]
+    *mixed_refs, spans_ref, window_ref = refs[:-5]
+    keep_ref, send_ref, ordered_ref, flat_ref, result_ref = refs[-5:]
     devices, rows, share = ordered_ref.shape
     _, requests, span, width = window_ref.shape
     steps = rows // requests
@@ -222,11 +264,6 @@
         if d * share < width:
             flat_ref[:, d * share : (d + 1) * share] = ordered_ref[d].astype(jnp.float32)
     own_head = head_masks(block_rows, width, steps)
-    for r in range(requests):
-        queries = flat_ref[r * steps : (r + 1) * steps, 0:width]
-        query_ref[r] = (jnp.concatenate([queries] * BLOCK_HEADS, axis=0) * own_head).astype(
-            jnp.bfloat16
-        )
     base = place * span
     scale = HD ** (-0.5)
     pair = 2 * steps
@@ -239,8 +276,10 @@
 
     def score(r):
         keys = window_ref.at[0, r]
+        queries = flat_ref[r * steps : (r + 1) * steps, 0:width]
+        queries = (jnp.concatenate([queries] * BLOCK_HEADS, axis=0) * own_head).astype(jnp.bfloat16)
         return jnp.concatenate(
-            [dot(query_ref[r, :, c], keys[:, c], ROWS_BY_ROWS) for c in cols], axis=0
+            [dot(queries[:, c], keys[:, c], ROWS_BY_ROWS) for c in cols], axis=0
         )
 
     scores = score(0)
@@ -265,15 +304,17 @@
         stats = jnp.where(stat_lane == stat_head + HEADS, total.reshape(HEADS * steps, 1), stats)
         stats = jnp.sum(stats.reshape(tiles, pair, LANES), axis=0)
         outs.append(stats[:steps] + stats[steps:])
-        flat_ref[r * steps : (r + 1) * steps, :] = jnp.concatenate(outs, axis=1)
+        result_ref[r * steps : (r + 1) * steps, :] = jnp.concatenate(outs, axis=1)
         scores = following
-    out_ref[:, :width] = flat_ref[:, :width].astype(jnp.bfloat16)
-    parts = []
-    for first in (0, HEADS):
-        parts += split(flat_ref[:, width + first : width + first + HEADS], PIECES)
-    blank = jnp.zeros((rows, LANES - 2 * PIECES * HEADS), jnp.float32)
-    parts = [part.astype(jnp.float32) for part in parts] + [blank]
-    out_ref[:, width:] = jnp.concatenate(parts, axis=1).astype(jnp.bfloat16)
+    halves = []
+    for c in range(CORES):
+        first = width + c * HALF_HEADS
+        peak = result_ref[:, first : first + HALF_HEADS]
+        total = result_ref[:, first + HEADS : first + HEADS + HALF_HEADS]
+        halves.append(pack(peak, total, result_ref[:, c * HALF : (c + 1) * HALF]))
+    odd = place % CORES == 1
+    keep_ref[...] = jnp.where(odd, halves[1], halves[0])
+    send_ref[...] = jnp.where(odd, halves[0], halves[1])
 
 
 def extra_kernel(*refs):
@@ -332,40 +373,39 @@
         stats_ref[r * steps : (r + 1) * steps, :] = stats[r]
 
 
+def pair_kernel(keep_ref, other_ref, extra_ref, extra_stats_ref, out_ref):
+    odd = lax.axis_index("seq") % CORES == 1
+    first = lax.axis_index("seq") // CORES == 0
+
+    def own_half(value, at, width):
+        return jnp.where(odd, value[:, at + width : at + 2 * width], value[:, at : at + width])
+
+    extra_peak = jnp.where(first, own_half(extra_stats_ref[...], 0, HALF_HEADS), MASKED)
+    extra_total = jnp.where(first, own_half(extra_stats_ref[...], HEADS, HALF_HEADS), 0.0)
+    extra = jnp.where(first, own_half(extra_ref[...], 0, HALF), 0.0)
+    parts = [unpack(keep_ref[...]), unpack(other_ref[...]), (extra_peak, extra_total, extra)]
+    out_ref[...] = pack(*merge(parts))
+
+
 def project_kernel(*refs):
-    *part_refs, extra_ref, extra_stats_ref, weight_ref, columns_ref, turned_ref = refs[:-2]
-    out_ref, residual_ref = refs[-2:]
-    devices = len(part_refs)
-    rows, width = extra_ref.shape
-    stats = [part_ref[:, width:].astype(jnp.float32) for part_ref in part_refs]
-
-    def joined(stat, first):
-        return sum(
-            stat[:, (first + i) * HEADS : (first + i + 1) * HEADS] for i in range(PIECES)
-        )
-
-    peaks = [joined(stat, 0) for stat in stats] + [extra_stats_ref[:, :HEADS]]
-    totals = [joined(stat, PIECES) for stat in stats] + [extra_stats_ref[:, HEADS : 2 * HEADS]]
-    overall = functools.reduce(jnp.maximum, peaks)
-    factors = [jnp.exp(peak - overall) for peak in peaks]
-    total = sum(f * t for f, t in zip(factors, totals))
-    inverse = 1.0 / total
-    head_of_row = lax.broadcasted_iota(jnp.int32, (HEADS, width), 0)
-    head_of_col = lax.broadcasted_iota(jnp.int32, (HEADS, width), 1) // HD
-    expand = (head_of_row == head_of_col).astype(jnp.bfloat16)
-
-    spread = jnp.concatenate([factor * inverse for factor in factors], axis=0)
-    spread = exact_dot(spread, expand)
-    attended = spread[devices * rows :] * extra_ref[...]
-    for d in range(devices):
-        share = spread[d * rows : (d + 1) * rows]
-        attended = attended + share * part_refs[d][:, :width].astype(jnp.float32)
-    projected = dot(attended.astype(jnp.bfloat16), weight_ref[...], ROWS_BY_ROWS).astype(jnp.bfloat16)
-    residual = columns_ref[...] + projected.astype(jnp.float32)
+    *part_refs, weight_ref, other_weight_ref, columns_ref, turned_ref, out_ref, residual_ref = refs
+    devices = lax.axis_size("seq")
+    groups = lax.axis_size("exp")
+    local_experts = EXPERTS // groups
+    odd = lax.axis_index("seq") % CORES == 1
+    attended = attend([unpack(part_ref[...]) for part_ref in part_refs]).astype(jnp.bfloat16)
+
+    def project(weight):
+        weight = jnp.where(odd, weight[:, HALF:], weight[:, :HALF])
+        return dot(attended, weight, ROWS_BY_ROWS)
+
+    mine = project(weight_ref[...]) + columns_ref[...]
+    others = project(other_weight_ref[...])
+    residual = jnp.concatenate(
+        [jnp.where(odd, others, mine), jnp.where(odd, mine, others)], axis=1
+    )
     residual_ref[...] = residual
     table = dot(turned_ref[...].astype(jnp.bfloat16), residual.astype(jnp.bfloat16))
-    groups = lax.axis_size("exp")
-    local_experts = EXPERTS // groups
     for s in range(devices):
         for x in range(groups):
             row = (x * local_experts + s // (devices // local_experts)) * CAP
@@ -376,7 +416,9 @@
     residual_refs, refs = refs[:devices], refs[devices:]
     gain_ref, router_ref, select_ref, chosen_ref, residual_ref, gates_ref, ordered_ref = refs
     in_order(residual_refs, ordered_ref)
-    residual = jnp.concatenate([ordered_ref[d] for d in range(devices)], axis=1)
+    residual = jnp.concatenate(
+        [ordered_ref[d] + ordered_ref[d + 1] for d in range(0, devices, CORES)], axis=1
+    )
     residual_ref[...] = residual
     normed = rms_rows(residual, gain_ref[...])
     logits = dot(normed, router_ref[...], ROWS_BY_ROWS)
@@ -421,12 +463,14 @@
     devices = lax.axis_size("seq")
     groups = lax.axis_size("exp")
     columns = []
-    for s in range(devices):
-        columns.append(
+    for s in range(0, devices, CORES):
+        pieces_of_chip = [
             jnp.concatenate(
-                [received_ref[s * groups + g].astype(jnp.float32) for g in range(groups)], axis=0
+                [received_ref[d * groups + g].astype(jnp.float32) for g in range(groups)], axis=0
             )
-        )
+            for d in range(s, s + CORES)
+        ]
+        columns.append(sum(pieces_of_chip))
     rows = rms_rows(jnp.concatenate(columns, axis=1), gain_ref[...])
 
     def layer(gate_weight, up_weight):
@@ -484,16 +528,19 @@
         out_ref[r] = total[r * steps : (r + 1) * steps].astype(jnp.bfloat16)
 
 
-def gather_seq(values, meanwhile=None):
-    count = lax.axis_size("seq")
-
-    def exchange(value, bits):
-        return lax.ppermute(value, "seq", [(i, i ^ bits) for i in range(count)])
-
-    near = [exchange(values, k) for k in range(2, count, 2)]
+def exchange(value, bits):
+    return lax.ppermute(value, "seq", [(i, i ^ bits) for i in range(lax.axis_size("seq"))])
+
+
+def from_chips(values, meanwhile=None):
+    others = [exchange(values, k) for k in range(2, lax.axis_size("seq"), 2)]
     if meanwhile is not None:
         values = meanwhile(values)
-    near = [values] + near
+    return [values] + others
+
+
+def gather_seq(values, meanwhile=None):
+    near = from_chips(values, meanwhile)
     return [part for value in near for part in (value, exchange(value, 1))]
 
 
@@ -532,90 +579,38 @@
     hbm = pl.BlockSpec(memory_space=pltpu.HBM)
 
     gain_row = attn_gain.reshape(1, width)
-    local_mix = pl.pallas_call(
+    local_mix, spans = pl.pallas_call(
         qkv_kernel,
-        in_specs=[hbm] * 4,
-        out_shape=shape((rows, share), bf16),
+        in_specs=[hbm] * 5,
+        out_shape=(shape((rows, share), bf16), shape((requests, LANES), jnp.int32)),
         scratch_shapes=[
             pltpu.VMEM(tokens.shape, bf16),
             pltpu.VMEM(gain_row.shape, f32),
             pltpu.VMEM(w_qkv.shape, bf16),
             pltpu.VMEM((rows, width), f32),
+            pltpu.SMEM((requests,), jnp.int32),
             pltpu.SemaphoreType.DMA((4,)),
         ],
         compiler_params=params(4),
         name="qkv",
-    )(in_hbm(tokens), in_hbm(gain_row), in_hbm(w_qkv), in_hbm(window_cache))
-
-    fetched = []
-
-    def routing(values):
-        held, *outputs = pl.pallas_call(
-            routing_kernel,
-            in_specs=[vmem] + [hbm] * 4,
-            out_shape=(
-                shape(values.shape, bf16),
-                shape((requests, LANES), jnp.int32),
-                shape((TOPK, rows, slots), f32),
-                shape((TOPK, rows, LANES), f32),
-                shape((slots, rows), f32),
-                shape((rows, w_out.shape[0]), f32),
-            ),
-            scratch_shapes=[
-                pltpu.SMEM((requests,), jnp.int32),
-                pltpu.VMEM((steps, TOPK, requests), jnp.int32),
-                pltpu.VMEM(slot_order.shape, jnp.int32),
-                pltpu.VMEM(tokens.shape, bf16),
-                pltpu.VMEM((rows, width), f32),
-                pltpu.SemaphoreType.DMA((4,)),
-            ],
-            compiler_params=params(8),
-            name="routing",
-        )(
-            values,
-            in_hbm(lengths),
-            in_hbm(expert_ids.transpose(1, 2, 0)),
-            in_hbm(slot_order),
-            in_hbm(tokens),
-        )
-        fetched.extend(outputs)
-        return held
-
-    mixed = gather_seq(local_mix, routing)
-    spans, select, chosen, turned, token_columns = fetched
+    )(in_hbm(tokens), in_hbm(gain_row), in_hbm(w_qkv), in_hbm(window_cache), in_hbm(lengths))
+
+    mixed = gather_seq(local_mix)
 
     padded = width + LANES
-    part = pl.pallas_call(
+    kept, sent = pl.pallas_call(
         attention_kernel,
         in_specs=[vmem] * (seq_count + 2),
-        out_shape=shape((rows, padded), bf16),
+        out_shape=(shape((rows, PACKED), bf16), shape((rows, PACKED), bf16)),
         scratch_shapes=[
             pltpu.VMEM((seq_count, rows, share), bf16),
             pltpu.VMEM((rows, padded), f32),
-            pltpu.VMEM((requests, BLOCK_HEADS * steps, width), bf16),
+            pltpu.VMEM((rows, padded), f32),
         ],
         compiler_params=params(8),
         name="attention",
     )(*mixed, spans, window_cache)
-    hidden_units = expert_down.shape[1]
-    held_units = min(HELD, hidden_units)
-    late_units = max(hidden_units - held_units, 16)
-
-    def fetch_expert(values):
-        held, piece = pl.pallas_call(
-            fetch_expert_kernel,
-            in_specs=[vmem, hbm],
-            out_shape=(shape(values.shape, bf16), shape((2, held_units, width), bf16)),
-            scratch_shapes=[pltpu.SemaphoreType.DMA((2,))],
-            compiler_params=params(8),
-            cost_estimate=moving(4 * held_units * width),
-            name="fetch_expert",
-        )(values, in_hbm(expert_in))
-        fetched.append(piece)
-        return held
-
-    parts = gather_seq(part, fetch_expert)
-    piece = fetched[-1]
+    other = exchange(sent, 1)
 
     extra, extra_stats = pl.pallas_call(
         extra_kernel,
@@ -630,15 +625,64 @@
         name="extra",
     )(*mixed, sink_cache)
 
+    part = pl.pallas_call(
+        pair_kernel,
+        out_shape=shape((rows, PACKED), bf16),
+        compiler_params=params(8),
+        name="pair",
+    )(kept, other, extra, extra_stats)
+
+    hidden_units = expert_down.shape[1]
+    held_units = min(HELD, hidden_units)
+    late_units = max(hidden_units - held_units, 16)
+
+    fetched = []
+
+    def fetch_expert(values):
+        held, *outputs = pl.pallas_call(
+            fetch_expert_kernel,
+            in_specs=[vmem] + [hbm] * 4,
+            out_shape=(
+                shape(values.shape, bf16),
+                shape((2, held_units, width), bf16),
+                shape((TOPK, rows, slots), f32),
+                shape((TOPK, rows, LANES), f32),
+                shape((slots, rows), f32),
+                shape((rows, w_out.shape[0]), f32),
+            ),
+            scratch_shapes=[
+                pltpu.VMEM((steps, TOPK, requests), jnp.int32),
+                pltpu.VMEM(slot_order.shape, jnp.int32),
+                pltpu.VMEM(tokens.shape, bf16),
+                pltpu.VMEM((rows, width), f32),
+                pltpu.SemaphoreType.DMA((5,)),
+            ],
+            compiler_params=params(8),
+            cost_estimate=moving(4 * held_units * width),
+            name="fetch_expert",
+        )(
+            values,
+            in_hbm(expert_in),
+            in_hbm(expert_ids.transpose(1, 2, 0)),
+            in_hbm(slot_order),
+            in_hbm(tokens),
+        )
+        fetched.extend(outputs)
+        return held
+
+    parts = from_chips(part, fetch_expert)
+    other_weight = exchange(lax.optimization_barrier((w_out, part))[0], 1)
+    piece, select, chosen, turned, token_columns = fetched
+
     outgoing, residual_columns = pl.pallas_call(
         project_kernel,
         out_shape=(
-            shape((seq_count * groups, CAP, w_out.shape[0]), bf16),
-            shape((rows, w_out.shape[0]), f32),
+            shape((seq_count * groups, CAP, CORES * w_out.shape[0]), bf16),
+            shape((rows, CORES * w_out.shape[0]), f32),
         ),
         compiler_params=params(16),
         name="project",
-    )(*parts, extra, extra_stats, w_out, token_columns, turned)
+    )(*parts, w_out, other_weight, token_columns, turned)
     received = lax.all_to_all(outgoing, ("seq", "exp"), split_axis=0, concat_axis=0, tiled=True)
     columns = gather_seq(residual_columns)
 
@@ -687,7 +731,7 @@
     residual, gates = pl.pallas_call(
         functools.partial(home_kernel, seq_count),
         out_shape=(shape((rows, width), f32), shape((rows, slots), f32)),
-        scratch_shapes=[pltpu.VMEM((seq_count, rows, w_out.shape[0]), f32)],
+        scratch_shapes=[pltpu.VMEM((seq_count, rows, CORES * w_out.shape[0]), f32)],
         compiler_params=params(8),
         name="home",
     )(*columns, moe_row, router.T, select, chosen)

time: 59.2 us -> 58.8 us (level)
  Pallas kernels: 18 us -> 16.2 us
  blocking collectives: 12.5 us -> 13.8 us
    pallas_call x3, Pallas kernels: 5.74 us -> 4.22 us  [the longest x1 2.01 us: fetch_expert(): pl.pallas_call(fetch_expert_kernel, in_specs=[vmem] + [hbm] * 4, out_shap...]
    all_to_all x1, blocking collectives: 12.5 us -> 13.8 us  [body(): lax.all_to_all(outgoing, ('seq', 'exp'), split_axis=0, concat_axis=0, til...]
    ppermute x21 -> x19, waiting for transfers between devices: 9.88 us -> 11.1 us  [exchange(): lax.ppermute(value, 'seq', [(i, i ^ bits) for i in range(lax.axis_size('s...]
    all_to_all x1, waiting for transfers between devices: 1.54 us -> 0.79 us  [body(): lax.all_to_all(outgoing, ('seq', 'exp'), split_axis=0, concat_axis=0, til...]
    ppermute x21 -> x19, starting transfers between devices: 13 us -> 12.7 us  [exchange(): lax.ppermute(value, 'seq', [(i, i ^ bits) for i in range(lax.axis_size('s...]
  transfers between devices with their start and end apart: 23 -> 21, of which waited for: 14 -> 14; matrix products, arithmetic and copies ran while one was open for 0% -> 0% of each run, Pallas kernels for 9% -> 6%
where the time goes in v9:
time: 58.8 us; the launch traced here: 58.6 us
  Pallas kernels  16.2 us (28%)
  starting transfers between devices  15.3 us (26%)
  blocking collectives  13.8 us (23%)
  waiting for transfers between devices  13.1 us (22%)
    all_to_all x1, blocking collectives, body(): lax.all_to_all(outgoing, ('seq', 'exp'), split_axis=0, concat_axis=0, til...  13.8 us
    ppermute x19, starting transfers between devices, exchange(): lax.ppermute(value, 'seq', [(i, i ^ bits) for i in range(lax.axis_size('s...  12.7 us
    ppermute x19, waiting for transfers between devices, exchange(): lax.ppermute(value, 'seq', [(i, i ^ bits) for i in range(lax.axis_size('s...  11.1 us
    pallas_call x1, Pallas kernels, body(): pl.pallas_call(attention_kernel, in_specs=[vmem] * (seq_count + 2), out_s...  5.16 us
    pallas_call x1, Pallas kernels, body(): pl.pallas_call(expert_kernel, in_specs=[vmem, vmem, vmem, hbm, hbm], out_...  3.24 us
    all_to_all x1, starting transfers between devices, body(): lax.all_to_all(outgoing, ('seq', 'exp'), split_axis=0, concat_axis=0, til...  2.58 us
    pallas_call x1, Pallas kernels, fetch_expert(): pl.pallas_call(fetch_expert_kernel, in_specs=[vmem] + [hbm] * 4, out_shap...  2.01 us
    pallas_call x1, Pallas kernels, body(): pl.pallas_call(qkv_kernel, in_specs=[hbm] * 5, out_shape=(shape((rows, sh...  1.73 us
  transfers between devices with their start and end apart: 21, of which 14 were waited for; matrix products, arithmetic and copies ran while one was open for 0% of the time, Pallas kernels for 6%

profile of v9, /device:TPU:0, one launch (start us, length us, event | category | flops | bytes accessed | tf_op | source)
XLA Modules:
  0.0 58.6 jit_solution(9843528827143650493)
XLA Ops:
  0.0 1.7 %qkv.1 = (bf16[48,384]{1,0:T(8,128)(2,1)S(1)}, s32[12,128]{1,0:T(8,128)S(1)}) custom-call(bf16[12,4,1024]{2,1,0:T(4,128)(2,1)} %tokens_ref.3, f32[1,1024]{1,0:T(1,128)} %bitcast.9, bf16[384,1024]{1,0:T(8,128)(2,1)} %weight_ref.1, bf16[2,12,512,1024]{3,2,1,0:T(8,128)(2,1)} %refs_9_.1, s32[12]{0:T(128)} %lengths_ref.1), custom_call_target="tpu_custom_call" | custom-call | tf_op jit(solution)/shard_map/qkv/pallas_call | solution.py:582
  1.7 4.0 %collective-permute-start.5 = (bf16[48,384]{1,0:T(8,128)(2,1)S(1)}, bf16[48,384]{1,0:T(8,128)(2,1)S(1)}, u32[]{:S(2)}, u32[]{:S(2)}) collective-permute-start(bf16[48,384]{1,0:T(8,128)(2,1)S(1)} %get-tuple-element.32.refs_0_), channel_id=1, source_target_pairs={{0,24},{4,28},{8,16},{12,20},{16,8},{20,12},{24,0},{28,4},{1,25},{... | collective-permute-start | bytes 110600 | tf_op jit(solution)/shard_map/ppermute | solution.py:532
  5.7 0.5 collective-permute-start.3
  6.2 0.1 collective-permute-start.1
  6.3 0.0 collective-permute-start
  6.3 1.3 %collective-permute-done.5.refs_6_ = bf16[48,384]{1,0:T(8,128)(2,1)S(1)} collective-permute-done((bf16[48,384]{1,0:T(8,128)(2,1)S(1)}, bf16[48,384]{1,0:T(8,128)(2,1)S(1)}, u32[]{:S(2)}, u32[]{:S(2)}) %collective-permute-start.5) | collective-permute-done | bytes 36896 | tf_op jit(solution)/shard_map/ppermute | solution.py:532
  7.6 0.0 collective-permute-start.6
  7.6 2.0 %collective-permute-done.3.refs_4_ = bf16[48,384]{1,0:T(8,128)(2,1)S(1)} collective-permute-done((bf16[48,384]{1,0:T(8,128)(2,1)S(1)}, bf16[48,384]{1,0:T(8,128)(2,1)S(1)}, u32[]{:S(2)}, u32[]{:S(2)}) %collective-permute-start.3) | collective-permute-done | bytes 36896 | tf_op jit(solution)/shard_map/ppermute | solution.py:532
  9.7 0.5 collective-permute-done.1.refs_2_
  10.2 0.0 collective-permute-start.2
  10.2 0.0 collective-permute-done.6.refs_7_
  10.2 0.7 %collective-permute-done.4.refs_5_ = bf16[48,384]{1,0:T(8,128)(2,1)S(1)} collective-permute-done((bf16[48,384]{1,0:T(8,128)(2,1)S(1)}, bf16[48,384]{1,0:T(8,128)(2,1)S(1)}, u32[]{:S(2)}, u32[]{:S(2)}) %collective-permute-start.4) | collective-permute-done | bytes 36896 | tf_op jit(solution)/shard_map/ppermute | solution.py:532
  10.9 0.5 collective-permute-done.2.refs_3_
  11.4 5.2 %attention.1 = (bf16[48,640]{1,0:T(8,128)(2,1)S(1)}, bf16[48,640]{1,0:T(8,128)(2,1)S(1)}) custom-call(bf16[48,384]{1,0:T(8,128)(2,1)S(1)} %get-tuple-element.32.refs_0_, bf16[48,384]{1,0:T(8,128)(2,1)S(1)} %collective-permute-done.refs_1_, bf16[48,384]{1,0:T(8,128)(2,1)S(1)} %collective-permute-done.1.refs_2_, ...), custom_call_target="tpu_custom_call" | custom-call | tf_op jit(solution)/shard_map/attention/pallas_call | solution.py:601
  16.6 0.0 copy-start.4
  16.6 0.2 collective-permute-start.7
  16.8 0.9 %extra.1 = (f32[48,1024]{1,0:T(8,128)S(1)}, f32[48,128]{1,0:T(8,128)S(1)}) custom-call(bf16[48,384]{1,0:T(8,128)(2,1)S(1)} %get-tuple-element.32.refs_0_, bf16[48,384]{1,0:T(8,128)(2,1)S(1)} %collective-permute-done.refs_1_, bf16[48,384]{1,0:T(8,128)(2,1)S(1)} %collective-permute-done.1.refs_2_, bf16[48,384]{1,0:T(8,128)(2,1)S(1)} %collective-permute-done.2.refs_3_, ...), custom_call_target="tpu_custom_call" | custom-call | tf_op jit(solution)/shard_map/extra/pallas_call | solution.py:615
  17.7 0.2 collective-permute-done.7.other_ref
  17.9 0.5 pair.1.sent_ref
  18.4 0.3 collective-permute-start.11
  18.6 1.5 %collective-permute-start.10 = (bf16[48,640]{1,0:T(8,128)(2,1)S(1)}, bf16[48,640]{1,0:T(8,128)(2,1)S(1)}, u32[]{:S(2)}, u32[]{:S(2)}) collective-permute-start(bf16[48,640]{1,0:T(8,128)(2,1)S(1)} %pair.1.sent_ref), channel_id=1, source_target_pairs={{0,24},{4,28},{8,16},{12,20},{16,8},{20,12},{24,0},{28,4},{1,25},{... | collective-permute-start | bytes 184328 | tf_op jit(solution)/shard_map/ppermute | solution.py:532
  20.1 0.3 collective-permute-start.9
  20.5 1.7 %collective-permute-start.8 = (bf16[48,640]{1,0:T(8,128)(2,1)S(1)}, bf16[48,640]{1,0:T(8,128)(2,1)S(1)}, u32[]{:S(2)}, u32[]{:S(2)}) collective-permute-start(bf16[48,640]{1,0:T(8,128)(2,1)S(1)} %pair.1.sent_ref), channel_id=1, source_target_pairs={{0,8},{4,12},{8,0},{12,4},{16,24},{20,28},{24,16},{28,20},{1,9},{5... | collective-permute-start | bytes 184328 | tf_op jit(solution)/shard_map/ppermute | solution.py:532
  22.1 2.0 %fetch_expert.1 = (bf16[48,640]{1,0:T(8,128)(2,1)S(1)}, bf16[2,768,1024]{2,1,0:T(8,128)(2,1)S(1)}, f32[2,48,128]{2,1,0:T(8,128)S(1)}, f32[2,48,128]{2,1,0:T(8,12...) custom-call(bf16[48,640]{1,0:T(8,128)(2,1)S(1)} %pair.1.sent_ref, bf16[2,1,1408,1024]{3,2,1,0:T(8,128)(2,1)} %in_ref.3, ...), custom_call_target="tpu_custom_call" | custom-call | bytes 3145728 | tf_op jit(solution)/shard_map/fetch_expert/pallas_call | solution.py:642
  24.1 0.0 collective-permute-done.10.refs_3_
  24.2 0.9 %collective-permute-done.9.refs_2_ = bf16[48,640]{1,0:T(8,128)(2,1)S(1)} collective-permute-done((bf16[48,640]{1,0:T(8,128)(2,1)S(1)}, bf16[48,640]{1,0:T(8,128)(2,1)S(1)}, u32[]{:S(2)}, u32[]{:S(2)}) %collective-permute-start.9) | collective-permute-done | bytes 61472 | tf_op jit(solution)/shard_map/ppermute | solution.py:532
  25.1 0.1 collective-permute-done.8.refs_1_
  25.1 0.0 collective-permute-done.11.refs_5_
  25.1 0.7 %project.1 = (bf16[32,8,256]{2,1,0:T(8,128)(2,1)S(1)}, f32[48,256]{1,0:T(8,128)S(1)}) custom-call(bf16[48,640]{1,0:T(8,128)(2,1)S(1)} %get-tuple-element.38.refs_0_, bf16[48,640]{1,0:T(8,128)(2,1)S(1)} %collective-permute-done.8.refs_1_, bf16[48,640]{1,0:T(8,128)(2,1)S(1)} %collective-permute-done.9.refs_2_, ...), custom_call_target="tpu_custom_call" | custom-call | tf_op jit(solution)/shard_map/project/pallas_call | solution.py:677
  25.9 13.8 %all_to_all.10.received_ref = bf16[32,8,256]{2,1,0:T(8,128)(2,1)S(1)} all-to-all(bf16[32,8,256]{2,1,0:T(8,128)(2,1)S(1)} %get-tuple-element.43), channel_id=1, replica_groups=mesh['seq'=8,'exp'=4] {'seq','exp'}, dimensions={0} | all-to-all | bytes 262144 | tf_op jit(solution)/shard_map/all_to_all | solution.py:686
  39.6 3.2 %expert.1 = (f32[32,512]{1,0:T(8,128)S(1)}, f32[32,512]{1,0:T(8,128)S(1)}) custom-call(bf16[32,8,256]{2,1,0:T(8,128)(2,1)S(1)} %all_to_all.10.received_ref, f32[1,1024]{1,0:T(1,128)S(1)} %bitcast.7, bf16[2,768,1024]{2,1,0:T(8,128)(2,1)S(1)} %get-tuple-element.44.piece_ref, bf16[2,1,1408,1024]{3,2,1,0:T(8,128)(2,1)} %in_ref.3, bf16[1,1408,1024]{2,1,0:T(8,128)(2,1)} %down_ref.1), custom_call_target="tpu_custom_call" | custom-call | tf_op jit(solution)/shard_map/expert/pallas_call | solution.py:690
  42.9 0.1 collective-permute-start.19
  43.0 1.2 %collective-permute-done.19.other_ref = f32[32,512]{1,0:T(8,128)S(1)} collective-permute-done((f32[32,512]{1,0:T(8,128)S(1)}, f32[32,512]{1,0:T(8,128)S(1)}, u32[]{:S(2)}, u32[]{:S(2)}) %collective-permute-start.19) | collective-permute-done | bytes 65568 | tf_op jit(solution)/shard_map/ppermute | solution.py:708
  44.2 0.7 %spread.1 = bf16[32,8,512]{2,1,0:T(8,128)(2,1)} custom-call(f32[32,512]{1,0:T(8,128)S(1)} %get-tuple-element.45.kept_ref, f32[32,512]{1,0:T(8,128)S(1)} %collective-permute-done.19.other_ref), custom_call_target="tpu_custom_call" | custom-call | tf_op jit(solution)/shard_map/spread/pallas_call | solution.py:716
  44.9 2.6 %all-to-all-start.1 = ((bf16[32,8,512]{2,1,0:T(8,128)(2,1)}), bf16[32,8,512]{2,1,0:T(8,128)(2,1)S(1)}, u32[]{:S(2)}, u32[]{:S(2)}) async-start(bf16[32,8,512]{2,1,0:T(8,128)(2,1)} %spread.1), calls=%async_computation.1 | async-start | bytes 524288 | tf_op jit(solution)/shard_map/all_to_all | solution.py:722
  47.5 2.6 %collective-permute-start.17 = (f32[48,256]{1,0:T(8,128)S(1)}, f32[48,256]{1,0:T(8,128)S(1)}, u32[]{:S(2)}, u32[]{:S(2)}) collective-permute-start(f32[48,256]{1,0:T(8,128)S(1)} %get-tuple-element.47.refs_0_), channel_id=1, source_target_pairs={{0,24},{4,28},{8,16},{12,20},{16,8},{20,12},{24,0},{28,4},{1,25},{... | collective-permute-start | bytes 147464 | tf_op jit(solution)/shard_map/ppermute | solution.py:532
  50.2 0.5 collective-permute-start.15
  50.7 0.4 collective-permute-start.13
  51.1 0.0 collective-permute-start.12
  51.1 2.8 %collective-permute-done.17.refs_6_ = f32[48,256]{1,0:T(8,128)S(1)} collective-permute-done((f32[48,256]{1,0:T(8,128)S(1)}, f32[48,256]{1,0:T(8,128)S(1)}, u32[]{:S(2)}, u32[]{:S(2)}) %collective-permute-start.17) | collective-permute-done | bytes 49184 | tf_op jit(solution)/shard_map/ppermute | solution.py:532
  53.9 0.0 collective-permute-start.18
  53.9 1.3 %collective-permute-done.15.refs_4_ = f32[48,256]{1,0:T(8,128)S(1)} collective-permute-done((f32[48,256]{1,0:T(8,128)S(1)}, f32[48,256]{1,0:T(8,128)S(1)}, u32[]{:S(2)}, u32[]{:S(2)}) %collective-permute-start.15) | collective-permute-done | bytes 49184 | tf_op jit(solution)/shard_map/ppermute | solution.py:532
  55.2 0.5 collective-permute-start.14
  55.7 0.7 %collective-permute-done.16.refs_5_ = f32[48,256]{1,0:T(8,128)S(1)} collective-permute-done((f32[48,256]{1,0:T(8,128)S(1)}, f32[48,256]{1,0:T(8,128)S(1)}, u32[]{:S(2)}, u32[]{:S(2)}) %collective-permute-start.16) | collective-permute-done | bytes 49184 | tf_op jit(solution)/shard_map/ppermute | solution.py:532
  56.4 0.2 collective-permute-done.14.refs_3_
  56.5 0.4 home.1
  56.9 0.8 %all-to-all-done.1 = bf16[32,8,512]{2,1,0:T(8,128)(2,1)S(1)} async-done(((bf16[32,8,512]{2,1,0:T(8,128)(2,1)}), bf16[32,8,512]{2,1,0:T(8,128)(2,1)S(1)}, u32[]{:S(2)}, u32[]{:S(2)}) %all-to-all-start.1) | async-done | bytes 262176 | tf_op jit(solution)/shard_map/all_to_all | solution.py:722
  57.7 0.8 %final.1 = bf16[12,4,1024]{2,1,0:T(4,128)(2,1)} custom-call(f32[48,128]{1,0:T(8,128)S(1)} %get-tuple-element.57.gates_ref, bf16[8,4,8,512]{3,2,1,0:T(8,128)(2,1)S(1)} %bitcast.5, f32[48,1024]{1,0:T(8,128)S(1)} %get-tuple-element.58.residual_ref), custom_call_target="tpu_custom_call" | custom-call | tf_op jit(solution)/shard_map/final/pallas_call | solution.py:739
  (15 shorter events, 0.0 us)
Async XLA Ops:
  0.0 11.4 %copy-start = (bf16[2,12,512,1024]{3,2,1,0:T(8,128)(2,1)S(1)}, bf16[2,12,512,1024]{3,2,1,0:T(8,128)(2,1)}, u32[]{:S(2)}) copy-start(bf16[2,12,512,1024]{3,2,1,0:T(8,128)(2,1)} %refs_9_.1) | copy-start | bytes 75497472
  1.7 5.9 %collective-permute-start.5 = (bf16[48,384]{1,0:T(8,128)(2,1)S(1)}, bf16[48,384]{1,0:T(8,128)(2,1)S(1)}, u32[]{:S(2)}, u32[]{:S(2)}) collective-permute-start(bf16[48,384]{1,0:T(8,128)(2,1)S(1)} %get-tuple-element.32.refs_0_), channel_id=1, source_target_pairs={{0,24},{4,28},{8,16},{12,20},{16,8},{20,12},{24,0},{28,4},{1,25},{... | collective-permute-start | bytes 110600 | tf_op jit(solution)/shard_map/ppermute | solution.py:532
  5.7 4.0 %collective-permute-start.3 = (bf16[48,384]{1,0:T(8,128)(2,1)S(1)}, bf16[48,384]{1,0:T(8,128)(2,1)S(1)}, u32[]{:S(2)}, u32[]{:S(2)}) collective-permute-start(bf16[48,384]{1,0:T(8,128)(2,1)S(1)} %get-tuple-element.32.refs_0_), channel_id=1, source_target_pairs={{0,16},{4,20},{8,24},{12,28},{16,0},{20,4},{24,8},{28,12},{1,17},{... | collective-permute-start | bytes 110600 | tf_op jit(solution)/shard_map/ppermute | solution.py:532
  6.2 4.0 %collective-permute-start.1 = (bf16[48,384]{1,0:T(8,128)(2,1)S(1)}, bf16[48,384]{1,0:T(8,128)(2,1)S(1)}, u32[]{:S(2)}, u32[]{:S(2)}) collective-permute-start(bf16[48,384]{1,0:T(8,128)(2,1)S(1)} %get-tuple-element.32.refs_0_), channel_id=1, source_target_pairs={{0,8},{4,12},{8,0},{12,4},{16,24},{20,28},{24,16},{28,20},{1,9},{5... | collective-permute-start | bytes 110600 | tf_op jit(solution)/shard_map/ppermute | solution.py:532
  6.3 3.8 %collective-permute-start = (bf16[48,384]{1,0:T(8,128)(2,1)S(1)}, bf16[48,384]{1,0:T(8,128)(2,1)S(1)}, u32[]{:S(2)}, u32[]{:S(2)}) collective-permute-start(bf16[48,384]{1,0:T(8,128)(2,1)S(1)} %get-tuple-element.32.refs_0_), channel_id=1, source_target_pairs={{0,4},{4,0},{8,12},{12,8},{16,20},{20,16},{24,28},{28,24},{1,5},{5... | collective-permute-start | bytes 110600 | tf_op jit(solution)/shard_map/ppermute | solution.py:532
  7.6 2.5 %collective-permute-start.6 = (bf16[48,384]{1,0:T(8,128)(2,1)S(1)}, bf16[48,384]{1,0:T(8,128)(2,1)S(1)}, u32[]{:S(2)}, u32[]{:S(2)}) collective-permute-start(bf16[48,384]{1,0:T(8,128)(2,1)S(1)} %collective-permute-done.5.refs_6_), channel_id=1, source_target_pairs={{0,4},{4,0},{8,12},{12,8},{16,20},{20,16},{24,28},{28,24},{1,5},{5... | collective-permute-start | bytes 110600 | tf_op jit(solution)/shard_map/ppermute | solution.py:532
  9.7 1.2 %collective-permute-start.4 = (bf16[48,384]{1,0:T(8,128)(2,1)S(1)}, bf16[48,384]{1,0:T(8,128)(2,1)S(1)}, u32[]{:S(2)}, u32[]{:S(2)}) collective-permute-start(bf16[48,384]{1,0:T(8,128)(2,1)S(1)} %collective-permute-done.3.refs_4_), channel_id=1, source_target_pairs={{0,4},{4,0},{8,12},{12,8},{16,20},{20,16},{24,28},{28,24},{1,5},{5... | collective-permute-start | bytes 110600 | tf_op jit(solution)/shard_map/ppermute | solution.py:532
  10.2 1.2 %collective-permute-start.2 = (bf16[48,384]{1,0:T(8,128)(2,1)S(1)}, bf16[48,384]{1,0:T(8,128)(2,1)S(1)}, u32[]{:S(2)}, u32[]{:S(2)}) collective-permute-start(bf16[48,384]{1,0:T(8,128)(2,1)S(1)} %collective-permute-done.1.refs_2_), channel_id=1, source_target_pairs={{0,4},{4,0},{8,12},{12,8},{16,20},{20,16},{24,28},{28,24},{1,5},{5... | collective-permute-start | bytes 110600 | tf_op jit(solution)/shard_map/ppermute | solution.py:532
  11.4 5.4 %copy-start.2 = (bf16[2,12,4,1024]{3,2,1,0:T(4,128)(2,1)S(1)}, bf16[2,12,4,1024]{3,2,1,0:T(4,128)(2,1)}, u32[]{:S(2)}) copy-start(bf16[2,12,4,1024]{3,2,1,0:T(4,128)(2,1)} %refs_8_.1) | copy-start | bytes 589828
  11.4 7.0 %copy-start.1 = (bf16[128,1024]{1,0:T(8,128)(2,1)S(1)}, bf16[128,1024]{1,0:T(8,128)(2,1)}, u32[]{:S(2)}) copy-start(bf16[128,1024]{1,0:T(8,128)(2,1)} %refs_4_.1) | copy-start | bytes 786436
  16.6 23.1 %copy-start.4 = (f32[1024]{0:T(1024)S(1)}, f32[1024]{0:T(1024)}, u32[]{:S(2)}) copy-start(f32[1024]{0:T(1024)} %param.20) | copy-start | bytes 12292
  16.6 1.3 %collective-permute-start.7 = (bf16[48,640]{1,0:T(8,128)(2,1)S(1)}, bf16[48,640]{1,0:T(8,128)(2,1)S(1)}, u32[]{:S(2)}, u32[]{:S(2)}) collective-permute-start(bf16[48,640]{1,0:T(8,128)(2,1)S(1)} %get-tuple-element.35), channel_id=1, source_target_pairs={{0,4},{4,0},{8,12},{12,8},{16,20},{20,16},{24,28},{28,24},{1,5},{5... | collective-permute-start | bytes 184328 | tf_op jit(solution)/shard_map/ppermute | solution.py:532
  18.4 6.8 %collective-permute-start.11 = (bf16[128,1024]{1,0:T(8,128)(2,1)S(1)}, bf16[128,1024]{1,0:T(8,128)(2,1)S(1)}, u32[]{:S(2)}, u32[]{:S(2)}) collective-permute-start(bf16[128,1024]{1,0:T(8,128)(2,1)S(1)} %copy-done.1), channel_id=1, source_target_pairs={{0,4},{4,0},{8,12},{12,8},{16,20},{20,16},{24,28},{28,24},{1,5},{5... | collective-permute-start | bytes 786440 | tf_op jit(solution)/shard_map/ppermute | solution.py:532
  18.6 5.5 %collective-permute-start.10 = (bf16[48,640]{1,0:T(8,128)(2,1)S(1)}, bf16[48,640]{1,0:T(8,128)(2,1)S(1)}, u32[]{:S(2)}, u32[]{:S(2)}) collective-permute-start(bf16[48,640]{1,0:T(8,128)(2,1)S(1)} %pair.1.sent_ref), channel_id=1, source_target_pairs={{0,24},{4,28},{8,16},{12,20},{16,8},{20,12},{24,0},{28,4},{1,25},{... | collective-permute-start | bytes 184328 | tf_op jit(solution)/shard_map/ppermute | solution.py:532
  20.1 5.0 %collective-permute-start.9 = (bf16[48,640]{1,0:T(8,128)(2,1)S(1)}, bf16[48,640]{1,0:T(8,128)(2,1)S(1)}, u32[]{:S(2)}, u32[]{:S(2)}) collective-permute-start(bf16[48,640]{1,0:T(8,128)(2,1)S(1)} %pair.1.sent_ref), channel_id=1, source_target_pairs={{0,16},{4,20},{8,24},{12,28},{16,0},{20,4},{24,8},{28,12},{1,17},{... | collective-permute-start | bytes 184328 | tf_op jit(solution)/shard_map/ppermute | solution.py:532
  20.5 4.7 %collective-permute-start.8 = (bf16[48,640]{1,0:T(8,128)(2,1)S(1)}, bf16[48,640]{1,0:T(8,128)(2,1)S(1)}, u32[]{:S(2)}, u32[]{:S(2)}) collective-permute-start(bf16[48,640]{1,0:T(8,128)(2,1)S(1)} %pair.1.sent_ref), channel_id=1, source_target_pairs={{0,8},{4,12},{8,0},{12,4},{16,24},{20,28},{24,16},{28,20},{1,9},{5... | collective-permute-start | bytes 184328 | tf_op jit(solution)/shard_map/ppermute | solution.py:532
  39.6 16.9 %copy-start.3 = (bf16[1024,16]{0,1:T(8,128)(2,1)S(1)}, bf16[1024,16]{0,1:T(8,128)(2,1)}, u32[]{:S(2)}) copy-start(bf16[1024,16]{0,1:T(8,128)(2,1)} %param.21) | copy-start | bytes 98308
  42.9 1.3 %collective-permute-start.19 = (f32[32,512]{1,0:T(8,128)S(1)}, f32[32,512]{1,0:T(8,128)S(1)}, u32[]{:S(2)}, u32[]{:S(2)}) collective-permute-start(f32[32,512]{1,0:T(8,128)S(1)} %get-tuple-element.46), channel_id=1, source_target_pairs={{0,4},{4,0},{8,12},{12,8},{16,20},{20,16},{24,28},{28,24},{1,5},{5... | collective-permute-start | bytes 196616 | tf_op jit(solution)/shard_map/ppermute | solution.py:708
  44.9 12.8 %all-to-all-start.1 = ((bf16[32,8,512]{2,1,0:T(8,128)(2,1)}), bf16[32,8,512]{2,1,0:T(8,128)(2,1)S(1)}, u32[]{:S(2)}, u32[]{:S(2)}) async-start(bf16[32,8,512]{2,1,0:T(8,128)(2,1)} %spread.1), calls=%async_computation.1 | async-start | bytes 524288 | tf_op jit(solution)/shard_map/all_to_all | solution.py:722
  47.5 6.4 %collective-permute-start.17 = (f32[48,256]{1,0:T(8,128)S(1)}, f32[48,256]{1,0:T(8,128)S(1)}, u32[]{:S(2)}, u32[]{:S(2)}) collective-permute-start(f32[48,256]{1,0:T(8,128)S(1)} %get-tuple-element.47.refs_0_), channel_id=1, source_target_pairs={{0,24},{4,28},{8,16},{12,20},{16,8},{20,12},{24,0},{28,4},{1,25},{... | collective-permute-start | bytes 147464 | tf_op jit(solution)/shard_map/ppermute | solution.py:532
  50.2 5.0 %collective-permute-start.15 = (f32[48,256]{1,0:T(8,128)S(1)}, f32[48,256]{1,0:T(8,128)S(1)}, u32[]{:S(2)}, u32[]{:S(2)}) collective-permute-start(f32[48,256]{1,0:T(8,128)S(1)} %get-tuple-element.47.refs_0_), channel_id=1, source_target_pairs={{0,16},{4,20},{8,24},{12,28},{16,0},{20,4},{24,8},{28,12},{1,17},{... | collective-permute-start | bytes 147464 | tf_op jit(solution)/shard_map/ppermute | solution.py:532
  50.7 4.5 %collective-permute-start.13 = (f32[48,256]{1,0:T(8,128)S(1)}, f32[48,256]{1,0:T(8,128)S(1)}, u32[]{:S(2)}, u32[]{:S(2)}) collective-permute-start(f32[48,256]{1,0:T(8,128)S(1)} %get-tuple-element.47.refs_0_), channel_id=1, source_target_pairs={{0,8},{4,12},{8,0},{12,4},{16,24},{20,28},{24,16},{28,20},{1,9},{5... | collective-permute-start | bytes 147464 | tf_op jit(solution)/shard_map/ppermute | solution.py:532
  51.1 4.6 %collective-permute-start.12 = (f32[48,256]{1,0:T(8,128)S(1)}, f32[48,256]{1,0:T(8,128)S(1)}, u32[]{:S(2)}, u32[]{:S(2)}) collective-permute-start(f32[48,256]{1,0:T(8,128)S(1)} %get-tuple-element.47.refs_0_), channel_id=1, source_target_pairs={{0,4},{4,0},{8,12},{12,8},{16,20},{20,16},{24,28},{28,24},{1,5},{5... | collective-permute-start | bytes 147464 | tf_op jit(solution)/shard_map/ppermute | solution.py:532
  53.9 1.8 %collective-permute-start.18 = (f32[48,256]{1,0:T(8,128)S(1)}, f32[48,256]{1,0:T(8,128)S(1)}, u32[]{:S(2)}, u32[]{:S(2)}) collective-permute-start(f32[48,256]{1,0:T(8,128)S(1)} %collective-permute-done.17.refs_6_), channel_id=1, source_target_pairs={{0,4},{4,0},{8,12},{12,8},{16,20},{20,16},{24,28},{28,24},{1,5},{5... | collective-permute-start | bytes 147464 | tf_op jit(solution)/shard_map/ppermute | solution.py:532
  55.1 1.2 %collective-permute-start.16 = (f32[48,256]{1,0:T(8,128)S(1)}, f32[48,256]{1,0:T(8,128)S(1)}, u32[]{:S(2)}, u32[]{:S(2)}) collective-permute-start(f32[48,256]{1,0:T(8,128)S(1)} %collective-permute-done.15.refs_4_), channel_id=1, source_target_pairs={{0,4},{4,0},{8,12},{12,8},{16,20},{20,16},{24,28},{28,24},{1,5},{5... | collective-permute-start | bytes 147464 | tf_op jit(solution)/shard_map/ppermute | solution.py:532
  55.2 1.4 %collective-permute-start.14 = (f32[48,256]{1,0:T(8,128)S(1)}, f32[48,256]{1,0:T(8,128)S(1)}, u32[]{:S(2)}, u32[]{:S(2)}) collective-permute-start(f32[48,256]{1,0:T(8,128)S(1)} %collective-permute-done.13.refs_2_), channel_id=1, source_target_pairs={{0,4},{4,0},{8,12},{12,8},{16,20},{20,16},{24,28},{28,24},{1,5},{5... | collective-permute-start | bytes 147464 | tf_op jit(solution)/shard_map/ppermute | solution.py:532

commit v10 on v9

--- a/solution.py
+++ b/solution.py
@@ -251,9 +251,9 @@
         copy.wait()
 
 
-def attention_kernel(*refs):
-    *mixed_refs, spans_ref, window_ref = refs[:-5]
-    keep_ref, send_ref, ordered_ref, flat_ref, result_ref = refs[-5:]
+def attention_kernel(of_own, *refs):
+    *mixed_refs, spans_ref, window_ref = refs[:-4]
+    out_ref, ordered_ref, flat_ref, result_ref = refs[-4:]
     devices, rows, share = ordered_ref.shape
     _, requests, span, width = window_ref.shape
     steps = rows // requests
@@ -263,20 +263,22 @@
     for d in range(devices):
         if d * share < width:
             flat_ref[:, d * share : (d + 1) * share] = ordered_ref[d].astype(jnp.float32)
-    own_head = head_masks(block_rows, width, steps)
+    own_head = head_masks(block_rows, HALF, steps)
+    half = place % CORES if of_own else 1 - place % CORES
+    heads = pl.ds(pl.multiple_of(half * HALF, HALF), HALF)
     base = place * span
     scale = HD ** (-0.5)
     pair = 2 * steps
-    tiles = HEADS * steps // pair
+    tiles = HALF_HEADS * steps // pair
     slot = base + lax.broadcasted_iota(jnp.int32, (pair, span), 1)
     step = lax.broadcasted_iota(jnp.int32, (pair, span), 0) % steps
-    stat_lane = lax.broadcasted_iota(jnp.int32, (HEADS * steps, LANES), 1)
-    stat_head = lax.broadcasted_iota(jnp.int32, (HEADS * steps, LANES), 0) // steps
-    cols = [slice(c, c + BLOCK) for c in range(0, width, BLOCK)]
+    stat_lane = lax.broadcasted_iota(jnp.int32, (HALF_HEADS * steps, LANES), 1)
+    stat_head = lax.broadcasted_iota(jnp.int32, (HALF_HEADS * steps, LANES), 0) // steps
+    cols = [slice(c, c + BLOCK) for c in range(0, HALF, BLOCK)]
 
     def score(r):
-        keys = window_ref.at[0, r]
-        queries = flat_ref[r * steps : (r + 1) * steps, 0:width]
+        keys = window_ref[0, r, :, heads]
+        queries = flat_ref[r * steps : (r + 1) * steps, heads]
         queries = (jnp.concatenate([queries] * BLOCK_HEADS, axis=0) * own_head).astype(jnp.bfloat16)
         return jnp.concatenate(
             [dot(queries[:, c], keys[:, c], ROWS_BY_ROWS) for c in cols], axis=0
@@ -292,29 +294,23 @@
         peak = jnp.max(scores, axis=-1, keepdims=True)
         weight = jnp.where(live, jnp.exp(scores - peak), 0.0)
         total = jnp.sum(weight, axis=-1, keepdims=True)
-        weight = weight.reshape(HEADS * steps, span).astype(jnp.bfloat16)
-        values = window_ref.at[1, r]
+        weight = weight.reshape(HALF_HEADS * steps, span).astype(jnp.bfloat16)
+        values = window_ref[1, r, :, heads]
         outs = []
         for b, c in enumerate(cols):
             own = slice(b * block_rows, (b + 1) * block_rows)
             mixed = dot(weight[own], values[:, c]) * own_head[:, c]
             mixed = sum(mixed[i : i + pair] for i in range(0, block_rows, pair))
             outs.append(mixed[:steps] + mixed[steps:])
-        stats = jnp.where(stat_lane == stat_head, peak.reshape(HEADS * steps, 1), 0.0)
-        stats = jnp.where(stat_lane == stat_head + HEADS, total.reshape(HEADS * steps, 1), stats)
+        stats = jnp.where(stat_lane == stat_head, peak.reshape(HALF_HEADS * steps, 1), 0.0)
+        stats = jnp.where(stat_lane == stat_head + HALF_HEADS, total.reshape(HALF_HEADS * steps, 1), stats)
         stats = jnp.sum(stats.reshape(tiles, pair, LANES), axis=0)
         outs.append(stats[:steps] + stats[steps:])
         result_ref[r * steps : (r + 1) * steps, :] = jnp.concatenate(outs, axis=1)
         scores = following
-    halves = []
-    for c in range(CORES):
-        first = width + c * HALF_HEADS
-        peak = result_ref[:, first : first + HALF_HEADS]
-        total = result_ref[:, first + HEADS : first + HEADS + HALF_HEADS]
-        halves.append(pack(peak, total, result_ref[:, c * HALF : (c + 1) * HALF]))
-    odd = place % CORES == 1
-    keep_ref[...] = jnp.where(odd, halves[1], halves[0])
-    send_ref[...] = jnp.where(odd, halves[0], halves[1])
+    peak = result_ref[:, HALF : HALF + HALF_HEADS]
+    total = result_ref[:, HALF + HALF_HEADS : HALF + 2 * HALF_HEADS]
+    out_ref[...] = pack(peak, total, result_ref[:, :HALF])
 
 
 def extra_kernel(*refs):
@@ -373,27 +369,30 @@
         stats_ref[r * steps : (r + 1) * steps, :] = stats[r]
 
 
-def pair_kernel(keep_ref, other_ref, extra_ref, extra_stats_ref, out_ref):
-    odd = lax.axis_index("seq") % CORES == 1
-    first = lax.axis_index("seq") // CORES == 0
-
-    def own_half(value, at, width):
-        return jnp.where(odd, value[:, at + width : at + 2 * width], value[:, at : at + width])
-
-    extra_peak = jnp.where(first, own_half(extra_stats_ref[...], 0, HALF_HEADS), MASKED)
-    extra_total = jnp.where(first, own_half(extra_stats_ref[...], HEADS, HALF_HEADS), 0.0)
-    extra = jnp.where(first, own_half(extra_ref[...], 0, HALF), 0.0)
-    parts = [unpack(keep_ref[...]), unpack(other_ref[...]), (extra_peak, extra_total, extra)]
-    out_ref[...] = pack(*merge(parts))
+def pair_kernel(keep_ref, other_ref, out_ref):
+    out_ref[...] = pack(*merge([unpack(keep_ref[...]), unpack(other_ref[...])]))
 
 
 def project_kernel(*refs):
-    *part_refs, weight_ref, other_weight_ref, columns_ref, turned_ref, out_ref, residual_ref = refs
+    *part_refs, extra_ref, extra_stats_ref, weight_ref, other_weight_ref, columns_ref = refs[:-3]
+    turned_ref, out_ref, residual_ref = refs[-3:]
     devices = lax.axis_size("seq")
     groups = lax.axis_size("exp")
     local_experts = EXPERTS // groups
     odd = lax.axis_index("seq") % CORES == 1
-    attended = attend([unpack(part_ref[...]) for part_ref in part_refs]).astype(jnp.bfloat16)
+
+    def own_half(value, at, width):
+        return jnp.where(odd, value[:, at + width : at + 2 * width], value[:, at : at + width])
+
+    parts = [unpack(part_ref[...]) for part_ref in part_refs]
+    parts.append(
+        (
+            own_half(extra_stats_ref[...], 0, HALF_HEADS),
+            own_half(extra_stats_ref[...], HEADS, HALF_HEADS),
+            own_half(extra_ref[...], 0, HALF),
+        )
+    )
+    attended = attend(parts).astype(jnp.bfloat16)
 
     def project(weight):
         weight = jnp.where(odd, weight[:, HALF:], weight[:, :HALF])
@@ -598,19 +597,23 @@
     mixed = gather_seq(local_mix)
 
     padded = width + LANES
-    kept, sent = pl.pallas_call(
-        attention_kernel,
-        in_specs=[vmem] * (seq_count + 2),
-        out_shape=(shape((rows, PACKED), bf16), shape((rows, PACKED), bf16)),
-        scratch_shapes=[
-            pltpu.VMEM((seq_count, rows, share), bf16),
-            pltpu.VMEM((rows, padded), f32),
-            pltpu.VMEM((rows, padded), f32),
-        ],
-        compiler_params=params(8),
-        name="attention",
-    )(*mixed, spans, window_cache)
+    def attention(of_own):
+        return pl.pallas_call(
+            functools.partial(attention_kernel, of_own),
+            in_specs=[vmem] * (seq_count + 2),
+            out_shape=shape((rows, PACKED), bf16),
+            scratch_shapes=[
+                pltpu.VMEM((seq_count, rows, share), bf16),
+                pltpu.VMEM((rows, padded), f32),
+                pltpu.VMEM((rows, PACKED), f32),
+            ],
+            compiler_params=params(8),
+            name="attention_own" if of_own else "attention_other",
+        )(*mixed, spans, window_cache)
+
+    sent = attention(False)
     other = exchange(sent, 1)
+    kept = attention(True)
 
     extra, extra_stats = pl.pallas_call(
         extra_kernel,
@@ -630,7 +633,7 @@
         out_shape=shape((rows, PACKED), bf16),
         compiler_params=params(8),
         name="pair",
-    )(kept, other, extra, extra_stats)
+    )(kept, other)
 
     hidden_units = expert_down.shape[1]
     held_units = min(HELD, hidden_units)
@@ -682,7 +685,7 @@
         ),
         compiler_params=params(16),
         name="project",
-    )(*parts, w_out, other_weight, token_columns, turned)
+    )(*parts, extra, extra_stats, w_out, other_weight, token_columns, turned)
     received = lax.all_to_all(outgoing, ("seq", "exp"), split_axis=0, concat_axis=0, tiled=True)
     columns = gather_seq(residual_columns)
 

time: 58.8 us -> 58.5 us (level)
  waiting for transfers between devices: 13.1 us -> 12 us
    ppermute x19, waiting for transfers between devices: 11.1 us -> 9.97 us  [exchange(): lax.ppermute(value, 'seq', [(i, i ^ bits) for i in range(lax.axis_size('s...]
    pallas_call x1 -> x2, Pallas kernels: 5.16 us -> 5.73 us  [attention(): pl.pallas_call(functools.partial(attention_kernel, of_own), in_specs=[vme...]
  transfers between devices with their start and end apart: 21 -> 21, of which waited for: 14 -> 11; matrix products, arithmetic and copies ran while one was open for 0% -> 0% of each run, Pallas kernels for 6% -> 11%
where the time goes in v10:
time: 58.5 us; the launch traced here: 58.2 us
  Pallas kernels  16.7 us (29%)
  starting transfers between devices  15.5 us (26%)
  blocking collectives  13.8 us (24%)
  waiting for transfers between devices  12 us (21%)
    all_to_all x1, blocking collectives, body(): lax.all_to_all(outgoing, ('seq', 'exp'), split_axis=0, concat_axis=0, til...  13.8 us
    ppermute x19, starting transfers between devices, exchange(): lax.ppermute(value, 'seq', [(i, i ^ bits) for i in range(lax.axis_size('s...  12.8 us
    ppermute x19, waiting for transfers between devices, exchange(): lax.ppermute(value, 'seq', [(i, i ^ bits) for i in range(lax.axis_size('s...  9.97 us
    pallas_call x2, Pallas kernels, attention(): pl.pallas_call(functools.partial(attention_kernel, of_own), in_specs=[vme...  5.73 us
    pallas_call x1, Pallas kernels, body(): pl.pallas_call(expert_kernel, in_specs=[vmem, vmem, vmem, hbm, hbm], out_...  3.24 us
    all_to_all x1, starting transfers between devices, body(): lax.all_to_all(outgoing, ('seq', 'exp'), split_axis=0, concat_axis=0, til...  2.58 us
    pallas_call x1, Pallas kernels, fetch_expert(): pl.pallas_call(fetch_expert_kernel, in_specs=[vmem] + [hbm] * 4, out_shap...  2.02 us
    pallas_call x1, Pallas kernels, body(): pl.pallas_call(qkv_kernel, in_specs=[hbm] * 5, out_shape=(shape((rows, sh...  1.73 us
  transfers between devices with their start and end apart: 21, of which 11 were waited for; matrix products, arithmetic and copies ran while one was open for 0% of the time, Pallas kernels for 11%

profile of v10, /device:TPU:0, one launch (start us, length us, event | category | flops | bytes accessed | tf_op | source)
XLA Modules:
  0.0 58.2 jit_solution(223770350250176767)
XLA Ops:
  0.0 1.7 %qkv.1 = (bf16[48,384]{1,0:T(8,128)(2,1)S(1)}, s32[12,128]{1,0:T(8,128)S(1)}) custom-call(bf16[12,4,1024]{2,1,0:T(4,128)(2,1)} %tokens_ref.3, f32[1,1024]{1,0:T(1,128)} %bitcast.9, bf16[384,1024]{1,0:T(8,128)(2,1)} %weight_ref.1, bf16[2,12,512,1024]{3,2,1,0:T(8,128)(2,1)} %refs_9_.3, s32[12]{0:T(128)} %lengths_ref.1), custom_call_target="tpu_custom_call" | custom-call | tf_op jit(solution)/shard_map/qkv/pallas_call | solution.py:581
  1.7 4.0 %collective-permute-start.5 = (bf16[48,384]{1,0:T(8,128)(2,1)S(1)}, bf16[48,384]{1,0:T(8,128)(2,1)S(1)}, u32[]{:S(2)}, u32[]{:S(2)}) collective-permute-start(bf16[48,384]{1,0:T(8,128)(2,1)S(1)} %get-tuple-element.30.refs_0_), channel_id=1, source_target_pairs={{0,24},{4,28},{8,16},{12,20},{16,8},{20,12},{24,0},{28,4},{1,25},{... | collective-permute-start | bytes 110600 | tf_op jit(solution)/shard_map/ppermute | solution.py:531
  5.7 0.5 collective-permute-start.3
  6.2 0.1 collective-permute-start.1
  6.3 0.0 collective-permute-start
  6.3 1.3 %collective-permute-done.5.refs_6_ = bf16[48,384]{1,0:T(8,128)(2,1)S(1)} collective-permute-done((bf16[48,384]{1,0:T(8,128)(2,1)S(1)}, bf16[48,384]{1,0:T(8,128)(2,1)S(1)}, u32[]{:S(2)}, u32[]{:S(2)}) %collective-permute-start.5) | collective-permute-done | bytes 36896 | tf_op jit(solution)/shard_map/ppermute | solution.py:531
  7.6 0.0 collective-permute-start.6
  7.6 2.0 %collective-permute-done.3.refs_4_ = bf16[48,384]{1,0:T(8,128)(2,1)S(1)} collective-permute-done((bf16[48,384]{1,0:T(8,128)(2,1)S(1)}, bf16[48,384]{1,0:T(8,128)(2,1)S(1)}, u32[]{:S(2)}, u32[]{:S(2)}) %collective-permute-start.3) | collective-permute-done | bytes 36896 | tf_op jit(solution)/shard_map/ppermute | solution.py:531
  9.7 0.5 collective-permute-done.1.refs_2_
  10.2 0.0 collective-permute-start.2
  10.2 0.0 collective-permute-done.6.refs_7_
  10.2 0.7 %collective-permute-done.4.refs_5_ = bf16[48,384]{1,0:T(8,128)(2,1)S(1)} collective-permute-done((bf16[48,384]{1,0:T(8,128)(2,1)S(1)}, bf16[48,384]{1,0:T(8,128)(2,1)S(1)}, u32[]{:S(2)}, u32[]{:S(2)}) %collective-permute-start.4) | collective-permute-done | bytes 36896 | tf_op jit(solution)/shard_map/ppermute | solution.py:531
  10.9 0.5 collective-permute-done.2.refs_3_
  11.4 2.9 %attention_other.1 = bf16[48,640]{1,0:T(8,128)(2,1)S(1)} custom-call(bf16[48,384]{1,0:T(8,128)(2,1)S(1)} %get-tuple-element.30.refs_0_, bf16[48,384]{1,0:T(8,128)(2,1)S(1)} %collective-permute-done.refs_1_, bf16[48,384]{1,0:T(8,128)(2,1)S(1)} %collective-permute-done.1.refs_2_, bf16[48,384]{1,0:T(8,128)(2,1)S(1)} %collective-permute-done.2.refs_3_, ...), custom_call_target="tpu_custom_call" | custom-call | tf_op jit(solution)/shard_map/attention_other/pallas_call | solution.py:601
  14.3 0.0 copy-start.1
  14.3 0.0 copy-start.2
  14.3 0.2 collective-permute-start.7
  14.5 2.9 %attention_own.1.keep_ref = bf16[48,640]{1,0:T(8,128)(2,1)S(1)} custom-call(bf16[48,384]{1,0:T(8,128)(2,1)S(1)} %get-tuple-element.30.refs_0_, bf16[48,384]{1,0:T(8,128)(2,1)S(1)} %collective-permute-done.refs_1_, bf16[48,384]{1,0:T(8,128)(2,1)S(1)} %collective-permute-done.1.refs_2_, bf16[48,384]{1,0:T(8,128)(2,1)S(1)} %collective-permute-done.2.refs_3_, ...), custom_call_target="tpu_custom_call" | custom-call | tf_op jit(solution)/shard_map/attention_own/pallas_call | solution.py:601
  17.4 0.0 copy-start.4
  17.4 0.0 collective-permute-done.7.other_ref
  17.4 0.3 pair.1.sent_ref
  17.7 0.4 collective-permute-start.11
  18.1 1.5 %collective-permute-start.10 = (bf16[48,640]{1,0:T(8,128)(2,1)S(1)}, bf16[48,640]{1,0:T(8,128)(2,1)S(1)}, u32[]{:S(2)}, u32[]{:S(2)}) collective-permute-start(bf16[48,640]{1,0:T(8,128)(2,1)S(1)} %pair.1.sent_ref), channel_id=1, source_target_pairs={{0,24},{4,28},{8,16},{12,20},{16,8},{20,12},{24,0},{28,4},{1,25},{... | collective-permute-start | bytes 184328 | tf_op jit(solution)/shard_map/ppermute | solution.py:531
  19.6 0.2 collective-permute-start.9
  19.8 1.8 %collective-permute-start.8 = (bf16[48,640]{1,0:T(8,128)(2,1)S(1)}, bf16[48,640]{1,0:T(8,128)(2,1)S(1)}, u32[]{:S(2)}, u32[]{:S(2)}) collective-permute-start(bf16[48,640]{1,0:T(8,128)(2,1)S(1)} %pair.1.sent_ref), channel_id=1, source_target_pairs={{0,8},{4,12},{8,0},{12,4},{16,24},{20,28},{24,16},{28,20},{1,9},{5... | collective-permute-start | bytes 184328 | tf_op jit(solution)/shard_map/ppermute | solution.py:531
  21.6 0.9 %extra.1 = (f32[48,1024]{1,0:T(8,128)S(1)}, f32[48,128]{1,0:T(8,128)S(1)}) custom-call(bf16[48,384]{1,0:T(8,128)(2,1)S(1)} %get-tuple-element.30.refs_0_, bf16[48,384]{1,0:T(8,128)(2,1)S(1)} %collective-permute-done.refs_1_, bf16[48,384]{1,0:T(8,128)(2,1)S(1)} %collective-permute-done.1.refs_2_, bf16[48,384]{1,0:T(8,128)(2,1)S(1)} %collective-permute-done.2.refs_3_, ...), custom_call_target="tpu_custom_call" | custom-call | tf_op jit(solution)/shard_map/extra/pallas_call | solution.py:618
  22.5 2.0 %fetch_expert.1 = (bf16[48,640]{1,0:T(8,128)(2,1)S(1)}, bf16[2,768,1024]{2,1,0:T(8,128)(2,1)S(1)}, f32[2,48,128]{2,1,0:T(8,128)S(1)}, f32[2,48,128]{2,1,0:T(8,12...) custom-call(bf16[48,640]{1,0:T(8,128)(2,1)S(1)} %pair.1.sent_ref, bf16[2,1,1408,1024]{3,2,1,0:T(8,128)(2,1)} %in_ref.3, ...), custom_call_target="tpu_custom_call" | custom-call | bytes 3145728 | tf_op jit(solution)/shard_map/fetch_expert/pallas_call | solution.py:645
  24.5 0.0 collective-permute-done.10.refs_3_
  24.5 0.0 collective-permute-done.9.refs_2_
  24.6 0.0 collective-permute-done.11.refs_7_
  24.6 0.9 %project.1 = (bf16[32,8,256]{2,1,0:T(8,128)(2,1)S(1)}, f32[48,256]{1,0:T(8,128)S(1)}) custom-call(bf16[48,640]{1,0:T(8,128)(2,1)S(1)} %get-tuple-element.32.refs_0_, bf16[48,640]{1,0:T(8,128)(2,1)S(1)} %collective-permute-done.8.refs_1_, bf16[48,640]{1,0:T(8,128)(2,1)S(1)} %collective-permute-done.9.refs_2_, ...), custom_call_target="tpu_custom_call" | custom-call | tf_op jit(solution)/shard_map/project/pallas_call | solution.py:680
  25.5 13.8 %all_to_all.10.received_ref = bf16[32,8,256]{2,1,0:T(8,128)(2,1)S(1)} all-to-all(bf16[32,8,256]{2,1,0:T(8,128)(2,1)S(1)} %get-tuple-element.39), channel_id=1, replica_groups=mesh['seq'=8,'exp'=4] {'seq','exp'}, dimensions={0} | all-to-all | bytes 262144 | tf_op jit(solution)/shard_map/all_to_all | solution.py:689
  39.3 3.2 %expert.1 = (f32[32,512]{1,0:T(8,128)S(1)}, f32[32,512]{1,0:T(8,128)S(1)}) custom-call(bf16[32,8,256]{2,1,0:T(8,128)(2,1)S(1)} %all_to_all.10.received_ref, f32[1,1024]{1,0:T(1,128)S(1)} %bitcast.7, bf16[2,768,1024]{2,1,0:T(8,128)(2,1)S(1)} %get-tuple-element.40.piece_ref, bf16[2,1,1408,1024]{3,2,1,0:T(8,128)(2,1)} %in_ref.3, bf16[1,1408,1024]{2,1,0:T(8,128)(2,1)} %down_ref.1), custom_call_target="tpu_custom_call" | custom-call | tf_op jit(solution)/shard_map/expert/pallas_call | solution.py:693
  42.5 0.1 collective-permute-start.19
  42.6 1.2 %collective-permute-done.19.other_ref = f32[32,512]{1,0:T(8,128)S(1)} collective-permute-done((f32[32,512]{1,0:T(8,128)S(1)}, f32[32,512]{1,0:T(8,128)S(1)}, u32[]{:S(2)}, u32[]{:S(2)}) %collective-permute-start.19) | collective-permute-done | bytes 65568 | tf_op jit(solution)/shard_map/ppermute | solution.py:711
  43.9 0.7 %spread.1 = bf16[32,8,512]{2,1,0:T(8,128)(2,1)} custom-call(f32[32,512]{1,0:T(8,128)S(1)} %get-tuple-element.41.kept_ref, f32[32,512]{1,0:T(8,128)S(1)} %collective-permute-done.19.other_ref), custom_call_target="tpu_custom_call" | custom-call | tf_op jit(solution)/shard_map/spread/pallas_call | solution.py:719
  44.6 2.6 %all-to-all-start.1 = ((bf16[32,8,512]{2,1,0:T(8,128)(2,1)}), bf16[32,8,512]{2,1,0:T(8,128)(2,1)S(1)}, u32[]{:S(2)}, u32[]{:S(2)}) async-start(bf16[32,8,512]{2,1,0:T(8,128)(2,1)} %spread.1), calls=%async_computation.1 | async-start | bytes 524288 | tf_op jit(solution)/shard_map/all_to_all | solution.py:725
  47.2 2.6 %collective-permute-start.17 = (f32[48,256]{1,0:T(8,128)S(1)}, f32[48,256]{1,0:T(8,128)S(1)}, u32[]{:S(2)}, u32[]{:S(2)}) collective-permute-start(f32[48,256]{1,0:T(8,128)S(1)} %get-tuple-element.43.refs_0_), channel_id=1, source_target_pairs={{0,24},{4,28},{8,16},{12,20},{16,8},{20,12},{24,0},{28,4},{1,25},{... | collective-permute-start | bytes 147464 | tf_op jit(solution)/shard_map/ppermute | solution.py:531
  49.8 0.5 collective-permute-start.15
  50.3 0.4 collective-permute-start.13
  50.7 2.8 %collective-permute-done.17.refs_6_ = f32[48,256]{1,0:T(8,128)S(1)} collective-permute-done((f32[48,256]{1,0:T(8,128)S(1)}, f32[48,256]{1,0:T(8,128)S(1)}, u32[]{:S(2)}, u32[]{:S(2)}) %collective-permute-start.17) | collective-permute-done | bytes 49184 | tf_op jit(solution)/shard_map/ppermute | solution.py:531
  53.5 1.3 %collective-permute-done.15.refs_4_ = f32[48,256]{1,0:T(8,128)S(1)} collective-permute-done((f32[48,256]{1,0:T(8,128)S(1)}, f32[48,256]{1,0:T(8,128)S(1)}, u32[]{:S(2)}, u32[]{:S(2)}) %collective-permute-start.15) | collective-permute-done | bytes 49184 | tf_op jit(solution)/shard_map/ppermute | solution.py:531
  54.8 0.5 collective-permute-start.14
  55.3 0.7 %collective-permute-done.16.refs_5_ = f32[48,256]{1,0:T(8,128)S(1)} collective-permute-done((f32[48,256]{1,0:T(8,128)S(1)}, f32[48,256]{1,0:T(8,128)S(1)}, u32[]{:S(2)}, u32[]{:S(2)}) %collective-permute-start.16) | collective-permute-done | bytes 49184 | tf_op jit(solution)/shard_map/ppermute | solution.py:531
  56.0 0.2 collective-permute-done.14.refs_3_
  56.2 0.4 home.1
  56.6 0.8 %all-to-all-done.1 = bf16[32,8,512]{2,1,0:T(8,128)(2,1)S(1)} async-done(((bf16[32,8,512]{2,1,0:T(8,128)(2,1)}), bf16[32,8,512]{2,1,0:T(8,128)(2,1)S(1)}, u32[]{:S(2)}, u32[]{:S(2)}) %all-to-all-start.1) | async-done | bytes 262176 | tf_op jit(solution)/shard_map/all_to_all | solution.py:725
  57.4 0.8 %final.1 = bf16[12,4,1024]{2,1,0:T(4,128)(2,1)} custom-call(f32[48,128]{1,0:T(8,128)S(1)} %get-tuple-element.53.gates_ref, bf16[8,4,8,512]{3,2,1,0:T(8,128)(2,1)S(1)} %bitcast.5, f32[48,1024]{1,0:T(8,128)S(1)} %get-tuple-element.54.residual_ref), custom_call_target="tpu_custom_call" | custom-call | tf_op jit(solution)/shard_map/final/pallas_call | solution.py:742
  (16 shorter events, 0.0 us)
Async XLA Ops:
  0.0 11.4 %copy-start = (bf16[2,12,512,1024]{3,2,1,0:T(8,128)(2,1)S(1)}, bf16[2,12,512,1024]{3,2,1,0:T(8,128)(2,1)}, u32[]{:S(2)}) copy-start(bf16[2,12,512,1024]{3,2,1,0:T(8,128)(2,1)} %refs_9_.3) | copy-start | bytes 75497472
  1.7 5.9 %collective-permute-start.5 = (bf16[48,384]{1,0:T(8,128)(2,1)S(1)}, bf16[48,384]{1,0:T(8,128)(2,1)S(1)}, u32[]{:S(2)}, u32[]{:S(2)}) collective-permute-start(bf16[48,384]{1,0:T(8,128)(2,1)S(1)} %get-tuple-element.30.refs_0_), channel_id=1, source_target_pairs={{0,24},{4,28},{8,16},{12,20},{16,8},{20,12},{24,0},{28,4},{1,25},{... | collective-permute-start | bytes 110600 | tf_op jit(solution)/shard_map/ppermute | solution.py:531
  5.7 4.0 %collective-permute-start.3 = (bf16[48,384]{1,0:T(8,128)(2,1)S(1)}, bf16[48,384]{1,0:T(8,128)(2,1)S(1)}, u32[]{:S(2)}, u32[]{:S(2)}) collective-permute-start(bf16[48,384]{1,0:T(8,128)(2,1)S(1)} %get-tuple-element.30.refs_0_), channel_id=1, source_target_pairs={{0,16},{4,20},{8,24},{12,28},{16,0},{20,4},{24,8},{28,12},{1,17},{... | collective-permute-start | bytes 110600 | tf_op jit(solution)/shard_map/ppermute | solution.py:531
  6.2 4.0 %collective-permute-start.1 = (bf16[48,384]{1,0:T(8,128)(2,1)S(1)}, bf16[48,384]{1,0:T(8,128)(2,1)S(1)}, u32[]{:S(2)}, u32[]{:S(2)}) collective-permute-start(bf16[48,384]{1,0:T(8,128)(2,1)S(1)} %get-tuple-element.30.refs_0_), channel_id=1, source_target_pairs={{0,8},{4,12},{8,0},{12,4},{16,24},{20,28},{24,16},{28,20},{1,9},{5... | collective-permute-start | bytes 110600 | tf_op jit(solution)/shard_map/ppermute | solution.py:531
  6.3 3.8 %collective-permute-start = (bf16[48,384]{1,0:T(8,128)(2,1)S(1)}, bf16[48,384]{1,0:T(8,128)(2,1)S(1)}, u32[]{:S(2)}, u32[]{:S(2)}) collective-permute-start(bf16[48,384]{1,0:T(8,128)(2,1)S(1)} %get-tuple-element.30.refs_0_), channel_id=1, source_target_pairs={{0,4},{4,0},{8,12},{12,8},{16,20},{20,16},{24,28},{28,24},{1,5},{5... | collective-permute-start | bytes 110600 | tf_op jit(solution)/shard_map/ppermute | solution.py:531
  7.6 2.5 %collective-permute-start.6 = (bf16[48,384]{1,0:T(8,128)(2,1)S(1)}, bf16[48,384]{1,0:T(8,128)(2,1)S(1)}, u32[]{:S(2)}, u32[]{:S(2)}) collective-permute-start(bf16[48,384]{1,0:T(8,128)(2,1)S(1)} %collective-permute-done.5.refs_6_), channel_id=1, source_target_pairs={{0,4},{4,0},{8,12},{12,8},{16,20},{20,16},{24,28},{28,24},{1,5},{5... | collective-permute-start | bytes 110600 | tf_op jit(solution)/shard_map/ppermute | solution.py:531
  9.7 1.2 %collective-permute-start.4 = (bf16[48,384]{1,0:T(8,128)(2,1)S(1)}, bf16[48,384]{1,0:T(8,128)(2,1)S(1)}, u32[]{:S(2)}, u32[]{:S(2)}) collective-permute-start(bf16[48,384]{1,0:T(8,128)(2,1)S(1)} %collective-permute-done.3.refs_4_), channel_id=1, source_target_pairs={{0,4},{4,0},{8,12},{12,8},{16,20},{20,16},{24,28},{28,24},{1,5},{5... | collective-permute-start | bytes 110600 | tf_op jit(solution)/shard_map/ppermute | solution.py:531
  10.2 1.2 %collective-permute-start.2 = (bf16[48,384]{1,0:T(8,128)(2,1)S(1)}, bf16[48,384]{1,0:T(8,128)(2,1)S(1)}, u32[]{:S(2)}, u32[]{:S(2)}) collective-permute-start(bf16[48,384]{1,0:T(8,128)(2,1)S(1)} %collective-permute-done.1.refs_2_), channel_id=1, source_target_pairs={{0,4},{4,0},{8,12},{12,8},{16,20},{20,16},{24,28},{28,24},{1,5},{5... | collective-permute-start | bytes 110600 | tf_op jit(solution)/shard_map/ppermute | solution.py:531
  14.3 3.4 %copy-start.1 = (bf16[128,1024]{1,0:T(8,128)(2,1)S(1)}, bf16[128,1024]{1,0:T(8,128)(2,1)}, u32[]{:S(2)}) copy-start(bf16[128,1024]{1,0:T(8,128)(2,1)} %refs_6_.1) | copy-start | bytes 786436
  14.3 7.3 %copy-start.2 = (bf16[2,12,4,1024]{3,2,1,0:T(4,128)(2,1)S(1)}, bf16[2,12,4,1024]{3,2,1,0:T(4,128)(2,1)}, u32[]{:S(2)}) copy-start(bf16[2,12,4,1024]{3,2,1,0:T(4,128)(2,1)} %refs_8_.1) | copy-start | bytes 589828
  14.3 3.1 %collective-permute-start.7 = (bf16[48,640]{1,0:T(8,128)(2,1)S(1)}, bf16[48,640]{1,0:T(8,128)(2,1)S(1)}, u32[]{:S(2)}, u32[]{:S(2)}) collective-permute-start(bf16[48,640]{1,0:T(8,128)(2,1)S(1)} %attention_other.1), channel_id=1, source_target_pairs={{0,4},{4,0},{8,12},{12,8},{16,20},{20,16},{24,28},{28,24},{1,5},{5... | collective-permute-start | bytes 184328 | tf_op jit(solution)/shard_map/ppermute | solution.py:531
  17.4 21.9 %copy-start.4 = (f32[1024]{0:T(1024)S(1)}, f32[1024]{0:T(1024)}, u32[]{:S(2)}) copy-start(f32[1024]{0:T(1024)} %param.20) | copy-start | bytes 12292
  17.7 6.9 %collective-permute-start.11 = (bf16[128,1024]{1,0:T(8,128)(2,1)S(1)}, bf16[128,1024]{1,0:T(8,128)(2,1)S(1)}, u32[]{:S(2)}, u32[]{:S(2)}) collective-permute-start(bf16[128,1024]{1,0:T(8,128)(2,1)S(1)} %copy-done.1), channel_id=1, source_target_pairs={{0,4},{4,0},{8,12},{12,8},{16,20},{20,16},{24,28},{28,24},{1,5},{5... | collective-permute-start | bytes 786440 | tf_op jit(solution)/shard_map/ppermute | solution.py:531
  18.1 6.4 %collective-permute-start.10 = (bf16[48,640]{1,0:T(8,128)(2,1)S(1)}, bf16[48,640]{1,0:T(8,128)(2,1)S(1)}, u32[]{:S(2)}, u32[]{:S(2)}) collective-permute-start(bf16[48,640]{1,0:T(8,128)(2,1)S(1)} %pair.1.sent_ref), channel_id=1, source_target_pairs={{0,24},{4,28},{8,16},{12,20},{16,8},{20,12},{24,0},{28,4},{1,25},{... | collective-permute-start | bytes 184328 | tf_op jit(solution)/shard_map/ppermute | solution.py:531
  19.6 5.0 %collective-permute-start.9 = (bf16[48,640]{1,0:T(8,128)(2,1)S(1)}, bf16[48,640]{1,0:T(8,128)(2,1)S(1)}, u32[]{:S(2)}, u32[]{:S(2)}) collective-permute-start(bf16[48,640]{1,0:T(8,128)(2,1)S(1)} %pair.1.sent_ref), channel_id=1, source_target_pairs={{0,16},{4,20},{8,24},{12,28},{16,0},{20,4},{24,8},{28,12},{1,17},{... | collective-permute-start | bytes 184328 | tf_op jit(solution)/shard_map/ppermute | solution.py:531
  19.8 4.8 %collective-permute-start.8 = (bf16[48,640]{1,0:T(8,128)(2,1)S(1)}, bf16[48,640]{1,0:T(8,128)(2,1)S(1)}, u32[]{:S(2)}, u32[]{:S(2)}) collective-permute-start(bf16[48,640]{1,0:T(8,128)(2,1)S(1)} %pair.1.sent_ref), channel_id=1, source_target_pairs={{0,8},{4,12},{8,0},{12,4},{16,24},{20,28},{24,16},{28,20},{1,9},{5... | collective-permute-start | bytes 184328 | tf_op jit(solution)/shard_map/ppermute | solution.py:531
  39.3 16.9 %copy-start.3 = (bf16[1024,16]{0,1:T(8,128)(2,1)S(1)}, bf16[1024,16]{0,1:T(8,128)(2,1)}, u32[]{:S(2)}) copy-start(bf16[1024,16]{0,1:T(8,128)(2,1)} %param.21) | copy-start | bytes 98308
  42.5 1.3 %collective-permute-start.19 = (f32[32,512]{1,0:T(8,128)S(1)}, f32[32,512]{1,0:T(8,128)S(1)}, u32[]{:S(2)}, u32[]{:S(2)}) collective-permute-start(f32[32,512]{1,0:T(8,128)S(1)} %get-tuple-element.42), channel_id=1, source_target_pairs={{0,4},{4,0},{8,12},{12,8},{16,20},{20,16},{24,28},{28,24},{1,5},{5... | collective-permute-start | bytes 196616 | tf_op jit(solution)/shard_map/ppermute | solution.py:711
  44.6 12.8 %all-to-all-start.1 = ((bf16[32,8,512]{2,1,0:T(8,128)(2,1)}), bf16[32,8,512]{2,1,0:T(8,128)(2,1)S(1)}, u32[]{:S(2)}, u32[]{:S(2)}) async-start(bf16[32,8,512]{2,1,0:T(8,128)(2,1)} %spread.1), calls=%async_computation.1 | async-start | bytes 524288 | tf_op jit(solution)/shard_map/all_to_all | solution.py:725
  47.2 6.4 %collective-permute-start.17 = (f32[48,256]{1,0:T(8,128)S(1)}, f32[48,256]{1,0:T(8,128)S(1)}, u32[]{:S(2)}, u32[]{:S(2)}) collective-permute-start(f32[48,256]{1,0:T(8,128)S(1)} %get-tuple-element.43.refs_0_), channel_id=1, source_target_pairs={{0,24},{4,28},{8,16},{12,20},{16,8},{20,12},{24,0},{28,4},{1,25},{... | collective-permute-start | bytes 147464 | tf_op jit(solution)/shard_map/ppermute | solution.py:531
  49.8 5.0 %collective-permute-start.15 = (f32[48,256]{1,0:T(8,128)S(1)}, f32[48,256]{1,0:T(8,128)S(1)}, u32[]{:S(2)}, u32[]{:S(2)}) collective-permute-start(f32[48,256]{1,0:T(8,128)S(1)} %get-tuple-element.43.refs_0_), channel_id=1, source_target_pairs={{0,16},{4,20},{8,24},{12,28},{16,0},{20,4},{24,8},{28,12},{1,17},{... | collective-permute-start | bytes 147464 | tf_op jit(solution)/shard_map/ppermute | solution.py:531
  50.3 4.5 %collective-permute-start.13 = (f32[48,256]{1,0:T(8,128)S(1)}, f32[48,256]{1,0:T(8,128)S(1)}, u32[]{:S(2)}, u32[]{:S(2)}) collective-permute-start(f32[48,256]{1,0:T(8,128)S(1)} %get-tuple-element.43.refs_0_), channel_id=1, source_target_pairs={{0,8},{4,12},{8,0},{12,4},{16,24},{20,28},{24,16},{28,20},{1,9},{5... | collective-permute-start | bytes 147464 | tf_op jit(solution)/shard_map/ppermute | solution.py:531
  50.7 4.6 %collective-permute-start.12 = (f32[48,256]{1,0:T(8,128)S(1)}, f32[48,256]{1,0:T(8,128)S(1)}, u32[]{:S(2)}, u32[]{:S(2)}) collective-permute-start(f32[48,256]{1,0:T(8,128)S(1)} %get-tuple-element.43.refs_0_), channel_id=1, source_target_pairs={{0,4},{4,0},{8,12},{12,8},{16,20},{20,16},{24,28},{28,24},{1,5},{5... | collective-permute-start | bytes 147464 | tf_op jit(solution)/shard_map/ppermute | solution.py:531
  53.5 1.8 %collective-permute-start.18 = (f32[48,256]{1,0:T(8,128)S(1)}, f32[48,256]{1,0:T(8,128)S(1)}, u32[]{:S(2)}, u32[]{:S(2)}) collective-permute-start(f32[48,256]{1,0:T(8,128)S(1)} %collective-permute-done.17.refs_6_), channel_id=1, source_target_pairs={{0,4},{4,0},{8,12},{12,8},{16,20},{20,16},{24,28},{28,24},{1,5},{5... | collective-permute-start | bytes 147464 | tf_op jit(solution)/shard_map/ppermute | solution.py:531
  54.8 1.2 %collective-permute-start.16 = (f32[48,256]{1,0:T(8,128)S(1)}, f32[48,256]{1,0:T(8,128)S(1)}, u32[]{:S(2)}, u32[]{:S(2)}) collective-permute-start(f32[48,256]{1,0:T(8,128)S(1)} %collective-permute-done.15.refs_4_), channel_id=1, source_target_pairs={{0,4},{4,0},{8,12},{12,8},{16,20},{20,16},{24,28},{28,24},{1,5},{5... | collective-permute-start | bytes 147464 | tf_op jit(solution)/shard_map/ppermute | solution.py:531
  54.8 1.4 %collective-permute-start.14 = (f32[48,256]{1,0:T(8,128)S(1)}, f32[48,256]{1,0:T(8,128)S(1)}, u32[]{:S(2)}, u32[]{:S(2)}) collective-permute-start(f32[48,256]{1,0:T(8,128)S(1)} %collective-permute-done.13.refs_2_), channel_id=1, source_target_pairs={{0,4},{4,0},{8,12},{12,8},{16,20},{20,16},{24,28},{28,24},{1,5},{5... | collective-permute-start | bytes 147464 | tf_op jit(solution)/shard_map/ppermute | solution.py:531

commit v11 on v10

--- a/solution.py
+++ b/solution.py
@@ -23,8 +23,8 @@
 HALF_HEADS = HEADS // CORES
 HALF = HALF_HEADS * HD
 PACKED = HALF + LANES
-HELD = 768
-PIECE = 320
+HELD = 800
+PIECE = 304
 AHEAD = 10
 BLOCK = 256
 BLOCK_HEADS = BLOCK // HD

time: 58.5 us -> 58.3 us (level)
  no operation moved by 1% of the time
where the time goes in v11:
time: 58.3 us; the launch traced here: 58 us
  Pallas kernels  16.6 us (28%)
  starting transfers between devices  15.5 us (27%)
  blocking collectives  13.8 us (24%)
  waiting for transfers between devices  12 us (21%)
    all_to_all x1, blocking collectives, body(): lax.all_to_all(outgoing, ('seq', 'exp'), split_axis=0, concat_axis=0, til...  13.8 us
    ppermute x19, starting transfers between devices, exchange(): lax.ppermute(value, 'seq', [(i, i ^ bits) for i in range(lax.axis_size('s...  12.8 us
    ppermute x19, waiting for transfers between devices, exchange(): lax.ppermute(value, 'seq', [(i, i ^ bits) for i in range(lax.axis_size('s...  9.97 us
    pallas_call x2, Pallas kernels, attention(): pl.pallas_call(functools.partial(attention_kernel, of_own), in_specs=[vme...  5.73 us
    pallas_call x1, Pallas kernels, body(): pl.pallas_call(expert_kernel, in_specs=[vmem, vmem, vmem, hbm, hbm], out_...  3.05 us
    all_to_all x1, starting transfers between devices, body(): lax.all_to_all(outgoing, ('seq', 'exp'), split_axis=0, concat_axis=0, til...  2.58 us
    pallas_call x1, Pallas kernels, fetch_expert(): pl.pallas_call(fetch_expert_kernel, in_specs=[vmem] + [hbm] * 4, out_shap...  2.06 us
    pallas_call x1, Pallas kernels, body(): pl.pallas_call(qkv_kernel, in_specs=[hbm] * 5, out_shape=(shape((rows, sh...  1.73 us
  transfers between devices with their start and end apart: 21, of which 11 were waited for; matrix products, arithmetic and copies ran while one was open for 0% of the time, Pallas kernels for 11%

profile of v11, /device:TPU:0, one launch (start us, length us, event | category | flops | bytes accessed | tf_op | source)
XLA Modules:
  0.0 58.0 jit_solution(5197181193364892562)
XLA Ops:
  0.0 1.7 %qkv.1 = (bf16[48,384]{1,0:T(8,128)(2,1)S(1)}, s32[12,128]{1,0:T(8,128)S(1)}) custom-call(bf16[12,4,1024]{2,1,0:T(4,128)(2,1)} %tokens_ref.3, f32[1,1024]{1,0:T(1,128)} %bitcast.9, bf16[384,1024]{1,0:T(8,128)(2,1)} %weight_ref.1, bf16[2,12,512,1024]{3,2,1,0:T(8,128)(2,1)} %refs_9_.3, s32[12]{0:T(128)} %lengths_ref.1), custom_call_target="tpu_custom_call" | custom-call | tf_op jit(solution)/shard_map/qkv/pallas_call | solution.py:581
  1.7 4.0 %collective-permute-start.5 = (bf16[48,384]{1,0:T(8,128)(2,1)S(1)}, bf16[48,384]{1,0:T(8,128)(2,1)S(1)}, u32[]{:S(2)}, u32[]{:S(2)}) collective-permute-start(bf16[48,384]{1,0:T(8,128)(2,1)S(1)} %get-tuple-element.30.refs_0_), channel_id=1, source_target_pairs={{0,24},{4,28},{8,16},{12,20},{16,8},{20,12},{24,0},{28,4},{1,25},{... | collective-permute-start | bytes 110600 | tf_op jit(solution)/shard_map/ppermute | solution.py:531
  5.7 0.5 collective-permute-start.3
  6.2 0.1 collective-permute-start.1
  6.3 1.3 %collective-permute-done.5.refs_6_ = bf16[48,384]{1,0:T(8,128)(2,1)S(1)} collective-permute-done((bf16[48,384]{1,0:T(8,128)(2,1)S(1)}, bf16[48,384]{1,0:T(8,128)(2,1)S(1)}, u32[]{:S(2)}, u32[]{:S(2)}) %collective-permute-start.5) | collective-permute-done | bytes 36896 | tf_op jit(solution)/shard_map/ppermute | solution.py:531
  7.6 0.0 collective-permute-start.6
  7.6 2.0 %collective-permute-done.3.refs_4_ = bf16[48,384]{1,0:T(8,128)(2,1)S(1)} collective-permute-done((bf16[48,384]{1,0:T(8,128)(2,1)S(1)}, bf16[48,384]{1,0:T(8,128)(2,1)S(1)}, u32[]{:S(2)}, u32[]{:S(2)}) %collective-permute-start.3) | collective-permute-done | bytes 36896 | tf_op jit(solution)/shard_map/ppermute | solution.py:531
  9.7 0.0 collective-permute-start.4
  9.7 0.5 collective-permute-done.1.refs_2_
  10.2 0.0 collective-permute-start.2
  10.2 0.0 collective-permute-done.refs_1_
  10.2 0.0 collective-permute-done.6.refs_7_
  10.2 0.7 %collective-permute-done.4.refs_5_ = bf16[48,384]{1,0:T(8,128)(2,1)S(1)} collective-permute-done((bf16[48,384]{1,0:T(8,128)(2,1)S(1)}, bf16[48,384]{1,0:T(8,128)(2,1)S(1)}, u32[]{:S(2)}, u32[]{:S(2)}) %collective-permute-start.4) | collective-permute-done | bytes 36896 | tf_op jit(solution)/shard_map/ppermute | solution.py:531
  10.9 0.5 collective-permute-done.2.refs_3_
  11.4 2.9 %attention_other.1 = bf16[48,640]{1,0:T(8,128)(2,1)S(1)} custom-call(bf16[48,384]{1,0:T(8,128)(2,1)S(1)} %get-tuple-element.30.refs_0_, bf16[48,384]{1,0:T(8,128)(2,1)S(1)} %collective-permute-done.refs_1_, bf16[48,384]{1,0:T(8,128)(2,1)S(1)} %collective-permute-done.1.refs_2_, bf16[48,384]{1,0:T(8,128)(2,1)S(1)} %collective-permute-done.2.refs_3_, ...), custom_call_target="tpu_custom_call" | custom-call | tf_op jit(solution)/shard_map/attention_other/pallas_call | solution.py:601
  14.3 0.0 copy-start.1
  14.3 0.0 copy-start.2
  14.3 0.2 collective-permute-start.7
  14.5 2.9 %attention_own.1.keep_ref = bf16[48,640]{1,0:T(8,128)(2,1)S(1)} custom-call(bf16[48,384]{1,0:T(8,128)(2,1)S(1)} %get-tuple-element.30.refs_0_, bf16[48,384]{1,0:T(8,128)(2,1)S(1)} %collective-permute-done.refs_1_, bf16[48,384]{1,0:T(8,128)(2,1)S(1)} %collective-permute-done.1.refs_2_, bf16[48,384]{1,0:T(8,128)(2,1)S(1)} %collective-permute-done.2.refs_3_, ...), custom_call_target="tpu_custom_call" | custom-call | tf_op jit(solution)/shard_map/attention_own/pallas_call | solution.py:601
  17.4 0.0 copy-start.4
  17.4 0.3 pair.1.sent_ref
  17.7 0.4 collective-permute-start.11
  18.1 1.5 %collective-permute-start.10 = (bf16[48,640]{1,0:T(8,128)(2,1)S(1)}, bf16[48,640]{1,0:T(8,128)(2,1)S(1)}, u32[]{:S(2)}, u32[]{:S(2)}) collective-permute-start(bf16[48,640]{1,0:T(8,128)(2,1)S(1)} %pair.1.sent_ref), channel_id=1, source_target_pairs={{0,24},{4,28},{8,16},{12,20},{16,8},{20,12},{24,0},{28,4},{1,25},{... | collective-permute-start | bytes 184328 | tf_op jit(solution)/shard_map/ppermute | solution.py:531
  19.6 0.2 collective-permute-start.9
  19.8 1.8 %collective-permute-start.8 = (bf16[48,640]{1,0:T(8,128)(2,1)S(1)}, bf16[48,640]{1,0:T(8,128)(2,1)S(1)}, u32[]{:S(2)}, u32[]{:S(2)}) collective-permute-start(bf16[48,640]{1,0:T(8,128)(2,1)S(1)} %pair.1.sent_ref), channel_id=1, source_target_pairs={{0,8},{4,12},{8,0},{12,4},{16,24},{20,28},{24,16},{28,20},{1,9},{5... | collective-permute-start | bytes 184328 | tf_op jit(solution)/shard_map/ppermute | solution.py:531
  21.6 0.9 %extra.1 = (f32[48,1024]{1,0:T(8,128)S(1)}, f32[48,128]{1,0:T(8,128)S(1)}) custom-call(bf16[48,384]{1,0:T(8,128)(2,1)S(1)} %get-tuple-element.30.refs_0_, bf16[48,384]{1,0:T(8,128)(2,1)S(1)} %collective-permute-done.refs_1_, bf16[48,384]{1,0:T(8,128)(2,1)S(1)} %collective-permute-done.1.refs_2_, bf16[48,384]{1,0:T(8,128)(2,1)S(1)} %collective-permute-done.2.refs_3_, ...), custom_call_target="tpu_custom_call" | custom-call | tf_op jit(solution)/shard_map/extra/pallas_call | solution.py:618
  22.5 2.1 %fetch_expert.1 = (bf16[48,640]{1,0:T(8,128)(2,1)S(1)}, bf16[2,800,1024]{2,1,0:T(8,128)(2,1)S(1)}, f32[2,48,128]{2,1,0:T(8,128)S(1)}, f32[2,48,128]{2,1,0:T(8,12...) custom-call(bf16[48,640]{1,0:T(8,128)(2,1)S(1)} %pair.1.sent_ref, bf16[2,1,1408,1024]{3,2,1,0:T(8,128)(2,1)} %in_ref.3, ...), custom_call_target="tpu_custom_call" | custom-call | bytes 3276800 | tf_op jit(solution)/shard_map/fetch_expert/pallas_call | solution.py:645
  24.6 0.0 collective-permute-done.10.refs_3_
  24.6 0.0 collective-permute-done.8.refs_1_
  24.6 0.0 collective-permute-done.11.refs_7_
  24.6 0.9 %project.1 = (bf16[32,8,256]{2,1,0:T(8,128)(2,1)S(1)}, f32[48,256]{1,0:T(8,128)S(1)}) custom-call(bf16[48,640]{1,0:T(8,128)(2,1)S(1)} %get-tuple-element.32.refs_0_, bf16[48,640]{1,0:T(8,128)(2,1)S(1)} %collective-permute-done.8.refs_1_, bf16[48,640]{1,0:T(8,128)(2,1)S(1)} %collective-permute-done.9.refs_2_, ...), custom_call_target="tpu_custom_call" | custom-call | tf_op jit(solution)/shard_map/project/pallas_call | solution.py:680
  25.5 13.8 %all_to_all.10.received_ref = bf16[32,8,256]{2,1,0:T(8,128)(2,1)S(1)} all-to-all(bf16[32,8,256]{2,1,0:T(8,128)(2,1)S(1)} %get-tuple-element.39), channel_id=1, replica_groups=mesh['seq'=8,'exp'=4] {'seq','exp'}, dimensions={0} | all-to-all | bytes 262144 | tf_op jit(solution)/shard_map/all_to_all | solution.py:689
  39.3 3.0 %expert.1 = (f32[32,512]{1,0:T(8,128)S(1)}, f32[32,512]{1,0:T(8,128)S(1)}) custom-call(bf16[32,8,256]{2,1,0:T(8,128)(2,1)S(1)} %all_to_all.10.received_ref, f32[1,1024]{1,0:T(1,128)S(1)} %bitcast.7, bf16[2,800,1024]{2,1,0:T(8,128)(2,1)S(1)} %get-tuple-element.40.piece_ref, bf16[2,1,1408,1024]{3,2,1,0:T(8,128)(2,1)} %in_ref.3, bf16[1,1408,1024]{2,1,0:T(8,128)(2,1)} %down_ref.1), custom_call_target="tpu_custom_call" | custom-call | tf_op jit(solution)/shard_map/expert/pallas_call | solution.py:693
  42.4 0.1 collective-permute-start.19
  42.4 1.2 %collective-permute-done.19.other_ref = f32[32,512]{1,0:T(8,128)S(1)} collective-permute-done((f32[32,512]{1,0:T(8,128)S(1)}, f32[32,512]{1,0:T(8,128)S(1)}, u32[]{:S(2)}, u32[]{:S(2)}) %collective-permute-start.19) | collective-permute-done | bytes 65568 | tf_op jit(solution)/shard_map/ppermute | solution.py:711
  43.7 0.7 %spread.1 = bf16[32,8,512]{2,1,0:T(8,128)(2,1)} custom-call(f32[32,512]{1,0:T(8,128)S(1)} %get-tuple-element.41.kept_ref, f32[32,512]{1,0:T(8,128)S(1)} %collective-permute-done.19.other_ref), custom_call_target="tpu_custom_call" | custom-call | tf_op jit(solution)/shard_map/spread/pallas_call | solution.py:719
  44.4 2.6 %all-to-all-start.1 = ((bf16[32,8,512]{2,1,0:T(8,128)(2,1)}), bf16[32,8,512]{2,1,0:T(8,128)(2,1)S(1)}, u32[]{:S(2)}, u32[]{:S(2)}) async-start(bf16[32,8,512]{2,1,0:T(8,128)(2,1)} %spread.1), calls=%async_computation.1 | async-start | bytes 524288 | tf_op jit(solution)/shard_map/all_to_all | solution.py:725
  47.0 2.6 %collective-permute-start.17 = (f32[48,256]{1,0:T(8,128)S(1)}, f32[48,256]{1,0:T(8,128)S(1)}, u32[]{:S(2)}, u32[]{:S(2)}) collective-permute-start(f32[48,256]{1,0:T(8,128)S(1)} %get-tuple-element.43.refs_0_), channel_id=1, source_target_pairs={{0,24},{4,28},{8,16},{12,20},{16,8},{20,12},{24,0},{28,4},{1,25},{... | collective-permute-start | bytes 147464 | tf_op jit(solution)/shard_map/ppermute | solution.py:531
  49.6 0.5 collective-permute-start.15
  50.1 0.4 collective-permute-start.13
  50.5 2.8 %collective-permute-done.17.refs_6_ = f32[48,256]{1,0:T(8,128)S(1)} collective-permute-done((f32[48,256]{1,0:T(8,128)S(1)}, f32[48,256]{1,0:T(8,128)S(1)}, u32[]{:S(2)}, u32[]{:S(2)}) %collective-permute-start.17) | collective-permute-done | bytes 49184 | tf_op jit(solution)/shard_map/ppermute | solution.py:531
  53.4 1.3 %collective-permute-done.15.refs_4_ = f32[48,256]{1,0:T(8,128)S(1)} collective-permute-done((f32[48,256]{1,0:T(8,128)S(1)}, f32[48,256]{1,0:T(8,128)S(1)}, u32[]{:S(2)}, u32[]{:S(2)}) %collective-permute-start.15) | collective-permute-done | bytes 49184 | tf_op jit(solution)/shard_map/ppermute | solution.py:531
  54.6 0.5 collective-permute-start.14
  55.1 0.7 %collective-permute-done.16.refs_5_ = f32[48,256]{1,0:T(8,128)S(1)} collective-permute-done((f32[48,256]{1,0:T(8,128)S(1)}, f32[48,256]{1,0:T(8,128)S(1)}, u32[]{:S(2)}, u32[]{:S(2)}) %collective-permute-start.16) | collective-permute-done | bytes 49184 | tf_op jit(solution)/shard_map/ppermute | solution.py:531
  55.8 0.2 collective-permute-done.14.refs_3_
  56.0 0.4 home.1
  56.4 0.8 %all-to-all-done.1 = bf16[32,8,512]{2,1,0:T(8,128)(2,1)S(1)} async-done(((bf16[32,8,512]{2,1,0:T(8,128)(2,1)}), bf16[32,8,512]{2,1,0:T(8,128)(2,1)S(1)}, u32[]{:S(2)}, u32[]{:S(2)}) %all-to-all-start.1) | async-done | bytes 262176 | tf_op jit(solution)/shard_map/all_to_all | solution.py:725
  57.2 0.8 %final.1 = bf16[12,4,1024]{2,1,0:T(4,128)(2,1)} custom-call(f32[48,128]{1,0:T(8,128)S(1)} %get-tuple-element.53.gates_ref, bf16[8,4,8,512]{3,2,1,0:T(8,128)(2,1)S(1)} %bitcast.5, f32[48,1024]{1,0:T(8,128)S(1)} %get-tuple-element.54.residual_ref), custom_call_target="tpu_custom_call" | custom-call | tf_op jit(solution)/shard_map/final/pallas_call | solution.py:742
  (16 shorter events, 0.0 us)
Async XLA Ops:
  0.0 11.4 %copy-start = (bf16[2,12,512,1024]{3,2,1,0:T(8,128)(2,1)S(1)}, bf16[2,12,512,1024]{3,2,1,0:T(8,128)(2,1)}, u32[]{:S(2)}) copy-start(bf16[2,12,512,1024]{3,2,1,0:T(8,128)(2,1)} %refs_9_.3) | copy-start | bytes 75497472
  1.7 5.9 %collective-permute-start.5 = (bf16[48,384]{1,0:T(8,128)(2,1)S(1)}, bf16[48,384]{1,0:T(8,128)(2,1)S(1)}, u32[]{:S(2)}, u32[]{:S(2)}) collective-permute-start(bf16[48,384]{1,0:T(8,128)(2,1)S(1)} %get-tuple-element.30.refs_0_), channel_id=1, source_target_pairs={{0,24},{4,28},{8,16},{12,20},{16,8},{20,12},{24,0},{28,4},{1,25},{... | collective-permute-start | bytes 110600 | tf_op jit(solution)/shard_map/ppermute | solution.py:531
  5.7 4.0 %collective-permute-start.3 = (bf16[48,384]{1,0:T(8,128)(2,1)S(1)}, bf16[48,384]{1,0:T(8,128)(2,1)S(1)}, u32[]{:S(2)}, u32[]{:S(2)}) collective-permute-start(bf16[48,384]{1,0:T(8,128)(2,1)S(1)} %get-tuple-element.30.refs_0_), channel_id=1, source_target_pairs={{0,16},{4,20},{8,24},{12,28},{16,0},{20,4},{24,8},{28,12},{1,17},{... | collective-permute-start | bytes 110600 | tf_op jit(solution)/shard_map/ppermute | solution.py:531
  6.2 4.0 %collective-permute-start.1 = (bf16[48,384]{1,0:T(8,128)(2,1)S(1)}, bf16[48,384]{1,0:T(8,128)(2,1)S(1)}, u32[]{:S(2)}, u32[]{:S(2)}) collective-permute-start(bf16[48,384]{1,0:T(8,128)(2,1)S(1)} %get-tuple-element.30.refs_0_), channel_id=1, source_target_pairs={{0,8},{4,12},{8,0},{12,4},{16,24},{20,28},{24,16},{28,20},{1,9},{5... | collective-permute-start | bytes 110600 | tf_op jit(solution)/shard_map/ppermute | solution.py:531
  6.3 3.8 %collective-permute-start = (bf16[48,384]{1,0:T(8,128)(2,1)S(1)}, bf16[48,384]{1,0:T(8,128)(2,1)S(1)}, u32[]{:S(2)}, u32[]{:S(2)}) collective-permute-start(bf16[48,384]{1,0:T(8,128)(2,1)S(1)} %get-tuple-element.30.refs_0_), channel_id=1, source_target_pairs={{0,4},{4,0},{8,12},{12,8},{16,20},{20,16},{24,28},{28,24},{1,5},{5... | collective-permute-start | bytes 110600 | tf_op jit(solution)/shard_map/ppermute | solution.py:531
  7.6 2.5 %collective-permute-start.6 = (bf16[48,384]{1,0:T(8,128)(2,1)S(1)}, bf16[48,384]{1,0:T(8,128)(2,1)S(1)}, u32[]{:S(2)}, u32[]{:S(2)}) collective-permute-start(bf16[48,384]{1,0:T(8,128)(2,1)S(1)} %collective-permute-done.5.refs_6_), channel_id=1, source_target_pairs={{0,4},{4,0},{8,12},{12,8},{16,20},{20,16},{24,28},{28,24},{1,5},{5... | collective-permute-start | bytes 110600 | tf_op jit(solution)/shard_map/ppermute | solution.py:531
  9.7 1.2 %collective-permute-start.4 = (bf16[48,384]{1,0:T(8,128)(2,1)S(1)}, bf16[48,384]{1,0:T(8,128)(2,1)S(1)}, u32[]{:S(2)}, u32[]{:S(2)}) collective-permute-start(bf16[48,384]{1,0:T(8,128)(2,1)S(1)} %collective-permute-done.3.refs_4_), channel_id=1, source_target_pairs={{0,4},{4,0},{8,12},{12,8},{16,20},{20,16},{24,28},{28,24},{1,5},{5... | collective-permute-start | bytes 110600 | tf_op jit(solution)/shard_map/ppermute | solution.py:531
  10.2 1.2 %collective-permute-start.2 = (bf16[48,384]{1,0:T(8,128)(2,1)S(1)}, bf16[48,384]{1,0:T(8,128)(2,1)S(1)}, u32[]{:S(2)}, u32[]{:S(2)}) collective-permute-start(bf16[48,384]{1,0:T(8,128)(2,1)S(1)} %collective-permute-done.1.refs_2_), channel_id=1, source_target_pairs={{0,4},{4,0},{8,12},{12,8},{16,20},{20,16},{24,28},{28,24},{1,5},{5... | collective-permute-start | bytes 110600 | tf_op jit(solution)/shard_map/ppermute | solution.py:531
  14.3 3.4 %copy-start.1 = (bf16[128,1024]{1,0:T(8,128)(2,1)S(1)}, bf16[128,1024]{1,0:T(8,128)(2,1)}, u32[]{:S(2)}) copy-start(bf16[128,1024]{1,0:T(8,128)(2,1)} %refs_6_.1) | copy-start | bytes 786436
  14.3 7.3 %copy-start.2 = (bf16[2,12,4,1024]{3,2,1,0:T(4,128)(2,1)S(1)}, bf16[2,12,4,1024]{3,2,1,0:T(4,128)(2,1)}, u32[]{:S(2)}) copy-start(bf16[2,12,4,1024]{3,2,1,0:T(4,128)(2,1)} %refs_8_.1) | copy-start | bytes 589828
  14.3 3.1 %collective-permute-start.7 = (bf16[48,640]{1,0:T(8,128)(2,1)S(1)}, bf16[48,640]{1,0:T(8,128)(2,1)S(1)}, u32[]{:S(2)}, u32[]{:S(2)}) collective-permute-start(bf16[48,640]{1,0:T(8,128)(2,1)S(1)} %attention_other.1), channel_id=1, source_target_pairs={{0,4},{4,0},{8,12},{12,8},{16,20},{20,16},{24,28},{28,24},{1,5},{5... | collective-permute-start | bytes 184328 | tf_op jit(solution)/shard_map/ppermute | solution.py:531
  17.4 21.9 %copy-start.4 = (f32[1024]{0:T(1024)S(1)}, f32[1024]{0:T(1024)}, u32[]{:S(2)}) copy-start(f32[1024]{0:T(1024)} %param.20) | copy-start | bytes 12292
  17.7 6.9 %collective-permute-start.11 = (bf16[128,1024]{1,0:T(8,128)(2,1)S(1)}, bf16[128,1024]{1,0:T(8,128)(2,1)S(1)}, u32[]{:S(2)}, u32[]{:S(2)}) collective-permute-start(bf16[128,1024]{1,0:T(8,128)(2,1)S(1)} %copy-done.1), channel_id=1, source_target_pairs={{0,4},{4,0},{8,12},{12,8},{16,20},{20,16},{24,28},{28,24},{1,5},{5... | collective-permute-start | bytes 786440 | tf_op jit(solution)/shard_map/ppermute | solution.py:531
  18.1 6.5 %collective-permute-start.10 = (bf16[48,640]{1,0:T(8,128)(2,1)S(1)}, bf16[48,640]{1,0:T(8,128)(2,1)S(1)}, u32[]{:S(2)}, u32[]{:S(2)}) collective-permute-start(bf16[48,640]{1,0:T(8,128)(2,1)S(1)} %pair.1.sent_ref), channel_id=1, source_target_pairs={{0,24},{4,28},{8,16},{12,20},{16,8},{20,12},{24,0},{28,4},{1,25},{... | collective-permute-start | bytes 184328 | tf_op jit(solution)/shard_map/ppermute | solution.py:531
  19.6 5.0 %collective-permute-start.9 = (bf16[48,640]{1,0:T(8,128)(2,1)S(1)}, bf16[48,640]{1,0:T(8,128)(2,1)S(1)}, u32[]{:S(2)}, u32[]{:S(2)}) collective-permute-start(bf16[48,640]{1,0:T(8,128)(2,1)S(1)} %pair.1.sent_ref), channel_id=1, source_target_pairs={{0,16},{4,20},{8,24},{12,28},{16,0},{20,4},{24,8},{28,12},{1,17},{... | collective-permute-start | bytes 184328 | tf_op jit(solution)/shard_map/ppermute | solution.py:531
  19.8 4.8 %collective-permute-start.8 = (bf16[48,640]{1,0:T(8,128)(2,1)S(1)}, bf16[48,640]{1,0:T(8,128)(2,1)S(1)}, u32[]{:S(2)}, u32[]{:S(2)}) collective-permute-start(bf16[48,640]{1,0:T(8,128)(2,1)S(1)} %pair.1.sent_ref), channel_id=1, source_target_pairs={{0,8},{4,12},{8,0},{12,4},{16,24},{20,28},{24,16},{28,20},{1,9},{5... | collective-permute-start | bytes 184328 | tf_op jit(solution)/shard_map/ppermute | solution.py:531
  39.3 16.7 %copy-start.3 = (bf16[1024,16]{0,1:T(8,128)(2,1)S(1)}, bf16[1024,16]{0,1:T(8,128)(2,1)}, u32[]{:S(2)}) copy-start(bf16[1024,16]{0,1:T(8,128)(2,1)} %param.21) | copy-start | bytes 98308
  42.4 1.3 %collective-permute-start.19 = (f32[32,512]{1,0:T(8,128)S(1)}, f32[32,512]{1,0:T(8,128)S(1)}, u32[]{:S(2)}, u32[]{:S(2)}) collective-permute-start(f32[32,512]{1,0:T(8,128)S(1)} %get-tuple-element.42), channel_id=1, source_target_pairs={{0,4},{4,0},{8,12},{12,8},{16,20},{20,16},{24,28},{28,24},{1,5},{5... | collective-permute-start | bytes 196616 | tf_op jit(solution)/shard_map/ppermute | solution.py:711
  44.4 12.8 %all-to-all-start.1 = ((bf16[32,8,512]{2,1,0:T(8,128)(2,1)}), bf16[32,8,512]{2,1,0:T(8,128)(2,1)S(1)}, u32[]{:S(2)}, u32[]{:S(2)}) async-start(bf16[32,8,512]{2,1,0:T(8,128)(2,1)} %spread.1), calls=%async_computation.1 | async-start | bytes 524288 | tf_op jit(solution)/shard_map/all_to_all | solution.py:725
  47.0 6.4 %collective-permute-start.17 = (f32[48,256]{1,0:T(8,128)S(1)}, f32[48,256]{1,0:T(8,128)S(1)}, u32[]{:S(2)}, u32[]{:S(2)}) collective-permute-start(f32[48,256]{1,0:T(8,128)S(1)} %get-tuple-element.43.refs_0_), channel_id=1, source_target_pairs={{0,24},{4,28},{8,16},{12,20},{16,8},{20,12},{24,0},{28,4},{1,25},{... | collective-permute-start | bytes 147464 | tf_op jit(solution)/shard_map/ppermute | solution.py:531
  49.6 5.0 %collective-permute-start.15 = (f32[48,256]{1,0:T(8,128)S(1)}, f32[48,256]{1,0:T(8,128)S(1)}, u32[]{:S(2)}, u32[]{:S(2)}) collective-permute-start(f32[48,256]{1,0:T(8,128)S(1)} %get-tuple-element.43.refs_0_), channel_id=1, source_target_pairs={{0,16},{4,20},{8,24},{12,28},{16,0},{20,4},{24,8},{28,12},{1,17},{... | collective-permute-start | bytes 147464 | tf_op jit(solution)/shard_map/ppermute | solution.py:531
  50.1 4.5 %collective-permute-start.13 = (f32[48,256]{1,0:T(8,128)S(1)}, f32[48,256]{1,0:T(8,128)S(1)}, u32[]{:S(2)}, u32[]{:S(2)}) collective-permute-start(f32[48,256]{1,0:T(8,128)S(1)} %get-tuple-element.43.refs_0_), channel_id=1, source_target_pairs={{0,8},{4,12},{8,0},{12,4},{16,24},{20,28},{24,16},{28,20},{1,9},{5... | collective-permute-start | bytes 147464 | tf_op jit(solution)/shard_map/ppermute | solution.py:531
  50.5 4.6 %collective-permute-start.12 = (f32[48,256]{1,0:T(8,128)S(1)}, f32[48,256]{1,0:T(8,128)S(1)}, u32[]{:S(2)}, u32[]{:S(2)}) collective-permute-start(f32[48,256]{1,0:T(8,128)S(1)} %get-tuple-element.43.refs_0_), channel_id=1, source_target_pairs={{0,4},{4,0},{8,12},{12,8},{16,20},{20,16},{24,28},{28,24},{1,5},{5... | collective-permute-start | bytes 147464 | tf_op jit(solution)/shard_map/ppermute | solution.py:531
  53.3 1.8 %collective-permute-start.18 = (f32[48,256]{1,0:T(8,128)S(1)}, f32[48,256]{1,0:T(8,128)S(1)}, u32[]{:S(2)}, u32[]{:S(2)}) collective-permute-start(f32[48,256]{1,0:T(8,128)S(1)} %collective-permute-done.17.refs_6_), channel_id=1, source_target_pairs={{0,4},{4,0},{8,12},{12,8},{16,20},{20,16},{24,28},{28,24},{1,5},{5... | collective-permute-start | bytes 147464 | tf_op jit(solution)/shard_map/ppermute | solution.py:531
  54.6 1.2 %collective-permute-start.16 = (f32[48,256]{1,0:T(8,128)S(1)}, f32[48,256]{1,0:T(8,128)S(1)}, u32[]{:S(2)}, u32[]{:S(2)}) collective-permute-start(f32[48,256]{1,0:T(8,128)S(1)} %collective-permute-done.15.refs_4_), channel_id=1, source_target_pairs={{0,4},{4,0},{8,12},{12,8},{16,20},{20,16},{24,28},{28,24},{1,5},{5... | collective-permute-start | bytes 147464 | tf_op jit(solution)/shard_map/ppermute | solution.py:531
  54.6 1.4 %collective-permute-start.14 = (f32[48,256]{1,0:T(8,128)S(1)}, f32[48,256]{1,0:T(8,128)S(1)}, u32[]{:S(2)}, u32[]{:S(2)}) collective-permute-start(f32[48,256]{1,0:T(8,128)S(1)} %collective-permute-done.13.refs_2_), channel_id=1, source_target_pairs={{0,4},{4,0},{8,12},{12,8},{16,20},{20,16},{24,28},{28,24},{1,5},{5... | collective-permute-start | bytes 147464 | tf_op jit(solution)/shard_map/ppermute | solution.py:531

commit v12 on v11

--- a/solution.py
+++ b/solution.py
@@ -252,17 +252,22 @@
 
 
 def attention_kernel(of_own, *refs):
-    *mixed_refs, spans_ref, window_ref = refs[:-4]
-    out_ref, ordered_ref, flat_ref, result_ref = refs[-4:]
-    devices, rows, share = ordered_ref.shape
+    if of_own:
+        flat_ref, spans_ref, window_ref, out_ref, result_ref = refs
+    else:
+        *mixed_refs, spans_ref, window_ref = refs[:-4]
+        out_ref, flat_ref, ordered_ref, result_ref = refs[-4:]
+        devices, _, share = ordered_ref.shape
+    rows = result_ref.shape[0]
     _, requests, span, width = window_ref.shape
     steps = rows // requests
     block_rows = BLOCK_HEADS * steps
     place = lax.axis_index("seq")
-    in_order(mixed_refs, ordered_ref)
-    for d in range(devices):
-        if d * share < width:
-            flat_ref[:, d * share : (d + 1) * share] = ordered_ref[d].astype(jnp.float32)
+    if not of_own:
+        in_order(mixed_refs, ordered_ref)
+        for d in range(devices):
+            if d * share < width:
+                flat_ref[:, d * share : (d + 1) * share] = ordered_ref[d].astype(jnp.float32)
     own_head = head_masks(block_rows, HALF, steps)
     half = place % CORES if of_own else 1 - place % CORES
     heads = pl.ds(pl.multiple_of(half * HALF, HALF), HALF)
@@ -597,23 +602,29 @@
     mixed = gather_seq(local_mix)
 
     padded = width + LANES
-    def attention(of_own):
-        return pl.pallas_call(
-            functools.partial(attention_kernel, of_own),
-            in_specs=[vmem] * (seq_count + 2),
-            out_shape=shape((rows, PACKED), bf16),
-            scratch_shapes=[
-                pltpu.VMEM((seq_count, rows, share), bf16),
-                pltpu.VMEM((rows, padded), f32),
-                pltpu.VMEM((rows, PACKED), f32),
-            ],
-            compiler_params=params(8),
-            name="attention_own" if of_own else "attention_other",
-        )(*mixed, spans, window_cache)
-
-    sent = attention(False)
+    packed_shape = shape((rows, PACKED), bf16)
+    sent, queries = pl.pallas_call(
+        functools.partial(attention_kernel, False),
+        in_specs=[vmem] * (seq_count + 2),
+        out_shape=(packed_shape, shape((rows, padded), f32)),
+        scratch_shapes=[
+            pltpu.VMEM((seq_count, rows, share), bf16),
+            pltpu.VMEM((rows, PACKED), f32),
+        ],
+        compiler_params=params(8),
+        cost_estimate=moving(2 * window_cache.size),
+        name="attention_other",
+    )(*mixed, spans, window_cache)
     other = exchange(sent, 1)
-    kept = attention(True)
+    kept = pl.pallas_call(
+        functools.partial(attention_kernel, True),
+        in_specs=[vmem] * 3,
+        out_shape=packed_shape,
+        scratch_shapes=[pltpu.VMEM((rows, PACKED), f32)],
+        compiler_params=params(8),
+        cost_estimate=moving(2 * window_cache.size),
+        name="attention_own",
+    )(queries, spans, window_cache)
 
     extra, extra_stats = pl.pallas_call(
         extra_kernel,

time: 58.3 us -> 58.2 us (level)
  no operation moved by 1% of the time
where the time goes in v12:
time: 58.2 us; the launch traced here: 58 us
  Pallas kernels  16.6 us (29%)
  starting transfers between devices  15.5 us (27%)
  blocking collectives  13.8 us (24%)
  waiting for transfers between devices  12 us (21%)
    all_to_all x1, blocking collectives, body(): lax.all_to_all(outgoing, ('seq', 'exp'), split_axis=0, concat_axis=0, til...  13.8 us
    ppermute x19, starting transfers between devices, exchange(): lax.ppermute(value, 'seq', [(i, i ^ bits) for i in range(lax.axis_size('s...  12.8 us
    ppermute x19, waiting for transfers between devices, exchange(): lax.ppermute(value, 'seq', [(i, i ^ bits) for i in range(lax.axis_size('s...  9.97 us
    pallas_call x1, Pallas kernels, body(): pl.pallas_call(expert_kernel, in_specs=[vmem, vmem, vmem, hbm, hbm], out_...  3.05 us
    pallas_call x1, Pallas kernels, body(): pl.pallas_call(functools.partial(attention_kernel, False), in_specs=[vmem...  2.86 us
    pallas_call x1, Pallas kernels, body(): pl.pallas_call(functools.partial(attention_kernel, True), in_specs=[vmem]...  2.85 us
    all_to_all x1, starting transfers between devices, body(): lax.all_to_all(outgoing, ('seq', 'exp'), split_axis=0, concat_axis=0, til...  2.58 us
    pallas_call x1, Pallas kernels, fetch_expert(): pl.pallas_call(fetch_expert_kernel, in_specs=[vmem] + [hbm] * 4, out_shap...  2.06 us
  transfers between devices with their start and end apart: 21, of which 11 were waited for; matrix products, arithmetic and copies ran while one was open for 0% of the time, Pallas kernels for 11%

profile of v12, /device:TPU:0, one launch (start us, length us, event | category | flops | bytes accessed | tf_op | source)
XLA Modules:
  0.0 58.0 jit_solution(606889834732745956)
XLA Ops:
  0.0 1.7 %qkv.1 = (bf16[48,384]{1,0:T(8,128)(2,1)S(1)}, s32[12,128]{1,0:T(8,128)S(1)}) custom-call(bf16[12,4,1024]{2,1,0:T(4,128)(2,1)} %tokens_ref.3, f32[1,1024]{1,0:T(1,128)} %bitcast.9, bf16[384,1024]{1,0:T(8,128)(2,1)} %weight_ref.1, bf16[2,12,512,1024]{3,2,1,0:T(8,128)(2,1)} %refs_2_.1, s32[12]{0:T(128)} %lengths_ref.1), custom_call_target="tpu_custom_call" | custom-call | tf_op jit(solution)/shard_map/qkv/pallas_call | solution.py:586
  1.7 4.0 %collective-permute-start.5 = (bf16[48,384]{1,0:T(8,128)(2,1)S(1)}, bf16[48,384]{1,0:T(8,128)(2,1)S(1)}, u32[]{:S(2)}, u32[]{:S(2)}) collective-permute-start(bf16[48,384]{1,0:T(8,128)(2,1)S(1)} %get-tuple-element.32.refs_0_), channel_id=1, source_target_pairs={{0,24},{4,28},{8,16},{12,20},{16,8},{20,12},{24,0},{28,4},{1,25},{... | collective-permute-start | bytes 110600 | tf_op jit(solution)/shard_map/ppermute | solution.py:536
  5.7 0.5 collective-permute-start.3
  6.2 0.1 collective-permute-start.1
  6.3 0.0 collective-permute-start
  6.3 1.3 %collective-permute-done.5.refs_6_ = bf16[48,384]{1,0:T(8,128)(2,1)S(1)} collective-permute-done((bf16[48,384]{1,0:T(8,128)(2,1)S(1)}, bf16[48,384]{1,0:T(8,128)(2,1)S(1)}, u32[]{:S(2)}, u32[]{:S(2)}) %collective-permute-start.5) | collective-permute-done | bytes 36896 | tf_op jit(solution)/shard_map/ppermute | solution.py:536
  7.6 0.0 collective-permute-start.6
  7.6 2.0 %collective-permute-done.3.refs_4_ = bf16[48,384]{1,0:T(8,128)(2,1)S(1)} collective-permute-done((bf16[48,384]{1,0:T(8,128)(2,1)S(1)}, bf16[48,384]{1,0:T(8,128)(2,1)S(1)}, u32[]{:S(2)}, u32[]{:S(2)}) %collective-permute-start.3) | collective-permute-done | bytes 36896 | tf_op jit(solution)/shard_map/ppermute | solution.py:536
  9.7 0.5 collective-permute-done.1.refs_2_
  10.2 0.0 collective-permute-start.2
  10.2 0.0 collective-permute-done.6.refs_7_
  10.2 0.7 %collective-permute-done.4.refs_5_ = bf16[48,384]{1,0:T(8,128)(2,1)S(1)} collective-permute-done((bf16[48,384]{1,0:T(8,128)(2,1)S(1)}, bf16[48,384]{1,0:T(8,128)(2,1)S(1)}, u32[]{:S(2)}, u32[]{:S(2)}) %collective-permute-start.4) | collective-permute-done | bytes 36896 | tf_op jit(solution)/shard_map/ppermute | solution.py:536
  10.9 0.5 collective-permute-done.2.refs_3_
  11.4 2.9 %attention_other.1 = (bf16[48,640]{1,0:T(8,128)(2,1)S(1)}, f32[48,1152]{1,0:T(8,128)S(1)}) custom-call(bf16[48,384]{1,0:T(8,128)(2,1)S(1)} %get-tuple-element.32.refs_0_, bf16[48,384]{1,0:T(8,128)(2,1)S(1)} %collective-permute-done.refs_1_, bf16[48,384]{1,0:T(8,128)(2,1)S(1)} %collective-permute-done.1.refs_2_, ...), custom_call_target="tpu_custom_call" | custom-call | bytes 25165824 | tf_op jit(solution)/shard_map/attention_other/pallas_call | solution.py:606
  14.3 0.2 collective-permute-start.7
  14.5 2.9 %attention_own.1.keep_ref = bf16[48,640]{1,0:T(8,128)(2,1)S(1)} custom-call(f32[48,1152]{1,0:T(8,128)S(1)} %get-tuple-element.34.refs_0_, s32[12,128]{1,0:T(8,128)S(1)} %get-tuple-element.33.refs_8_.refs_1_, bf16[2,12,512,1024]{3,2,1,0:T(8,128)(2,1)S(1)} %copy-done), custom_call_target="tpu_custom_call" | custom-call | bytes 25165824 | tf_op jit(solution)/shard_map/attention_own/pallas_call | solution.py:619
  17.3 0.0 copy-start.4
  17.3 0.0 collective-permute-done.7.other_ref
  17.4 0.3 pair.1.sent_ref
  17.7 0.4 collective-permute-start.11
  18.1 1.5 %collective-permute-start.10 = (bf16[48,640]{1,0:T(8,128)(2,1)S(1)}, bf16[48,640]{1,0:T(8,128)(2,1)S(1)}, u32[]{:S(2)}, u32[]{:S(2)}) collective-permute-start(bf16[48,640]{1,0:T(8,128)(2,1)S(1)} %pair.1.sent_ref), channel_id=1, source_target_pairs={{0,24},{4,28},{8,16},{12,20},{16,8},{20,12},{24,0},{28,4},{1,25},{... | collective-permute-start | bytes 184328 | tf_op jit(solution)/shard_map/ppermute | solution.py:536
  19.6 0.2 collective-permute-start.9
  19.7 1.8 %collective-permute-start.8 = (bf16[48,640]{1,0:T(8,128)(2,1)S(1)}, bf16[48,640]{1,0:T(8,128)(2,1)S(1)}, u32[]{:S(2)}, u32[]{:S(2)}) collective-permute-start(bf16[48,640]{1,0:T(8,128)(2,1)S(1)} %pair.1.sent_ref), channel_id=1, source_target_pairs={{0,8},{4,12},{8,0},{12,4},{16,24},{20,28},{24,16},{28,20},{1,9},{5... | collective-permute-start | bytes 184328 | tf_op jit(solution)/shard_map/ppermute | solution.py:536
  21.6 0.9 %extra.1 = (f32[48,1024]{1,0:T(8,128)S(1)}, f32[48,128]{1,0:T(8,128)S(1)}) custom-call(bf16[48,384]{1,0:T(8,128)(2,1)S(1)} %get-tuple-element.32.refs_0_, bf16[48,384]{1,0:T(8,128)(2,1)S(1)} %collective-permute-done.refs_1_, bf16[48,384]{1,0:T(8,128)(2,1)S(1)} %collective-permute-done.1.refs_2_, bf16[48,384]{1,0:T(8,128)(2,1)S(1)} %collective-permute-done.2.refs_3_, ...), custom_call_target="tpu_custom_call" | custom-call | tf_op jit(solution)/shard_map/extra/pallas_call | solution.py:629
  22.5 2.1 %fetch_expert.1 = (bf16[48,640]{1,0:T(8,128)(2,1)S(1)}, bf16[2,800,1024]{2,1,0:T(8,128)(2,1)S(1)}, f32[2,48,128]{2,1,0:T(8,128)S(1)}, f32[2,48,128]{2,1,0:T(8,12...) custom-call(bf16[48,640]{1,0:T(8,128)(2,1)S(1)} %pair.1.sent_ref, bf16[2,1,1408,1024]{3,2,1,0:T(8,128)(2,1)} %in_ref.3, ...), custom_call_target="tpu_custom_call" | custom-call | bytes 3276800 | tf_op jit(solution)/shard_map/fetch_expert/pallas_call | solution.py:656
  24.5 0.0 collective-permute-done.10.refs_3_
  24.6 0.0 collective-permute-done.8.refs_1_
  24.6 0.0 collective-permute-done.11.refs_7_
  24.6 0.9 %project.1 = (bf16[32,8,256]{2,1,0:T(8,128)(2,1)S(1)}, f32[48,256]{1,0:T(8,128)S(1)}) custom-call(bf16[48,640]{1,0:T(8,128)(2,1)S(1)} %get-tuple-element.36.refs_0_, bf16[48,640]{1,0:T(8,128)(2,1)S(1)} %collective-permute-done.8.refs_1_, bf16[48,640]{1,0:T(8,128)(2,1)S(1)} %collective-permute-done.9.refs_2_, ...), custom_call_target="tpu_custom_call" | custom-call | tf_op jit(solution)/shard_map/project/pallas_call | solution.py:691
  25.5 13.8 %all_to_all.10.received_ref = bf16[32,8,256]{2,1,0:T(8,128)(2,1)S(1)} all-to-all(bf16[32,8,256]{2,1,0:T(8,128)(2,1)S(1)} %get-tuple-element.43), channel_id=1, replica_groups=mesh['seq'=8,'exp'=4] {'seq','exp'}, dimensions={0} | all-to-all | bytes 262144 | tf_op jit(solution)/shard_map/all_to_all | solution.py:700
  39.3 3.0 %expert.1 = (f32[32,512]{1,0:T(8,128)S(1)}, f32[32,512]{1,0:T(8,128)S(1)}) custom-call(bf16[32,8,256]{2,1,0:T(8,128)(2,1)S(1)} %all_to_all.10.received_ref, f32[1,1024]{1,0:T(1,128)S(1)} %bitcast.7, bf16[2,800,1024]{2,1,0:T(8,128)(2,1)S(1)} %get-tuple-element.44.piece_ref, bf16[2,1,1408,1024]{3,2,1,0:T(8,128)(2,1)} %in_ref.3, bf16[1,1408,1024]{2,1,0:T(8,128)(2,1)} %down_ref.1), custom_call_target="tpu_custom_call" | custom-call | tf_op jit(solution)/shard_map/expert/pallas_call | solution.py:704
  42.3 0.1 collective-permute-start.19
  42.4 1.2 %collective-permute-done.19.other_ref = f32[32,512]{1,0:T(8,128)S(1)} collective-permute-done((f32[32,512]{1,0:T(8,128)S(1)}, f32[32,512]{1,0:T(8,128)S(1)}, u32[]{:S(2)}, u32[]{:S(2)}) %collective-permute-start.19) | collective-permute-done | bytes 65568 | tf_op jit(solution)/shard_map/ppermute | solution.py:722
  43.6 0.7 %spread.1 = bf16[32,8,512]{2,1,0:T(8,128)(2,1)} custom-call(f32[32,512]{1,0:T(8,128)S(1)} %get-tuple-element.45.kept_ref, f32[32,512]{1,0:T(8,128)S(1)} %collective-permute-done.19.other_ref), custom_call_target="tpu_custom_call" | custom-call | tf_op jit(solution)/shard_map/spread/pallas_call | solution.py:730
  44.3 2.6 %all-to-all-start.1 = ((bf16[32,8,512]{2,1,0:T(8,128)(2,1)}), bf16[32,8,512]{2,1,0:T(8,128)(2,1)S(1)}, u32[]{:S(2)}, u32[]{:S(2)}) async-start(bf16[32,8,512]{2,1,0:T(8,128)(2,1)} %spread.1), calls=%async_computation.1 | async-start | bytes 524288 | tf_op jit(solution)/shard_map/all_to_all | solution.py:736
  46.9 2.6 %collective-permute-start.17 = (f32[48,256]{1,0:T(8,128)S(1)}, f32[48,256]{1,0:T(8,128)S(1)}, u32[]{:S(2)}, u32[]{:S(2)}) collective-permute-start(f32[48,256]{1,0:T(8,128)S(1)} %get-tuple-element.47.refs_0_), channel_id=1, source_target_pairs={{0,24},{4,28},{8,16},{12,20},{16,8},{20,12},{24,0},{28,4},{1,25},{... | collective-permute-start | bytes 147464 | tf_op jit(solution)/shard_map/ppermute | solution.py:536
  49.6 0.5 collective-permute-start.15
  50.1 0.4 collective-permute-start.13
  50.5 0.0 collective-permute-start.12
  50.5 2.8 %collective-permute-done.17.refs_6_ = f32[48,256]{1,0:T(8,128)S(1)} collective-permute-done((f32[48,256]{1,0:T(8,128)S(1)}, f32[48,256]{1,0:T(8,128)S(1)}, u32[]{:S(2)}, u32[]{:S(2)}) %collective-permute-start.17) | collective-permute-done | bytes 49184 | tf_op jit(solution)/shard_map/ppermute | solution.py:536
  53.3 1.3 %collective-permute-done.15.refs_4_ = f32[48,256]{1,0:T(8,128)S(1)} collective-permute-done((f32[48,256]{1,0:T(8,128)S(1)}, f32[48,256]{1,0:T(8,128)S(1)}, u32[]{:S(2)}, u32[]{:S(2)}) %collective-permute-start.15) | collective-permute-done | bytes 49184 | tf_op jit(solution)/shard_map/ppermute | solution.py:536
  54.6 0.0 collective-permute-start.16
  54.6 0.5 collective-permute-start.14
  55.1 0.7 %collective-permute-done.16.refs_5_ = f32[48,256]{1,0:T(8,128)S(1)} collective-permute-done((f32[48,256]{1,0:T(8,128)S(1)}, f32[48,256]{1,0:T(8,128)S(1)}, u32[]{:S(2)}, u32[]{:S(2)}) %collective-permute-start.16) | collective-permute-done | bytes 49184 | tf_op jit(solution)/shard_map/ppermute | solution.py:536
  55.8 0.2 collective-permute-done.14.refs_3_
  56.0 0.4 home.1
  56.3 0.8 %all-to-all-done.1 = bf16[32,8,512]{2,1,0:T(8,128)(2,1)S(1)} async-done(((bf16[32,8,512]{2,1,0:T(8,128)(2,1)}), bf16[32,8,512]{2,1,0:T(8,128)(2,1)S(1)}, u32[]{:S(2)}, u32[]{:S(2)}) %all-to-all-start.1) | async-done | bytes 262176 | tf_op jit(solution)/shard_map/all_to_all | solution.py:736
  57.1 0.8 %final.1 = bf16[12,4,1024]{2,1,0:T(4,128)(2,1)} custom-call(f32[48,128]{1,0:T(8,128)S(1)} %get-tuple-element.57.gates_ref, bf16[8,4,8,512]{3,2,1,0:T(8,128)(2,1)S(1)} %bitcast.5, f32[48,1024]{1,0:T(8,128)S(1)} %get-tuple-element.58.residual_ref), custom_call_target="tpu_custom_call" | custom-call | tf_op jit(solution)/shard_map/final/pallas_call | solution.py:753
  (16 shorter events, 0.0 us)
Async XLA Ops:
  0.0 11.4 %copy-start = (bf16[2,12,512,1024]{3,2,1,0:T(8,128)(2,1)S(1)}, bf16[2,12,512,1024]{3,2,1,0:T(8,128)(2,1)}, u32[]{:S(2)}) copy-start(bf16[2,12,512,1024]{3,2,1,0:T(8,128)(2,1)} %refs_2_.1) | copy-start | bytes 75497472
  1.7 5.9 %collective-permute-start.5 = (bf16[48,384]{1,0:T(8,128)(2,1)S(1)}, bf16[48,384]{1,0:T(8,128)(2,1)S(1)}, u32[]{:S(2)}, u32[]{:S(2)}) collective-permute-start(bf16[48,384]{1,0:T(8,128)(2,1)S(1)} %get-tuple-element.32.refs_0_), channel_id=1, source_target_pairs={{0,24},{4,28},{8,16},{12,20},{16,8},{20,12},{24,0},{28,4},{1,25},{... | collective-permute-start | bytes 110600 | tf_op jit(solution)/shard_map/ppermute | solution.py:536
  5.7 4.0 %collective-permute-start.3 = (bf16[48,384]{1,0:T(8,128)(2,1)S(1)}, bf16[48,384]{1,0:T(8,128)(2,1)S(1)}, u32[]{:S(2)}, u32[]{:S(2)}) collective-permute-start(bf16[48,384]{1,0:T(8,128)(2,1)S(1)} %get-tuple-element.32.refs_0_), channel_id=1, source_target_pairs={{0,16},{4,20},{8,24},{12,28},{16,0},{20,4},{24,8},{28,12},{1,17},{... | collective-permute-start | bytes 110600 | tf_op jit(solution)/shard_map/ppermute | solution.py:536
  6.2 4.0 %collective-permute-start.1 = (bf16[48,384]{1,0:T(8,128)(2,1)S(1)}, bf16[48,384]{1,0:T(8,128)(2,1)S(1)}, u32[]{:S(2)}, u32[]{:S(2)}) collective-permute-start(bf16[48,384]{1,0:T(8,128)(2,1)S(1)} %get-tuple-element.32.refs_0_), channel_id=1, source_target_pairs={{0,8},{4,12},{8,0},{12,4},{16,24},{20,28},{24,16},{28,20},{1,9},{5... | collective-permute-start | bytes 110600 | tf_op jit(solution)/shard_map/ppermute | solution.py:536
  6.3 3.8 %collective-permute-start = (bf16[48,384]{1,0:T(8,128)(2,1)S(1)}, bf16[48,384]{1,0:T(8,128)(2,1)S(1)}, u32[]{:S(2)}, u32[]{:S(2)}) collective-permute-start(bf16[48,384]{1,0:T(8,128)(2,1)S(1)} %get-tuple-element.32.refs_0_), channel_id=1, source_target_pairs={{0,4},{4,0},{8,12},{12,8},{16,20},{20,16},{24,28},{28,24},{1,5},{5... | collective-permute-start | bytes 110600 | tf_op jit(solution)/shard_map/ppermute | solution.py:536
  7.6 2.5 %collective-permute-start.6 = (bf16[48,384]{1,0:T(8,128)(2,1)S(1)}, bf16[48,384]{1,0:T(8,128)(2,1)S(1)}, u32[]{:S(2)}, u32[]{:S(2)}) collective-permute-start(bf16[48,384]{1,0:T(8,128)(2,1)S(1)} %collective-permute-done.5.refs_6_), channel_id=1, source_target_pairs={{0,4},{4,0},{8,12},{12,8},{16,20},{20,16},{24,28},{28,24},{1,5},{5... | collective-permute-start | bytes 110600 | tf_op jit(solution)/shard_map/ppermute | solution.py:536
  9.7 1.2 %collective-permute-start.4 = (bf16[48,384]{1,0:T(8,128)(2,1)S(1)}, bf16[48,384]{1,0:T(8,128)(2,1)S(1)}, u32[]{:S(2)}, u32[]{:S(2)}) collective-permute-start(bf16[48,384]{1,0:T(8,128)(2,1)S(1)} %collective-permute-done.3.refs_4_), channel_id=1, source_target_pairs={{0,4},{4,0},{8,12},{12,8},{16,20},{20,16},{24,28},{28,24},{1,5},{5... | collective-permute-start | bytes 110600 | tf_op jit(solution)/shard_map/ppermute | solution.py:536
  10.2 1.2 %collective-permute-start.2 = (bf16[48,384]{1,0:T(8,128)(2,1)S(1)}, bf16[48,384]{1,0:T(8,128)(2,1)S(1)}, u32[]{:S(2)}, u32[]{:S(2)}) collective-permute-start(bf16[48,384]{1,0:T(8,128)(2,1)S(1)} %collective-permute-done.1.refs_2_), channel_id=1, source_target_pairs={{0,4},{4,0},{8,12},{12,8},{16,20},{20,16},{24,28},{28,24},{1,5},{5... | collective-permute-start | bytes 110600 | tf_op jit(solution)/shard_map/ppermute | solution.py:536
  14.3 3.1 %collective-permute-start.7 = (bf16[48,640]{1,0:T(8,128)(2,1)S(1)}, bf16[48,640]{1,0:T(8,128)(2,1)S(1)}, u32[]{:S(2)}, u32[]{:S(2)}) collective-permute-start(bf16[48,640]{1,0:T(8,128)(2,1)S(1)} %get-tuple-element.35), channel_id=1, source_target_pairs={{0,4},{4,0},{8,12},{12,8},{16,20},{20,16},{24,28},{28,24},{1,5},{5... | collective-permute-start | bytes 184328 | tf_op jit(solution)/shard_map/ppermute | solution.py:536
  14.5 3.2 %copy-start.1 = (bf16[128,1024]{1,0:T(8,128)(2,1)S(1)}, bf16[128,1024]{1,0:T(8,128)(2,1)}, u32[]{:S(2)}) copy-start(bf16[128,1024]{1,0:T(8,128)(2,1)} %refs_6_.1) | copy-start | bytes 786436
  14.5 7.1 %copy-start.2 = (bf16[2,12,4,1024]{3,2,1,0:T(4,128)(2,1)S(1)}, bf16[2,12,4,1024]{3,2,1,0:T(4,128)(2,1)}, u32[]{:S(2)}) copy-start(bf16[2,12,4,1024]{3,2,1,0:T(4,128)(2,1)} %refs_8_.1) | copy-start | bytes 589828
  17.3 21.9 %copy-start.4 = (f32[1024]{0:T(1024)S(1)}, f32[1024]{0:T(1024)}, u32[]{:S(2)}) copy-start(f32[1024]{0:T(1024)} %param.20) | copy-start | bytes 12292
  17.7 6.9 %collective-permute-start.11 = (bf16[128,1024]{1,0:T(8,128)(2,1)S(1)}, bf16[128,1024]{1,0:T(8,128)(2,1)S(1)}, u32[]{:S(2)}, u32[]{:S(2)}) collective-permute-start(bf16[128,1024]{1,0:T(8,128)(2,1)S(1)} %copy-done.1), channel_id=1, source_target_pairs={{0,4},{4,0},{8,12},{12,8},{16,20},{20,16},{24,28},{28,24},{1,5},{5... | collective-permute-start | bytes 786440 | tf_op jit(solution)/shard_map/ppermute | solution.py:536
  18.1 6.5 %collective-permute-start.10 = (bf16[48,640]{1,0:T(8,128)(2,1)S(1)}, bf16[48,640]{1,0:T(8,128)(2,1)S(1)}, u32[]{:S(2)}, u32[]{:S(2)}) collective-permute-start(bf16[48,640]{1,0:T(8,128)(2,1)S(1)} %pair.1.sent_ref), channel_id=1, source_target_pairs={{0,24},{4,28},{8,16},{12,20},{16,8},{20,12},{24,0},{28,4},{1,25},{... | collective-permute-start | bytes 184328 | tf_op jit(solution)/shard_map/ppermute | solution.py:536
  19.6 5.0 %collective-permute-start.9 = (bf16[48,640]{1,0:T(8,128)(2,1)S(1)}, bf16[48,640]{1,0:T(8,128)(2,1)S(1)}, u32[]{:S(2)}, u32[]{:S(2)}) collective-permute-start(bf16[48,640]{1,0:T(8,128)(2,1)S(1)} %pair.1.sent_ref), channel_id=1, source_target_pairs={{0,16},{4,20},{8,24},{12,28},{16,0},{20,4},{24,8},{28,12},{1,17},{... | collective-permute-start | bytes 184328 | tf_op jit(solution)/shard_map/ppermute | solution.py:536
  19.7 4.8 %collective-permute-start.8 = (bf16[48,640]{1,0:T(8,128)(2,1)S(1)}, bf16[48,640]{1,0:T(8,128)(2,1)S(1)}, u32[]{:S(2)}, u32[]{:S(2)}) collective-permute-start(bf16[48,640]{1,0:T(8,128)(2,1)S(1)} %pair.1.sent_ref), channel_id=1, source_target_pairs={{0,8},{4,12},{8,0},{12,4},{16,24},{20,28},{24,16},{28,20},{1,9},{5... | collective-permute-start | bytes 184328 | tf_op jit(solution)/shard_map/ppermute | solution.py:536
  39.3 16.7 %copy-start.3 = (bf16[1024,16]{0,1:T(8,128)(2,1)S(1)}, bf16[1024,16]{0,1:T(8,128)(2,1)}, u32[]{:S(2)}) copy-start(bf16[1024,16]{0,1:T(8,128)(2,1)} %param.21) | copy-start | bytes 98308
  42.3 1.3 %collective-permute-start.19 = (f32[32,512]{1,0:T(8,128)S(1)}, f32[32,512]{1,0:T(8,128)S(1)}, u32[]{:S(2)}, u32[]{:S(2)}) collective-permute-start(f32[32,512]{1,0:T(8,128)S(1)} %get-tuple-element.46), channel_id=1, source_target_pairs={{0,4},{4,0},{8,12},{12,8},{16,20},{20,16},{24,28},{28,24},{1,5},{5... | collective-permute-start | bytes 196616 | tf_op jit(solution)/shard_map/ppermute | solution.py:722
  44.3 12.8 %all-to-all-start.1 = ((bf16[32,8,512]{2,1,0:T(8,128)(2,1)}), bf16[32,8,512]{2,1,0:T(8,128)(2,1)S(1)}, u32[]{:S(2)}, u32[]{:S(2)}) async-start(bf16[32,8,512]{2,1,0:T(8,128)(2,1)} %spread.1), calls=%async_computation.1 | async-start | bytes 524288 | tf_op jit(solution)/shard_map/all_to_all | solution.py:736
  46.9 6.4 %collective-permute-start.17 = (f32[48,256]{1,0:T(8,128)S(1)}, f32[48,256]{1,0:T(8,128)S(1)}, u32[]{:S(2)}, u32[]{:S(2)}) collective-permute-start(f32[48,256]{1,0:T(8,128)S(1)} %get-tuple-element.47.refs_0_), channel_id=1, source_target_pairs={{0,24},{4,28},{8,16},{12,20},{16,8},{20,12},{24,0},{28,4},{1,25},{... | collective-permute-start | bytes 147464 | tf_op jit(solution)/shard_map/ppermute | solution.py:536
  49.6 5.0 %collective-permute-start.15 = (f32[48,256]{1,0:T(8,128)S(1)}, f32[48,256]{1,0:T(8,128)S(1)}, u32[]{:S(2)}, u32[]{:S(2)}) collective-permute-start(f32[48,256]{1,0:T(8,128)S(1)} %get-tuple-element.47.refs_0_), channel_id=1, source_target_pairs={{0,16},{4,20},{8,24},{12,28},{16,0},{20,4},{24,8},{28,12},{1,17},{... | collective-permute-start | bytes 147464 | tf_op jit(solution)/shard_map/ppermute | solution.py:536
  50.1 4.5 %collective-permute-start.13 = (f32[48,256]{1,0:T(8,128)S(1)}, f32[48,256]{1,0:T(8,128)S(1)}, u32[]{:S(2)}, u32[]{:S(2)}) collective-permute-start(f32[48,256]{1,0:T(8,128)S(1)} %get-tuple-element.47.refs_0_), channel_id=1, source_target_pairs={{0,8},{4,12},{8,0},{12,4},{16,24},{20,28},{24,16},{28,20},{1,9},{5... | collective-permute-start | bytes 147464 | tf_op jit(solution)/shard_map/ppermute | solution.py:536
  50.5 4.6 %collective-permute-start.12 = (f32[48,256]{1,0:T(8,128)S(1)}, f32[48,256]{1,0:T(8,128)S(1)}, u32[]{:S(2)}, u32[]{:S(2)}) collective-permute-start(f32[48,256]{1,0:T(8,128)S(1)} %get-tuple-element.47.refs_0_), channel_id=1, source_target_pairs={{0,4},{4,0},{8,12},{12,8},{16,20},{20,16},{24,28},{28,24},{1,5},{5... | collective-permute-start | bytes 147464 | tf_op jit(solution)/shard_map/ppermute | solution.py:536
  53.3 1.8 %collective-permute-start.18 = (f32[48,256]{1,0:T(8,128)S(1)}, f32[48,256]{1,0:T(8,128)S(1)}, u32[]{:S(2)}, u32[]{:S(2)}) collective-permute-start(f32[48,256]{1,0:T(8,128)S(1)} %collective-permute-done.17.refs_6_), channel_id=1, source_target_pairs={{0,4},{4,0},{8,12},{12,8},{16,20},{20,16},{24,28},{28,24},{1,5},{5... | collective-permute-start | bytes 147464 | tf_op jit(solution)/shard_map/ppermute | solution.py:536
  54.6 1.2 %collective-permute-start.16 = (f32[48,256]{1,0:T(8,128)S(1)}, f32[48,256]{1,0:T(8,128)S(1)}, u32[]{:S(2)}, u32[]{:S(2)}) collective-permute-start(f32[48,256]{1,0:T(8,128)S(1)} %collective-permute-done.15.refs_4_), channel_id=1, source_target_pairs={{0,4},{4,0},{8,12},{12,8},{16,20},{20,16},{24,28},{28,24},{1,5},{5... | collective-permute-start | bytes 147464 | tf_op jit(solution)/shard_map/ppermute | solution.py:536
  54.6 1.4 %collective-permute-start.14 = (f32[48,256]{1,0:T(8,128)S(1)}, f32[48,256]{1,0:T(8,128)S(1)}, u32[]{:S(2)}, u32[]{:S(2)}) collective-permute-start(f32[48,256]{1,0:T(8,128)S(1)} %collective-permute-done.13.refs_2_), channel_id=1, source_target_pairs={{0,4},{4,0},{8,12},{12,8},{16,20},{20,16},{24,28},{28,24},{1,5},{5... | collective-permute-start | bytes 147464 | tf_op jit(solution)/shard_map/ppermute | solution.py:536
